TPU v7x, 32 devices: a whole 2x2x4 slice. The times are simulated.
32 devices in a mesh: dp: 8 (over z, y), expert: 4 (over x, core).
Axes of the slice: x: 2, y: 2, z: 4, core: 2. Of those that a mesh axis runs over, the one named last changes fastest.
Arguments:
- tokens: bfloat16 [12288, 1536], P(('dp', 'expert')), may hold values from -6 to 6
- cotangent: bfloat16 [12288, 1536], P(('dp', 'expert')), may hold values from -6 to 6
- lengths: int32 [32], P(('dp', 'expert')), may hold values from 96 to 384, as said below
- routes: int32 [12288, 8], P(('dp', 'expert')), may hold values from 0 to 39, as said below
- slots: int32 [12288, 8], P(('dp', 'expert')), may hold values from 0 to 151, as said below
- first_gain: bfloat16 [1536], P(('dp', 'expert')), may hold values from 0.5 to 1.5
- qkv_weight: bfloat16 [1536, 2560], P(('dp', 'expert')), may hold values from -0.4375 to 0.4375
- out_weight: bfloat16 [1536, 1536], P(None, ('dp', 'expert')), may hold values from -2.5 to 2.5
- second_gain: bfloat16 [1536], P(('dp', 'expert')), may hold values from 0.5 to 1.5
- router_weight: bfloat16 [1536, 40], P(('dp', 'expert')), may hold values from -0.078125 to 0.078125
- gate_up_weight: bfloat16 [40, 1536, 1024], P('expert', 'dp'), may hold values from -0.15625 to 0.15625
- down_weight: bfloat16 [40, 512, 1536], P('expert', None, 'dp'), may hold values from -4 to 4
Outputs:
- output: bfloat16 [12288, 1536], P(('dp', 'expert'))
- input_grad: float32 [12288, 1536], P(('dp', 'expert'))
- first_gain_grad: float32 [1536], P(('dp', 'expert'))
- qkv_grad: float32 [1536, 2560], P(('dp', 'expert'))
- out_grad: float32 [1536, 1536], P(None, ('dp', 'expert'))
- second_gain_grad: float32 [1536], P(('dp', 'expert'))
- router_grad: float32 [1536, 40], P(('dp', 'expert'))
- gate_up_grad: float32 [40, 1536, 1024], P('expert', 'dp')
- down_grad: float32 [40, 512, 1536], P('expert', None, 'dp')
Inputs may be any that keep to these rules, and one draw needn't show every extreme that they name: `lengths`: in every draw one sequence has exactly 384 valid tokens. `routes`: A token's 8 experts are distinct. Among the rows of one device no expert is named more than 152 times; in every draw, for each index of dp, some expert is named exactly 152 times by every one of the 4 devices of that index. `slots`: for one device and one expert, the places of the rows naming it are distinct and run from 0 to that expert's count of rows less one.
All inputs are finite; a program needn't handle non-finite values.
Results may differ from a plain program's by a relative error of at most 0.017.
Values may be sent and summed in bfloat16 or wider, within the bound.
No kernel may reach another device: no remote copies, remote signals or barrier semaphores. Data moves between devices by JAX's collectives and lax.ppermute only.
A program may use at most 320 MiB of HBM per device.

v0:
```python
import jax
import jax.numpy as jnp
from jax import lax
from jax.sharding import PartitionSpec as P

QUERY_HEADS = 24
KEY_VALUE_HEADS = 8
HEAD_SIZE = 64
FF = 512
EXPERTS = 40
TOP = 8
CAP = 152


epsilon = 1e-06
residual_scale = 0.22
score_scale = 0.015625
rope_base = 10000.0
masked_score = -1e30


def rope_tables(length):
    half = HEAD_SIZE // 2
    freqs = jnp.power(rope_base, -2.0 * jnp.arange(half, dtype=jnp.float32) / HEAD_SIZE)
    angles = jnp.arange(length, dtype=jnp.float32)[:, None] * freqs[None, :]
    cosine_table = jnp.concatenate([jnp.cos(angles), jnp.cos(angles)], axis=-1)
    sine_table = jnp.concatenate([jnp.sin(angles), jnp.sin(angles)], axis=-1)
    return (cosine_table, sine_table)


def rotate_half(value_rows):
    half = value_rows.shape[-1] // 2
    return jnp.concatenate([-value_rows[..., half:], value_rows[..., :half]], axis=-1)


def rotate_pairs(value_rows, cosine_table, sine_table):
    return value_rows * cosine_table[:, None, :] + rotate_half(value_rows) * sine_table[:, None, :]


def unrotate(grads, cosine_table, sine_table):
    return grads * cosine_table[:, None, :] - rotate_half(grads * sine_table[:, None, :])


def rms_inverse(value_rows):
    return lax.rsqrt(jnp.mean(value_rows * value_rows, axis=-1, keepdims=True) + epsilon)


def norm_backward(grad_normed, normal, inverse, gain):
    gain_term = jnp.sum(grad_normed * normal, axis=0)
    scaled = grad_normed * gain
    grad_input = inverse * (scaled - normal * jnp.mean(scaled * normal, axis=-1, keepdims=True))
    return (gain_term, grad_input)


def contract_rows(left, right):
    return lax.dot_general(
        left, right, (((0,), (0,)), ((), ())), preferred_element_type=jnp.float32
    )


def multiply_transposed(left, right):
    return lax.dot_general(
        left, right, (((1,), (1,)), ((), ())), preferred_element_type=jnp.float32
    )


def fetch_expert(gate_up_shard, down_shard):
    return (
        lax.all_gather(gate_up_shard, "dp", axis=0, tiled=True),
        lax.all_gather(down_shard, "dp", axis=1, tiled=True),
    )


def gate_values(hidden_rows, router_full, route_rows):
    logits = jnp.dot(hidden_rows, router_full, preferred_element_type=jnp.float32)
    chosen_mask = route_rows[:, :, None] == jnp.arange(EXPERTS)[None, None, :]
    chosen = jnp.sum(jnp.where(chosen_mask, logits[:, None, :], 0.0), axis=-1)
    return (chosen_mask, jax.nn.softmax(chosen, axis=-1))


def body(
    tokens,
    cotangent,
    lengths,
    routes,
    slots,
    first_gain,
    qkv_weight,
    out_weight,
    second_gain,
    router_weight,
    gate_up_weight,
    down_weight,
):
    sequence_length = tokens.shape[0]
    width = tokens.shape[1]
    query_group = QUERY_HEADS // KEY_VALUE_HEADS
    length = lengths[0]
    gathered = (
        lax.all_gather(first_gain, ("dp", "expert"), axis=0, tiled=True),
        lax.all_gather(qkv_weight, ("dp", "expert"), axis=0, tiled=True),
        lax.all_gather(out_weight, ("dp", "expert"), axis=1, tiled=True),
        lax.all_gather(second_gain, ("dp", "expert"), axis=0, tiled=True),
        lax.all_gather(router_weight, ("dp", "expert"), axis=0, tiled=True),
    )
    gain_one, qkv_full, out_full, gain_two, router_full = gathered
    inputs = tokens.astype(jnp.float32)
    inverse_one = rms_inverse(inputs)
    normal_one = inputs * inverse_one
    hidden_one = (normal_one * gain_one.astype(jnp.float32)).astype(jnp.bfloat16)
    projected_rows = jnp.dot(hidden_one, qkv_full, preferred_element_type=jnp.float32)
    cosine_table, sine_table = rope_tables(sequence_length)
    query_width_total = QUERY_HEADS * HEAD_SIZE
    key_width_total = KEY_VALUE_HEADS * HEAD_SIZE
    query_rows = rotate_pairs(
        projected_rows[:, :query_width_total].reshape(sequence_length, QUERY_HEADS, HEAD_SIZE),
        cosine_table,
        sine_table,
    ).astype(jnp.bfloat16)
    keys = rotate_pairs(
        projected_rows[:, query_width_total : query_width_total + key_width_total].reshape(
            sequence_length, KEY_VALUE_HEADS, HEAD_SIZE
        ),
        cosine_table,
        sine_table,
    ).astype(jnp.bfloat16)
    value_rows = (
        projected_rows[:, query_width_total + key_width_total :]
        .reshape(sequence_length, KEY_VALUE_HEADS, HEAD_SIZE)
        .astype(jnp.bfloat16)
    )
    row_index = jnp.arange(sequence_length)[:, None]
    column_index = jnp.arange(sequence_length)[None, :]
    allowed = (column_index <= row_index) & (column_index < length)

    def head_scores(head):
        head_query = lax.dynamic_slice_in_dim(query_rows, head * query_group, query_group, 1)
        head_key = lax.dynamic_index_in_dim(keys, head, 1, keepdims=False)
        head_value = lax.dynamic_index_in_dim(value_rows, head, 1, keepdims=False)
        scores = (
            jnp.einsum("qgd,kd->gqk", head_query, head_key, preferred_element_type=jnp.float32)
            * score_scale
        )
        return (head_query, head_key, head_value, jnp.where(allowed[None], scores, masked_score))

    def attention_head_forward(head):
        head_query, head_key, head_value, scores = head_scores(head)
        peak = jnp.max(scores, axis=-1, keepdims=True)
        exponent = jnp.exp(scores - peak)
        total = jnp.sum(exponent, axis=-1, keepdims=True)
        weights = (exponent / total).astype(jnp.bfloat16)
        head_mixed = jnp.einsum(
            "gqk,kd->qgd", weights, head_value, preferred_element_type=jnp.float32
        ).astype(jnp.bfloat16)
        return (head_mixed, (peak + jnp.log(total))[..., 0])

    mixed_head_output, log_sum_totals = lax.map(attention_head_forward, jnp.arange(KEY_VALUE_HEADS))
    mixed = mixed_head_output.transpose(1, 0, 2, 3).reshape(
        sequence_length, QUERY_HEADS * HEAD_SIZE
    )
    branch = jnp.dot(mixed, out_full, preferred_element_type=jnp.float32)
    middle = inputs + residual_scale * branch
    inverse_two = rms_inverse(middle)
    normal_two = middle * inverse_two
    hidden_two = (normal_two * gain_two.astype(jnp.float32)).astype(jnp.bfloat16)
    chosen_mask, gates = gate_values(hidden_two, router_full, routes)
    grad_out = cotangent.astype(jnp.float32)
    grad_mixture = residual_scale * grad_out

    def expert_forward(carry, pieces):
        rows, gate_up_shard, down_shard = pieces
        gate_up_full, down_full = fetch_expert(gate_up_shard, down_shard)
        gate_up = jnp.dot(rows, gate_up_full, preferred_element_type=jnp.float32)
        hidden = (jax.nn.silu(gate_up[:, :FF]) * gate_up[:, FF:]).astype(jnp.bfloat16)
        return (
            carry,
            jnp.dot(hidden, down_full, preferred_element_type=jnp.float32).astype(jnp.bfloat16),
        )

    copies = jnp.broadcast_to(hidden_two[:, None, :], (sequence_length, TOP, width))
    outgoing = jnp.zeros((EXPERTS, CAP, width), jnp.bfloat16).at[routes, slots].set(copies)
    received = lax.all_to_all(outgoing, "expert", split_axis=0, concat_axis=1, tiled=True)
    _, produced = lax.scan(expert_forward, None, (received, gate_up_weight, down_weight))
    returned = lax.all_to_all(produced, "expert", split_axis=1, concat_axis=0, tiled=True)
    expert_rows = returned[routes, slots].astype(jnp.float32)
    mixture = jnp.sum(gates[:, :, None] * expert_rows, axis=1)
    grad_gates = jnp.sum(expert_rows * grad_mixture[:, None, :], axis=-1)
    grad_rows = (gates[:, :, None] * grad_mixture[:, None, :]).astype(jnp.bfloat16)
    outgoing_grad = jnp.zeros((EXPERTS, CAP, width), jnp.bfloat16).at[routes, slots].set(grad_rows)
    grad_received = lax.all_to_all(outgoing_grad, "expert", split_axis=0, concat_axis=1, tiled=True)
    output = (middle + residual_scale * mixture).astype(jnp.bfloat16)
    again = (
        lax.all_gather(first_gain, ("dp", "expert"), axis=0, tiled=True),
        lax.all_gather(qkv_weight, ("dp", "expert"), axis=0, tiled=True),
        lax.all_gather(out_weight, ("dp", "expert"), axis=1, tiled=True),
        lax.all_gather(second_gain, ("dp", "expert"), axis=0, tiled=True),
        lax.all_gather(router_weight, ("dp", "expert"), axis=0, tiled=True),
    )
    gain_back, qkv_back, output_gradient, gain_two_back, router_back = again
    grad_chosen = gates * (grad_gates - jnp.sum(gates * grad_gates, axis=-1, keepdims=True))
    grad_logits = jnp.sum(jnp.where(chosen_mask, grad_chosen[:, :, None], 0.0), axis=1).astype(
        jnp.bfloat16
    )

    def expert_backward(carry, pieces):
        rows, grad_produced, gate_up_shard, down_shard = pieces
        gate_up_full, down_full = fetch_expert(gate_up_shard, down_shard)
        gate_up = jnp.dot(rows, gate_up_full, preferred_element_type=jnp.float32)
        gate = gate_up[:, :FF]
        upper = gate_up[:, FF:]
        sigmoid = jax.nn.sigmoid(gate)
        swish = gate * sigmoid
        hidden = (swish * upper).astype(jnp.bfloat16)
        grad_hidden = multiply_transposed(grad_produced, down_full)
        grad_gate_up = jnp.concatenate(
            [grad_hidden * upper * sigmoid * (1.0 + gate * (1.0 - sigmoid)), grad_hidden * swish],
            axis=-1,
        ).astype(jnp.bfloat16)
        grad_copy = multiply_transposed(grad_gate_up, gate_up_full).astype(jnp.bfloat16)
        gate_up_part = lax.psum_scatter(
            contract_rows(rows, grad_gate_up).astype(jnp.bfloat16),
            "dp",
            scatter_dimension=0,
            tiled=True,
        ).astype(jnp.float32)
        down_part = lax.psum_scatter(
            contract_rows(grad_produced, hidden).astype(jnp.bfloat16),
            "dp",
            scatter_dimension=0,
            tiled=True,
        ).astype(jnp.float32)
        return (carry, (grad_copy, gate_up_part, down_part.T))

    _, (grad_copies, gate_up_grads, down_grads) = lax.scan(
        expert_backward, None, (received, grad_received, gate_up_weight, down_weight)
    )
    grad_back = lax.all_to_all(grad_copies, "expert", split_axis=1, concat_axis=0, tiled=True)
    copy_sum = jnp.sum(grad_back[routes, slots].astype(jnp.float32), axis=1)
    grad_hidden_two = copy_sum + multiply_transposed(grad_logits, router_back)
    router_term = contract_rows(hidden_two, grad_logits)
    second_term, grad_norm_two = norm_backward(
        grad_hidden_two, normal_two, inverse_two, gain_two_back.astype(jnp.float32)
    )
    grad_middle = grad_out + grad_norm_two
    branch_gradient = (residual_scale * grad_middle).astype(jnp.bfloat16)
    out_term = contract_rows(mixed, branch_gradient)
    grad_mixed = (
        multiply_transposed(branch_gradient, output_gradient)
        .astype(jnp.bfloat16)
        .reshape(sequence_length, KEY_VALUE_HEADS, query_group, HEAD_SIZE)
    )

    def attention_head_backward(head):
        head_query, head_key, head_value, scores = head_scores(head)
        head_grad = lax.dynamic_index_in_dim(grad_mixed, head, 1, keepdims=False)
        head_total = lax.dynamic_index_in_dim(log_sum_totals, head, 0, keepdims=False)
        probs = jnp.exp(scores - head_total[..., None])
        grad_weights = jnp.einsum(
            "qgd,kd->gqk", head_grad, head_value, preferred_element_type=jnp.float32
        )
        grad_scores = (
            probs * (grad_weights - jnp.sum(probs * grad_weights, axis=-1, keepdims=True))
        ).astype(jnp.bfloat16)
        grad_query = (
            jnp.einsum("gqk,kd->qgd", grad_scores, head_key, preferred_element_type=jnp.float32)
            * score_scale
        )
        grad_key = (
            jnp.einsum("gqk,qgd->kd", grad_scores, head_query, preferred_element_type=jnp.float32)
            * score_scale
        )
        grad_value = jnp.einsum(
            "gqk,qgd->kd", probs.astype(jnp.bfloat16), head_grad, preferred_element_type=jnp.float32
        )
        return (grad_query, grad_key, grad_value)

    query_head_rows, key_head_rows, value_head_rows = lax.map(
        attention_head_backward, jnp.arange(KEY_VALUE_HEADS)
    )
    grad_query = unrotate(
        query_head_rows.transpose(1, 0, 2, 3).reshape(sequence_length, QUERY_HEADS, HEAD_SIZE),
        cosine_table,
        sine_table,
    )
    grad_key = unrotate(key_head_rows.transpose(1, 0, 2), cosine_table, sine_table)
    grad_value = value_head_rows.transpose(1, 0, 2)
    grad_projected = jnp.concatenate(
        [
            grad_query.reshape(sequence_length, query_width_total),
            grad_key.reshape(sequence_length, key_width_total),
            grad_value.reshape(sequence_length, key_width_total),
        ],
        axis=-1,
    ).astype(jnp.bfloat16)
    qkv_term = contract_rows(hidden_one, grad_projected)
    grad_hidden_one = multiply_transposed(grad_projected, qkv_back)
    first_term, grad_norm_one = norm_backward(
        grad_hidden_one, normal_one, inverse_one, gain_back.astype(jnp.float32)
    )
    grad_input = grad_middle + grad_norm_one
    summed = (
        lax.psum_scatter(first_term, ("dp", "expert"), scatter_dimension=0, tiled=True),
        lax.psum_scatter(qkv_term, ("dp", "expert"), scatter_dimension=0, tiled=True),
        lax.psum_scatter(out_term, ("dp", "expert"), scatter_dimension=1, tiled=True),
        lax.psum_scatter(second_term, ("dp", "expert"), scatter_dimension=0, tiled=True),
        lax.psum_scatter(router_term, ("dp", "expert"), scatter_dimension=0, tiled=True),
    )
    return (
        output,
        grad_input,
        summed[0],
        summed[1],
        summed[2],
        summed[3],
        summed[4],
        gate_up_grads,
        down_grads,
    )


def solution(mesh):
    in_specs = (
        P(("dp", "expert"), None),
        P(("dp", "expert"), None),
        P(("dp", "expert")),
        P(("dp", "expert"), None),
        P(("dp", "expert"), None),
        P(("dp", "expert")),
        P(("dp", "expert"), None),
        P(None, ("dp", "expert")),
        P(("dp", "expert")),
        P(("dp", "expert"), None),
        P("expert", "dp", None),
        P("expert", None, "dp"),
    )
    out_specs = (
        P(("dp", "expert"), None),
        P(("dp", "expert"), None),
        P(("dp", "expert")),
        P(("dp", "expert"), None),
        P(None, ("dp", "expert")),
        P(("dp", "expert")),
        P(("dp", "expert"), None),
        P("expert", "dp", None),
        P("expert", None, "dp"),
    )
    return jax.shard_map(body, mesh=mesh, in_specs=in_specs, out_specs=out_specs, check_vma=False)
```

profile of v0, /device:TPU:0, one launch (start us, length us, event | category | flops | bytes accessed | tf_op | source)
XLA Modules:
  0.0 5170.3 jit_solution(13333880766658947321)
XLA Ops:
  111.5 59.9 %while.54 = (s32[]{:T(128)}, bf16[8,384,3,64]{1,3,2,0:T(8,128)(2,1)}, f32[8,3,384]{2,1,0:T(4,128)}, s32[8]{0:T(128)S(1)}, bf16[384,8,64]{0,2,1:T(8,128)(2,1)}, /...) while((s32[]{:T(128)}, ...), condition=%wide.region_4.5_spmd.clone, body=%wide.region_1.4_spmd.clone.sunk | while | flops 117152648 | bytes 6036581 | solution.py:157
  211.2 235.5 %all-gather.4 = bf16[32,48,40]{1,2,0:T(8,128)(2,1)S(1)} all-gather(bf16[1,48,40]{1,2,0:T(8,128)(2,1)S(1)} %bitcast.308), channel_id=1, replica_groups=mesh['dp'=8,'expert'=4] {'dp','expert'}, dimensions={0}, use_global_device_ids=true | all-gather | bytes 126720 | tf_op jit(solution)/shard_map/all_gather | solution.py:104
  505.0 1118.7 %while.52 = (s32[]{:T(128)}, bf16[10,608,1536]{2,1,0:T(8,128)(2,1)}, bf16[10,608,1536]{2,1,0:T(8,128)(2,1)}, bf16[10,192,1024]{2,1,0:T(8,128)(2,1)}, bf16[10,512,192]{1,2,0:T(8,128)(2,1)}, /*index=5*/s32[]{:T(128)}) while((s32[]{:T(128)}, bf16[10,608,1536]{2,1,0:T(8,128)(2,1)}, bf16[10,608,1536]{2,1,0:T(8,128)(2,1)}, ...), condition=%wide.region_11.12_spmd, body=%wide.region_10.11_spmd.sunk | while | flops 2871705600 | bytes 30539948 | solution.py:183
  730.9 59.6 %all-gather.26.cloned.1.call-done = bf16[1,1536,1024]{2,1,0:T(8,128)(2,1)} async-done(((bf16[1,192,1024]{2,1,0:T(8,128)(2,1)}), bf16[1,1536,1024]{2,1,0:T(8,128)(2,1)}) %all-gather.26.cloned.1.call-update) | async-done | bytes 3145744 | tf_op jit(solution)/shard_map/while/body/eval_jaxpr/all_gather | solution.py:69
  843.1 59.6 %all-gather.26.cloned.1.call-done = bf16[1,1536,1024]{2,1,0:T(8,128)(2,1)} async-done(((bf16[1,192,1024]{2,1,0:T(8,128)(2,1)}), bf16[1,1536,1024]{2,1,0:T(8,128)(2,1)}) %all-gather.26.cloned.1.call-update) | async-done | bytes 3145744 | tf_op jit(solution)/shard_map/while/body/eval_jaxpr/all_gather | solution.py:69
  955.1 59.6 %all-gather.26.cloned.1.call-done = bf16[1,1536,1024]{2,1,0:T(8,128)(2,1)} async-done(((bf16[1,192,1024]{2,1,0:T(8,128)(2,1)}), bf16[1,1536,1024]{2,1,0:T(8,128)(2,1)}) %all-gather.26.cloned.1.call-update) | async-done | bytes 3145744 | tf_op jit(solution)/shard_map/while/body/eval_jaxpr/all_gather | solution.py:69
  1067.3 59.6 %all-gather.26.cloned.1.call-done = bf16[1,1536,1024]{2,1,0:T(8,128)(2,1)} async-done(((bf16[1,192,1024]{2,1,0:T(8,128)(2,1)}), bf16[1,1536,1024]{2,1,0:T(8,128)(2,1)}) %all-gather.26.cloned.1.call-update) | async-done | bytes 3145744 | tf_op jit(solution)/shard_map/while/body/eval_jaxpr/all_gather | solution.py:69
  1402.9 59.6 %all-gather.26.cloned.1.call-done = bf16[1,1536,1024]{2,1,0:T(8,128)(2,1)} async-done(((bf16[1,192,1024]{2,1,0:T(8,128)(2,1)}), bf16[1,1536,1024]{2,1,0:T(8,128)(2,1)}) %all-gather.26.cloned.1.call-update) | async-done | bytes 3145744 | tf_op jit(solution)/shard_map/while/body/eval_jaxpr/all_gather | solution.py:69
  1514.9 59.6 %all-gather.26.cloned.1.call-done = bf16[1,1536,1024]{2,1,0:T(8,128)(2,1)} async-done(((bf16[1,192,1024]{2,1,0:T(8,128)(2,1)}), bf16[1,1536,1024]{2,1,0:T(8,128)(2,1)}) %all-gather.26.cloned.1.call-update) | async-done | bytes 3145744 | tf_op jit(solution)/shard_map/while/body/eval_jaxpr/all_gather | solution.py:69
  1705.8 2545.5 %while.53 = (s32[]{:T(128)}, bf16[10,608,1536]{2,1,0:T(8,128)(2,1)}, f32[10,192,1024]{2,1,0:T(8,128)}, f32[10,512,192]{1,2,0:T(8,128)}, bf16[10,608,1536]{2,1,0:...) while((s32[]{:T(128)}, ...), condition=%wide.region_17.18_spmd, body=%wide.region_14.17_spmd.sunk | while | flops 7664893952 | bytes 85492096 | solution.py:234
  1709.3 60.1 %all-gather.28.cloned.1.call-done = bf16[1,1536,1024]{2,1,0:T(8,128)(2,1)} async-done(((bf16[1,192,1024]{2,1,0:T(8,128)(2,1)}), bf16[1,1536,1024]{2,1,0:T(8,128)(2,1)}) %all-gather.28.cloned.1.call-update) | async-done | bytes 3145744 | tf_op jit(solution)/shard_map/while/body/eval_jaxpr/all_gather | solution.py:69
  1883.4 75.1 %reduce-scatter.14.cloned.1.call-done = bf16[192,1024]{1,0:T(8,128)(2,1)} async-done(((bf16[1536,1024]{1,0:T(8,128)(2,1)}), bf16[192,1024]{1,0:T(8,128)(2,1)}) %reduce-scatter.14.cloned.1.call-update) | async-done | bytes 393232 | tf_op jit(solution)/shard_map/while/body/eval_jaxpr/reduce_scatter | solution.py:220
  1964.0 59.6 %all-gather.28.cloned.1.call-done = bf16[1,1536,1024]{2,1,0:T(8,128)(2,1)} async-done(((bf16[1,192,1024]{2,1,0:T(8,128)(2,1)}), bf16[1,1536,1024]{2,1,0:T(8,128)(2,1)}) %all-gather.28.cloned.1.call-update) | async-done | bytes 3145744 | tf_op jit(solution)/shard_map/while/body/eval_jaxpr/all_gather | solution.py:69
  2138.1 74.9 %reduce-scatter.14.cloned.1.call-done = bf16[192,1024]{1,0:T(8,128)(2,1)} async-done(((bf16[1536,1024]{1,0:T(8,128)(2,1)}), bf16[192,1024]{1,0:T(8,128)(2,1)}) %reduce-scatter.14.cloned.1.call-update) | async-done | bytes 393232 | tf_op jit(solution)/shard_map/while/body/eval_jaxpr/reduce_scatter | solution.py:220
  2218.4 59.8 %all-gather.28.cloned.1.call-done = bf16[1,1536,1024]{2,1,0:T(8,128)(2,1)} async-done(((bf16[1,192,1024]{2,1,0:T(8,128)(2,1)}), bf16[1,1536,1024]{2,1,0:T(8,128)(2,1)}) %all-gather.28.cloned.1.call-update) | async-done | bytes 3145744 | tf_op jit(solution)/shard_map/while/body/eval_jaxpr/all_gather | solution.py:69
  2392.4 75.0 %reduce-scatter.14.cloned.1.call-done = bf16[192,1024]{1,0:T(8,128)(2,1)} async-done(((bf16[1536,1024]{1,0:T(8,128)(2,1)}), bf16[192,1024]{1,0:T(8,128)(2,1)}) %reduce-scatter.14.cloned.1.call-update) | async-done | bytes 393232 | tf_op jit(solution)/shard_map/while/body/eval_jaxpr/reduce_scatter | solution.py:220
  2472.9 59.8 %all-gather.28.cloned.1.call-done = bf16[1,1536,1024]{2,1,0:T(8,128)(2,1)} async-done(((bf16[1,192,1024]{2,1,0:T(8,128)(2,1)}), bf16[1,1536,1024]{2,1,0:T(8,128)(2,1)}) %all-gather.28.cloned.1.call-update) | async-done | bytes 3145744 | tf_op jit(solution)/shard_map/while/body/eval_jaxpr/all_gather | solution.py:69
  2646.9 75.2 %reduce-scatter.14.cloned.1.call-done = bf16[192,1024]{1,0:T(8,128)(2,1)} async-done(((bf16[1536,1024]{1,0:T(8,128)(2,1)}), bf16[192,1024]{1,0:T(8,128)(2,1)}) %reduce-scatter.14.cloned.1.call-update) | async-done | bytes 393232 | tf_op jit(solution)/shard_map/while/body/eval_jaxpr/reduce_scatter | solution.py:220
  2901.4 75.3 %reduce-scatter.14.cloned.1.call-done = bf16[192,1024]{1,0:T(8,128)(2,1)} async-done(((bf16[1536,1024]{1,0:T(8,128)(2,1)}), bf16[192,1024]{1,0:T(8,128)(2,1)}) %reduce-scatter.14.cloned.1.call-update) | async-done | bytes 393232 | tf_op jit(solution)/shard_map/while/body/eval_jaxpr/reduce_scatter | solution.py:220
  2982.2 59.6 %all-gather.28.cloned.1.call-done = bf16[1,1536,1024]{2,1,0:T(8,128)(2,1)} async-done(((bf16[1,192,1024]{2,1,0:T(8,128)(2,1)}), bf16[1,1536,1024]{2,1,0:T(8,128)(2,1)}) %all-gather.28.cloned.1.call-update) | async-done | bytes 3145744 | tf_op jit(solution)/shard_map/while/body/eval_jaxpr/all_gather | solution.py:69
  3156.0 75.1 %reduce-scatter.14.cloned.1.call-done = bf16[192,1024]{1,0:T(8,128)(2,1)} async-done(((bf16[1536,1024]{1,0:T(8,128)(2,1)}), bf16[192,1024]{1,0:T(8,128)(2,1)}) %reduce-scatter.14.cloned.1.call-update) | async-done | bytes 393232 | tf_op jit(solution)/shard_map/while/body/eval_jaxpr/reduce_scatter | solution.py:220
  3410.3 75.4 %reduce-scatter.14.cloned.1.call-done = bf16[192,1024]{1,0:T(8,128)(2,1)} async-done(((bf16[1536,1024]{1,0:T(8,128)(2,1)}), bf16[192,1024]{1,0:T(8,128)(2,1)}) %reduce-scatter.14.cloned.1.call-update) | async-done | bytes 393232 | tf_op jit(solution)/shard_map/while/body/eval_jaxpr/reduce_scatter | solution.py:220
  3664.8 75.2 %reduce-scatter.14.cloned.1.call-done = bf16[192,1024]{1,0:T(8,128)(2,1)} async-done(((bf16[1536,1024]{1,0:T(8,128)(2,1)}), bf16[192,1024]{1,0:T(8,128)(2,1)}) %reduce-scatter.14.cloned.1.call-update) | async-done | bytes 393232 | tf_op jit(solution)/shard_map/while/body/eval_jaxpr/reduce_scatter | solution.py:220
  3745.5 59.9 %all-gather.28.cloned.1.call-done = bf16[1,1536,1024]{2,1,0:T(8,128)(2,1)} async-done(((bf16[1,192,1024]{2,1,0:T(8,128)(2,1)}), bf16[1,1536,1024]{2,1,0:T(8,128)(2,1)}) %all-gather.28.cloned.1.call-update) | async-done | bytes 3145744 | tf_op jit(solution)/shard_map/while/body/eval_jaxpr/all_gather | solution.py:69
  3919.8 74.9 %reduce-scatter.14.cloned.1.call-done = bf16[192,1024]{1,0:T(8,128)(2,1)} async-done(((bf16[1536,1024]{1,0:T(8,128)(2,1)}), bf16[192,1024]{1,0:T(8,128)(2,1)}) %reduce-scatter.14.cloned.1.call-update) | async-done | bytes 393232 | tf_op jit(solution)/shard_map/while/body/eval_jaxpr/reduce_scatter | solution.py:220
  4174.0 75.3 %reduce-scatter.14.cloned.1.call-done = bf16[192,1024]{1,0:T(8,128)(2,1)} async-done(((bf16[1536,1024]{1,0:T(8,128)(2,1)}), bf16[192,1024]{1,0:T(8,128)(2,1)}) %reduce-scatter.14.cloned.1.call-update) | async-done | bytes 393232 | tf_op jit(solution)/shard_map/while/body/eval_jaxpr/reduce_scatter | solution.py:220
  4334.1 69.0 %gather_fusion = bf16[3072,1536]{1,0:T(8,128)(2,1)} fusion(bf16[40,152,1536]{2,1,0:T(8,128)(2,1)} %bitcast.291, s32[3072]{0:T(1024)S(1)} %reshape.219), kind=kCustom, calls=%fused_computation | custom fusion | bytes 18898944 | tf_op jit(solution)/shard_map/gather | solution.py:185
  4417.0 218.8 %all-to-all-done.3 = bf16[10,608,1536]{2,0,1:T(8,128)(2,1)} async-done(((bf16[10,608,1536]{2,0,1:T(8,128)(2,1)}), bf16[10,608,1536]{2,0,1:T(8,128)(2,1)}, u32[]{:S(2)}, u32[]{:S(2)}) %all-to-all-start.3) | async-done | bytes 18677792 | tf_op jit(solution)/shard_map/all_to_all | solution.py:237
  4656.8 69.1 %gather_fusion.1 = bf16[3072,1536]{1,0:T(8,128)(2,1)} fusion(bf16[40,152,1536]{2,1,0:T(8,128)(2,1)} %bitcast.290, s32[3072]{0:T(1024)S(1)} %reshape.219), kind=kCustom, calls=%fused_computation.1 | custom fusion | bytes 18898944 | tf_op jit(solution)/shard_map/gather | solution.py:238
  4758.9 91.5 %while.55 = (s32[]{:T(128)}, f32[8,384,3,64]{1,3,2,0:T(8,128)}, f32[8,384,64]{1,2,0:T(8,128)}, bf16[8,384,64]{1,2,0:T(8,128)(2,1)S(1)}, s32[8]{0:T(128)S(1)}, /*...) while((s32[]{:T(128)}, f32[8,384,3,64]{1,3,2,0:T(8,128)}, ...), condition=%wide.region_25.26_spmd.clone, body=%wide.region_23.25_spmd.clone.sunk | while | flops 287488896 | bytes 14820493 | solution.py:277
  4923.6 62.5 %reduce-scatter.10.cloned.1.call-done = f32[1536,48]{0,1:T(8,128)} async-done(((f32[1536,1536]{0,1:T(8,128)}), f32[1536,48]{0,1:T(8,128)}) %reduce-scatter.10.cloned.1.call-update) | async-done | bytes 294928 | tf_op jit(solution)/shard_map/reduce_scatter | solution.py:304
  4986.1 177.2 %reduce-scatter.8.cloned.1.call-done = f32[48,2560]{1,0:T(8,128)} async-done(((f32[1536,2560]{1,0:T(8,128)}), f32[48,2560]{1,0:T(8,128)}) %reduce-scatter.8.cloned.1.call-update) | async-done | bytes 491536 | tf_op jit(solution)/shard_map/reduce_scatter | solution.py:303
  (686 shorter events, 2811.3 us)
Async XLA Ops:
  7.9 163.5 %all-gather.22.cloned.1.call-start = ((), (), s32[]{:S(2)}) async-start(), calls=%async_computation.10 | async-start | bytes 4866048 | tf_op jit(solution)/shard_map/all_gather | solution.py:102
  203.7 273.1 %all-to-all-start = ((bf16[40,152,1536]{2,1,0:T(8,128)(2,1)}), bf16[40,152,1536]{2,1,0:T(8,128)(2,1)}, u32[]{:S(2)}, u32[]{:S(2)}) async-start(bf16[40,152,1536]{2,1,0:T(8,128)(2,1)} %bitcast.293), calls=%async_computation.2 | async-start | bytes 37355520 | tf_op jit(solution)/shard_map/all_to_all | solution.py:182
  476.8 1198.6 %all-to-all-start.2 = ((bf16[40,152,1536]{2,1,0:T(8,128)(2,1)}), bf16[40,152,1536]{2,1,0:T(8,128)(2,1)}, u32[]{:S(2)}, u32[]{:S(2)}) async-start(bf16[40,152,1536]{2,1,0:T(8,128)(2,1)} %bitcast.292), calls=%async_computation.4 | async-start | bytes 37355520 | tf_op jit(solution)/shard_map/all_to_all | solution.py:190
  1675.5 2627.6 %all-to-all-start.1 = ((bf16[10,608,1536]{2,0,1:T(8,128)(2,1)}), bf16[10,608,1536]{2,0,1:T(8,128)(2,1)}, u32[]{:S(2)}, u32[]{:S(2)}) async-start(bf16[10,608,1536]{2,0,1:T(8,128)(2,1)} %copy.116), calls=%async_computation.3 | async-start | bytes 59768832 | tf_op jit(solution)/shard_map/all_to_all | solution.py:184
  1707.6 106.6 %all-gather.30.cloned.1.call-start = ((), (), s32[]{:S(2)}) async-start(), calls=%async_computation.17 | async-start | bytes 1769472 | tf_op jit(solution)/shard_map/while/body/eval_jaxpr/all_gather | solution.py:70
  1709.3 172.4 %reduce-scatter.16.cloned.1.call-start = ((), (), s32[]{:S(2)}) async-start(), calls=%async_computation.19 | async-start | bytes 1769472 | tf_op jit(solution)/shard_map/while/body/eval_jaxpr/reduce_scatter | solution.py:226
  1778.2 180.3 %reduce-scatter.14.cloned.1.call-start = ((), (), s32[]{:S(2)}) async-start(), calls=%async_computation.18 | async-start | bytes 3538944 | tf_op jit(solution)/shard_map/while/body/eval_jaxpr/reduce_scatter | solution.py:220
  1964.0 172.4 %reduce-scatter.16.cloned.1.call-start = ((), (), s32[]{:S(2)}) async-start(), calls=%async_computation.19 | async-start | bytes 1769472 | tf_op jit(solution)/shard_map/while/body/eval_jaxpr/reduce_scatter | solution.py:226
  2032.3 180.6 %reduce-scatter.14.cloned.1.call-start = ((), (), s32[]{:S(2)}) async-start(), calls=%async_computation.18 | async-start | bytes 3538944 | tf_op jit(solution)/shard_map/while/body/eval_jaxpr/reduce_scatter | solution.py:220
  2216.7 106.6 %all-gather.30.cloned.1.call-start = ((), (), s32[]{:S(2)}) async-start(), calls=%async_computation.17 | async-start | bytes 1769472 | tf_op jit(solution)/shard_map/while/body/eval_jaxpr/all_gather | solution.py:70
  2218.4 172.3 %reduce-scatter.16.cloned.1.call-start = ((), (), s32[]{:S(2)}) async-start(), calls=%async_computation.19 | async-start | bytes 1769472 | tf_op jit(solution)/shard_map/while/body/eval_jaxpr/reduce_scatter | solution.py:226
  2287.0 180.4 %reduce-scatter.14.cloned.1.call-start = ((), (), s32[]{:S(2)}) async-start(), calls=%async_computation.18 | async-start | bytes 3538944 | tf_op jit(solution)/shard_map/while/body/eval_jaxpr/reduce_scatter | solution.py:220
  2471.1 106.7 %all-gather.30.cloned.1.call-start = ((), (), s32[]{:S(2)}) async-start(), calls=%async_computation.17 | async-start | bytes 1769472 | tf_op jit(solution)/shard_map/while/body/eval_jaxpr/all_gather | solution.py:70
  2472.8 172.3 %reduce-scatter.16.cloned.1.call-start = ((), (), s32[]{:S(2)}) async-start(), calls=%async_computation.19 | async-start | bytes 1769472 | tf_op jit(solution)/shard_map/while/body/eval_jaxpr/reduce_scatter | solution.py:226
  2541.5 180.6 %reduce-scatter.14.cloned.1.call-start = ((), (), s32[]{:S(2)}) async-start(), calls=%async_computation.18 | async-start | bytes 3538944 | tf_op jit(solution)/shard_map/while/body/eval_jaxpr/reduce_scatter | solution.py:220
  2727.6 172.1 %reduce-scatter.16.cloned.1.call-start = ((), (), s32[]{:S(2)}) async-start(), calls=%async_computation.19 | async-start | bytes 1769472 | tf_op jit(solution)/shard_map/while/body/eval_jaxpr/reduce_scatter | solution.py:226
  2795.9 180.8 %reduce-scatter.14.cloned.1.call-start = ((), (), s32[]{:S(2)}) async-start(), calls=%async_computation.18 | async-start | bytes 3538944 | tf_op jit(solution)/shard_map/while/body/eval_jaxpr/reduce_scatter | solution.py:220
  2982.1 172.2 %reduce-scatter.16.cloned.1.call-start = ((), (), s32[]{:S(2)}) async-start(), calls=%async_computation.19 | async-start | bytes 1769472 | tf_op jit(solution)/shard_map/while/body/eval_jaxpr/reduce_scatter | solution.py:226
  3050.5 180.6 %reduce-scatter.14.cloned.1.call-start = ((), (), s32[]{:S(2)}) async-start(), calls=%async_computation.18 | async-start | bytes 3538944 | tf_op jit(solution)/shard_map/while/body/eval_jaxpr/reduce_scatter | solution.py:220
  3236.6 172.0 %reduce-scatter.16.cloned.1.call-start = ((), (), s32[]{:S(2)}) async-start(), calls=%async_computation.19 | async-start | bytes 1769472 | tf_op jit(solution)/shard_map/while/body/eval_jaxpr/reduce_scatter | solution.py:226
  3304.9 180.7 %reduce-scatter.14.cloned.1.call-start = ((), (), s32[]{:S(2)}) async-start(), calls=%async_computation.18 | async-start | bytes 3538944 | tf_op jit(solution)/shard_map/while/body/eval_jaxpr/reduce_scatter | solution.py:220
  3491.1 172.0 %reduce-scatter.16.cloned.1.call-start = ((), (), s32[]{:S(2)}) async-start(), calls=%async_computation.19 | async-start | bytes 1769472 | tf_op jit(solution)/shard_map/while/body/eval_jaxpr/reduce_scatter | solution.py:226
  3559.4 180.6 %reduce-scatter.14.cloned.1.call-start = ((), (), s32[]{:S(2)}) async-start(), calls=%async_computation.18 | async-start | bytes 3538944 | tf_op jit(solution)/shard_map/while/body/eval_jaxpr/reduce_scatter | solution.py:220
  3743.7 106.9 %all-gather.30.cloned.1.call-start = ((), (), s32[]{:S(2)}) async-start(), calls=%async_computation.17 | async-start | bytes 1769472 | tf_op jit(solution)/shard_map/while/body/eval_jaxpr/all_gather | solution.py:70
  3745.4 172.7 %reduce-scatter.16.cloned.1.call-start = ((), (), s32[]{:S(2)}) async-start(), calls=%async_computation.19 | async-start | bytes 1769472 | tf_op jit(solution)/shard_map/while/body/eval_jaxpr/reduce_scatter | solution.py:226
  3814.1 180.6 %reduce-scatter.14.cloned.1.call-start = ((), (), s32[]{:S(2)}) async-start(), calls=%async_computation.18 | async-start | bytes 3538944 | tf_op jit(solution)/shard_map/while/body/eval_jaxpr/reduce_scatter | solution.py:220
  4000.2 172.1 %reduce-scatter.16.cloned.1.call-start = ((), (), s32[]{:S(2)}) async-start(), calls=%async_computation.19 | async-start | bytes 1769472 | tf_op jit(solution)/shard_map/while/body/eval_jaxpr/reduce_scatter | solution.py:226
  4068.5 180.8 %reduce-scatter.14.cloned.1.call-start = ((), (), s32[]{:S(2)}) async-start(), calls=%async_computation.18 | async-start | bytes 3538944 | tf_op jit(solution)/shard_map/while/body/eval_jaxpr/reduce_scatter | solution.py:220
  4303.1 332.8 %all-to-all-start.3 = ((bf16[10,608,1536]{2,0,1:T(8,128)(2,1)}), bf16[10,608,1536]{2,0,1:T(8,128)(2,1)}, u32[]{:S(2)}, u32[]{:S(2)}) async-start(bf16[10,608,1536]{2,0,1:T(8,128)(2,1)} %copy.120), calls=%async_computation.5 | async-start | bytes 59768832 | tf_op jit(solution)/shard_map/all_to_all | solution.py:237
  4312.3 609.8 %reduce-scatter.12.cloned.1.call-start = ((), (), s32[]{:S(2)}) async-start(), calls=%async_computation.13 | async-start | bytes 811008
  4751.3 234.8 %reduce-scatter.10.cloned.1.call-start = ((), (), s32[]{:S(2)}) async-start(), calls=%async_computation.12 | async-start | bytes 9732096 | tf_op jit(solution)/shard_map/reduce_scatter | solution.py:304
  4757.9 405.5 %reduce-scatter.8.cloned.1.call-start = ((), (), s32[]{:S(2)}) async-start(), calls=%async_computation.11 | async-start | bytes 16220160 | tf_op jit(solution)/shard_map/reduce_scatter | solution.py:303
  (119 other events, 4162.9 us)
Sparse Core Ops, SparseCore 0:
  10.9 78.2 all-gather.19
  92.1 62.1 all-gather.21
  1709.6 59.7 all-gather.27
  1818.0 63.6 reduce-scatter.15
  1885.1 73.3 reduce-scatter.13
  1964.0 59.5 all-gather.27
  2072.6 63.6 reduce-scatter.15
  2139.8 73.1 reduce-scatter.13
  2218.7 59.5 all-gather.27
  2327.0 63.6 reduce-scatter.15
  2394.2 73.1 reduce-scatter.13
  2473.2 59.5 all-gather.27
  2581.5 63.6 reduce-scatter.15
  2648.7 73.3 reduce-scatter.13
  2836.0 63.6 reduce-scatter.15
  2903.2 73.3 reduce-scatter.13
  2982.1 59.5 all-gather.27
  3090.6 63.6 reduce-scatter.15
  3157.8 73.3 reduce-scatter.13
  3344.9 63.6 reduce-scatter.15
  3412.2 73.4 reduce-scatter.13
  3599.4 63.6 reduce-scatter.15
  3666.7 73.2 reduce-scatter.13
  3745.8 59.5 all-gather.27
  3854.4 63.6 reduce-scatter.15
  3921.6 73.1 reduce-scatter.13
  4000.2 59.5 all-gather.27
  4108.6 63.6 reduce-scatter.15
  4175.9 73.3 reduce-scatter.13
  4751.4 93.6 reduce-scatter.11
  4851.5 134.6 reduce-scatter.9
  4993.8 169.5 reduce-scatter.7
  (33 shorter events, 1622.6 us)
where the time goes:
time: 5190 us; the launch traced here: 5170 us
  waiting for transfers between devices  3710 us (71%)
  local copies, waits for them, and re-layouts  491 us (9%)
  matrix products  437 us (8%)
  blocking collectives  318 us (6%)
  other arithmetic  121 us (2%)
    all_gather x20, waiting for transfers between devices, fetch_expert(): lax.all_gather(gate_up_shard, 'dp', axis=0, tiled=True)  1190 us
    all_gather x20, waiting for transfers between devices, fetch_expert(): lax.all_gather(down_shard, 'dp', axis=1, tiled=True)  768 us
    reduce_scatter x10, waiting for transfers between devices, expert_backward(): lax.psum_scatter(contract_rows(rows, grad_gate_up).astype(jnp.bfloat16),...  751 us
    reduce_scatter x10, waiting for transfers between devices, expert_backward(): lax.psum_scatter(contract_rows(grad_produced, hidden).astype(jnp.bfloat16...  507 us
    all_gather x1, blocking collectives, body(): lax.all_gather(router_weight, ('dp', 'expert'), axis=0, tiled=True)  235 us
    all_to_all x1, waiting for transfers between devices, body(): lax.all_to_all(grad_copies, 'expert', split_axis=1, concat_axis=0, tiled=...  219 us
    reduce_scatter x1, waiting for transfers between devices, body(): lax.psum_scatter(qkv_term, ('dp', 'expert'), scatter_dimension=0, tiled=T...  177 us
    dot_general x22, matrix products, contract_rows(): lax.dot_general(left, right, (((0,), (0,)), ((), ())), preferred_element_...  114 us
  transfers between devices with their start and end apart: 69, of which 64 were waited for; matrix products, arithmetic and copies ran while one was open for 17% of the time, Pallas kernels for 0%

commit v1 on v0

--- a/solution.py
+++ b/solution.py
@@ -78,7 +78,7 @@
     return (chosen_mask, jax.nn.softmax(chosen, axis=-1))
 
 
-def body(
+def general_body(
     tokens,
     cotangent,
     lengths,
@@ -318,6 +318,508 @@
     )
 
 
+WIDE = 160
+Z_SIZE, Y_SIZE, X_SIZE, C_SIZE = 4, 2, 2, 2
+MESH_AXES = ("dp", "expert")
+
+
+def device_index(z, y, x, c):
+    return ((z * Y_SIZE + y) * X_SIZE + x) * C_SIZE + c
+
+
+def device_pairs(target):
+    pairs = []
+    for z in range(Z_SIZE):
+        for y in range(Y_SIZE):
+            for x in range(X_SIZE):
+                for c in range(C_SIZE):
+                    to = target(z, y, x, c)
+                    if to is not None:
+                        pairs.append((device_index(z, y, x, c), device_index(*to)))
+    return pairs
+
+
+PAIRS_X = device_pairs(lambda z, y, x, c: (z, y, 1 - x, c))
+PAIRS_Y = device_pairs(lambda z, y, x, c: (z, 1 - y, x, c))
+PAIRS_C = device_pairs(lambda z, y, x, c: (z, y, x, 1 - c))
+
+
+def pairs_shift(step):
+    return device_pairs(lambda z, y, x, c: ((z + step) % Z_SIZE, y, x, c))
+
+
+def pairs_up(first):
+    return device_pairs(
+        lambda z, y, x, c: (z + 1, y, x, c) if first <= z < Z_SIZE - 1 else None
+    )
+
+
+def pairs_up_below(last):
+    return device_pairs(lambda z, y, x, c: (z + 1, y, x, c) if z <= last else None)
+
+
+def pairs_down(last):
+    return device_pairs(lambda z, y, x, c: (z - 1, y, x, c) if 1 <= z <= last else None)
+
+
+def pairs_down_above(first):
+    return device_pairs(lambda z, y, x, c: (z - 1, y, x, c) if z >= first else None)
+
+
+def move(value, pairs):
+    return lax.ppermute(value, MESH_AXES, pairs)
+
+
+def line_gather(block, z):
+    ups, downs = [None], [None]
+    up = down = block
+    for step in range(1, Z_SIZE):
+        up = move(up, pairs_up(step - 1))
+        down = move(down, pairs_down(Z_SIZE - step))
+        ups.append(up)
+        downs.append(down)
+    blocks = [block] + [
+        jnp.where(z >= s, ups[s], downs[Z_SIZE - s]) for s in range(1, Z_SIZE)
+    ]
+    return [(part, move(part, PAIRS_C)) for part in blocks]
+
+
+def line_scatter(parts):
+    low = jnp.bfloat16
+    terms = [own + move(other.astype(low), PAIRS_C).astype(jnp.float32) for own, other in parts]
+
+    def sent(value, pairs):
+        return move(value.astype(low), pairs).astype(jnp.float32)
+
+    up = terms[2] + sent(terms[1], pairs_up_below(0))
+    down = terms[2] + sent(terms[3], pairs_down_above(3))
+    up = terms[3] + sent(up, pairs_up_below(1))
+    down = terms[1] + sent(down, pairs_down_above(2))
+    return terms[0] + sent(up, pairs_up_below(2)) + sent(down, pairs_down_above(1))
+
+
+def half_order(z_to):
+    first = 10 * (z_to // 2)
+    if z_to % 2 == 0:
+        return [first, first + 1, first + 2, first + 3, first + 4]
+    return [first + 6, first + 7, first + 8, first + 9, first + 5]
+
+
+HALF_ORDER = [half_order(z_to) for z_to in range(Z_SIZE)]
+HALF_PLACE = [0] * (Z_SIZE * 5)
+for order_z in range(Z_SIZE):
+    for order_q in range(5):
+        HALF_PLACE[HALF_ORDER[order_z][order_q]] = order_z * 5 + order_q
+UNIT_HALVES = ((0, 2), (2, 4), (4, 5))
+
+
+def shift_exchange(chunks, z):
+    own = lax.dynamic_index_in_dim(chunks, z, 0, keepdims=True)
+    result = lax.dynamic_update_slice_in_dim(jnp.zeros_like(chunks), own, z, 0)
+    for step in range(1, Z_SIZE):
+        chunk = lax.dynamic_index_in_dim(chunks, (z + step) % Z_SIZE, 0, keepdims=True)
+        got = move(chunk, pairs_shift(step))
+        result = lax.dynamic_update_slice_in_dim(result, got, (z + Z_SIZE - step) % Z_SIZE, 0)
+    return result
+
+
+def gather_weights(gate_up_weight, down_weight, z):
+    experts, rows = gate_up_weight.shape[0], gate_up_weight.shape[1]
+    gate, upper = gate_up_weight[..., :FF], gate_up_weight[..., FF:]
+    down_t = down_weight.transpose(0, 2, 1)
+    half = FF // 2
+    halves = jnp.concatenate(
+        [part.reshape(experts, rows, 2, half) for part in (gate, upper, down_t)], axis=-1
+    ).transpose(0, 2, 1, 3).reshape(2 * experts, rows, 3 * half)
+    chunks = jnp.stack(
+        [jnp.stack([halves[q] for q in HALF_ORDER[z_to]]) for z_to in range(Z_SIZE)]
+    )
+    mine = shift_exchange(chunks, z)
+    mine = mine.transpose(1, 0, 2, 3).reshape(5, Z_SIZE * rows, 3 * half)
+    own_units, other_units = [], []
+    middle = Z_SIZE * rows // 2
+    for first, last in UNIT_HALVES:
+        piece = mine[first:last]
+        from_y = move(piece, PAIRS_Y)
+        from_x = move(piece, PAIRS_X)
+        far_a = move(from_y[:, :middle], PAIRS_X)
+        far_b = move(from_x[:, middle:], PAIRS_Y)
+        own_units.append(jnp.concatenate([piece, from_y], axis=1))
+        other_units.append(jnp.concatenate([from_x, far_a, far_b], axis=1))
+    return other_units + own_units
+
+
+def scatter_grads(other_grads, own_grads, z, rows):
+    span = Z_SIZE * rows
+    middle = span // 2
+    low = jnp.bfloat16
+    full = jnp.float32
+    sums = []
+    for other, own in zip(other_grads, own_grads):
+        via_x = move(other[:, span : span + middle], PAIRS_X)
+        via_y = move(other[:, span + middle :], PAIRS_Y)
+        to_x = jnp.concatenate(
+            [
+                other[:, :middle],
+                (other[:, middle:span].astype(full) + via_y.astype(full)).astype(low),
+            ],
+            axis=1,
+        )
+        to_y = jnp.concatenate(
+            [
+                (own[:, span : span + middle].astype(full) + via_x.astype(full)).astype(low),
+                own[:, span + middle :],
+            ],
+            axis=1,
+        )
+        got_x = move(to_x, PAIRS_X)
+        got_y = move(to_y, PAIRS_Y)
+        sums.append(
+            (own[:, :span].astype(full) + got_x.astype(full) + got_y.astype(full)).astype(low)
+        )
+    total = jnp.concatenate(sums, axis=0)
+    chunks = total.reshape(5, Z_SIZE, rows, total.shape[-1]).transpose(1, 0, 2, 3)
+    back = shift_exchange(chunks, z).reshape(Z_SIZE * 5, rows, total.shape[-1])
+    return jnp.stack([back[HALF_PLACE[q]] for q in range(Z_SIZE * 5)]).astype(full)
+
+
+def swap_features(value, y, rows):
+    lead = value.shape[:-1]
+    parts = value.reshape(*lead, Z_SIZE, Y_SIZE, rows)
+    first = jnp.where(y == 0, parts[..., 0, :], parts[..., 1, :])
+    second = jnp.where(y == 0, parts[..., 1, :], parts[..., 0, :])
+    return jnp.concatenate(
+        [first.reshape(*lead, Z_SIZE * rows), second.reshape(*lead, Z_SIZE * rows)], axis=-1
+    )
+
+
+def unswap_features(value, y, rows):
+    lead = value.shape[:-1]
+    first = value[..., : Z_SIZE * rows].reshape(*lead, Z_SIZE, rows)
+    second = value[..., Z_SIZE * rows :].reshape(*lead, Z_SIZE, rows)
+    even = jnp.where(y == 0, first, second)
+    odd = jnp.where(y == 0, second, first)
+    return jnp.stack([even, odd], axis=-2).reshape(*lead, Z_SIZE * Y_SIZE * rows)
+
+
+def dense_gates(logits, chosen):
+    peak = jnp.max(jnp.where(chosen, logits, -jnp.inf), axis=-1, keepdims=True)
+    exponent = jnp.where(chosen, jnp.exp(logits - peak), 0.0)
+    return exponent / jnp.sum(exponent, axis=-1, keepdims=True)
+
+
+def expert_unit(weights, slot_rows, gate_rows, rows_in, grads_in):
+    half = FF // 2
+    low = jnp.bfloat16
+    full = jnp.float32
+    sources, length = slot_rows.shape
+    width = rows_in.shape[-1]
+    pick = slot_rows[:, None, :] == jnp.arange(WIDE, dtype=jnp.int32)[None, :, None]
+    one_hot = pick.astype(low)
+    picked = jnp.einsum("ist,itd->isd", one_hot, rows_in, preferred_element_type=full)
+    picked = picked.astype(low).reshape(sources * WIDE, width)
+    dys = jnp.einsum("ist,itd->isd", one_hot, grads_in, preferred_element_type=full)
+    dys = dys.reshape(sources * WIDE, width)
+    gate_of = jnp.sum(jnp.where(pick, gate_rows[:, None, :], 0.0), axis=-1).reshape(-1, 1)
+    grad_rows = (residual_scale * gate_of * dys).astype(low)
+    dys = dys.astype(low)
+    produced = jnp.zeros((sources * WIDE, width), full)
+    grad_copy = jnp.zeros((sources * WIDE, width), full)
+    grad_gate = jnp.zeros((sources * WIDE,), full)
+    grads = []
+    for part in range(weights.shape[0]):
+        gate_up_w = weights[part, :, : 2 * half]
+        down_t = weights[part, :, 2 * half :]
+        gate_up = jnp.dot(picked, gate_up_w, preferred_element_type=full)
+        gate = gate_up[:, :half]
+        upper = gate_up[:, half:]
+        sigmoid = jax.nn.sigmoid(gate)
+        swish = gate * sigmoid
+        hidden_full = swish * upper
+        hidden = hidden_full.astype(low)
+        produced = produced + multiply_transposed(hidden, down_t)
+        grad_plain = residual_scale * jnp.dot(dys, down_t, preferred_element_type=full)
+        grad_gate = grad_gate + jnp.sum(hidden.astype(full) * grad_plain, axis=-1)
+        grad_hidden = grad_plain * gate_of
+        grad_gate_up = jnp.concatenate(
+            [grad_hidden * upper * sigmoid * (1.0 + gate * (1.0 - sigmoid)), grad_hidden * swish],
+            axis=-1,
+        ).astype(low)
+        grad_copy = grad_copy + multiply_transposed(grad_gate_up, gate_up_w)
+        grads.append(
+            jnp.concatenate(
+                [contract_rows(picked, grad_gate_up), contract_rows(grad_rows, hidden)], axis=-1
+            ).astype(low)
+        )
+    produced = (produced * gate_of).astype(low).reshape(sources, WIDE, width)
+    grad_copy = grad_copy.astype(low).reshape(sources, WIDE, width)
+    grad_gate = jnp.sum(jnp.where(pick, grad_gate.reshape(sources, WIDE, 1), 0.0), axis=1)
+    return one_hot, produced, grad_copy, grad_gate, jnp.stack(grads)
+
+
+def body(
+    tokens,
+    cotangent,
+    lengths,
+    routes,
+    slots,
+    first_gain,
+    qkv_weight,
+    out_weight,
+    second_gain,
+    router_weight,
+    gate_up_weight,
+    down_weight,
+):
+    low = jnp.bfloat16
+    full = jnp.float32
+    dp_index = lax.axis_index("dp")
+    expert_index = lax.axis_index("expert")
+    z, y = dp_index // Y_SIZE, dp_index % Y_SIZE
+    x, c = expert_index // C_SIZE, expert_index % C_SIZE
+    sequence_length = tokens.shape[0]
+    width = tokens.shape[1]
+    rows = gate_up_weight.shape[1]
+    query_group = QUERY_HEADS // KEY_VALUE_HEADS
+    query_width_total = QUERY_HEADS * HEAD_SIZE
+    key_width_total = KEY_VALUE_HEADS * HEAD_SIZE
+    length = lengths[0]
+
+    chosen_by = routes[None, :, :] == jnp.arange(EXPERTS, dtype=jnp.int32)[:, None, None]
+    slot_table = jnp.sum(jnp.where(chosen_by, slots[None, :, :] + 1, 0), axis=-1) - 1
+    slot_tables = lax.all_gather(slot_table, MESH_AXES, axis=0, tiled=False)
+
+    small = jnp.concatenate(
+        [router_weight, first_gain[:, None], second_gain[:, None]], axis=1
+    )
+    small = jnp.pad(small, ((0, 0), (0, 128 - small.shape[1])))
+    first_pack = lax.all_gather(
+        jnp.concatenate([qkv_weight, small], axis=1), MESH_AXES, axis=0, tiled=True
+    )
+    out_t = lax.all_gather(out_weight.T, MESH_AXES, axis=0, tiled=True)
+    qkv_full = first_pack[:, : qkv_weight.shape[1]]
+    small_full = first_pack[:, qkv_weight.shape[1] :]
+    router_full = small_full[:, :EXPERTS]
+    gain_one = small_full[:, EXPERTS].astype(full)
+    gain_two = small_full[:, EXPERTS + 1].astype(full)
+
+    inputs = tokens.astype(full)
+    inverse_one = rms_inverse(inputs)
+    normal_one = inputs * inverse_one
+    hidden_one = (normal_one * gain_one).astype(low)
+    projected_rows = jnp.dot(hidden_one, qkv_full, preferred_element_type=full)
+    cosine_table, sine_table = rope_tables(sequence_length)
+    query_rows = rotate_pairs(
+        projected_rows[:, :query_width_total].reshape(sequence_length, QUERY_HEADS, HEAD_SIZE),
+        cosine_table,
+        sine_table,
+    ).astype(low)
+    keys = rotate_pairs(
+        projected_rows[:, query_width_total : query_width_total + key_width_total].reshape(
+            sequence_length, KEY_VALUE_HEADS, HEAD_SIZE
+        ),
+        cosine_table,
+        sine_table,
+    ).astype(low)
+    value_rows = (
+        projected_rows[:, query_width_total + key_width_total :]
+        .reshape(sequence_length, KEY_VALUE_HEADS, HEAD_SIZE)
+        .astype(low)
+    )
+    row_index = jnp.arange(sequence_length)[:, None]
+    column_index = jnp.arange(sequence_length)[None, :]
+    allowed = (column_index <= row_index) & (column_index < length)
+
+    def head_scores(head):
+        head_query = lax.dynamic_slice_in_dim(query_rows, head * query_group, query_group, 1)
+        head_key = lax.dynamic_index_in_dim(keys, head, 1, keepdims=False)
+        head_value = lax.dynamic_index_in_dim(value_rows, head, 1, keepdims=False)
+        scores = (
+            jnp.einsum("qgd,kd->gqk", head_query, head_key, preferred_element_type=full)
+            * score_scale
+        )
+        return (head_query, head_key, head_value, jnp.where(allowed[None], scores, masked_score))
+
+    def attention_head_forward(head):
+        head_query, head_key, head_value, scores = head_scores(head)
+        peak = jnp.max(scores, axis=-1, keepdims=True)
+        exponent = jnp.exp(scores - peak)
+        total = jnp.sum(exponent, axis=-1, keepdims=True)
+        weights = (exponent / total).astype(low)
+        head_mixed = jnp.einsum(
+            "gqk,kd->qgd", weights, head_value, preferred_element_type=full
+        ).astype(low)
+        return (head_mixed, (peak + jnp.log(total))[..., 0])
+
+    mixed_head_output, log_sum_totals = lax.map(attention_head_forward, jnp.arange(KEY_VALUE_HEADS))
+    mixed = mixed_head_output.transpose(1, 0, 2, 3).reshape(
+        sequence_length, QUERY_HEADS * HEAD_SIZE
+    )
+    branch = multiply_transposed(mixed, out_t)
+    middle = inputs + residual_scale * branch
+    inverse_two = rms_inverse(middle)
+    normal_two = middle * inverse_two
+    hidden_two = (normal_two * gain_two).astype(low)
+    grad_out = cotangent.astype(full)
+
+    grad_blocks = line_gather(swap_features(cotangent, y, rows), z)
+    row_blocks = line_gather(swap_features(hidden_two, y, rows), z)
+    grads_in = jnp.stack([part for pair in grad_blocks for part in pair])
+    rows_in = jnp.stack([part for pair in row_blocks for part in pair])
+    sources = [
+        device_index((z + Z_SIZE - s) % Z_SIZE, y, x, c if k == 0 else 1 - c)
+        for s in range(Z_SIZE)
+        for k in range(C_SIZE)
+    ]
+    slots_in = jnp.stack(
+        [lax.dynamic_index_in_dim(slot_tables, source, 0, keepdims=False) for source in sources]
+    )
+    router_t = router_full.T
+    logits_in = jnp.einsum(
+        "ed,itd->iet", swap_features(router_t, y, rows), rows_in, preferred_element_type=full
+    )
+    chosen_in = slots_in >= 0
+    peak_in = jnp.max(jnp.where(chosen_in, logits_in, -jnp.inf), axis=1, keepdims=True)
+    exponent_in = jnp.where(chosen_in, jnp.exp(logits_in - peak_in), 0.0)
+    gates_in = exponent_in / jnp.sum(exponent_in, axis=1, keepdims=True)
+
+    units = gather_weights(gate_up_weight, down_weight, z)
+    even = z % 2 == 0
+    ids = []
+    for group in (1 - x, x):
+        base = EXPERTS // (X_SIZE * C_SIZE) * (group * C_SIZE + c) + 5 * (z // 2)
+        ids += [base + jnp.where(even, 0, 3), base + jnp.where(even, 1, 4), base + 2]
+    hots, outs, copies, gate_grads, weight_grads = [], [], [], [], []
+    for unit, expert in zip(units, ids):
+        hot, produced, grad_copy, grad_gate, grads = expert_unit(
+            unit,
+            lax.dynamic_index_in_dim(slots_in, expert, 1, keepdims=False),
+            lax.dynamic_index_in_dim(gates_in, expert, 1, keepdims=False),
+            rows_in,
+            grads_in,
+        )
+        hots.append(hot)
+        outs.append(produced)
+        copies.append(grad_copy)
+        gate_grads.append(grad_gate)
+        weight_grads.append(grads)
+    hot_all = jnp.concatenate(hots, axis=1)
+    copy_parts = jnp.einsum(
+        "ist,isd->itd", hot_all, jnp.concatenate(copies, axis=1), preferred_element_type=full
+    )
+    out_parts = jnp.einsum(
+        "ist,isd->itd", hot_all, jnp.concatenate(outs, axis=1), preferred_element_type=full
+    )
+    expert_iota = jnp.arange(64, dtype=jnp.int32)[None, None, :]
+    gate_parts = sum(
+        jnp.where(expert_iota == expert, grad_gate[:, :, None], 0.0)
+        for expert, grad_gate in zip(ids, gate_grads)
+    )
+    gate_high = gate_parts.astype(low).astype(full)
+    copy_parts = jnp.concatenate([copy_parts, gate_high, gate_parts - gate_high], axis=-1)
+    pairs_of = lambda parts: [(parts[2 * s], parts[2 * s + 1]) for s in range(Z_SIZE)]
+    copy_sum = line_scatter(pairs_of(copy_parts))
+    mixture = unswap_features(line_scatter(pairs_of(out_parts)), y, rows)
+    output = (middle + residual_scale * mixture).astype(low)
+    grad_gates = copy_sum[:, width : width + EXPERTS] + copy_sum[:, width + 64 : width + 64 + EXPERTS]
+    copy_sum = unswap_features(copy_sum[:, :width], y, rows)
+
+    chosen = (slot_table >= 0).T
+    gates = dense_gates(jnp.dot(hidden_two, router_full, preferred_element_type=full), chosen)
+    grad_logits = (
+        gates * (grad_gates - jnp.sum(gates * grad_gates, axis=-1, keepdims=True))
+    ).astype(low)
+    grad_hidden_two = copy_sum + multiply_transposed(grad_logits, router_full)
+    router_term = contract_rows(hidden_two, grad_logits)
+    second_term, grad_norm_two = norm_backward(
+        grad_hidden_two, normal_two, inverse_two, gain_two
+    )
+    grad_middle = grad_out + grad_norm_two
+    branch_gradient = (residual_scale * grad_middle).astype(low)
+    out_term = contract_rows(branch_gradient, mixed)
+    grad_mixed = (
+        jnp.dot(branch_gradient, out_t, preferred_element_type=full)
+        .astype(low)
+        .reshape(sequence_length, KEY_VALUE_HEADS, query_group, HEAD_SIZE)
+    )
+
+    def attention_head_backward(head):
+        head_query, head_key, head_value, scores = head_scores(head)
+        head_grad = lax.dynamic_index_in_dim(grad_mixed, head, 1, keepdims=False)
+        head_total = lax.dynamic_index_in_dim(log_sum_totals, head, 0, keepdims=False)
+        probs = jnp.exp(scores - head_total[..., None])
+        grad_weights = jnp.einsum(
+            "qgd,kd->gqk", head_grad, head_value, preferred_element_type=full
+        )
+        grad_scores = (
+            probs * (grad_weights - jnp.sum(probs * grad_weights, axis=-1, keepdims=True))
+        ).astype(low)
+        grad_query = (
+            jnp.einsum("gqk,kd->qgd", grad_scores, head_key, preferred_element_type=full)
+            * score_scale
+        )
+        grad_key = (
+            jnp.einsum("gqk,qgd->kd", grad_scores, head_query, preferred_element_type=full)
+            * score_scale
+        )
+        grad_value = jnp.einsum(
+            "gqk,qgd->kd", probs.astype(low), head_grad, preferred_element_type=full
+        )
+        return (grad_query, grad_key, grad_value)
+
+    query_head_rows, key_head_rows, value_head_rows = lax.map(
+        attention_head_backward, jnp.arange(KEY_VALUE_HEADS)
+    )
+    grad_query = unrotate(
+        query_head_rows.transpose(1, 0, 2, 3).reshape(sequence_length, QUERY_HEADS, HEAD_SIZE),
+        cosine_table,
+        sine_table,
+    )
+    grad_key = unrotate(key_head_rows.transpose(1, 0, 2), cosine_table, sine_table)
+    grad_value = value_head_rows.transpose(1, 0, 2)
+    grad_projected = jnp.concatenate(
+        [
+            grad_query.reshape(sequence_length, query_width_total),
+            grad_key.reshape(sequence_length, key_width_total),
+            grad_value.reshape(sequence_length, key_width_total),
+        ],
+        axis=-1,
+    ).astype(low)
+    qkv_term = contract_rows(hidden_one, grad_projected)
+    grad_hidden_one = multiply_transposed(grad_projected, qkv_full)
+    first_term, grad_norm_one = norm_backward(
+        grad_hidden_one, normal_one, inverse_one, gain_one
+    )
+    grad_input = grad_middle + grad_norm_one
+
+    weight_sums = scatter_grads(weight_grads[:3], weight_grads[3:], z, rows)
+    weight_sums = weight_sums.reshape(EXPERTS // (X_SIZE * C_SIZE), 2, rows, 3 * FF // 2)
+    parts = [
+        weight_sums[..., i * FF // 2 : (i + 1) * FF // 2].transpose(0, 2, 1, 3).reshape(-1, rows, FF)
+        for i in range(3)
+    ]
+    gate_up_grads = jnp.concatenate(parts[:2], axis=-1)
+    down_grads = parts[2].transpose(0, 2, 1)
+
+    small_term = jnp.concatenate(
+        [router_term, first_term[:, None], second_term[:, None]], axis=1
+    )
+    small_sum = lax.psum_scatter(small_term, MESH_AXES, scatter_dimension=0, tiled=True)
+    out_sum = lax.psum_scatter(out_term.astype(low), MESH_AXES, scatter_dimension=0, tiled=True)
+    qkv_sum = lax.psum_scatter(qkv_term.astype(low), MESH_AXES, scatter_dimension=0, tiled=True)
+    return (
+        output,
+        grad_input,
+        small_sum[:, EXPERTS],
+        qkv_sum.astype(full),
+        out_sum.astype(full).T,
+        small_sum[:, EXPERTS + 1],
+        small_sum[:, :EXPERTS],
+        gate_up_grads,
+        down_grads,
+    )
+
+
 def solution(mesh):
     in_specs = (
         P(("dp", "expert"), None),
@@ -344,4 +846,6 @@
         P("expert", "dp", None),
         P("expert", None, "dp"),
     )
-    return jax.shard_map(body, mesh=mesh, in_specs=in_specs, out_specs=out_specs, check_vma=False)
+    fits = mesh.shape["dp"] == Z_SIZE * Y_SIZE and mesh.shape["expert"] == X_SIZE * C_SIZE
+    chosen = body if fits else general_body
+    return jax.shard_map(chosen, mesh=mesh, in_specs=in_specs, out_specs=out_specs, check_vma=False)

time: 5190 us -> 1880 us (0.36)
  waiting for transfers between devices: 3710 us -> 736 us
  blocking collectives: 318 us -> 0 us
  local copies, waits for them, and re-layouts: 491 us -> 251 us
  starting transfers between devices: 36 us -> 129 us
  other arithmetic: 121 us -> 211 us
    all_gather x42 -> x3, waiting for transfers between devices: 1990 us -> 0.01 us  [the longest x1 0.01 us: body(): slot_tables = lax.all_gather(slot_table, MESH_AXES, axis=0, tiled=False)]
    reduce_scatter x22 -> x2, waiting for transfers between devices: 1500 us -> 99.9 us  [the longest x1 99.9 us: body(): lax.psum_scatter(qkv_term.astype(low), MESH_AXES, scatter_dimension=0, ti...]
    ppermute x0 -> x70, waiting for transfers between devices: none -> 636 us  [move(): return lax.ppermute(value, MESH_AXES, pairs)]
    all_gather x1 -> x0, blocking collectives: 235 us -> none  [body(): lax.all_gather(router_weight, ('dp', 'expert'), axis=0, tiled=True)]
    all_to_all x4 -> x0, waiting for transfers between devices: 219 us -> none  [the longest x1 219 us: body(): lax.all_to_all(grad_copies, 'expert', split_axis=1, concat_axis=0, tiled=...]
    gather x2 -> x0, local copies, waits for them, and re-layouts: 138 us -> none  [the longest x1 69.1 us: body(): copy_sum = jnp.sum(grad_back[routes, slots].astype(jnp.float32), axis=1)]
    while x62 -> x0, local copies, waits for them, and re-layouts: 133 us -> none  [the longest x1 51.8 us: body(): lax.scan(expert_forward, None, (received, gate_up_weight, down_weight))]
    ppermute x0 -> x70, starting transfers between devices: none -> 129 us  [move(): return lax.ppermute(value, MESH_AXES, pairs)]
  transfers between devices with their start and end apart: 69 -> 76, of which waited for: 64 -> 22; matrix products, arithmetic and copies ran while one was open for 17% -> 28% of each run, Pallas kernels for 0% -> 0%
where the time goes in v1:
time: 1880 us; the launch traced here: 1870 us
  waiting for transfers between devices  736 us (39%)
  matrix products  477 us (25%)
  local copies, waits for them, and re-layouts  251 us (13%)
  other arithmetic  211 us (11%)
  starting transfers between devices  129 us (7%)
  loops' own time  42 us (2%)
  between operations  19.1 us (1%)
    ppermute x70, waiting for transfers between devices, move(): return lax.ppermute(value, MESH_AXES, pairs)  636 us
    ppermute x70, starting transfers between devices, move(): return lax.ppermute(value, MESH_AXES, pairs)  129 us
    reduce_scatter x1, waiting for transfers between devices, body(): lax.psum_scatter(qkv_term.astype(low), MESH_AXES, scatter_dimension=0, ti...  99.9 us
    dot_general x23, matrix products, multiply_transposed(): lax.dot_general(left, right, (((1,), (1,)), ((), ())), preferred_element_...  99.3 us
    unnamed x577, local copies, waits for them, and re-layouts  95.1 us
    dot_general x23, matrix products, contract_rows(): lax.dot_general(left, right, (((0,), (0,)), ((), ())), preferred_element_...  68.7 us
    dot_general x6, matrix products, expert_unit(): jnp.einsum('ist,itd->isd', one_hot, grads_in, preferred_element_type=full)  64.7 us
    dot_general x10, matrix products, expert_unit(): jnp.dot(dys, down_t, preferred_element_type=full)  40.4 us
  transfers between devices with their start and end apart: 76, of which 22 were waited for; matrix products, arithmetic and copies ran while one was open for 28% of the time, Pallas kernels for 0%

profile of v1, /device:TPU:0, one launch (start us, length us, event | category | flops | bytes accessed | tf_op | source)
XLA Modules:
  0.0 1866.3 jit_solution(3826795029841939714)
XLA Ops:
  79.9 20.1 %collective-permute-done.10 = bf16[1,5,192,768]{3,2,1,0:T(8,128)(2,1)} collective-permute-done((bf16[1,5,192,768]{3,2,1,0:T(8,128)(2,1)}, bf16[1,5,192,768]{3,2,1,0:T(8,128)(2,1)}, u32[]{:S(2)}, u32[]{:S(2)}) %collective-permute-start.10) | collective-permute-done | bytes 1474592 | tf_op jit(solution)/shard_map/ppermute | solution.py:370
  104.9 62.2 %collective-permute-done.11 = bf16[1,5,192,768]{3,2,1,0:T(8,128)(2,1)} collective-permute-done((bf16[1,5,192,768]{3,2,1,0:T(8,128)(2,1)}, bf16[1,5,192,768]{3,2,1,0:T(8,128)(2,1)}, u32[]{:S(2)}, u32[]{:S(2)}) %collective-permute-start.11) | collective-permute-done | bytes 1474592 | tf_op jit(solution)/shard_map/ppermute | solution.py:370
  178.0 15.5 collective-permute-done.38
  211.2 72.8 %collective-permute-done.39 = bf16[384,1536]{1,0:T(8,128)(2,1)S(1)} collective-permute-done((bf16[384,1536]{1,0:T(8,128)(2,1)}, bf16[384,1536]{1,0:T(8,128)(2,1)S(1)}, u32[]{:S(2)}, u32[]{:S(2)}) %collective-permute-start.39) | collective-permute-done | bytes 1179680 | tf_op jit(solution)/shard_map/ppermute | solution.py:370
  326.3 37.0 %collective-permute-done.18 = bf16[2,768,768]{2,1,0:T(8,128)(2,1)} collective-permute-done((bf16[2,768,768]{2,1,0:T(8,128)(2,1)S(1)}, bf16[2,768,768]{2,1,0:T(8,128)(2,1)}, u32[]{:S(2)}, u32[]{:S(2)}) %collective-permute-start.18) | collective-permute-done | bytes 2359328 | tf_op jit(solution)/shard_map/ppermute | solution.py:370
  401.8 64.1 %while.30 = (s32[]{:T(128)}, bf16[8,384,3,64]{1,3,2,0:T(8,128)(2,1)}, f32[8,3,384]{2,1,0:T(4,128)}, s32[8]{0:T(128)}, bf16[384,8,64]{0,2,1:T(8,128)(2,1)}, /*ind...) while((s32[]{:T(128)}, ...), condition=%wide.region_4.5_spmd.clone.clone, body=%wide.region_1.4_spmd.clone.sunk.clone | while | flops 117152648 | bytes 6036541 | solution.py:654
  492.6 35.7 %collective-permute-done.2 = bf16[384,1536]{1,0:T(8,128)(2,1)S(1)} collective-permute-done((bf16[384,1536]{1,0:T(8,128)(2,1)S(1)}, bf16[384,1536]{1,0:T(8,128)(2,1)S(1)}, u32[]{:S(2)}, u32[]{:S(2)}) %collective-permute-start.2) | collective-permute-done | bytes 1179680 | tf_op jit(solution)/shard_map/ppermute | solution.py:370
  544.2 12.6 collective-permute-done.3
  558.2 10.2 fusion.303
  568.7 15.6 collective-permute-done.4
  584.7 10.3 fusion.306
  595.8 10.2 fusion.302
  607.0 10.1 fusion.305
  618.0 10.4 fusion.304
  629.2 13.5 fusion.300
  878.5 20.7 %fusion.311 = f32[8,384,1536]{1,2,0:T(8,128)} fusion(pred[8,960,384]{2,1,0:T(8,128)(4,1)S(1)} %copy-done.193, bf16[8,960,1536]{2,1,0:T(8,128)(2,1)} %constant_dynamic-update-slice_fusion.23), kind=kOutput, calls=%fused_computation.700 | convolution fusion | flops 9059696640 | bytes 45416448 | tf_op jit(solution)/shard_map/ist,isd->itd/dot_general | solution.py:707
  899.8 13.6 fusion.290
  915.3 9.6 pad_maximum_fusion
  1003.8 24.9 %fusion.307 = (bf16[8,384,1536]{1,2,0:T(8,128)(2,1)}, f32[8,384,1536]{1,2,0:T(8,128)}) fusion(pred[8,960,384]{2,1,0:T(8,128)(4,1)S(1)} %copy-done.194, bf16[8,960,1536]{2,1,0:T(8,128)(2,1)} %constant_dynamic-update-slice_fusion.17), kind=kOutput, calls=%fused_computation.695 | convolution fusion | flops 9064415232 | bytes 54853632 | tf_op jit(solution)/shard_map/ist,isd->itd/dot_general | solution.py:710
  1048.7 18.8 %collective-permute-start.29 = (bf16[384,1536]{0,1:T(8,128)(2,1)}, bf16[384,1536]{0,1:T(8,128)(2,1)}, u32[]{:S(2)}, u32[]{:S(2)}) collective-permute-start(bf16[384,1536]{0,1:T(8,128)(2,1)} %fusion.161), channel_id=1, source_target_pairs={{0,8},{1,9},{2,10},{3,11},{4,12},{5,13},{6,14},{7,15}} | collective-permute-start | bytes 3538952 | tf_op jit(solution)/shard_map/ppermute | solution.py:370
  1072.8 20.4 %collective-permute-done.29 = bf16[384,1536]{0,1:T(8,128)(2,1)} collective-permute-done((bf16[384,1536]{0,1:T(8,128)(2,1)}, bf16[384,1536]{0,1:T(8,128)(2,1)}, u32[]{:S(2)}, u32[]{:S(2)}) %collective-permute-start.29) | collective-permute-done | bytes 1179680 | tf_op jit(solution)/shard_map/ppermute | solution.py:370
  1102.0 18.4 collective-permute-done.49
  1130.5 15.3 collective-permute-done.30
  1151.7 20.6 %collective-permute-done.50 = bf16[384,1664]{0,1:T(8,128)(2,1)} collective-permute-done((bf16[384,1664]{0,1:T(8,128)(2,1)S(1)}, bf16[384,1664]{0,1:T(8,128)(2,1)}, u32[]{:S(2)}, u32[]{:S(2)}) %collective-permute-start.50) | collective-permute-done | bytes 1277984 | tf_op jit(solution)/shard_map/ppermute | solution.py:370
  1200.1 20.3 %collective-permute-start.51 = (bf16[384,1664]{0,1:T(8,128)(2,1)S(1)}, bf16[384,1664]{0,1:T(8,128)(2,1)S(1)}, u32[]{:S(2)}, u32[]{:S(2)}) collective-permute-start(bf16[384,1664]{0,1:T(8,128)(2,1)S(1)} %copy-done.142), channel_id=1, source_target_pairs={{0,8},{1,9},{2,10},{3,11},{4,12},{5,13},{6,14},{7,15},{8,16},{9,17... | collective-permute-start | bytes 3833864 | tf_op jit(solution)/shard_map/ppermute | solution.py:370
  1230.8 43.1 %collective-permute-done.34 = bf16[384,1536]{0,1:T(8,128)(2,1)S(1)} collective-permute-done((bf16[384,1536]{0,1:T(8,128)(2,1)}, bf16[384,1536]{0,1:T(8,128)(2,1)S(1)}, u32[]{:S(2)}, u32[]{:S(2)}) %collective-permute-start.34) | collective-permute-done | bytes 1179680 | tf_op jit(solution)/shard_map/ppermute | solution.py:370
  1279.4 20.3 %collective-permute-done.54 = bf16[384,1664]{0,1:T(8,128)(2,1)S(1)} collective-permute-done((bf16[384,1664]{0,1:T(8,128)(2,1)S(1)}, bf16[384,1664]{0,1:T(8,128)(2,1)S(1)}, u32[]{:S(2)}, u32[]{:S(2)}) %collective-permute-start.54) | collective-permute-done | bytes 1277984 | tf_op jit(solution)/shard_map/ppermute | solution.py:370
  1323.8 91.2 %while.31 = (s32[]{:T(128)}, f32[8,384,3,64]{1,3,2,0:T(8,128)}, f32[8,384,64]{1,2,0:T(8,128)}, bf16[8,384,64]{1,2,0:T(8,128)(2,1)S(1)}, s32[8]{0:T(128)S(1)}, /*...) while((s32[]{:T(128)}, f32[8,384,3,64]{1,3,2,0:T(8,128)}, ...), condition=%wide.region_37.38_spmd.clone.clone, body=%wide.region_35.37_spmd.clone.sunk.clone | while | flops 287488896 | bytes 14820453 | solution.py:770
  1498.6 105.7 %collective-permute-done.66 = bf16[1,768,768]{1,2,0:T(8,128)(2,1)S(1)} collective-permute-done((bf16[1,768,768]{1,2,0:T(8,128)(2,1)S(1)}, bf16[1,768,768]{1,2,0:T(8,128)(2,1)S(1)}, u32[]{:S(2)}, u32[]{:S(2)}) %collective-permute-start.66) | collective-permute-done | bytes 1179680 | tf_op jit(solution)/shard_map/ppermute | solution.py:370
  1631.4 30.7 %collective-permute-done.67 = bf16[1,5,192,768]{3,2,0,1:T(8,128)(2,1)S(1)} collective-permute-done((bf16[1,5,192,768]{3,2,0,1:T(8,128)(2,1)S(1)}, bf16[1,5,192,768]{3,2,0,1:T(8,128)(2,1)S(1)}, u32[]{:S(2)}, u32[]{:S(2)}) %collective-permute-start.67) | collective-permute-done | bytes 1474592 | tf_op jit(solution)/shard_map/ppermute | solution.py:370
  1662.3 62.4 %collective-permute-done.68 = bf16[1,5,192,768]{3,2,0,1:T(8,128)(2,1)S(1)} collective-permute-done((bf16[1,5,192,768]{3,2,0,1:T(8,128)(2,1)S(1)}, bf16[1,5,192,768]{3,2,0,1:T(8,128)(2,1)S(1)}, u32[]{:S(2)}, u32[]{:S(2)}) %collective-permute-start.68) | collective-permute-done | bytes 1474592 | tf_op jit(solution)/shard_map/ppermute | solution.py:370
  1757.3 99.9 %reduce-scatter.6.cloned.1.call-done = bf16[48,2560]{1,0:T(8,128)(2,1)} async-done(((bf16[1536,2560]{1,0:T(8,128)(2,1)}), bf16[48,2560]{1,0:T(8,128)(2,1)}) %reduce-scatter.6.cloned.1.call-update) | async-done | bytes 245776 | tf_op jit(solution)/shard_map/reduce_scatter | solution.py:809
  (1150 shorter events, 924.0 us)
Async XLA Ops:
  7.2 295.5 %all-gather.9.cloned.1.call-start = ((), (), s32[]{:S(2)}) async-start(), calls=%async_computation.7 | async-start | bytes 2027520 | tf_op jit(solution)/shard_map/all_gather | solution.py:590
  10.1 367.0 %all-gather.5.cloned.1.call-start = ((), (), s32[]{:S(2)}) async-start(), calls=%async_computation.3 | async-start | bytes 8515584 | tf_op jit(solution)/shard_map/all_gather | solution.py:596
  12.7 453.2 %all-gather.7.cloned.1.call-start = ((), (), s32[]{:S(2)}) async-start(), calls=%async_computation.4 | async-start | bytes 4866048 | tf_op jit(solution)/shard_map/all_gather | solution.py:599
  16.2 180.4 %collective-permute-start.35 = (bf16[384,1536]{1,0:T(8,128)(2,1)}, bf16[384,1536]{1,0:T(8,128)(2,1)}, u32[]{:S(2)}, u32[]{:S(2)}) collective-permute-start(bf16[384,1536]{1,0:T(8,128)(2,1)} %pad_maximum_fusion.20), channel_id=1, source_target_pairs={{0,1},{1,0},{2,3},{3,2},{4,5},{5,4},{6,7},{7,6},{8,9},{9,8},{10,11... | collective-permute-start | bytes 3538952 | tf_op jit(solution)/shard_map/ppermute | solution.py:370
  61.7 105.4 %collective-permute-start.11 = (bf16[1,5,192,768]{3,2,1,0:T(8,128)(2,1)}, bf16[1,5,192,768]{3,2,1,0:T(8,128)(2,1)}, u32[]{:S(2)}, u32[]{:S(2)}) collective-permute-start(bf16[1,5,192,768]{3,2,1,0:T(8,128)(2,1)} %get-tuple-element.338), channel_id=1, source_target_pairs={{0,16},{1,17},{2,18},{3,19},{4,20},{5,21},{6,22},{7,23},{8,24},{9,... | collective-permute-start | bytes 4423688 | tf_op jit(solution)/shard_map/ppermute | solution.py:370
  66.0 103.6 %collective-permute-start.12 = (bf16[1,5,192,768]{3,2,1,0:T(8,128)(2,1)S(1)}, bf16[1,5,192,768]{3,2,1,0:T(8,128)(2,1)}, u32[]{:S(2)}, u32[]{:S(2)}) collective-permute-start(bf16[1,5,192,768]{3,2,1,0:T(8,128)(2,1)S(1)} %get-tuple-element.337), channel_id=1, source_target_pairs={{0,24},{1,25},{2,26},{3,27},{4,28},{5,29},{6,30},{7,31},{8,0},{9,1... | collective-permute-start | bytes 4423688 | tf_op jit(solution)/shard_map/ppermute | solution.py:370
  66.2 1686.0 %reduce-scatter.10.cloned.1.call-start = ((), (), s32[]{:S(2)}) async-start(), calls=%async_computation.8 | async-start | bytes 811008
  78.0 115.5 %collective-permute-start.38 = (bf16[384,1536]{1,0:T(8,128)(2,1)}, bf16[384,1536]{1,0:T(8,128)(2,1)}, u32[]{:S(2)}, u32[]{:S(2)}) collective-permute-start(bf16[384,1536]{1,0:T(8,128)(2,1)} %collective-permute-done.37), channel_id=1, source_target_pairs={{8,0},{9,1},{10,2},{11,3},{12,4},{13,5},{14,6},{15,7},{16,8},{17,9... | collective-permute-start | bytes 3538952 | tf_op jit(solution)/shard_map/ppermute | solution.py:370
  100.0 94.8 %collective-permute-start.36 = (bf16[384,1536]{1,0:T(8,128)(2,1)}, bf16[384,1536]{1,0:T(8,128)(2,1)}, u32[]{:S(2)}, u32[]{:S(2)}) collective-permute-start(bf16[384,1536]{1,0:T(8,128)(2,1)} %pad_maximum_fusion.20), channel_id=1, source_target_pairs={{0,8},{1,9},{2,10},{3,11},{4,12},{5,13},{6,14},{7,15},{8,16},{9,17... | collective-permute-start | bytes 3538952 | tf_op jit(solution)/shard_map/ppermute | solution.py:370
  194.9 119.4 %collective-permute-start.41 = (bf16[384,1536]{1,0:T(8,128)(2,1)}, bf16[384,1536]{1,0:T(8,128)(2,1)}, u32[]{:S(2)}, u32[]{:S(2)}) collective-permute-start(bf16[384,1536]{1,0:T(8,128)(2,1)} %collective-permute-done.36), channel_id=1, source_target_pairs={{8,16},{9,17},{10,18},{11,19},{12,20},{13,21},{14,22},{15,23},{16,... | collective-permute-start | bytes 3538952 | tf_op jit(solution)/shard_map/ppermute | solution.py:370
  203.1 115.4 %collective-permute-start.14 = (bf16[2,768,768]{2,1,0:T(8,128)(2,1)}, bf16[2,768,768]{2,1,0:T(8,128)(2,1)}, u32[]{:S(2)}, u32[]{:S(2)}) collective-permute-start(bf16[2,768,768]{2,1,0:T(8,128)(2,1)} %bitcast.36), channel_id=1, source_target_pairs={{0,4},{1,5},{2,6},{3,7},{4,0},{5,1},{6,2},{7,3},{8,12},{9,13},{10,... | collective-permute-start | bytes 7077896 | tf_op jit(solution)/shard_map/ppermute | solution.py:370
  204.6 118.7 %collective-permute-start.13 = (bf16[2,768,768]{2,1,0:T(8,128)(2,1)}, bf16[2,768,768]{2,1,0:T(8,128)(2,1)}, u32[]{:S(2)}, u32[]{:S(2)}) collective-permute-start(bf16[2,768,768]{2,1,0:T(8,128)(2,1)} %bitcast.36), channel_id=1, source_target_pairs={{0,2},{1,3},{2,0},{3,1},{4,6},{5,7},{6,4},{7,5},{8,10},{9,11},{10,... | collective-permute-start | bytes 7077896 | tf_op jit(solution)/shard_map/ppermute | solution.py:370
  318.4 164.2 %collective-permute-start.43 = (bf16[384,1536]{1,0:T(8,128)(2,1)}, bf16[384,1536]{1,0:T(8,128)(2,1)}, u32[]{:S(2)}, u32[]{:S(2)}) collective-permute-start(bf16[384,1536]{1,0:T(8,128)(2,1)} %collective-permute-done.41), channel_id=1, source_target_pairs={{16,24},{17,25},{18,26},{19,27},{20,28},{21,29},{22,30},{23,31}} | collective-permute-start | bytes 3538952 | tf_op jit(solution)/shard_map/ppermute | solution.py:370
  323.2 163.4 %collective-permute-start.15 = (bf16[2,384,768]{2,1,0:T(8,128)(2,1)}, bf16[2,384,768]{2,1,0:T(8,128)(2,1)}, u32[]{:S(2)}, u32[]{:S(2)}) collective-permute-start(bf16[2,384,768]{2,1,0:T(8,128)(2,1)} %slice.637), channel_id=1, source_target_pairs={{0,2},{1,3},{2,0},{3,1},{4,6},{5,7},{6,4},{7,5},{8,10},{9,11},{10,... | collective-permute-start | bytes 3538952 | tf_op jit(solution)/shard_map/ppermute | solution.py:370
  363.3 167.8 %collective-permute-start.16 = (bf16[2,384,768]{2,1,0:T(8,128)(2,1)}, bf16[2,384,768]{2,1,0:T(8,128)(2,1)}, u32[]{:S(2)}, u32[]{:S(2)}) collective-permute-start(bf16[2,384,768]{2,1,0:T(8,128)(2,1)} %slice.638), channel_id=1, source_target_pairs={{0,4},{1,5},{2,6},{3,7},{4,0},{5,1},{6,2},{7,3},{8,12},{9,13},{10,... | collective-permute-start | bytes 3538952 | tf_op jit(solution)/shard_map/ppermute | solution.py:370
  372.8 159.7 %collective-permute-start.19 = (bf16[2,384,768]{2,1,0:T(8,128)(2,1)}, bf16[2,384,768]{2,1,0:T(8,128)(2,1)}, u32[]{:S(2)}, u32[]{:S(2)}) collective-permute-start(bf16[2,384,768]{2,1,0:T(8,128)(2,1)} %slice.651), channel_id=1, source_target_pairs={{0,2},{1,3},{2,0},{3,1},{4,6},{5,7},{6,4},{7,5},{8,10},{9,11},{10,... | collective-permute-start | bytes 3538952 | tf_op jit(solution)/shard_map/ppermute | solution.py:370
  375.3 159.5 %collective-permute-start.20 = (bf16[2,384,768]{2,1,0:T(8,128)(2,1)}, bf16[2,384,768]{2,1,0:T(8,128)(2,1)}, u32[]{:S(2)}, u32[]{:S(2)}) collective-permute-start(bf16[2,384,768]{2,1,0:T(8,128)(2,1)} %slice.652), channel_id=1, source_target_pairs={{0,4},{1,5},{2,6},{3,7},{4,0},{5,1},{6,2},{7,3},{8,12},{9,13},{10,... | collective-permute-start | bytes 3538952 | tf_op jit(solution)/shard_map/ppermute | solution.py:370
  1179.4 97.7 %collective-permute-start.45 = (bf16[384,1664]{0,1:T(8,128)(2,1)S(1)}, bf16[384,1664]{0,1:T(8,128)(2,1)S(1)}, u32[]{:S(2)}, u32[]{:S(2)}) collective-permute-start(bf16[384,1664]{0,1:T(8,128)(2,1)S(1)} %get-tuple-element.324), channel_id=1, source_target_pairs={{0,1},{1,0},{2,3},{3,2},{4,5},{5,4},{6,7},{7,6},{8,9},{9,8},{10,11... | collective-permute-start | bytes 3833864 | tf_op jit(solution)/shard_map/ppermute | solution.py:370
  1230.2 225.6 %collective-permute-start.55 = (bf16[2,384,768]{1,2,0:T(8,128)(2,1)}, bf16[2,384,768]{1,2,0:T(8,128)(2,1)}, u32[]{:S(2)}, u32[]{:S(2)}) collective-permute-start(bf16[2,384,768]{1,2,0:T(8,128)(2,1)} %get-tuple-element.348), channel_id=1, source_target_pairs={{0,4},{1,5},{2,6},{3,7},{4,0},{5,1},{6,2},{7,3},{8,12},{9,13},{10,... | collective-permute-start | bytes 3538952 | tf_op jit(solution)/shard_map/ppermute | solution.py:370
  1273.9 187.3 %collective-permute-start.57 = (bf16[2,384,768]{1,2,0:T(8,128)(2,1)}, bf16[2,384,768]{1,2,0:T(8,128)(2,1)}, u32[]{:S(2)}, u32[]{:S(2)}) collective-permute-start(bf16[2,384,768]{1,2,0:T(8,128)(2,1)} %get-tuple-element.347), channel_id=1, source_target_pairs={{0,2},{1,3},{2,0},{3,1},{4,6},{5,7},{6,4},{7,5},{8,10},{9,11},{10,... | collective-permute-start | bytes 3538952 | tf_op jit(solution)/shard_map/ppermute | solution.py:370
  1277.1 189.4 %collective-permute-start.59 = (bf16[2,384,768]{1,2,0:T(8,128)(2,1)}, bf16[2,384,768]{1,2,0:T(8,128)(2,1)}, u32[]{:S(2)}, u32[]{:S(2)}) collective-permute-start(bf16[2,384,768]{1,2,0:T(8,128)(2,1)} %get-tuple-element.351), channel_id=1, source_target_pairs={{0,4},{1,5},{2,6},{3,7},{4,0},{5,1},{6,2},{7,3},{8,12},{9,13},{10,... | collective-permute-start | bytes 3538952 | tf_op jit(solution)/shard_map/ppermute | solution.py:370
  1277.6 203.6 %collective-permute-start.61 = (bf16[2,384,768]{1,2,0:T(8,128)(2,1)}, bf16[2,384,768]{1,2,0:T(8,128)(2,1)}, u32[]{:S(2)}, u32[]{:S(2)}) collective-permute-start(bf16[2,384,768]{1,2,0:T(8,128)(2,1)} %get-tuple-element.350), channel_id=1, source_target_pairs={{0,2},{1,3},{2,0},{3,1},{4,6},{5,7},{6,4},{7,5},{8,10},{9,11},{10,... | collective-permute-start | bytes 3538952 | tf_op jit(solution)/shard_map/ppermute | solution.py:370
  1299.7 153.5 %collective-permute-start.63 = (bf16[1,384,768]{1,2,0:T(8,128)(2,1)}, bf16[1,384,768]{1,2,0:T(8,128)(2,1)}, u32[]{:S(2)}, u32[]{:S(2)}) collective-permute-start(bf16[1,384,768]{1,2,0:T(8,128)(2,1)} %get-tuple-element.378), channel_id=1, source_target_pairs={{0,4},{1,5},{2,6},{3,7},{4,0},{5,1},{6,2},{7,3},{8,12},{9,13},{10,... | collective-permute-start | bytes 1769480 | tf_op jit(solution)/shard_map/ppermute | solution.py:370
  1431.1 324.5 %reduce-scatter.8.cloned.1.call-start = ((), (), s32[]{:S(2)}) async-start(), calls=%async_computation.6 | async-start | bytes 4866048 | tf_op jit(solution)/shard_map/reduce_scatter | solution.py:808
  1437.7 419.5 %reduce-scatter.6.cloned.1.call-start = ((), (), s32[]{:S(2)}) async-start(), calls=%async_computation.5 | async-start | bytes 8110080 | tf_op jit(solution)/shard_map/reduce_scatter | solution.py:809
  1461.2 145.0 %collective-permute-start.56 = (bf16[2,768,768]{1,2,0:T(8,128)(2,1)}, bf16[2,768,768]{1,2,0:T(8,128)(2,1)}, u32[]{:S(2)}, u32[]{:S(2)}) collective-permute-start(bf16[2,768,768]{1,2,0:T(8,128)(2,1)} %pad_maximum_fusion.6), channel_id=1, source_target_pairs={{0,2},{1,3},{2,0},{3,1},{4,6},{5,7},{6,4},{7,5},{8,10},{9,11},{10,... | collective-permute-start | bytes 7077896 | tf_op jit(solution)/shard_map/ppermute | solution.py:370
  1466.6 139.6 %collective-permute-start.58 = (bf16[2,768,768]{1,2,0:T(8,128)(2,1)}, bf16[2,768,768]{1,2,0:T(8,128)(2,1)}, u32[]{:S(2)}, u32[]{:S(2)}) collective-permute-start(bf16[2,768,768]{1,2,0:T(8,128)(2,1)} %fusion.118), channel_id=1, source_target_pairs={{0,4},{1,5},{2,6},{3,7},{4,0},{5,1},{6,2},{7,3},{8,12},{9,13},{10,... | collective-permute-start | bytes 7077896 | tf_op jit(solution)/shard_map/ppermute | solution.py:370
  1481.2 128.3 %collective-permute-start.60 = (bf16[2,768,768]{1,2,0:T(8,128)(2,1)S(1)}, bf16[2,768,768]{1,2,0:T(8,128)(2,1)S(1)}, u32[]{:S(2)}, u32[]{:S(2)}) collective-permute-start(bf16[2,768,768]{1,2,0:T(8,128)(2,1)S(1)} %pad_maximum_fusion.7), channel_id=1, source_target_pairs={{0,2},{1,3},{2,0},{3,1},{4,6},{5,7},{6,4},{7,5},{8,10},{9,11},{10,... | collective-permute-start | bytes 7077896 | tf_op jit(solution)/shard_map/ppermute | solution.py:370
  1484.8 124.7 %collective-permute-start.62 = (bf16[2,768,768]{1,2,0:T(8,128)(2,1)S(1)}, bf16[2,768,768]{1,2,0:T(8,128)(2,1)S(1)}, u32[]{:S(2)}, u32[]{:S(2)}) collective-permute-start(bf16[2,768,768]{1,2,0:T(8,128)(2,1)S(1)} %fusion.122), channel_id=1, source_target_pairs={{0,4},{1,5},{2,6},{3,7},{4,0},{5,1},{6,2},{7,3},{8,12},{9,13},{10,... | collective-permute-start | bytes 7077896 | tf_op jit(solution)/shard_map/ppermute | solution.py:370
  1496.5 107.9 %collective-permute-start.66 = (bf16[1,768,768]{1,2,0:T(8,128)(2,1)S(1)}, bf16[1,768,768]{1,2,0:T(8,128)(2,1)S(1)}, u32[]{:S(2)}, u32[]{:S(2)}) collective-permute-start(bf16[1,768,768]{1,2,0:T(8,128)(2,1)S(1)} %fusion.185), channel_id=1, source_target_pairs={{0,4},{1,5},{2,6},{3,7},{4,0},{5,1},{6,2},{7,3},{8,12},{9,13},{10,... | collective-permute-start | bytes 3538952 | tf_op jit(solution)/shard_map/ppermute | solution.py:370
  1626.5 98.1 %collective-permute-start.68 = (bf16[1,5,192,768]{3,2,0,1:T(8,128)(2,1)S(1)}, bf16[1,5,192,768]{3,2,0,1:T(8,128)(2,1)S(1)}, u32[]{:S(2)}, u32[]{:S(2)}) collective-permute-start(bf16[1,5,192,768]{3,2,0,1:T(8,128)(2,1)S(1)} %get-tuple-element.333), channel_id=1, source_target_pairs={{0,16},{1,17},{2,18},{3,19},{4,20},{5,21},{6,22},{7,23},{8,24},{9,... | collective-permute-start | bytes 4423688 | tf_op jit(solution)/shard_map/ppermute | solution.py:370
  1626.5 98.3 %collective-permute-start.69 = (bf16[1,5,192,768]{3,2,0,1:T(8,128)(2,1)S(1)}, bf16[1,5,192,768]{3,2,0,1:T(8,128)(2,1)S(1)}, u32[]{:S(2)}, u32[]{:S(2)}) collective-permute-start(bf16[1,5,192,768]{3,2,0,1:T(8,128)(2,1)S(1)} %get-tuple-element.332), channel_id=1, source_target_pairs={{0,24},{1,25},{2,26},{3,27},{4,28},{5,29},{6,30},{7,31},{8,0},{9,1... | collective-permute-start | bytes 4423688 | tf_op jit(solution)/shard_map/ppermute | solution.py:370
  (306 other events, 4344.6 us)
Sparse Core Ops, SparseCore 0:
  11.5 122.1 all-gather.8
  137.2 137.5 all-gather.4
  277.7 77.9 all-gather.6
  1431.2 94.4 reduce-scatter.9
  1531.0 196.7 reduce-scatter.7
  1734.3 122.8 reduce-scatter.5

commit v2 on v0

--- a/solution.py
+++ b/solution.py
@@ -1,6 +1,10 @@
+import functools
+
 import jax
 import jax.numpy as jnp
 from jax import lax
+from jax.experimental import pallas as pl
+from jax.experimental.pallas import tpu as pltpu
 from jax.sharding import PartitionSpec as P
 
 QUERY_HEADS = 24
@@ -78,7 +82,7 @@
     return (chosen_mask, jax.nn.softmax(chosen, axis=-1))
 
 
-def body(
+def general_body(
     tokens,
     cotangent,
     lengths,
@@ -318,6 +322,1344 @@
     )
 
 
+WIDE = 160
+Z_SIZE, Y_SIZE, X_SIZE, C_SIZE = 4, 2, 2, 2
+MESH_AXES = ("dp", "expert")
+
+
+def device_index(z, y, x, c):
+    return ((z * Y_SIZE + y) * X_SIZE + x) * C_SIZE + c
+
+
+def device_pairs(target):
+    pairs = []
+    for z in range(Z_SIZE):
+        for y in range(Y_SIZE):
+            for x in range(X_SIZE):
+                for c in range(C_SIZE):
+                    to = target(z, y, x, c)
+                    if to is not None:
+                        pairs.append((device_index(z, y, x, c), device_index(*to)))
+    return pairs
+
+
+PAIRS_X = device_pairs(lambda z, y, x, c: (z, y, 1 - x, c))
+PAIRS_Y = device_pairs(lambda z, y, x, c: (z, 1 - y, x, c))
+PAIRS_C = device_pairs(lambda z, y, x, c: (z, y, x, 1 - c))
+
+
+def pairs_shift(step):
+    return device_pairs(lambda z, y, x, c: ((z + step) % Z_SIZE, y, x, c))
+
+
+def pairs_up(first):
+    return device_pairs(
+        lambda z, y, x, c: (z + 1, y, x, c) if first <= z < Z_SIZE - 1 else None
+    )
+
+
+def pairs_up_below(last):
+    return device_pairs(lambda z, y, x, c: (z + 1, y, x, c) if z <= last else None)
+
+
+def pairs_down(last):
+    return device_pairs(lambda z, y, x, c: (z - 1, y, x, c) if 1 <= z <= last else None)
+
+
+def pairs_down_above(first):
+    return device_pairs(lambda z, y, x, c: (z - 1, y, x, c) if z >= first else None)
+
+
+def tie_kernel(*refs):
+    del refs
+
+
+def tie(value, *after):
+    any_spec = pl.BlockSpec(memory_space=pl.ANY)
+    return pl.pallas_call(
+        tie_kernel,
+        in_specs=[any_spec] * (1 + len(after)),
+        out_specs=any_spec,
+        out_shape=jax.ShapeDtypeStruct(value.shape, value.dtype),
+        input_output_aliases={0: 0},
+        name="tie",
+    )(value, *after)
+
+
+def join_kernel(*refs):
+    refs[-1][...] = jnp.zeros_like(refs[-1])
+
+
+class Rounds:
+    def __init__(self):
+        self.token = None
+
+    def gate(self, value):
+        return value if self.token is None else tie(value, self.token)
+
+    def after(self):
+        return () if self.token is None else (self.token,)
+
+    def close(self, *arrays):
+        arrays = list(arrays) + list(self.after())
+        self.token = pl.pallas_call(
+            join_kernel,
+            in_specs=[pl.BlockSpec(memory_space=pl.ANY)] * len(arrays),
+            out_specs=pl.BlockSpec(memory_space=pltpu.VMEM),
+            out_shape=jax.ShapeDtypeStruct((8, 128), jnp.float32),
+            name="join",
+        )(*arrays)
+
+
+def move(value, pairs):
+    return lax.ppermute(value, MESH_AXES, pairs)
+
+
+def line_hop(step, up, down):
+    return move(up, pairs_up(step - 1)), move(down, pairs_down(Z_SIZE - step))
+
+
+def rows_kernel(info, own, u1, u2, u3, d1, d2, d3, *rest):
+    other, out, sem = rest[:7], rest[7], rest[8]
+    z = info[0]
+    mine = (own, u1, u2, u3, d1, d2, d3)
+    waits = []
+    for k, parts in enumerate((other, mine)):
+        ups, downs = parts[1:4], parts[4:7]
+        target = out.at[k * Z_SIZE]
+        first = pltpu.make_async_copy(parts[0], target, sem.at[k * Z_SIZE])
+        first.start()
+        waits.append(first)
+        for s in range(1, Z_SIZE):
+            target = out.at[k * Z_SIZE + s]
+            below = pltpu.make_async_copy(ups[s - 1], target, sem.at[k * Z_SIZE + s])
+            above = pltpu.make_async_copy(downs[Z_SIZE - s - 1], target, sem.at[k * Z_SIZE + s])
+            pl.when(z >= s)(below.start)
+            pl.when(z < s)(above.start)
+            waits.append(below)
+    for copy in waits:
+        copy.wait()
+
+
+def line_blocks(z, mine, other):
+    any_spec = pl.BlockSpec(memory_space=pl.ANY)
+    block = mine[0]
+    return pl.pallas_call(
+        rows_kernel,
+        grid_spec=pltpu.PrefetchScalarGridSpec(
+            num_scalar_prefetch=1,
+            grid=(),
+            in_specs=[any_spec] * 14,
+            out_specs=pl.BlockSpec(memory_space=pltpu.VMEM),
+            scratch_shapes=[pltpu.SemaphoreType.DMA((2 * Z_SIZE,))],
+        ),
+        out_shape=jax.ShapeDtypeStruct((2 * Z_SIZE, *block.shape), block.dtype),
+        cost_estimate=pl.CostEstimate(
+            flops=0, bytes_accessed=32 * block.size, transcendentals=0
+        ),
+        compiler_params=pltpu.CompilerParams(vmem_limit_bytes=32 * 1024 * 1024),
+        name="line_blocks",
+    )(z[None], *mine, *other)
+
+
+def dense_kernel(info, *refs):
+    pieces, out, sem = refs[:10], refs[10], refs[11]
+    y, x, c = info[0], info[1], info[2]
+    zs = Z_SIZE // 2
+    copies = []
+    for k in range(2):
+        at_c = c if k == 0 else 1 - c
+        block, from_x, from_y, far_a, far_b = pieces[5 * k : 5 * k + 5]
+        targets = [
+            (block, out.at[:, y, x, at_c]),
+            (from_x, out.at[:, y, 1 - x, at_c]),
+            (from_y, out.at[:, 1 - y, x, at_c]),
+            (far_a, out.at[pl.ds(0, zs), 1 - y, 1 - x, at_c]),
+            (far_b, out.at[pl.ds(zs, zs), 1 - y, 1 - x, at_c]),
+        ]
+        for piece, target in targets:
+            copies.append(pltpu.make_async_copy(piece, target, sem.at[len(copies)]))
+    for copy in copies:
+        copy.start()
+    for copy in copies:
+        copy.wait()
+
+
+def dense_assemble(place, mine, other):
+    z, y, x, c = place
+    any_spec = pl.BlockSpec(memory_space=pl.ANY)
+    block = mine[0]
+    rows, n = block.shape[1:]
+    full = pl.pallas_call(
+        dense_kernel,
+        grid_spec=pltpu.PrefetchScalarGridSpec(
+            num_scalar_prefetch=1,
+            grid=(),
+            in_specs=[any_spec] * 10,
+            out_specs=pl.BlockSpec(memory_space=pltpu.VMEM),
+            scratch_shapes=[pltpu.SemaphoreType.DMA((10,))],
+        ),
+        out_shape=jax.ShapeDtypeStruct((Z_SIZE, Y_SIZE, X_SIZE, C_SIZE, rows, n), block.dtype),
+        cost_estimate=pl.CostEstimate(
+            flops=0, bytes_accessed=32 * block.size, transcendentals=0
+        ),
+        compiler_params=pltpu.CompilerParams(vmem_limit_bytes=32 * 1024 * 1024),
+        name="dense_assemble",
+    )(jnp.stack([y, x, c]), *mine, *other)
+    return full.reshape(-1, n)
+
+
+def half_order(z_to):
+    first = 10 * (z_to // 2)
+    if z_to % 2 == 0:
+        return [first, first + 1, first + 2, first + 3, first + 4]
+    return [first + 6, first + 7, first + 8, first + 9, first + 5]
+
+
+HALF_ORDER = [half_order(z_to) for z_to in range(Z_SIZE)]
+HALF_PLACE = [0] * (Z_SIZE * 5)
+for order_z in range(Z_SIZE):
+    for order_q in range(5):
+        HALF_PLACE[HALF_ORDER[order_z][order_q]] = order_z * 5 + order_q
+UNIT_HALVES = ((0, 2), (2, 4), (4, 5))
+
+
+def dense_gates(logits, chosen):
+    peak = jnp.max(jnp.where(chosen, logits, -jnp.inf), axis=-1, keepdims=True)
+    exponent = jnp.where(chosen, jnp.exp(logits - peak), 0.0)
+    return exponent / jnp.sum(exponent, axis=-1, keepdims=True)
+
+
+def mm(left, right):
+    return jnp.dot(left, right, preferred_element_type=jnp.float32)
+
+
+def weight_loads(pieces, w_s, sem, y):
+    zs = Z_SIZE // 2
+    count = len(pieces) // w_s.shape[0]
+    copies = []
+    for h in range(w_s.shape[0]):
+        places = [w_s.at[h, :, y]]
+        if count == 2:
+            places.append(w_s.at[h, :, 1 - y])
+        else:
+            places += [w_s.at[h, pl.ds(0, zs), 1 - y], w_s.at[h, pl.ds(zs, zs), 1 - y]]
+        for piece, place in zip(pieces[h * count : (h + 1) * count], places):
+            copies.append(pltpu.make_async_copy(piece, place, sem.at[len(copies)]))
+    return copies
+
+
+def expert_forward_kernel(info, slots, gates, rows, *rest, count, waits):
+    pieces = rest[:count]
+    out, kept, gate_up_out, w_s, in_sem = rest[count + waits :]
+    low = jnp.bfloat16
+    step = pl.program_id(0)
+    half = FF // 2
+    halves = w_s.shape[0]
+    loads = weight_loads(pieces, w_s, in_sem, info[0])
+
+    @pl.when(step == 0)
+    def _():
+        for load in loads:
+            load.start()
+
+    group, length, width = rows.shape
+    span = group * WIDE
+    iota = lax.broadcasted_iota(jnp.int32, (WIDE, length), 0)
+    gate_cols = []
+    for j in range(group):
+        pick = iota == slots[j]
+        one_hot = jnp.where(pick, 1.0, 0.0).astype(low)
+        gate_cols.append(jnp.sum(jnp.where(pick, gates[j], 0.0), axis=1, keepdims=True))
+        kept[j * WIDE : (j + 1) * WIDE, :] = mm(one_hot, rows[j]).astype(low)
+    gate_col = jnp.concatenate(gate_cols, axis=0)
+
+    @pl.when(step == 0)
+    def _():
+        for load in loads:
+            load.wait()
+
+    produced = None
+    for h in range(halves):
+        gate_up_w = w_s[h, :, :, :, : 2 * half].reshape(width, 2 * half)
+        down_t = w_s[h, :, :, :, 2 * half :].reshape(width, half)
+        gate_up = mm(kept[...], gate_up_w)
+        gate_up_out[:, 2 * h * half : 2 * (h + 1) * half] = gate_up
+        gate = gate_up[:, :half]
+        hidden = (gate * (1.0 / (1.0 + jnp.exp(-gate))) * gate_up[:, half:]).astype(low)
+        term = multiply_transposed(hidden, down_t)
+        produced = term if produced is None else produced + term
+    out[...] = (produced * gate_col).astype(low).reshape(group, WIDE, width)
+
+
+def expert_forward(place, halves, y, slots, gates, rows_in, pieces, buffer, after):
+    sources, length, width = rows_in.shape
+    _, rows, lanes = pieces[0].shape
+    half = FF // 2
+    low = jnp.bfloat16
+    group = 2
+    units = 2 * len(UNIT_HALVES)
+    any_spec = pl.BlockSpec(memory_space=pl.ANY)
+    row_spec = pl.BlockSpec((group, 1, length), lambda i, info: (i, 0, 0))
+    waits = list(after)
+    aliases = {}
+    if buffer is not None:
+        aliases = {4 + len(pieces): 0}
+        waits = [buffer] + waits
+    total = sources * WIDE
+    span = group * WIDE
+    return pl.pallas_call(
+        functools.partial(expert_forward_kernel, count=len(pieces), waits=len(waits)),
+        grid_spec=pltpu.PrefetchScalarGridSpec(
+            num_scalar_prefetch=1,
+            grid=(sources // group,),
+            in_specs=[
+                row_spec,
+                row_spec,
+                pl.BlockSpec((group, length, width), lambda i, info: (i, 0, 0)),
+            ]
+            + [any_spec] * (len(pieces) + len(waits)),
+            out_specs=[
+                pl.BlockSpec((group, WIDE, width), lambda i, info: (i, place, 0)),
+                pl.BlockSpec((span, width), lambda i, info: (i, 0)),
+                pl.BlockSpec((span, 2 * half * halves), lambda i, info: (i, 0)),
+            ],
+            scratch_shapes=[
+                pltpu.VMEM((halves, Z_SIZE, Y_SIZE, rows, lanes), low),
+                pltpu.SemaphoreType.DMA((6,)),
+            ],
+        ),
+        out_shape=[
+            jax.ShapeDtypeStruct((sources, units * WIDE, width), low),
+            jax.ShapeDtypeStruct((total, width), low),
+            jax.ShapeDtypeStruct((total, 2 * half * halves), jnp.float32),
+        ],
+        input_output_aliases=aliases,
+        compiler_params=pltpu.CompilerParams(vmem_limit_bytes=48 * 1024 * 1024),
+        cost_estimate=pl.CostEstimate(
+            flops=2 * total * width * (3 * half * halves + length),
+            bytes_accessed=2 * (sources * length * width + 2 * total * width)
+            + 8 * total * half * halves
+            + 2 * halves * width * lanes,
+            transcendentals=total * half * halves,
+        ),
+        name="expert_forward",
+    )(y, slots, gates, rows_in, *pieces, *waits)
+
+
+def expert_back_kernel(info, slots, gates, dys, kept, gate_ups, *rest, count, waits):
+    pieces = rest[:count]
+    back, near_a_g, near_b_g, far_a_g, far_b_g = rest[count + waits : count + waits + 5]
+    w_s, x_s, gd_s, dgu_s, hid_s, g_s, in_sem, out_sem = rest[count + waits + 5 :]
+    low = jnp.bfloat16
+    full = jnp.float32
+    step = pl.program_id(0)
+    y = info[0]
+    expert = info[1]
+    half = FF // 2
+    zs = Z_SIZE // 2
+    halves = w_s.shape[0]
+    loads = weight_loads(pieces, w_s, in_sem, y)
+
+    @pl.when(step == 0)
+    def _():
+        for load in loads:
+            load.start()
+
+    group, length, width = dys.shape
+    span = group * WIDE
+    here = pl.ds(pl.multiple_of(step * span, span), span)
+    iota = lax.broadcasted_iota(jnp.int32, (WIDE, length), 0)
+    gate_cols = []
+    dy_parts = []
+    for j in range(group):
+        pick = iota == slots[j]
+        one_hot = jnp.where(pick, 1.0, 0.0).astype(low)
+        gate_col = jnp.sum(jnp.where(pick, gates[j], 0.0), axis=1, keepdims=True)
+        at = pl.multiple_of(step * span + j * WIDE, WIDE)
+        dy = mm(one_hot, dys[j])
+        gd_s[pl.ds(at, WIDE), :] = (dy * (residual_scale * gate_col)).astype(low)
+        dy_parts.append(dy.astype(low))
+        gate_cols.append(gate_col)
+    dy = jnp.concatenate(dy_parts, axis=0)
+    gate_col = jnp.concatenate(gate_cols, axis=0)
+    x_s[here, :] = kept[...]
+
+    @pl.when(step == 0)
+    def _():
+        for load in loads:
+            load.wait()
+
+    grad_copy = None
+    grad_gate = None
+    for h in range(halves):
+        gate_up_w = w_s[h, :, :, :, : 2 * half].reshape(width, 2 * half)
+        down_t = w_s[h, :, :, :, 2 * half :].reshape(width, half)
+        gate = gate_ups[:, 2 * h * half : (2 * h + 1) * half]
+        upper = gate_ups[:, (2 * h + 1) * half : (2 * h + 2) * half]
+        sigmoid = 1.0 / (1.0 + jnp.exp(-gate))
+        swish = gate * sigmoid
+        hidden = (swish * upper).astype(low)
+        hid_s[here, h * half : (h + 1) * half] = hidden
+        grad_plain = residual_scale * mm(dy, down_t)
+        term = jnp.sum(hidden.astype(full) * grad_plain, axis=1, keepdims=True)
+        grad_gate = term if grad_gate is None else grad_gate + term
+        grad_hidden = grad_plain * gate_col
+        dgu_s[here, 2 * h * half : (2 * h + 1) * half] = (
+            grad_hidden * upper * sigmoid * (1.0 + gate * (1.0 - sigmoid))
+        ).astype(low)
+        dgu_s[here, (2 * h + 1) * half : (2 * h + 2) * half] = (grad_hidden * swish).astype(low)
+        term = multiply_transposed(dgu_s[here, 2 * h * half : 2 * (h + 1) * half], gate_up_w)
+        grad_copy = term if grad_copy is None else grad_copy + term
+    back[:, :, :width] = grad_copy.astype(low).reshape(group, WIDE, width)
+    lane = lax.broadcasted_iota(jnp.int32, (span, 128), 1)
+    high = grad_gate.astype(low).astype(full)
+    extra = jnp.where(lane == expert, high, 0.0) + jnp.where(
+        lane == expert + 64, grad_gate - high, 0.0
+    )
+    back[:, :, width:] = extra.astype(low).reshape(group, WIDE, 128)
+
+    @pl.when(step == pl.num_programs(0) - 1)
+    def _():
+        piece = width // Z_SIZE
+        for h in range(halves):
+            for zz in range(Z_SIZE):
+                cols = slice(zz * piece, (zz + 1) * piece)
+                got = contract_rows(x_s[:, cols], dgu_s[:, 2 * h * half : 2 * (h + 1) * half])
+                g_s[h, zz, :, :, : 2 * half] = got.astype(low).reshape(2, piece // 2, 2 * half)
+                got = contract_rows(gd_s[:, cols], hid_s[:, h * half : (h + 1) * half])
+                g_s[h, zz, :, :, 2 * half :] = got.astype(low).reshape(2, piece // 2, half)
+        stores = [
+            (g_s.at[:, pl.ds(0, zs), y], near_a_g),
+            (g_s.at[:, pl.ds(zs, zs), y], near_b_g),
+            (g_s.at[:, pl.ds(0, zs), 1 - y], far_a_g),
+            (g_s.at[:, pl.ds(zs, zs), 1 - y], far_b_g),
+        ]
+        stores = [pltpu.make_async_copy(a, b, out_sem.at[i]) for i, (a, b) in enumerate(stores)]
+        for store in stores:
+            store.start()
+        for store in stores:
+            store.wait()
+
+
+def expert_backward(
+    place, halves, info, slots, gates, grads_in, kept, gate_ups, pieces, buffer, after
+):
+    sources, length, width = grads_in.shape
+    _, rows, lanes = pieces[0].shape
+    half = FF // 2
+    low = jnp.bfloat16
+    group = 2
+    units = 2 * len(UNIT_HALVES)
+    any_spec = pl.BlockSpec(memory_space=pl.ANY)
+    row_spec = pl.BlockSpec((group, 1, length), lambda i, info: (i, 0, 0))
+    waits = list(after)
+    aliases = {}
+    if buffer is not None:
+        aliases = {6 + len(pieces): 0}
+        waits = [buffer] + waits
+    total = sources * WIDE
+    span = group * WIDE
+    quarter = (halves, Z_SIZE // 2, rows, lanes)
+    result = pl.pallas_call(
+        functools.partial(expert_back_kernel, count=len(pieces), waits=len(waits)),
+        grid_spec=pltpu.PrefetchScalarGridSpec(
+            num_scalar_prefetch=1,
+            grid=(sources // group,),
+            in_specs=[
+                row_spec,
+                row_spec,
+                pl.BlockSpec((group, length, width), lambda i, info: (i, 0, 0)),
+                pl.BlockSpec((span, width), lambda i, info: (i, 0)),
+                pl.BlockSpec((span, 2 * half * halves), lambda i, info: (i, 0)),
+            ]
+            + [any_spec] * (len(pieces) + len(waits)),
+            out_specs=[
+                pl.BlockSpec((group, WIDE, width + 128), lambda i, info: (i, place, 0)),
+            ]
+            + [any_spec] * 4,
+            scratch_shapes=[
+                pltpu.VMEM((halves, Z_SIZE, Y_SIZE, rows, lanes), low),
+                pltpu.VMEM((total, width), low),
+                pltpu.VMEM((total, width), low),
+                pltpu.VMEM((total, 2 * half * halves), low),
+                pltpu.VMEM((total, half * halves), low),
+                pltpu.VMEM((halves, Z_SIZE, Y_SIZE, rows, lanes), low),
+                pltpu.SemaphoreType.DMA((6,)),
+                pltpu.SemaphoreType.DMA((4,)),
+            ],
+        ),
+        out_shape=[jax.ShapeDtypeStruct((sources, units * WIDE, width + 128), low)]
+        + [jax.ShapeDtypeStruct(quarter, low)] * 4,
+        input_output_aliases=aliases,
+        compiler_params=pltpu.CompilerParams(vmem_limit_bytes=60 * 1024 * 1024),
+        cost_estimate=pl.CostEstimate(
+            flops=2 * total * width * (6 * half * halves + length),
+            bytes_accessed=2 * (sources * length * width + 2 * total * width)
+            + 8 * total * half * halves
+            + 4 * halves * width * lanes,
+            transcendentals=total * half * halves,
+        ),
+        name="expert_backward",
+    )(info, slots, gates, grads_in, kept, gate_ups, *pieces, *waits)
+    return result[0], result[1:]
+
+
+def turn_halves(value):
+    lanes = value.shape[-1]
+    lane = lax.broadcasted_iota(jnp.int32, value.shape, 1)
+    ahead = pltpu.roll(value, lanes - HEAD_SIZE // 2, 1)
+    behind = pltpu.roll(value, HEAD_SIZE // 2, 1)
+    return jnp.where(lane % HEAD_SIZE < HEAD_SIZE // 2, -ahead, behind)
+
+
+def heads_of(value, first, count):
+    return jnp.concatenate(
+        [value[:, (first + i) * HEAD_SIZE : (first + i + 1) * HEAD_SIZE] for i in range(count)],
+        axis=0,
+    )
+
+
+ROW_BLOCK = 128
+PAIR = 2
+GROUP = QUERY_HEADS // KEY_VALUE_HEADS
+QUERY_LANES = PAIR * GROUP * HEAD_SIZE
+KEY_LANES = PAIR * HEAD_SIZE
+
+
+def block_mask(block, length):
+    shape = (ROW_BLOCK, (block + 1) * ROW_BLOCK)
+    row = lax.broadcasted_iota(jnp.int32, shape, 0) + block * ROW_BLOCK
+    column = lax.broadcasted_iota(jnp.int32, shape, 1)
+    allowed = jnp.where((column <= row) & (column < length), 1, 0)
+    return jnp.concatenate([allowed] * GROUP, axis=0) > 0
+
+
+def attention_kernel(
+    length, tokens, gain, wq, wk, wv, cosine, sine, *rest
+):
+    h1, q, k, v, mixed, lse, h_s, lse_s = rest[-8:]
+    step = pl.program_id(0)
+    low = jnp.bfloat16
+    rows = tokens.shape[0]
+
+    @pl.when(step == 0)
+    def _():
+        value = tokens[...].astype(jnp.float32)
+        hidden = (value * rms_inverse(value) * gain[...]).astype(low)
+        h_s[...] = hidden
+        h1[...] = hidden
+
+    lane = lax.broadcasted_iota(jnp.int32, (rows, 128), 1)
+    cos = cosine[...]
+    sin = sine[...]
+    query = mm(h_s[...], wq[...])
+    query = (query * cos + turn_halves(query) * sin).astype(low)
+    key = mm(h_s[...], wk[...])
+    key = (key * cos[:, :KEY_LANES] + turn_halves(key) * sin[:, :KEY_LANES]).astype(low)
+    value = mm(h_s[...], wv[...]).astype(low)
+    q[...] = query
+    k[...] = key
+    v[...] = value
+    blocks = rows // ROW_BLOCK
+    totals = [[] for _ in range(PAIR * GROUP)]
+    masks = [block_mask(block, length[0]) for block in range(blocks)]
+    outs = [[] for _ in range(PAIR * GROUP)]
+    for head in range(PAIR):
+        key_h = key[:, head * HEAD_SIZE : (head + 1) * HEAD_SIZE]
+        value_h = value[:, head * HEAD_SIZE : (head + 1) * HEAD_SIZE]
+        for block in range(blocks):
+            keys = (block + 1) * ROW_BLOCK
+            query_h = heads_of(
+                query[block * ROW_BLOCK : (block + 1) * ROW_BLOCK], head * GROUP, GROUP
+            )
+            scores = multiply_transposed(query_h, key_h[:keys]) * score_scale
+            scores = jnp.where(masks[block], scores, masked_score)
+            peak = jnp.max(scores, axis=1, keepdims=True)
+            exponent = jnp.exp(scores - peak)
+            total = jnp.sum(exponent, axis=1, keepdims=True)
+            weights = (exponent / total).astype(low)
+            out = mm(weights, value_h[:keys]).astype(low)
+            log_total = peak + jnp.log(total)
+            for i in range(GROUP):
+                part = slice(i * ROW_BLOCK, (i + 1) * ROW_BLOCK)
+                outs[head * GROUP + i].append(out[part])
+                totals[head * GROUP + i].append(log_total[part])
+    mixed[...] = jnp.concatenate([jnp.concatenate(o, axis=0) for o in outs], axis=1)
+
+    @pl.when(step == 0)
+    def _():
+        lse_s[...] = jnp.zeros_like(lse_s)
+
+    kept = lse_s[...]
+    for i in range(PAIR * GROUP):
+        column = jnp.concatenate(totals[i], axis=0)
+        kept = jnp.where(lane == step * PAIR * GROUP + i, column, kept)
+    lse_s[...] = kept
+    lse[...] = kept
+
+
+def attention_forward(length, tokens, gain, weight, cosine, sine, after=()):
+    rows, width = tokens.shape
+    steps = KEY_VALUE_HEADS // PAIR
+    low = jnp.bfloat16
+    query_total = QUERY_HEADS * HEAD_SIZE
+    key_total = KEY_VALUE_HEADS * HEAD_SIZE
+    key_at = query_total // KEY_LANES
+    value_at = key_at + steps
+    whole = lambda shape: pl.BlockSpec(shape, lambda i, n: (0, 0))
+    cols = lambda lanes, at: pl.BlockSpec((width, lanes), lambda i, n: (0, at + i))
+    part = lambda lanes: pl.BlockSpec((rows, lanes), lambda i, n: (0, i))
+    return pl.pallas_call(
+        attention_kernel,
+        grid_spec=pltpu.PrefetchScalarGridSpec(
+            num_scalar_prefetch=1,
+            grid=(steps,),
+            in_specs=[
+                whole((rows, width)),
+                whole((1, width)),
+                cols(QUERY_LANES, 0),
+                cols(KEY_LANES, key_at),
+                cols(KEY_LANES, value_at),
+                whole((rows, QUERY_LANES)),
+                whole((rows, QUERY_LANES)),
+            ]
+            + [pl.BlockSpec(memory_space=pl.ANY)] * len(after),
+            out_specs=[
+                whole((rows, width)),
+                part(QUERY_LANES),
+                part(KEY_LANES),
+                part(KEY_LANES),
+                part(QUERY_LANES),
+                whole((rows, 128)),
+            ],
+            scratch_shapes=[pltpu.VMEM((rows, width), low), pltpu.VMEM((rows, 128), jnp.float32)],
+        ),
+        out_shape=[
+            jax.ShapeDtypeStruct((rows, width), low),
+            jax.ShapeDtypeStruct((rows, query_total), low),
+            jax.ShapeDtypeStruct((rows, key_total), low),
+            jax.ShapeDtypeStruct((rows, key_total), low),
+            jax.ShapeDtypeStruct((rows, query_total), low),
+            jax.ShapeDtypeStruct((rows, 128), jnp.float32),
+        ],
+        compiler_params=pltpu.CompilerParams(vmem_limit_bytes=48 * 1024 * 1024),
+        cost_estimate=pl.CostEstimate(
+            flops=2 * rows * width * (query_total + 2 * key_total)
+            + 4 * QUERY_HEADS * rows * rows * HEAD_SIZE,
+            bytes_accessed=2 * width * (query_total + 2 * key_total) + 10 * rows * width,
+            transcendentals=QUERY_HEADS * rows * rows,
+        ),
+        name="attention_forward",
+    )(length, tokens, gain, weight, weight, weight, cosine, sine, *after)
+
+
+def attention_back_kernel(
+    length, dbranch, wo, q, k, v, lse, h1, wq, wk, wv, cosine, sine, *rest, first
+):
+    grads, dh1, dh_s = rest[-3:]
+    step = pl.program_id(0)
+    low = jnp.bfloat16
+    full = jnp.float32
+    rows = dbranch.shape[0]
+    blocks = rows // ROW_BLOCK
+    dmixed = mm(dbranch[...], wo[...]).astype(low)
+    lane = lax.broadcasted_iota(jnp.int32, (rows, 128), 1)
+    kept = lse[...]
+    query, key, value = q[...], k[...], v[...]
+    columns = [
+        jnp.sum(jnp.where(lane == (step + first) * PAIR * GROUP + i, kept, 0.0), axis=1, keepdims=True)
+        for i in range(PAIR * GROUP)
+    ]
+    masks = [block_mask(block, length[0]) for block in range(blocks)]
+    dq = [[] for _ in range(PAIR * GROUP)]
+    dks, dvs = [], []
+    for head in range(PAIR):
+        key_h = key[:, head * HEAD_SIZE : (head + 1) * HEAD_SIZE]
+        value_h = value[:, head * HEAD_SIZE : (head + 1) * HEAD_SIZE]
+        dk = [None] * blocks
+        dv = [None] * blocks
+        for block in range(blocks):
+            keys = (block + 1) * ROW_BLOCK
+            at = slice(block * ROW_BLOCK, (block + 1) * ROW_BLOCK)
+            query_h = heads_of(query[at], head * GROUP, GROUP)
+            dmixed_h = heads_of(dmixed[at], head * GROUP, GROUP)
+            log_total = jnp.concatenate(
+                [columns[head * GROUP + i][at] for i in range(GROUP)], axis=0
+            )
+            scores = multiply_transposed(query_h, key_h[:keys]) * score_scale
+            scores = jnp.where(masks[block], scores, masked_score)
+            probs = jnp.exp(scores - log_total)
+            dprobs = multiply_transposed(dmixed_h, value_h[:keys])
+            delta = jnp.sum(probs * dprobs, axis=1, keepdims=True)
+            dscores = (probs * (dprobs - delta)).astype(low)
+            dquery = mm(dscores, key_h[:keys]) * score_scale
+            dkey = contract_rows(dscores, query_h) * score_scale
+            dvalue = contract_rows(probs.astype(low), dmixed_h)
+            for i in range(GROUP):
+                dq[head * GROUP + i].append(dquery[i * ROW_BLOCK : (i + 1) * ROW_BLOCK])
+            for b in range(block + 1):
+                part = slice(b * ROW_BLOCK, (b + 1) * ROW_BLOCK)
+                dk[b] = dkey[part] if dk[b] is None else dk[b] + dkey[part]
+                dv[b] = dvalue[part] if dv[b] is None else dv[b] + dvalue[part]
+        dks.append(jnp.concatenate(dk, axis=0))
+        dvs.append(jnp.concatenate(dv, axis=0))
+    cos = cosine[...]
+    sin = sine[...]
+    dquery = jnp.concatenate([jnp.concatenate(o, axis=0) for o in dq], axis=1)
+    dquery = (dquery * cos - turn_halves(dquery * sin)).astype(low)
+    dkey = jnp.concatenate(dks, axis=1)
+    dkey = (dkey * cos[:, :KEY_LANES] - turn_halves(dkey * sin[:, :KEY_LANES])).astype(low)
+    dvalue = jnp.concatenate(dvs, axis=1).astype(low)
+    hidden = h1[...]
+    grads[:, :QUERY_LANES] = contract_rows(hidden, dquery).astype(low)
+    both = contract_rows(hidden, jnp.concatenate([dkey, dvalue], axis=1)).astype(low)
+    grads[:, QUERY_LANES:] = both
+    term = (
+        multiply_transposed(dquery, wq[...])
+        + multiply_transposed(dkey, wk[...])
+        + multiply_transposed(dvalue, wv[...])
+    )
+
+    @pl.when(step == 0)
+    def _():
+        dh_s[...] = term
+
+    @pl.when(step > 0)
+    def _():
+        dh_s[...] += term
+
+    @pl.when(step == pl.num_programs(0) - 1)
+    def _():
+        dh1[...] = dh_s[...]
+
+
+def attention_backward(
+    length, dbranch, out_t, q, k, v, lse, h1, weight, cosine, sine, first, steps, after=()
+):
+    rows, width = dbranch.shape
+    pairs = KEY_VALUE_HEADS // PAIR
+    low = jnp.bfloat16
+    full = jnp.float32
+    query_total = QUERY_HEADS * HEAD_SIZE
+    key_total = KEY_VALUE_HEADS * HEAD_SIZE
+    key_at = query_total // KEY_LANES
+    value_at = key_at + pairs
+    whole = lambda shape: pl.BlockSpec(shape, lambda i, n: (0, 0))
+    cols = lambda lanes, at: pl.BlockSpec((width, lanes), lambda i, n: (0, at + first + i))
+    part = lambda lanes: pl.BlockSpec((rows, lanes), lambda i, n: (0, first + i))
+    lanes = QUERY_LANES + 2 * KEY_LANES
+    return pl.pallas_call(
+        functools.partial(attention_back_kernel, first=first),
+        grid_spec=pltpu.PrefetchScalarGridSpec(
+            num_scalar_prefetch=1,
+            grid=(steps,),
+            in_specs=[
+                whole((rows, width)),
+                cols(QUERY_LANES, 0),
+                part(QUERY_LANES),
+                part(KEY_LANES),
+                part(KEY_LANES),
+                whole((rows, 128)),
+                whole((rows, width)),
+                cols(QUERY_LANES, 0),
+                cols(KEY_LANES, key_at),
+                cols(KEY_LANES, value_at),
+                whole((rows, QUERY_LANES)),
+                whole((rows, QUERY_LANES)),
+            ]
+            + [pl.BlockSpec(memory_space=pl.ANY)] * len(after),
+            out_specs=[pl.BlockSpec((width, lanes), lambda i, n: (0, i)), whole((rows, width))],
+            scratch_shapes=[pltpu.VMEM((rows, width), full)],
+        ),
+        out_shape=[
+            jax.ShapeDtypeStruct((width, steps * lanes), low),
+            jax.ShapeDtypeStruct((rows, width), full),
+        ],
+        compiler_params=pltpu.CompilerParams(vmem_limit_bytes=48 * 1024 * 1024),
+        cost_estimate=pl.CostEstimate(
+            flops=4 * rows * width * (query_total + 2 * key_total)
+            + 2 * rows * width * query_total
+            + 10 * QUERY_HEADS * rows * rows * HEAD_SIZE,
+            bytes_accessed=4 * width * (query_total + 2 * key_total) + 2 * width * width + 14 * rows * width,
+            transcendentals=QUERY_HEADS * rows * rows,
+        ),
+        name="attention_backward",
+    )(length, dbranch, out_t, q, k, v, lse, h1, weight, weight, weight, cosine, sine, *after)
+
+
+def combine_kernel(slots, values, *rest):
+    other, own, p_s = rest[-3:]
+    step = pl.program_id(0)
+    length = slots.shape[2]
+    iota = lax.broadcasted_iota(jnp.int32, (WIDE, length), 0)
+    for u in range(slots.shape[1]):
+        pick = iota == slots[0, u : u + 1, :]
+        p_s[u * WIDE : (u + 1) * WIDE, :] = jnp.where(pick, 1.0, 0.0).astype(jnp.bfloat16)
+    result = contract_rows(p_s[...], values[0]).astype(jnp.bfloat16)
+
+    @pl.when(step < Z_SIZE)
+    def _():
+        other[0] = result
+
+    @pl.when(step >= Z_SIZE)
+    def _():
+        own[0] = result
+
+
+def combine(slots, values, after=()):
+    sources, units, length = slots.shape
+    n = values.shape[-1]
+    low = jnp.bfloat16
+    return pl.pallas_call(
+        combine_kernel,
+        grid=(sources,),
+        in_specs=[
+            pl.BlockSpec((1, units, length), lambda i: (i, 0, 0)),
+            pl.BlockSpec((1, units * WIDE, n), lambda i: (i, 0, 0)),
+        ]
+        + [pl.BlockSpec(memory_space=pl.ANY)] * len(after),
+        out_specs=[
+            pl.BlockSpec((1, length, n), lambda i: (jnp.minimum(i, Z_SIZE - 1), 0, 0)),
+            pl.BlockSpec((1, length, n), lambda i: (jnp.maximum(i - Z_SIZE, 0), 0, 0)),
+        ],
+        out_shape=[jax.ShapeDtypeStruct((Z_SIZE, length, n), low)] * 2,
+        scratch_shapes=[pltpu.VMEM((units * WIDE, length), low)],
+        compiler_params=pltpu.CompilerParams(vmem_limit_bytes=60 * 1024 * 1024),
+        cost_estimate=pl.CostEstimate(
+            flops=2 * sources * units * WIDE * length * n,
+            bytes_accessed=sources * (units * WIDE + length) * n * 2,
+            transcendentals=0,
+        ),
+        name="combine",
+    )(slots, values, *after)
+
+
+def line_terms(own, moved):
+    return [own[0].astype(jnp.float32) + moved[0].astype(jnp.float32)] + [
+        plus(own[s], moved[s]).astype(jnp.bfloat16) for s in range(1, Z_SIZE)
+    ]
+
+
+def line_first(terms):
+    return terms[1], terms[3]
+
+
+def weight_chunks(gate_up_weight, down_weight):
+    experts, rows = gate_up_weight.shape[0], gate_up_weight.shape[1]
+    gate, upper = gate_up_weight[..., :FF], gate_up_weight[..., FF:]
+    down_t = down_weight.transpose(0, 2, 1)
+    half = FF // 2
+
+    def one(q):
+        cols = slice((q % 2) * half, (q % 2 + 1) * half)
+        return jnp.concatenate([part[q // 2, :, cols] for part in (gate, upper, down_t)], axis=-1)
+
+    return [
+        jnp.stack([one(HALF_ORDER[z_to][j]) for z_to in range(Z_SIZE)]) for j in range(5)
+    ]
+
+
+def along_z(own, got, z):
+    result = jnp.zeros((Z_SIZE, *own.shape), own.dtype)
+    result = lax.dynamic_update_slice_in_dim(result, own[None], z, 0)
+    for step in range(1, Z_SIZE):
+        result = lax.dynamic_update_slice_in_dim(
+            result, got[step - 1][None], (z + Z_SIZE - step) % Z_SIZE, 0
+        )
+    return result
+
+
+def shift_sends(rounds, chunk, z, steps=(1, 2, 3), axis=0):
+    return [
+        move(
+            rounds.gate(lax.dynamic_index_in_dim(chunk, (z + step) % Z_SIZE, axis, keepdims=False)),
+            pairs_shift(step),
+        )
+        for step in steps
+    ]
+
+
+class DenseScatter:
+    def __init__(self, rounds, term, place):
+        self.rounds, self.place = rounds, place
+        z, y, x, c = place
+        rows, n = term.shape
+        rows = rows // (Z_SIZE * Y_SIZE * X_SIZE * C_SIZE)
+        blocks = term.reshape(Z_SIZE, Y_SIZE, X_SIZE, C_SIZE, rows, n)
+
+        def block(at_y, at_x, at_c):
+            got = lax.dynamic_slice(
+                blocks, (0, at_y, at_x, at_c, 0, 0), (Z_SIZE, 1, 1, 1, rows, n)
+            )
+            return got.reshape(Z_SIZE, rows, n)
+
+        order = [(y, x), (y, 1 - x), (1 - y, x), (1 - y, 1 - x)]
+        self.mine = [block(at_y, at_x, c) for at_y, at_x in order]
+        self.theirs = jnp.stack([block(at_y, at_x, 1 - c) for at_y, at_x in order])
+
+    def cores(self):
+        self.got = move(self.rounds.gate(self.theirs), PAIRS_C)
+        return [self.got]
+
+    def first(self):
+        low = jnp.bfloat16
+        zs = Z_SIZE // 2
+        self.near, self.to_x, self.to_y, far = [
+            plus(self.mine[i], self.got[i]) for i in range(4)
+        ]
+        gate = self.rounds.gate
+        self.via_x = move(gate(far[:zs].astype(low)), PAIRS_X)
+        self.via_y = move(gate(far[zs:].astype(low)), PAIRS_Y)
+        self.x_a = move(gate(self.to_x[:zs].astype(low)), PAIRS_X)
+        self.y_b = move(gate(self.to_y[zs:].astype(low)), PAIRS_Y)
+        return [self.via_x, self.via_y, self.x_a, self.y_b]
+
+    def second(self):
+        low = jnp.bfloat16
+        zs = Z_SIZE // 2
+        gate = self.rounds.gate
+        self.x_b = move(gate(plus(self.to_x[zs:], self.via_y).astype(low)), PAIRS_X)
+        self.y_a = move(gate(plus(self.to_y[:zs], self.via_x).astype(low)), PAIRS_Y)
+        return [self.x_b, self.y_a]
+
+    def along(self):
+        zs = Z_SIZE // 2
+        z = self.place[0]
+        total = jnp.concatenate(
+            [
+                plus(self.near[:zs], self.x_a) + self.y_a.astype(jnp.float32),
+                plus(self.near[zs:], self.x_b) + self.y_b.astype(jnp.float32),
+            ]
+        ).astype(jnp.bfloat16)
+        self.own = lax.dynamic_index_in_dim(total, z, 0, keepdims=False)
+        self.parts = shift_sends(self.rounds, total, z)
+        return self.parts
+
+    def result(self):
+        return plus(self.own, self.parts[0]) + plus(self.parts[1], self.parts[2])
+
+
+def plus(a, b):
+    return a.astype(jnp.float32) + b.astype(jnp.float32)
+
+
+def ring_total(own, x_a, second):
+    y_b, y_a, x_b = second
+    return jnp.concatenate(
+        [plus(own[0], x_a) + y_a.astype(jnp.float32), plus(own[1], x_b) + y_b.astype(jnp.float32)],
+        axis=1,
+    ).astype(jnp.bfloat16)
+
+
+def body(
+    tokens,
+    cotangent,
+    lengths,
+    routes,
+    slots,
+    first_gain,
+    qkv_weight,
+    out_weight,
+    second_gain,
+    router_weight,
+    gate_up_weight,
+    down_weight,
+):
+    low = jnp.bfloat16
+    full = jnp.float32
+    dp_index = lax.axis_index("dp")
+    expert_index = lax.axis_index("expert")
+    z, y = dp_index // Y_SIZE, dp_index % Y_SIZE
+    x, c = expert_index // C_SIZE, expert_index % C_SIZE
+    sequence_length = tokens.shape[0]
+    width = tokens.shape[1]
+    rows = gate_up_weight.shape[1]
+
+    chosen_by = routes[None, :, :] == jnp.arange(EXPERTS, dtype=jnp.int32)[:, None, None]
+    slot_table = jnp.sum(jnp.where(chosen_by, slots[None, :, :] + 1, 0), axis=-1) - 1
+    place = (z, y, x, c)
+    zs = Z_SIZE // 2
+    steps = range(1, Z_SIZE)
+    rounds = Rounds()
+    gate = rounds.gate
+
+    small = jnp.concatenate(
+        [router_weight, first_gain[:, None], second_gain[:, None]], axis=1
+    )
+    small = jnp.pad(small, ((0, 0), (0, 128 - small.shape[1])))
+    shard = jnp.concatenate([qkv_weight, small], axis=1)
+    out_shard = out_weight.T
+    table = slot_table.astype(low)
+
+    got = [move(shard, pairs_shift(s)) for s in steps]
+    tables = [move(table, pairs_shift(s)) for s in steps]
+    cuts = weight_chunks(gate_up_weight, down_weight)
+    rounds.close(*got, *tables, *cuts)
+
+    near, far, moved = [None] * 5, [None] * 5, [None] * 5
+
+    def send_half(q):
+        return shift_sends(rounds, cuts[q], z)
+
+    def keep_half(q, got):
+        moved[q] = along_z(lax.dynamic_index_in_dim(cuts[q], z, 0, keepdims=False), got, z)
+
+    def send_near(q):
+        moved[q] = gate(moved[q])
+        near[q] = (move(moved[q], PAIRS_X), move(moved[q], PAIRS_Y))
+        return near[q]
+
+    def send_far(q):
+        far[q] = (move(gate(near[q][1][:zs]), PAIRS_X), move(gate(near[q][0][zs:]), PAIRS_Y))
+        return far[q]
+
+    block = gate(along_z(shard, got, z))
+    out_got = [move(s, pairs_shift(i + 1)) for i, s in enumerate([gate(out_shard)] * 3)]
+    half_got = send_half(0)
+    from_x, from_y = move(block, PAIRS_X), move(block, PAIRS_Y)
+    block_c = move(block, PAIRS_C)
+    tables = jnp.stack([table] + tables)
+    tables_c = move(gate(tables), PAIRS_C)
+    rounds.close(from_x, from_y, block_c, *out_got, *half_got, tables_c)
+    keep_half(0, half_got)
+    far_a, far_b = move(gate(from_y[:zs]), PAIRS_X), move(gate(from_x[zs:]), PAIRS_Y)
+    from_x_c, from_y_c = move(gate(from_x), PAIRS_C), move(gate(from_y), PAIRS_C)
+    out_block = gate(along_z(out_shard, out_got, z))
+    out_x, out_y = move(out_block, PAIRS_X), move(out_block, PAIRS_Y)
+    out_block_c = move(out_block, PAIRS_C)
+    half_got = send_half(1)
+    rounds.close(far_a, far_b, from_x_c, from_y_c, out_x, out_y, out_block_c, *half_got)
+    keep_half(1, half_got)
+    far_a_c, far_b_c = move(gate(far_a), PAIRS_C), move(gate(far_b), PAIRS_C)
+    out_far_a, out_far_b = move(gate(out_y[:zs]), PAIRS_X), move(gate(out_x[zs:]), PAIRS_Y)
+    out_x_c, out_y_c = move(gate(out_x), PAIRS_C), move(gate(out_y), PAIRS_C)
+    half_got = send_half(2)
+    rounds.close(far_a_c, far_b_c, out_far_a, out_far_b, out_x_c, out_y_c, *half_got, *send_near(0))
+    keep_half(2, half_got)
+    first_pack = dense_assemble(
+        place,
+        (block, from_x, from_y, far_a, far_b),
+        (block_c, from_x_c, from_y_c, far_a_c, far_b_c),
+    )
+    small_full = first_pack[:, qkv_weight.shape[1] :]
+    router_full = small_full[:, :EXPERTS]
+    gain_one = small_full[:, EXPERTS].astype(full)
+    gain_two = small_full[:, EXPERTS + 1].astype(full)
+
+    inputs = tokens.astype(full)
+    inverse_one = rms_inverse(inputs)
+    normal_one = inputs * inverse_one
+    cosine_table, sine_table = rope_tables(sequence_length)
+    cosine_table = jnp.tile(cosine_table, (1, QUERY_LANES // HEAD_SIZE))
+    sine_table = jnp.tile(sine_table, (1, QUERY_LANES // HEAD_SIZE))
+    out_far_a_c, out_far_b_c = move(gate(out_far_a), PAIRS_C), move(gate(out_far_b), PAIRS_C)
+    half_got = send_half(3)
+    hidden_one, query_rows, keys, value_rows, mixed, log_totals = attention_forward(
+        lengths, tokens, gain_one[None, :], first_pack, cosine_table, sine_table, rounds.after()
+    )
+    rounds.close(out_far_a_c, out_far_b_c, *half_got, *send_near(1), mixed)
+    keep_half(3, half_got)
+    out_t = dense_assemble(
+        place,
+        (out_block, out_x, out_y, out_far_a, out_far_b),
+        (out_block_c, out_x_c, out_y_c, out_far_a_c, out_far_b_c),
+    )
+    half_got = send_half(4)
+    branch = multiply_transposed(mixed, out_t)
+    middle = inputs + residual_scale * branch
+    inverse_two = rms_inverse(middle)
+    normal_two = middle * inverse_two
+    hidden_two = (normal_two * gain_two).astype(low)
+    grad_out = cotangent.astype(full)
+
+    rounds.close(*half_got, *send_near(2), hidden_two)
+    keep_half(4, half_got)
+    sent = gate(hidden_two)
+    up, down = line_hop(1, sent, sent)
+    own_c = move(sent, PAIRS_C)
+    rounds.close(up, down, own_c, *send_near(3), *send_far(0))
+    hops, hops_c = [(up, down)], []
+    for step, sends in ((2, lambda: (*send_near(4), *send_far(1))), (3, lambda: (*send_far(2), *send_far(3)))):
+        up, down = gate(hops[-1][0]), gate(hops[-1][1])
+        hops[-1] = (up, down)
+        hops_c.append((move(up, PAIRS_C), move(down, PAIRS_C)))
+        hops.append(line_hop(step, up, down))
+        rounds.close(*hops_c[-1], *hops[-1], *sends())
+    up, down = hops[-1]
+    hops_c.append((move(gate(up), PAIRS_C), move(gate(down), PAIRS_C)))
+    rounds.close(*hops_c[-1], *send_far(4))
+
+    def gathered(own, own_c, hops, hops_c):
+        return line_blocks(
+            z,
+            (own, *[h[0] for h in hops], *[h[1] for h in hops]),
+            (own_c, *[h[0] for h in hops_c], *[h[1] for h in hops_c]),
+        )
+
+    rows_in = gathered(hidden_two, own_c, hops, hops_c)
+    rings = [
+        (
+            [p for q in range(*cut) for p in (moved[q], near[q][1])],
+            [p for q in range(*cut) for p in (near[q][0], *far[q])],
+        )
+        for cut in UNIT_HALVES
+    ]
+    slots_in = jnp.concatenate([tables_c, tables], axis=0).astype(jnp.int32)
+    logits_in = jnp.einsum("de,itd->iet", router_full, rows_in, preferred_element_type=full)
+    chosen_in = slots_in >= 0
+    peak_in = jnp.max(jnp.where(chosen_in, logits_in, -jnp.inf), axis=1, keepdims=True)
+    exponent_in = jnp.where(chosen_in, jnp.exp(logits_in - peak_in), 0.0)
+    gates_in = exponent_in / jnp.sum(exponent_in, axis=1, keepdims=True)
+
+    units = range(len(UNIT_HALVES))
+    even = z % 2 == 0
+    ids = []
+    for group in (1 - x, x):
+        base = EXPERTS // (X_SIZE * C_SIZE) * (group * C_SIZE + c) + 5 * (z // 2)
+        ids += [base + jnp.where(even, 0, 3), base + jnp.where(even, 1, 4), base + 2]
+    unit_slots = [lax.dynamic_index_in_dim(slots_in, expert, 1, keepdims=True) for expert in ids]
+    unit_gates = [lax.dynamic_index_in_dim(gates_in, expert, 1, keepdims=True) for expert in ids]
+    pairs = len(UNIT_HALVES)
+    sizes = [end - first for first, end in UNIT_HALVES]
+    all_slots = jnp.concatenate(unit_slots, axis=1)
+    infos = [jnp.stack([y, expert]).astype(jnp.int32) for expert in ids]
+    buffer = None
+    saved = {}
+
+    def run_forward(pair, own):
+        nonlocal buffer
+        at = pair + (pairs if own else 0)
+        buffer, *saved[at] = expert_forward(
+            at,
+            sizes[pair],
+            infos[at],
+            unit_slots[at],
+            unit_gates[at],
+            rows_in,
+            rings[pair][0 if own else 1],
+            buffer,
+            rounds.after(),
+        )
+
+    sent = gate(cotangent)
+    dy_c = move(sent, PAIRS_C)
+    dy_hops, dy_hops_c = [], []
+    up = down = sent
+    for pair in range(pairs):
+        if pair > 0:
+            up, down = gate(up), gate(down)
+            dy_hops[-1] = (up, down)
+            dy_hops_c.append((move(up, PAIRS_C), move(down, PAIRS_C)))
+        up, down = line_hop(pair + 1, up, down)
+        dy_hops.append((up, down))
+        run_forward(pair, False)
+        run_forward(pair, True)
+        rounds.close(up, down, saved[pair + pairs][0], *(dy_hops_c[-1] if dy_hops_c else (dy_c,)))
+    up, down = gate(up), gate(down)
+    dy_hops[-1] = (up, down)
+    dy_hops_c.append((move(up, PAIRS_C), move(down, PAIRS_C)))
+    mix_other, mix_own = combine(all_slots, buffer, rounds.after())
+    rounds.close(mix_other, *dy_hops_c[-1])
+    mix_moved = move(gate(mix_other), PAIRS_C)
+    grads_in = gathered(cotangent, dy_c, dy_hops, dy_hops_c)
+    rounds.close(mix_moved, grads_in)
+
+    back = None
+    grads = [[None, None] for _ in units]
+
+    def run_back(pair, own):
+        nonlocal back
+        at = pair + (pairs if own else 0)
+        back, grads[pair][1 if own else 0] = expert_backward(
+            at,
+            sizes[pair],
+            infos[at],
+            unit_slots[at],
+            unit_gates[at],
+            grads_in,
+            *saved[at],
+            rings[pair][0 if own else 1],
+            back,
+            rounds.after(),
+        )
+
+    vias, firsts, seconds = [None] * 3, [None] * 3, [None] * 3
+
+    def send_via(u):
+        vias[u] = (move(gate(grads[u][0][2]), PAIRS_X), move(gate(grads[u][0][3]), PAIRS_Y))
+        return vias[u]
+
+    def send_first(u):
+        firsts[u] = (move(gate(grads[u][0][0]), PAIRS_X), move(gate(grads[u][1][3]), PAIRS_Y))
+        return firsts[u]
+
+    def send_second(u):
+        via_x, via_y = vias[u]
+        seconds[u] = (
+            move(gate(plus(grads[u][0][1], via_y).astype(low)), PAIRS_X),
+            move(gate(plus(grads[u][1][2], via_x).astype(low)), PAIRS_Y),
+        )
+        return seconds[u]
+
+    def total_of(u):
+        x_b, y_a = seconds[u]
+        x_a, y_b = firsts[u]
+        return ring_total(grads[u][1], x_a, (y_b, y_a, x_b))
+
+    def hop_sum(step, terms, up, down):
+        up = move(gate(up), pairs_up_below(step - 1))
+        down = move(gate(down), pairs_down_above(Z_SIZE - step))
+        return up, down
+
+    terms = line_terms(mix_own, mix_moved)
+    up, down = hop_sum(1, terms, terms[1], terms[3])
+    run_back(0, False)
+    rounds.close(up, down, grads[0][0][0])
+    up, down = hop_sum(2, terms, plus(terms[2], up).astype(low), plus(terms[2], down).astype(low))
+    run_back(0, True)
+    rounds.close(up, down, grads[0][1][0], *send_via(0))
+    up, down = hop_sum(3, terms, plus(terms[3], up).astype(low), plus(terms[1], down).astype(low))
+    run_back(1, False)
+    rounds.close(up, down, grads[1][0][0], *send_first(0))
+    output = (middle + residual_scale * (terms[0] + plus(up, down))).astype(low)
+    run_back(1, True)
+    rounds.close(grads[1][1][0], *send_second(0))
+    totals = [total_of(0), None, None]
+    backs = [[], [], []]
+
+    def send_back(u, step):
+        backs[u] += shift_sends(rounds, totals[u], z, (step,), 1)
+        return backs[u][-1:]
+
+    run_back(2, False)
+    rounds.close(grads[2][0][0], *send_via(1), *send_back(0, 1))
+    run_back(2, True)
+    rounds.close(grads[2][1][0], *send_first(1), *send_back(0, 2))
+    copy_other, copy_own = combine(all_slots, back, rounds.after())
+    rounds.close(copy_other, *send_second(1), *send_back(0, 3))
+    copy_moved = move(gate(copy_other), PAIRS_C)
+    rounds.close(copy_moved, *send_via(2))
+    terms = line_terms(copy_own, copy_moved)
+    up, down = hop_sum(1, terms, terms[1], terms[3])
+    totals[1] = total_of(1)
+    rounds.close(up, down, *send_first(2))
+    up, down = hop_sum(2, terms, plus(terms[2], up).astype(low), plus(terms[2], down).astype(low))
+    rounds.close(up, down, *send_second(2))
+    up, down = hop_sum(3, terms, plus(terms[3], up).astype(low), plus(terms[1], down).astype(low))
+    rounds.close(up, down)
+    copy_sum = terms[0] + plus(up, down)
+    totals[2] = total_of(2)
+    grad_gates = copy_sum[:, width : width + EXPERTS] + copy_sum[:, width + 64 : width + 64 + EXPERTS]
+    copy_sum = copy_sum[:, :width]
+
+    chosen = (slot_table >= 0).T
+    gates = dense_gates(jnp.dot(hidden_two, router_full, preferred_element_type=full), chosen)
+    grad_logits = (
+        gates * (grad_gates - jnp.sum(gates * grad_gates, axis=-1, keepdims=True))
+    ).astype(low)
+    grad_hidden_two = copy_sum + multiply_transposed(grad_logits, router_full)
+    router_term = contract_rows(hidden_two, grad_logits)
+    second_term, grad_norm_two = norm_backward(
+        grad_hidden_two, normal_two, inverse_two, gain_two
+    )
+    grad_middle = grad_out + grad_norm_two
+    branch_gradient = (residual_scale * grad_middle).astype(low)
+    small_term = jnp.concatenate([router_term, second_term[:, None]], axis=1)
+    out_pack = jnp.concatenate(
+        [
+            contract_rows(branch_gradient, mixed),
+            jnp.pad(small_term, ((0, 0), (0, 128 - small_term.shape[1]))),
+        ],
+        axis=1,
+    ).astype(low)
+    out_scatter = DenseScatter(rounds, out_pack, place)
+
+    def run_attention(first):
+        return attention_backward(
+            lengths,
+            branch_gradient,
+            out_t,
+            query_rows,
+            keys,
+            value_rows,
+            log_totals,
+            hidden_one,
+            first_pack,
+            cosine_table,
+            sine_table,
+            first,
+            2,
+            rounds.after(),
+        )
+
+    rounds.close(out_scatter.theirs, branch_gradient, *send_back(1, 1))
+    qkv_terms = [None, None]
+    qkv_terms[0], part_one = run_attention(0)
+    rounds.close(part_one, *out_scatter.cores(), *send_back(1, 2))
+    qkv_terms[1], part_two = run_attention(2)
+    qkv_scatter = [DenseScatter(rounds, qkv_terms[0], place)]
+    rounds.close(part_two, *out_scatter.first(), *qkv_scatter[0].cores(), *send_back(1, 3))
+    grad_hidden_one = part_one + part_two
+    first_term, grad_norm_one = norm_backward(
+        grad_hidden_one, normal_one, inverse_one, gain_one
+    )
+    grad_input = grad_middle + grad_norm_one
+
+    first_pack_term = jnp.pad(first_term[:, None], ((0, 0), (0, 127))).astype(low)
+    qkv_scatter.append(
+        DenseScatter(rounds, jnp.concatenate([qkv_terms[1], first_pack_term], axis=1), place)
+    )
+    sent = [*out_scatter.second(), *qkv_scatter[0].first(), *qkv_scatter[1].cores()]
+    for step in steps:
+        sent += send_back(2, step)
+    rounds.close(*sent)
+    rounds.close(*out_scatter.along(), *qkv_scatter[0].second(), *qkv_scatter[1].first())
+    rounds.close(*qkv_scatter[0].along(), *qkv_scatter[1].second())
+    qkv_scatter[1].along()
+    back = jnp.concatenate(
+        [
+            along_z(lax.dynamic_index_in_dim(totals[u], z, 1, keepdims=False), backs[u], z)
+            for u in units
+        ],
+        axis=1,
+    ).reshape(Z_SIZE * 5, rows, -1)
+    weight_sums = jnp.stack([back[HALF_PLACE[q]] for q in range(Z_SIZE * 5)]).astype(full)
+    weight_sums = weight_sums.reshape(EXPERTS // (X_SIZE * C_SIZE), 2, rows, 3 * FF // 2)
+    parts = [
+        weight_sums[..., i * FF // 2 : (i + 1) * FF // 2].transpose(0, 2, 1, 3).reshape(-1, rows, FF)
+        for i in range(3)
+    ]
+    gate_up_grads = jnp.concatenate(parts[:2], axis=-1)
+    down_grads = parts[2].transpose(0, 2, 1)
+
+    qkv_sums = [scatter.result() for scatter in qkv_scatter]
+    first_sum = qkv_sums[-1][:, -128]
+    qkv_sums[-1] = qkv_sums[-1][:, :-128]
+    qkv_sum = jnp.concatenate(qkv_sums, axis=1)
+    qkv_sum = qkv_sum.reshape(qkv_sum.shape[0], -1, QUERY_LANES + 2 * KEY_LANES)
+    qkv_sum = jnp.concatenate(
+        [
+            part.reshape(qkv_sum.shape[0], -1)
+            for part in jnp.split(qkv_sum, (QUERY_LANES, QUERY_LANES + KEY_LANES), axis=2)
+        ],
+        axis=1,
+    )
+    out_sum = out_scatter.result()
+    small_sum = out_sum[:, width:]
+    return (
+        output,
+        grad_input,
+        first_sum,
+        qkv_sum,
+        out_sum[:, :width].T,
+        small_sum[:, EXPERTS],
+        small_sum[:, :EXPERTS],
+        gate_up_grads,
+        down_grads,
+    )
+
+
 def solution(mesh):
     in_specs = (
         P(("dp", "expert"), None),
@@ -344,4 +1686,6 @@
         P("expert", "dp", None),
         P("expert", None, "dp"),
     )
-    return jax.shard_map(body, mesh=mesh, in_specs=in_specs, out_specs=out_specs, check_vma=False)
+    fits = mesh.shape["dp"] == Z_SIZE * Y_SIZE and mesh.shape["expert"] == X_SIZE * C_SIZE
+    chosen = body if fits else general_body
+    return jax.shard_map(chosen, mesh=mesh, in_specs=in_specs, out_specs=out_specs, check_vma=False)

time: 5190 us -> 1280 us (0.25)
  waiting for transfers between devices: 3710 us -> 307 us
  matrix products: 437 us -> 22.7 us
  Pallas kernels: 0 us -> 366 us
  blocking collectives: 318 us -> 0 us
  local copies, waits for them, and re-layouts: 491 us -> 211 us
  starting transfers between devices: 36 us -> 204 us
    all_gather x42 -> x0, waiting for transfers between devices: 1990 us -> none  [the longest x20 1190 us: fetch_expert(): lax.all_gather(gate_up_shard, 'dp', axis=0, tiled=True)]
    reduce_scatter x22 -> x0, waiting for transfers between devices: 1500 us -> none  [the longest x10 751 us: expert_backward(): lax.psum_scatter(contract_rows(rows, grad_gate_up).astype(jnp.bfloat16),...]
    pallas_call x0 -> x184, Pallas kernels: none -> 366 us  [the longest x6 143 us: expert_backward(): pl.pallas_call(functools.partial(expert_back_kernel, count=len(pieces), w...]
    ppermute x0 -> x160, waiting for transfers between devices: none -> 307 us  [move(): return lax.ppermute(value, MESH_AXES, pairs)]
    all_gather x1 -> x0, blocking collectives: 235 us -> none  [body(): lax.all_gather(router_weight, ('dp', 'expert'), axis=0, tiled=True)]
    all_to_all x4 -> x0, waiting for transfers between devices: 219 us -> none  [the longest x1 219 us: body(): lax.all_to_all(grad_copies, 'expert', split_axis=1, concat_axis=0, tiled=...]
    dot_general x89 -> x2, matrix products: 224 us -> 8.15 us  [the longest x1 6.6 us: body(): jnp.einsum('de,itd->iet', router_full, rows_in, preferred_element_type=full)]
    ppermute x0 -> x160, starting transfers between devices: none -> 204 us  [move(): return lax.ppermute(value, MESH_AXES, pairs)]
  transfers between devices with their start and end apart: 69 -> 160, of which waited for: 64 -> 48; matrix products, arithmetic and copies ran while one was open for 17% -> 24% of each run, Pallas kernels for 0% -> 26%
where the time goes in v2:
time: 1280 us; the launch traced here: 1260 us
  Pallas kernels  366 us (29%)
  waiting for transfers between devices  307 us (24%)
  local copies, waits for them, and re-layouts  211 us (16%)
  starting transfers between devices  204 us (16%)
  other arithmetic  146 us (11%)
  matrix products  22.7 us (2%)
    ppermute x160, waiting for transfers between devices, move(): return lax.ppermute(value, MESH_AXES, pairs)  307 us
    ppermute x160, starting transfers between devices, move(): return lax.ppermute(value, MESH_AXES, pairs)  204 us
    pallas_call x6, Pallas kernels, expert_backward(): pl.pallas_call(functools.partial(expert_back_kernel, count=len(pieces), w...  143 us
    unnamed x537, local copies, waits for them, and re-layouts  96.9 us
    pallas_call x6, Pallas kernels, expert_forward(): pl.pallas_call(functools.partial(expert_forward_kernel, count=len(pieces)...  88.4 us
    pallas_call x2, Pallas kernels, combine(): pl.pallas_call(combine_kernel, grid=(sources,), in_specs=[pl.BlockSpec((1...  38.5 us
    pallas_call x2, Pallas kernels, attention_backward(): pl.pallas_call(functools.partial(attention_back_kernel, first=first), gri...  37.4 us
    dynamic_update_slice x30, local copies, waits for them, and re-layouts, along_z(): lax.dynamic_update_slice_in_dim(result, got[step - 1][None], (z + Z_SIZE...  33.1 us
  transfers between devices with their start and end apart: 160, of which 48 were waited for; matrix products, arithmetic and copies ran while one was open for 24% of the time, Pallas kernels for 26%

profile of v2, /device:TPU:0, one launch (start us, length us, event | category | flops | bytes accessed | tf_op | source)
XLA Modules:
  0.0 1261.4 jit_solution(15645045845467655892)
XLA Ops:
  76.9 16.5 %collective-permute-done.13.refs_7_ = bf16[192,768]{1,0:T(8,128)(2,1)S(1)} collective-permute-done((bf16[192,768]{1,0:T(8,128)(2,1)}, bf16[192,768]{1,0:T(8,128)(2,1)S(1)}, u32[]{:S(2)}, u32[]{:S(2)}) %collective-permute-start.13) | collective-permute-done | bytes 294944 | tf_op jit(solution)/shard_map/ppermute | solution.py:415
  106.7 18.2 %collective-permute-done.24.refs_8_ = bf16[192,768]{1,0:T(8,128)(2,1)} collective-permute-done((bf16[192,768]{1,0:T(8,128)(2,1)}, bf16[192,768]{1,0:T(8,128)(2,1)}, u32[]{:S(2)}, u32[]{:S(2)}) %collective-permute-start.24) | collective-permute-done | bytes 294944 | tf_op jit(solution)/shard_map/ppermute | solution.py:415
  130.9 11.6 collective-permute-done.20.refs_4_.refs_1_
  220.2 18.6 %attention_forward.1 = (bf16[384,1536]{1,0:T(8,128)(2,1)S(1)}, bf16[384,1536]{1,0:T(8,128)(2,1)S(1)}, bf16[384,512]{1,0:T(8,128)(2,1)S(1)}, bf16[384,512]{1,0:T(...) custom-call(s32[1]{0:T(128)S(6)} %copy.553.length, bf16[384,1536]{1,0:T(8,128)(2,1)} %tokens.1, ...), custom_call_target="tpu_custom_call" | custom-call | flops 3925868544 | bytes 13762560 | tf_op jit(solution)/shard_map/attention_forward/pallas_call | solution.py:913
  267.1 15.4 %collective-permute-done.45.refs_1_ = bf16[192,768]{1,0:T(8,128)(2,1)S(1)} collective-permute-done((bf16[192,768]{1,0:T(8,128)(2,1)}, bf16[192,768]{1,0:T(8,128)(2,1)S(1)}, u32[]{:S(2)}, u32[]{:S(2)}) %collective-permute-start.45) | collective-permute-done | bytes 294944 | tf_op jit(solution)/shard_map/ppermute | solution.py:415
  303.9 20.4 %collective-permute-done.52.refs_3_.rest_3_ = bf16[4,192,768]{2,1,0:T(8,128)(2,1)} collective-permute-done((bf16[4,192,768]{2,1,0:T(8,128)(2,1)}, bf16[4,192,768]{2,1,0:T(8,128)(2,1)}, u32[]{:S(2)}, u32[]{:S(2)}) %collective-permute-start.52) | collective-permute-done | bytes 1179680 | tf_op jit(solution)/shard_map/ppermute | solution.py:415
  336.4 13.1 %collective-permute-done.63.refs_7_.rest_5_ = bf16[2,192,768]{2,1,0:T(8,128)(2,1)} collective-permute-done((bf16[2,192,768]{2,1,0:T(8,128)(2,1)}, bf16[2,192,768]{2,1,0:T(8,128)(2,1)}, u32[]{:S(2)}, u32[]{:S(2)}) %collective-permute-start.63) | collective-permute-done | bytes 589856 | tf_op jit(solution)/shard_map/ppermute | solution.py:415
  350.8 14.0 %collective-permute-done.62.refs_6_.rest_4_ = bf16[2,192,768]{2,1,0:T(8,128)(2,1)} collective-permute-done((bf16[2,192,768]{2,1,0:T(8,128)(2,1)}, bf16[2,192,768]{2,1,0:T(8,128)(2,1)}, u32[]{:S(2)}, u32[]{:S(2)}) %collective-permute-start.62) | collective-permute-done | bytes 589856 | tf_op jit(solution)/shard_map/ppermute | solution.py:415
  379.1 10.0 collective-permute-done.71.refs_7_.rest_5_
  392.8 20.2 %collective-permute-done.65.refs_3_.d3 = bf16[384,1536]{1,0:T(8,128)(2,1)S(1)} collective-permute-done((bf16[384,1536]{1,0:T(8,128)(2,1)}, bf16[384,1536]{1,0:T(8,128)(2,1)S(1)}, u32[]{:S(2)}, u32[]{:S(2)}) %collective-permute-start.65) | collective-permute-done | bytes 1179680 | tf_op jit(solution)/shard_map/ppermute | solution.py:415
  414.6 8.6 collective-permute-done.68.refs_4_.rest_1_
  447.2 8.6 collective-permute-done.75.refs_3_.rest_2_
  479.2 16.0 %expert_forward.6 = (bf16[8,960,1536]{2,1,0:T(8,128)(2,1)}, bf16[1280,1536]{1,0:T(8,128)(2,1)}, f32[1280,1024]{1,0:T(8,128)}) custom-call(s32[2]{0:T(128)S(1)} %copy-done.81, s32[8,1,384]{2,1,0:T(1,128)S(1)} %copy-done.59, f32[8,1,384]{2,1,0:T(1,128)S(1)} %get-tuple-element.335.gates, bf16[8,384,1536]{2,1,0:T(8,128)(2,1)} %line_blocks.2.rows, ...), custom_call_target="tpu_custom_call" | custom-call | flops 7549747200 | bytes 27262976 | tf_op jit(solution)/shard_map/expert_forward/pallas_call | solution.py:611
  495.2 16.0 %expert_forward.7 = (bf16[8,960,1536]{2,1,0:T(8,128)(2,1)}, bf16[1280,1536]{1,0:T(8,128)(2,1)}, f32[1280,1024]{1,0:T(8,128)}) custom-call(s32[2]{0:T(128)S(1)} %copy-done.65, s32[8,1,384]{2,1,0:T(1,128)S(1)} %copy-done.53, f32[8,1,384]{2,1,0:T(1,128)S(1)} %get-tuple-element.336.gates, ...), custom_call_target="tpu_custom_call", output_to_operand_aliasing={{0}: (8, {})} | custom-call | flops 7549747200 | bytes 27262976 | tf_op jit(solution)/shard_map/expert_forward/pallas_call | solution.py:611
  517.6 16.5 %expert_forward.8 = (bf16[8,960,1536]{2,1,0:T(8,128)(2,1)}, bf16[1280,1536]{1,0:T(8,128)(2,1)}, f32[1280,1024]{1,0:T(8,128)}) custom-call(s32[2]{0:T(128)S(1)} %copy-done.64, s32[8,1,384]{2,1,0:T(1,128)S(1)} %copy-done.52, f32[8,1,384]{2,1,0:T(1,128)S(1)} %copy-done.57, bf16[8,384,1536]{2,1,0:T(8,128)(2,1)} %line_blocks.2.rows, ...), custom_call_target="tpu_custom_call", output_to_operand_aliasing={{0}: (10, {})} | custom-call | flops 7549747200 | bytes 27262976 | tf_op jit(solution)/shard_map/expert_forward/pallas_call | solution.py:611
  534.2 15.7 %expert_forward.9 = (bf16[8,960,1536]{2,1,0:T(8,128)(2,1)}, bf16[1280,1536]{1,0:T(8,128)(2,1)}, f32[1280,1024]{1,0:T(8,128)}) custom-call(s32[2]{0:T(128)S(1)} %copy-done.63, s32[8,1,384]{2,1,0:T(1,128)S(1)} %copy-done.51, f32[8,1,384]{2,1,0:T(1,128)S(1)} %copy-done.56, bf16[8,384,1536]{2,1,0:T(8,128)(2,1)} %line_blocks.2.rows, ...), custom_call_target="tpu_custom_call", output_to_operand_aliasing={{0}: (8, {})} | custom-call | flops 7549747200 | bytes 27262976 | tf_op jit(solution)/shard_map/expert_forward/pallas_call | solution.py:611
  556.0 12.7 %expert_forward.10 = (bf16[8,960,1536]{2,1,0:T(8,128)(2,1)}, bf16[1280,1536]{1,0:T(8,128)(2,1)}, f32[1280,512]{1,0:T(8,128)S(1)}) custom-call(s32[2]{0:T(128)S(1)} %pad_add_fusion.2.info, s32[8,1,384]{2,1,0:T(1,128)S(1)} %copy-done.46, f32[8,1,384]{2,1,0:T(1,128)S(1)} %copy-done.50, ...), custom_call_target="tpu_custom_call", output_to_operand_aliasing={{0}: (7, {})} | custom-call | flops 4529848320 | bytes 22282240 | tf_op jit(solution)/shard_map/expert_forward/pallas_call | solution.py:611
  570.3 11.5 expert_forward.11
  590.0 18.2 %combine.2 = (bf16[4,384,1536]{2,1,0:T(8,128)(2,1)}, bf16[4,384,1536]{2,1,0:T(8,128)(2,1)}) custom-call(s32[8,6,384]{2,1,0:T(8,128)} %concatenate.164.slots, bf16[8,960,1536]{2,1,0:T(8,128)(2,1)} %get-tuple-element.79.values, f32[8,128]{1,0:T(8,128)} %join.44.rest_0_.refs_1_.refs_3_), custom_call_target="tpu_custom_call" | custom-call | flops 9059696640 | bytes 33030144 | tf_op jit(solution)/shard_map/combine/pallas_call | solution.py:1114
  628.6 8.7 collective-permute-start.90
  637.4 26.1 %expert_backward.6 = (bf16[8,960,1664]{2,1,0:T(8,128)(2,1)}, bf16[2,2,192,768]{3,2,1,0:T(8,128)(2,1)}, bf16[2,2,192,768]{3,2,1,0:T(8,128)(2,1)}, bf16[2,2,192,76...) custom-call(s32[2]{0:T(128)} %pad_add_fusion.6.info, s32[8,1,384]{2,1,0:T(1,128)} %get-tuple-element.346.slots, ...), custom_call_target="tpu_custom_call" | custom-call | flops 13589544960 | bytes 31981568 | tf_op jit(solution)/shard_map/expert_backward/pallas_call | solution.py:764
  677.4 26.1 %expert_backward.7 = (bf16[8,960,1664]{2,1,0:T(8,128)(2,1)}, bf16[2,2,192,768]{3,2,1,0:T(8,128)(2,1)}, bf16[2,2,192,768]{3,2,1,0:T(8,128)(2,1)}, bf16[2,2,192,76...) custom-call(s32[2]{0:T(128)} %pad_add_fusion.5.info, ...), custom_call_target="tpu_custom_call", output_to_operand_aliasing={{0}: (10, {})} | custom-call | flops 13589544960 | bytes 31981568 | tf_op jit(solution)/shard_map/expert_backward/pallas_call | solution.py:764
  722.5 26.0 %expert_backward.8 = (bf16[8,960,1664]{2,1,0:T(8,128)(2,1)}, bf16[2,2,192,768]{3,2,1,0:T(8,128)(2,1)}, bf16[2,2,192,768]{3,2,1,0:T(8,128)(2,1)}, bf16[2,2,192,76...) custom-call(s32[2]{0:T(128)} %pad_add_fusion.4.info, ...), custom_call_target="tpu_custom_call", output_to_operand_aliasing={{0}: (12, {})} | custom-call | flops 13589544960 | bytes 31981568 | tf_op jit(solution)/shard_map/expert_backward/pallas_call | solution.py:764
  753.3 26.4 %expert_backward.9 = (bf16[8,960,1664]{2,1,0:T(8,128)(2,1)}, bf16[2,2,192,768]{3,2,1,0:T(8,128)(2,1)}, bf16[2,2,192,768]{3,2,1,0:T(8,128)(2,1)}, bf16[2,2,192,76...) custom-call(s32[2]{0:T(128)} %pad_add_fusion.3.info, ...), custom_call_target="tpu_custom_call", output_to_operand_aliasing={{0}: (10, {})} | custom-call | flops 13589544960 | bytes 31981568 | tf_op jit(solution)/shard_map/expert_backward/pallas_call | solution.py:764
  790.2 19.3 %expert_backward.10 = (bf16[8,960,1664]{2,1,0:T(8,128)(2,1)}, bf16[1,2,192,768]{3,2,1,0:T(8,128)(2,1)}, bf16[1,2,192,768]{3,2,1,0:T(8,128)(2,1)}, bf16[1,2,192,7...) custom-call(s32[2]{0:T(128)} %copy-done.62, s32[8,1,384]{2,1,0:T(1,128)} %get-tuple-element.344.slots, ...), custom_call_target="tpu_custom_call", output_to_operand_aliasing={{0}: (9, {})} | custom-call | flops 7549747200 | bytes 24641536 | tf_op jit(solution)/shard_map/expert_backward/pallas_call | solution.py:764
  820.6 19.0 %expert_backward.11 = (bf16[8,960,1664]{2,1,0:T(8,128)(2,1)}, bf16[1,2,192,768]{3,2,1,0:T(8,128)(2,1)}, bf16[1,2,192,768]{3,2,1,0:T(8,128)(2,1)}, bf16[1,2,192,7...) custom-call(s32[2]{0:T(128)} %copy-done.61, s32[8,1,384]{2,1,0:T(1,128)} %copy-done.45, ...), custom_call_target="tpu_custom_call", output_to_operand_aliasing={{0}: (8, {})} | custom-call | flops 7549747200 | bytes 24641536 | tf_op jit(solution)/shard_map/expert_backward/pallas_call | solution.py:764
  844.2 20.3 %combine.3 = (bf16[4,384,1664]{2,1,0:T(8,128)(2,1)}, bf16[4,384,1664]{2,1,0:T(8,128)(2,1)}) custom-call(s32[8,6,384]{2,1,0:T(8,128)} %concatenate.164.slots, bf16[8,960,1664]{2,1,0:T(8,128)(2,1)} %get-tuple-element.110.values, f32[8,128]{1,0:T(8,128)} %join.52.rest_0_.refs_1_.refs_4_), custom_call_target="tpu_custom_call" | custom-call | flops 9814671360 | bytes 35782656 | tf_op jit(solution)/shard_map/combine/pallas_call | solution.py:1114
  895.3 23.8 %collective-permute-done.114.refs_0_ = bf16[384,1664]{1,0:T(8,128)(2,1)} collective-permute-done((bf16[384,1664]{1,0:T(8,128)(2,1)}, bf16[384,1664]{1,0:T(8,128)(2,1)}, u32[]{:S(2)}, u32[]{:S(2)}) %collective-permute-start.114) | collective-permute-done | bytes 1277984 | tf_op jit(solution)/shard_map/ppermute | solution.py:415
  944.3 12.8 %collective-permute-done.118.refs_0_ = bf16[384,1664]{1,0:T(8,128)(2,1)} collective-permute-done((bf16[384,1664]{1,0:T(8,128)(2,1)}, bf16[384,1664]{1,0:T(8,128)(2,1)}, u32[]{:S(2)}, u32[]{:S(2)}) %collective-permute-start.118) | collective-permute-done | bytes 1277984 | tf_op jit(solution)/shard_map/ppermute | solution.py:415
  961.7 9.0 collective-permute-start.122
  1039.5 18.5 %attention_backward.2 = (bf16[1536,1280]{1,0:T(8,128)(2,1)}, f32[384,1536]{1,0:T(8,128)}) custom-call(s32[1]{0:T(128)S(6)} %copy.553.length, bf16[384,1536]{1,0:T(8,128)(2,1)S(1)} %copy-done.27, bf16[1536,1536]{1,0:T(8,128)(2,1)} %bitcast.601, bf16[384,1536]{1,0:T(8,128)(2,1)S(1)} %copy-done.70, bf16[384,512]{1,0:T(8,128)(2,1)S(1)} %copy-done.73, ...), custom_call_target="tpu_custom_call" | custom-call | flops 10116661248 | bytes 28704768 | tf_op jit(solution)/shard_map/attention_backward/pallas_call | solution.py:1052
  1069.6 18.9 %attention_backward.3 = (bf16[1536,1280]{1,0:T(8,128)(2,1)}, f32[384,1536]{1,0:T(8,128)}) custom-call(s32[1]{0:T(128)S(6)} %copy.553.length, bf16[384,1536]{1,0:T(8,128)(2,1)S(1)} %copy-done.27, bf16[1536,1536]{1,0:T(8,128)(2,1)} %bitcast.602, bf16[384,1536]{1,0:T(8,128)(2,1)S(1)} %copy-done.71, bf16[384,512]{1,0:T(8,128)(2,1)S(1)} %copy-done.74, ...), custom_call_target="tpu_custom_call" | custom-call | flops 10116661248 | bytes 28704768 | tf_op jit(solution)/shard_map/attention_backward/pallas_call | solution.py:1052
  (1230 shorter events, 719.9 us)
Async XLA Ops:
  44.8 48.6 %collective-permute-start.6 = (bf16[4,48,2688]{2,1,0:T(8,128)(2,1)}, bf16[4,48,2688]{2,1,0:T(8,128)(2,1)S(1)}, u32[]{:S(2)}, u32[]{:S(2)}) collective-permute-start(bf16[4,48,2688]{2,1,0:T(8,128)(2,1)} %tie.131.refs_0_), channel_id=1, source_target_pairs={{0,2},{1,3},{2,0},{3,1},{4,6},{5,7},{6,4},{7,5},{8,10},{9,11},{10,... | collective-permute-start | bytes 3096584 | tf_op jit(solution)/shard_map/ppermute | solution.py:415
  46.3 47.2 %collective-permute-start.7 = (bf16[4,48,2688]{2,1,0:T(8,128)(2,1)}, bf16[4,48,2688]{2,1,0:T(8,128)(2,1)S(1)}, u32[]{:S(2)}, u32[]{:S(2)}) collective-permute-start(bf16[4,48,2688]{2,1,0:T(8,128)(2,1)} %tie.131.refs_0_), channel_id=1, source_target_pairs={{0,4},{1,5},{2,6},{3,7},{4,0},{5,1},{6,2},{7,3},{8,12},{9,13},{10,... | collective-permute-start | bytes 3096584 | tf_op jit(solution)/shard_map/ppermute | solution.py:415
  47.8 46.4 %collective-permute-start.8 = (bf16[4,48,2688]{2,1,0:T(8,128)(2,1)}, bf16[4,48,2688]{2,1,0:T(8,128)(2,1)}, u32[]{:S(2)}, u32[]{:S(2)}) collective-permute-start(bf16[4,48,2688]{2,1,0:T(8,128)(2,1)} %tie.131.refs_0_), channel_id=1, source_target_pairs={{0,1},{1,0},{2,3},{3,2},{4,5},{5,4},{6,7},{7,6},{8,9},{9,8},{10,11... | collective-permute-start | bytes 3096584 | tf_op jit(solution)/shard_map/ppermute | solution.py:415
  106.7 36.1 %collective-permute-start.19 = (bf16[4,48,2688]{2,1,0:T(8,128)(2,1)}, bf16[4,48,2688]{2,1,0:T(8,128)(2,1)}, u32[]{:S(2)}, u32[]{:S(2)}) collective-permute-start(bf16[4,48,2688]{2,1,0:T(8,128)(2,1)} %tie.140), channel_id=1, source_target_pairs={{0,1},{1,0},{2,3},{3,2},{4,5},{5,4},{6,7},{7,6},{8,9},{9,8},{10,11... | collective-permute-start | bytes 3096584 | tf_op jit(solution)/shard_map/ppermute | solution.py:415
  149.1 38.7 %collective-permute-start.27 = (bf16[2,48,2688]{2,1,0:T(8,128)(2,1)}, bf16[2,48,2688]{2,1,0:T(8,128)(2,1)}, u32[]{:S(2)}, u32[]{:S(2)}) collective-permute-start(bf16[2,48,2688]{2,1,0:T(8,128)(2,1)} %tie.146), channel_id=1, source_target_pairs={{0,1},{1,0},{2,3},{3,2},{4,5},{5,4},{6,7},{7,6},{8,9},{9,8},{10,11... | collective-permute-start | bytes 1548296 | tf_op jit(solution)/shard_map/ppermute | solution.py:415
  151.1 44.0 %collective-permute-start.35 = (bf16[4,192,768]{2,1,0:T(8,128)(2,1)}, bf16[4,192,768]{2,1,0:T(8,128)(2,1)}, u32[]{:S(2)}, u32[]{:S(2)}) collective-permute-start(bf16[4,192,768]{2,1,0:T(8,128)(2,1)} %tie.154.rest_0_), channel_id=1, source_target_pairs={{0,2},{1,3},{2,0},{3,1},{4,6},{5,7},{6,4},{7,5},{8,10},{9,11},{10,... | collective-permute-start | bytes 3538952 | tf_op jit(solution)/shard_map/ppermute | solution.py:415
  155.6 39.6 %collective-permute-start.36 = (bf16[4,192,768]{2,1,0:T(8,128)(2,1)}, bf16[4,192,768]{2,1,0:T(8,128)(2,1)}, u32[]{:S(2)}, u32[]{:S(2)}) collective-permute-start(bf16[4,192,768]{2,1,0:T(8,128)(2,1)} %tie.154.rest_0_), channel_id=1, source_target_pairs={{0,4},{1,5},{2,6},{3,7},{4,0},{5,1},{6,2},{7,3},{8,12},{9,13},{10,... | collective-permute-start | bytes 3538952 | tf_op jit(solution)/shard_map/ppermute | solution.py:415
  195.8 49.1 %collective-permute-start.42 = (bf16[4,192,768]{2,1,0:T(8,128)(2,1)}, bf16[4,192,768]{2,1,0:T(8,128)(2,1)}, u32[]{:S(2)}, u32[]{:S(2)}) collective-permute-start(bf16[4,192,768]{2,1,0:T(8,128)(2,1)} %tie.160.rest_2_), channel_id=1, source_target_pairs={{0,2},{1,3},{2,0},{3,1},{4,6},{5,7},{6,4},{7,5},{8,10},{9,11},{10,... | collective-permute-start | bytes 3538952 | tf_op jit(solution)/shard_map/ppermute | solution.py:415
  196.8 48.1 %collective-permute-start.43 = (bf16[4,192,768]{2,1,0:T(8,128)(2,1)}, bf16[4,192,768]{2,1,0:T(8,128)(2,1)}, u32[]{:S(2)}, u32[]{:S(2)}) collective-permute-start(bf16[4,192,768]{2,1,0:T(8,128)(2,1)} %tie.160.rest_2_), channel_id=1, source_target_pairs={{0,4},{1,5},{2,6},{3,7},{4,0},{5,1},{6,2},{7,3},{8,12},{9,13},{10,... | collective-permute-start | bytes 3538952 | tf_op jit(solution)/shard_map/ppermute | solution.py:415
  246.3 36.2 %collective-permute-start.47 = (bf16[4,192,768]{2,1,0:T(8,128)(2,1)}, bf16[4,192,768]{2,1,0:T(8,128)(2,1)}, u32[]{:S(2)}, u32[]{:S(2)}) collective-permute-start(bf16[4,192,768]{2,1,0:T(8,128)(2,1)} %tie.164.rest_0_), channel_id=1, source_target_pairs={{0,2},{1,3},{2,0},{3,1},{4,6},{5,7},{6,4},{7,5},{8,10},{9,11},{10,... | collective-permute-start | bytes 3538952 | tf_op jit(solution)/shard_map/ppermute | solution.py:415
  328.5 38.0 %collective-permute-start.60 = (bf16[4,192,768]{2,1,0:T(8,128)(2,1)}, bf16[4,192,768]{2,1,0:T(8,128)(2,1)}, u32[]{:S(2)}, u32[]{:S(2)}) collective-permute-start(bf16[4,192,768]{2,1,0:T(8,128)(2,1)} %tie.171.rest_0_), channel_id=1, source_target_pairs={{0,2},{1,3},{2,0},{3,1},{4,6},{5,7},{6,4},{7,5},{8,10},{9,11},{10,... | collective-permute-start | bytes 3538952 | tf_op jit(solution)/shard_map/ppermute | solution.py:415
  370.4 42.5 %collective-permute-start.65 = (bf16[384,1536]{1,0:T(8,128)(2,1)}, bf16[384,1536]{1,0:T(8,128)(2,1)S(1)}, u32[]{:S(2)}, u32[]{:S(2)}) collective-permute-start(bf16[384,1536]{1,0:T(8,128)(2,1)} %tie.175.d2), channel_id=1, source_target_pairs={{8,0},{9,1},{10,2},{11,3},{12,4},{13,5},{14,6},{15,7}} | collective-permute-start | bytes 3538952 | tf_op jit(solution)/shard_map/ppermute | solution.py:415
  377.3 45.9 %collective-permute-start.67 = (bf16[384,1536]{1,0:T(8,128)(2,1)}, bf16[384,1536]{1,0:T(8,128)(2,1)}, u32[]{:S(2)}, u32[]{:S(2)}) collective-permute-start(bf16[384,1536]{1,0:T(8,128)(2,1)} %tie.175.d2), channel_id=1, source_target_pairs={{0,1},{1,0},{2,3},{3,2},{4,5},{5,4},{6,7},{7,6},{8,9},{9,8},{10,11... | collective-permute-start | bytes 3538952 | tf_op jit(solution)/shard_map/ppermute | solution.py:415
  377.3 45.9 %collective-permute-start.64 = (bf16[384,1536]{1,0:T(8,128)(2,1)}, bf16[384,1536]{1,0:T(8,128)(2,1)}, u32[]{:S(2)}, u32[]{:S(2)}) collective-permute-start(bf16[384,1536]{1,0:T(8,128)(2,1)} %tie.174.u2), channel_id=1, source_target_pairs={{16,24},{17,25},{18,26},{19,27},{20,28},{21,29},{22,30},{23,31}} | collective-permute-start | bytes 3538952 | tf_op jit(solution)/shard_map/ppermute | solution.py:415
  457.8 53.4 %collective-permute-start.76 = (bf16[384,1536]{1,0:T(8,128)(2,1)}, bf16[384,1536]{1,0:T(8,128)(2,1)}, u32[]{:S(2)}, u32[]{:S(2)}) collective-permute-start(bf16[384,1536]{1,0:T(8,128)(2,1)} %tie.184), channel_id=1, source_target_pairs={{0,8},{1,9},{2,10},{3,11},{4,12},{5,13},{6,14},{7,15},{8,16},{9,17... | collective-permute-start | bytes 3538952 | tf_op jit(solution)/shard_map/ppermute | solution.py:415
  461.0 50.3 %collective-permute-start.77 = (bf16[384,1536]{1,0:T(8,128)(2,1)}, bf16[384,1536]{1,0:T(8,128)(2,1)}, u32[]{:S(2)}, u32[]{:S(2)}) collective-permute-start(bf16[384,1536]{1,0:T(8,128)(2,1)} %tie.184), channel_id=1, source_target_pairs={{8,0},{9,1},{10,2},{11,3},{12,4},{13,5},{14,6},{15,7},{16,8},{17,9... | collective-permute-start | bytes 3538952 | tf_op jit(solution)/shard_map/ppermute | solution.py:415
  462.2 49.0 %collective-permute-start.78 = (bf16[384,1536]{1,0:T(8,128)(2,1)}, bf16[384,1536]{1,0:T(8,128)(2,1)}, u32[]{:S(2)}, u32[]{:S(2)}) collective-permute-start(bf16[384,1536]{1,0:T(8,128)(2,1)} %tie.184), channel_id=1, source_target_pairs={{0,1},{1,0},{2,3},{3,2},{4,5},{5,4},{6,7},{7,6},{8,9},{9,8},{10,11... | collective-permute-start | bytes 3538952 | tf_op jit(solution)/shard_map/ppermute | solution.py:415
  511.8 38.0 %collective-permute-start.80 = (bf16[384,1536]{1,0:T(8,128)(2,1)}, bf16[384,1536]{1,0:T(8,128)(2,1)}, u32[]{:S(2)}, u32[]{:S(2)}) collective-permute-start(bf16[384,1536]{1,0:T(8,128)(2,1)} %tie.186.d1), channel_id=1, source_target_pairs={{8,0},{9,1},{10,2},{11,3},{12,4},{13,5},{14,6},{15,7},{16,8},{17,9... | collective-permute-start | bytes 3538952 | tf_op jit(solution)/shard_map/ppermute | solution.py:415
  513.3 36.6 %collective-permute-start.82 = (bf16[384,1536]{1,0:T(8,128)(2,1)}, bf16[384,1536]{1,0:T(8,128)(2,1)}, u32[]{:S(2)}, u32[]{:S(2)}) collective-permute-start(bf16[384,1536]{1,0:T(8,128)(2,1)} %tie.186.d1), channel_id=1, source_target_pairs={{0,1},{1,0},{2,3},{3,2},{4,5},{5,4},{6,7},{7,6},{8,9},{9,8},{10,11... | collective-permute-start | bytes 3538952 | tf_op jit(solution)/shard_map/ppermute | solution.py:415
  513.8 36.0 %collective-permute-start.79 = (bf16[384,1536]{1,0:T(8,128)(2,1)}, bf16[384,1536]{1,0:T(8,128)(2,1)}, u32[]{:S(2)}, u32[]{:S(2)}) collective-permute-start(bf16[384,1536]{1,0:T(8,128)(2,1)} %tie.185.u1), channel_id=1, source_target_pairs={{8,16},{9,17},{10,18},{11,19},{12,20},{13,21},{14,22},{15,23},{16,... | collective-permute-start | bytes 3538952 | tf_op jit(solution)/shard_map/ppermute | solution.py:415
  550.5 36.9 %collective-permute-start.84 = (bf16[384,1536]{1,0:T(8,128)(2,1)}, bf16[384,1536]{1,0:T(8,128)(2,1)}, u32[]{:S(2)}, u32[]{:S(2)}) collective-permute-start(bf16[384,1536]{1,0:T(8,128)(2,1)} %tie.188.d2), channel_id=1, source_target_pairs={{8,0},{9,1},{10,2},{11,3},{12,4},{13,5},{14,6},{15,7}} | collective-permute-start | bytes 3538952 | tf_op jit(solution)/shard_map/ppermute | solution.py:415
  624.5 38.9 %collective-permute-start.91 = (bf16[384,1536]{1,0:T(8,128)(2,1)}, bf16[384,1536]{1,0:T(8,128)(2,1)}, u32[]{:S(2)}, u32[]{:S(2)}) collective-permute-start(bf16[384,1536]{1,0:T(8,128)(2,1)} %tie.193), channel_id=1, source_target_pairs={{24,16},{25,17},{26,18},{27,19},{28,20},{29,21},{30,22},{31,23}} | collective-permute-start | bytes 3538952 | tf_op jit(solution)/shard_map/ppermute | solution.py:415
  664.1 39.5 %collective-permute-start.95 = (bf16[2,2,192,768]{3,2,1,0:T(8,128)(2,1)}, bf16[2,2,192,768]{3,2,1,0:T(8,128)(2,1)}, u32[]{:S(2)}, u32[]{:S(2)}) collective-permute-start(bf16[2,2,192,768]{3,2,1,0:T(8,128)(2,1)} %tie.197), channel_id=1, source_target_pairs={{0,4},{1,5},{2,6},{3,7},{4,0},{5,1},{6,2},{7,3},{8,12},{9,13},{10,... | collective-permute-start | bytes 3538952 | tf_op jit(solution)/shard_map/ppermute | solution.py:415
  665.8 37.7 %collective-permute-start.94 = (bf16[2,2,192,768]{3,2,1,0:T(8,128)(2,1)}, bf16[2,2,192,768]{3,2,1,0:T(8,128)(2,1)}, u32[]{:S(2)}, u32[]{:S(2)}) collective-permute-start(bf16[2,2,192,768]{3,2,1,0:T(8,128)(2,1)} %tie.196), channel_id=1, source_target_pairs={{0,2},{1,3},{2,0},{3,1},{4,6},{5,7},{6,4},{7,5},{8,10},{9,11},{10,... | collective-permute-start | bytes 3538952 | tf_op jit(solution)/shard_map/ppermute | solution.py:415
  704.1 44.4 %collective-permute-start.99 = (bf16[2,2,192,768]{3,2,1,0:T(8,128)(2,1)}, bf16[2,2,192,768]{3,2,1,0:T(8,128)(2,1)}, u32[]{:S(2)}, u32[]{:S(2)}) collective-permute-start(bf16[2,2,192,768]{3,2,1,0:T(8,128)(2,1)} %tie.201), channel_id=1, source_target_pairs={{0,4},{1,5},{2,6},{3,7},{4,0},{5,1},{6,2},{7,3},{8,12},{9,13},{10,... | collective-permute-start | bytes 3538952 | tf_op jit(solution)/shard_map/ppermute | solution.py:415
  704.4 44.1 %collective-permute-start.98 = (bf16[2,2,192,768]{3,2,1,0:T(8,128)(2,1)}, bf16[2,2,192,768]{3,2,1,0:T(8,128)(2,1)}, u32[]{:S(2)}, u32[]{:S(2)}) collective-permute-start(bf16[2,2,192,768]{3,2,1,0:T(8,128)(2,1)} %tie.200), channel_id=1, source_target_pairs={{0,2},{1,3},{2,0},{3,1},{4,6},{5,7},{6,4},{7,5},{8,10},{9,11},{10,... | collective-permute-start | bytes 3538952 | tf_op jit(solution)/shard_map/ppermute | solution.py:415
  708.0 40.6 %collective-permute-start.97 = (bf16[384,1536]{1,0:T(8,128)(2,1)}, bf16[384,1536]{1,0:T(8,128)(2,1)}, u32[]{:S(2)}, u32[]{:S(2)}) collective-permute-start(bf16[384,1536]{1,0:T(8,128)(2,1)} %tie.199), channel_id=1, source_target_pairs={{8,0},{9,1},{10,2},{11,3},{12,4},{13,5},{14,6},{15,7},{16,8},{17,9... | collective-permute-start | bytes 3538952 | tf_op jit(solution)/shard_map/ppermute | solution.py:415
  711.8 36.7 %collective-permute-start.96 = (bf16[384,1536]{1,0:T(8,128)(2,1)}, bf16[384,1536]{1,0:T(8,128)(2,1)S(1)}, u32[]{:S(2)}, u32[]{:S(2)}) collective-permute-start(bf16[384,1536]{1,0:T(8,128)(2,1)} %tie.198), channel_id=1, source_target_pairs={{0,8},{1,9},{2,10},{3,11},{4,12},{5,13},{6,14},{7,15},{8,16},{9,17... | collective-permute-start | bytes 3538952 | tf_op jit(solution)/shard_map/ppermute | solution.py:415
  1088.5 40.3 %collective-permute-start.132 = (bf16[2,192,768]{2,1,0:T(8,128)(2,1)}, bf16[2,192,768]{2,1,0:T(8,128)(2,1)}, u32[]{:S(2)}, u32[]{:S(2)}) collective-permute-start(bf16[2,192,768]{2,1,0:T(8,128)(2,1)} %tie.234), channel_id=1, source_target_pairs={{0,24},{1,25},{2,26},{3,27},{4,28},{5,29},{6,30},{7,31},{8,0},{9,1... | collective-permute-start | bytes 1769480 | tf_op jit(solution)/shard_map/ppermute | solution.py:415
  1137.0 48.5 %collective-permute-start.135 = (bf16[2,48,1664]{2,1,0:T(8,128)(2,1)}, bf16[2,48,1664]{2,1,0:T(8,128)(2,1)}, u32[]{:S(2)}, u32[]{:S(2)}) collective-permute-start(bf16[2,48,1664]{2,1,0:T(8,128)(2,1)} %tie.237), channel_id=1, source_target_pairs={{0,4},{1,5},{2,6},{3,7},{4,0},{5,1},{6,2},{7,3},{8,12},{9,13},{10,... | collective-permute-start | bytes 958472 | tf_op jit(solution)/shard_map/ppermute | solution.py:415
  1149.6 35.9 %collective-permute-start.134 = (bf16[2,48,1664]{2,1,0:T(8,128)(2,1)}, bf16[2,48,1664]{2,1,0:T(8,128)(2,1)S(1)}, u32[]{:S(2)}, u32[]{:S(2)}) collective-permute-start(bf16[2,48,1664]{2,1,0:T(8,128)(2,1)} %tie.236), channel_id=1, source_target_pairs={{0,2},{1,3},{2,0},{3,1},{4,6},{5,7},{6,4},{7,5},{8,10},{9,11},{10,... | collective-permute-start | bytes 958472 | tf_op jit(solution)/shard_map/ppermute | solution.py:415
  1151.6 36.4 %collective-permute-start.139 = (bf16[2,48,1280]{2,1,0:T(8,128)(2,1)}, bf16[2,48,1280]{2,1,0:T(8,128)(2,1)S(1)}, u32[]{:S(2)}, u32[]{:S(2)}) collective-permute-start(bf16[2,48,1280]{2,1,0:T(8,128)(2,1)} %tie.241), channel_id=1, source_target_pairs={{0,4},{1,5},{2,6},{3,7},{4,0},{5,1},{6,2},{7,3},{8,12},{9,13},{10,... | collective-permute-start | bytes 737288 | tf_op jit(solution)/shard_map/ppermute | solution.py:415
  (380 other events, 3981.3 us)

commit v3 on v2

--- a/solution.py
+++ b/solution.py
@@ -348,26 +348,7 @@
 PAIRS_C = device_pairs(lambda z, y, x, c: (z, y, x, 1 - c))
 
 
-def pairs_shift(step):
-    return device_pairs(lambda z, y, x, c: ((z + step) % Z_SIZE, y, x, c))
-
-
-def pairs_up(first):
-    return device_pairs(
-        lambda z, y, x, c: (z + 1, y, x, c) if first <= z < Z_SIZE - 1 else None
-    )
-
-
-def pairs_up_below(last):
-    return device_pairs(lambda z, y, x, c: (z + 1, y, x, c) if z <= last else None)
-
-
-def pairs_down(last):
-    return device_pairs(lambda z, y, x, c: (z - 1, y, x, c) if 1 <= z <= last else None)
-
-
-def pairs_down_above(first):
-    return device_pairs(lambda z, y, x, c: (z - 1, y, x, c) if z >= first else None)
+Z_GROUPS = [[z * Y_SIZE + y for z in range(Z_SIZE)] for y in range(Y_SIZE)]
 
 
 def tie_kernel(*refs):
@@ -386,6 +367,16 @@
     )(value, *after)
 
 
+def trade(value):
+    return lax.all_to_all(
+        value, "dp", split_axis=0, concat_axis=0, axis_index_groups=Z_GROUPS, tiled=True
+    )
+
+
+def spread(value):
+    return trade(jnp.broadcast_to(value[None], (Z_SIZE, *value.shape)))
+
+
 def join_kernel(*refs):
     refs[-1][...] = jnp.zeros_like(refs[-1])
 
@@ -415,98 +406,80 @@
     return lax.ppermute(value, MESH_AXES, pairs)
 
 
-def line_hop(step, up, down):
-    return move(up, pairs_up(step - 1)), move(down, pairs_down(Z_SIZE - step))
-
-
-def rows_kernel(info, own, u1, u2, u3, d1, d2, d3, *rest):
-    other, out, sem = rest[:7], rest[7], rest[8]
-    z = info[0]
-    mine = (own, u1, u2, u3, d1, d2, d3)
-    waits = []
-    for k, parts in enumerate((other, mine)):
-        ups, downs = parts[1:4], parts[4:7]
-        target = out.at[k * Z_SIZE]
-        first = pltpu.make_async_copy(parts[0], target, sem.at[k * Z_SIZE])
-        first.start()
-        waits.append(first)
-        for s in range(1, Z_SIZE):
-            target = out.at[k * Z_SIZE + s]
-            below = pltpu.make_async_copy(ups[s - 1], target, sem.at[k * Z_SIZE + s])
-            above = pltpu.make_async_copy(downs[Z_SIZE - s - 1], target, sem.at[k * Z_SIZE + s])
-            pl.when(z >= s)(below.start)
-            pl.when(z < s)(above.start)
-            waits.append(below)
-    for copy in waits:
-        copy.wait()
-
-
-def line_blocks(z, mine, other):
+def assemble(plan, info, arrays, shape, name):
     any_spec = pl.BlockSpec(memory_space=pl.ANY)
-    block = mine[0]
+
+    def kernel(info_ref, *refs):
+        *parts, out, sem = refs
+        copies = [
+            pltpu.make_async_copy(source, target, sem.at[i])
+            for i, (source, target) in enumerate(plan(info_ref, parts, out))
+        ]
+        for copy in copies:
+            copy.start()
+        for copy in copies:
+            copy.wait()
+
+    dtype = arrays[0].dtype
+    size = 1
+    for extent in shape:
+        size *= extent
     return pl.pallas_call(
-        rows_kernel,
+        kernel,
         grid_spec=pltpu.PrefetchScalarGridSpec(
             num_scalar_prefetch=1,
             grid=(),
-            in_specs=[any_spec] * 14,
+            in_specs=[any_spec] * len(arrays),
             out_specs=pl.BlockSpec(memory_space=pltpu.VMEM),
-            scratch_shapes=[pltpu.SemaphoreType.DMA((2 * Z_SIZE,))],
+            scratch_shapes=[pltpu.SemaphoreType.DMA((2 * len(arrays),))],
         ),
-        out_shape=jax.ShapeDtypeStruct((2 * Z_SIZE, *block.shape), block.dtype),
-        cost_estimate=pl.CostEstimate(
-            flops=0, bytes_accessed=32 * block.size, transcendentals=0
-        ),
+        out_shape=jax.ShapeDtypeStruct(shape, dtype),
         compiler_params=pltpu.CompilerParams(vmem_limit_bytes=32 * 1024 * 1024),
-        name="line_blocks",
-    )(z[None], *mine, *other)
-
-
-def dense_kernel(info, *refs):
-    pieces, out, sem = refs[:10], refs[10], refs[11]
-    y, x, c = info[0], info[1], info[2]
-    zs = Z_SIZE // 2
-    copies = []
-    for k in range(2):
-        at_c = c if k == 0 else 1 - c
-        block, from_x, from_y, far_a, far_b = pieces[5 * k : 5 * k + 5]
-        targets = [
-            (block, out.at[:, y, x, at_c]),
-            (from_x, out.at[:, y, 1 - x, at_c]),
-            (from_y, out.at[:, 1 - y, x, at_c]),
-            (far_a, out.at[pl.ds(0, zs), 1 - y, 1 - x, at_c]),
-            (far_b, out.at[pl.ds(zs, zs), 1 - y, 1 - x, at_c]),
-        ]
-        for piece, target in targets:
-            copies.append(pltpu.make_async_copy(piece, target, sem.at[len(copies)]))
-    for copy in copies:
-        copy.start()
-    for copy in copies:
-        copy.wait()
+        cost_estimate=pl.CostEstimate(flops=0, bytes_accessed=4 * size, transcendentals=0),
+        name=name,
+    )(info, *arrays)
 
 
 def dense_assemble(place, mine, other):
     z, y, x, c = place
-    any_spec = pl.BlockSpec(memory_space=pl.ANY)
-    block = mine[0]
-    rows, n = block.shape[1:]
-    full = pl.pallas_call(
-        dense_kernel,
-        grid_spec=pltpu.PrefetchScalarGridSpec(
-            num_scalar_prefetch=1,
-            grid=(),
-            in_specs=[any_spec] * 10,
-            out_specs=pl.BlockSpec(memory_space=pltpu.VMEM),
-            scratch_shapes=[pltpu.SemaphoreType.DMA((10,))],
-        ),
-        out_shape=jax.ShapeDtypeStruct((Z_SIZE, Y_SIZE, X_SIZE, C_SIZE, rows, n), block.dtype),
-        cost_estimate=pl.CostEstimate(
-            flops=0, bytes_accessed=32 * block.size, transcendentals=0
-        ),
-        compiler_params=pltpu.CompilerParams(vmem_limit_bytes=32 * 1024 * 1024),
-        name="dense_assemble",
-    )(jnp.stack([y, x, c]), *mine, *other)
+    rows, n = mine[0].shape[1:]
+    zs = Z_SIZE // 2
+
+    def plan(info, parts, out):
+        at_y, at_x = info[0], info[1]
+        copies = []
+        for k in range(2):
+            at_c = info[2] if k == 0 else 1 - info[2]
+            block, from_x, from_y, far_a, far_b = parts[5 * k : 5 * k + 5]
+            copies += [
+                (block, out.at[:, at_y, at_x, at_c]),
+                (from_x, out.at[:, at_y, 1 - at_x, at_c]),
+                (from_y, out.at[:, 1 - at_y, at_x, at_c]),
+                (far_a, out.at[pl.ds(0, zs), 1 - at_y, 1 - at_x, at_c]),
+                (far_b, out.at[pl.ds(zs, zs), 1 - at_y, 1 - at_x, at_c]),
+            ]
+        return copies
+
+    shape = (Z_SIZE, Y_SIZE, X_SIZE, C_SIZE, rows, n)
+    full = assemble(plan, jnp.stack([y, x, c]), (*mine, *other), shape, "dense_assemble")
     return full.reshape(-1, n)
+
+
+def join_rows(other, own):
+    counts = [part.shape[1] for part in own]
+
+    def plan(info, parts, out):
+        copies = []
+        for k in range(2):
+            at = 0
+            for i, count in enumerate(counts):
+                target = out.at[pl.ds(k * Z_SIZE, Z_SIZE), pl.ds(at, count)]
+                copies.append((parts[k * len(counts) + i], target))
+                at += count
+        return copies
+
+    shape = (2 * Z_SIZE, sum(counts), own[0].shape[2])
+    return assemble(plan, jnp.zeros((1,), jnp.int32), (*other, *own), shape, "join_rows")
 
 
 def half_order(z_to):
@@ -535,17 +508,12 @@
 
 
 def weight_loads(pieces, w_s, sem, y):
-    zs = Z_SIZE // 2
-    count = len(pieces) // w_s.shape[0]
     copies = []
     for h in range(w_s.shape[0]):
-        places = [w_s.at[h, :, y]]
-        if count == 2:
-            places.append(w_s.at[h, :, 1 - y])
-        else:
-            places += [w_s.at[h, pl.ds(0, zs), 1 - y], w_s.at[h, pl.ds(zs, zs), 1 - y]]
-        for piece, place in zip(pieces[h * count : (h + 1) * count], places):
-            copies.append(pltpu.make_async_copy(piece, place, sem.at[len(copies)]))
+        for piece, at_y in zip(pieces[2 * h : 2 * h + 2], (y, 1 - y)):
+            copies.append(
+                pltpu.make_async_copy(piece, w_s.at[h, :, at_y], sem.at[len(copies)])
+            )
     return copies
 
 
@@ -626,7 +594,7 @@
             ],
             scratch_shapes=[
                 pltpu.VMEM((halves, Z_SIZE, Y_SIZE, rows, lanes), low),
-                pltpu.SemaphoreType.DMA((6,)),
+                pltpu.SemaphoreType.DMA((4,)),
             ],
         ),
         out_shape=[
@@ -635,7 +603,7 @@
             jax.ShapeDtypeStruct((total, 2 * half * halves), jnp.float32),
         ],
         input_output_aliases=aliases,
-        compiler_params=pltpu.CompilerParams(vmem_limit_bytes=48 * 1024 * 1024),
+        compiler_params=pltpu.CompilerParams(vmem_limit_bytes=60 * 1024 * 1024),
         cost_estimate=pl.CostEstimate(
             flops=2 * total * width * (3 * half * halves + length),
             bytes_accessed=2 * (sources * length * width + 2 * total * width)
@@ -785,7 +753,7 @@
                 pltpu.VMEM((total, 2 * half * halves), low),
                 pltpu.VMEM((total, half * halves), low),
                 pltpu.VMEM((halves, Z_SIZE, Y_SIZE, rows, lanes), low),
-                pltpu.SemaphoreType.DMA((6,)),
+                pltpu.SemaphoreType.DMA((4,)),
                 pltpu.SemaphoreType.DMA((4,)),
             ],
         ),
@@ -803,6 +771,103 @@
         name="expert_backward",
     )(info, slots, gates, grads_in, kept, gate_ups, *pieces, *waits)
     return result[0], result[1:]
+
+
+def middle_back_kernel(
+    c_ref, got, gates, small, gain, middle, hidden, cotangent, mixed, dmiddle, dbranch, mine, theirs,
+    g_s, sem,
+):
+    full = jnp.float32
+    low = jnp.bfloat16
+    c = c_ref[0]
+    length, width = middle.shape
+    total = got[0].astype(full)
+    for z in range(1, Z_SIZE):
+        total = total + got[z].astype(full)
+    parts = total[:, width:]
+    grad_gates = parts + pltpu.roll(parts, 64, 1)
+    gate = gates[...]
+    grad_logits = gate * (grad_gates - jnp.sum(gate * grad_gates, axis=1, keepdims=True))
+    grad_logits = grad_logits.astype(low)
+    dh2 = total[:, :width] + multiply_transposed(grad_logits, small[...])
+    value = middle[...]
+    inverse = rms_inverse(value)
+    normal = value * inverse
+    scaled = dh2 * gain[...]
+    mean = jnp.mean(scaled * normal, axis=1, keepdims=True)
+    grad = cotangent[...].astype(full) + inverse * (scaled - normal * mean)
+    dmiddle[...] = grad
+    branch = (residual_scale * grad).astype(low)
+    dbranch[...] = branch
+    blocks = g_s.shape[0]
+    per = g_s.shape[2]
+    step = width // Z_SIZE
+    rows = blocks // Z_SIZE
+    for z in range(Z_SIZE):
+        part = slice(z * step, (z + 1) * step)
+        here = slice(z * rows, (z + 1) * rows)
+        term = contract_rows(branch[:, part], mixed[...]).astype(low)
+        g_s[here, :, :, :width] = term.reshape(rows, C_SIZE, per, width)
+        router = contract_rows(hidden[:, part], grad_logits)
+        product = (dh2[:, part] * normal[:, part]).astype(low)
+        second = contract_rows(product, jnp.ones((length, 128), low))
+        lane = lax.broadcasted_iota(jnp.int32, router.shape, 1)
+        router = jnp.where(lane == EXPERTS, second, router).astype(low)
+        g_s[here, :, :, width:] = router.reshape(rows, C_SIZE, per, 128)
+    copies = [
+        pltpu.make_async_copy(g_s.at[:, c], mine, sem.at[0]),
+        pltpu.make_async_copy(g_s.at[:, 1 - c], theirs, sem.at[1]),
+    ]
+    for copy in copies:
+        copy.start()
+    for copy in copies:
+        copy.wait()
+
+
+def middle_backward(c, got, gates, pack, small_at, gain, middle, hidden, cotangent, mixed):
+    length, width = middle.shape
+    low = jnp.bfloat16
+    blocks = Z_SIZE * Y_SIZE * X_SIZE
+    per = width // (blocks * C_SIZE)
+    any_spec = pl.BlockSpec(memory_space=pl.ANY)
+    whole = lambda a: pl.BlockSpec(a.shape, lambda i, n: (0,) * a.ndim)
+    split = jax.ShapeDtypeStruct((blocks, per, width + 128), low)
+    rows = pl.BlockSpec((length, width), lambda i, n: (0, 0))
+    return pl.pallas_call(
+        middle_back_kernel,
+        grid_spec=pltpu.PrefetchScalarGridSpec(
+            num_scalar_prefetch=1,
+            grid=(1,),
+            in_specs=[
+                whole(got),
+                whole(gates),
+                pl.BlockSpec((width, 128), lambda i, n: (0, small_at // 128)),
+                whole(gain),
+                rows,
+                rows,
+                rows,
+                rows,
+            ],
+            out_specs=[rows, rows, any_spec, any_spec],
+            scratch_shapes=[
+                pltpu.VMEM((blocks, C_SIZE, per, width + 128), low),
+                pltpu.SemaphoreType.DMA((2,)),
+            ],
+        ),
+        out_shape=[
+            jax.ShapeDtypeStruct((length, width), jnp.float32),
+            jax.ShapeDtypeStruct((length, width), low),
+            split,
+            split,
+        ],
+        compiler_params=pltpu.CompilerParams(vmem_limit_bytes=56 * 1024 * 1024),
+        cost_estimate=pl.CostEstimate(
+            flops=2 * length * width * (width + 384),
+            bytes_accessed=length * width * 24 + 4 * width * width,
+            transcendentals=0,
+        ),
+        name="middle_backward",
+    )(c[None], got, gates, pack, gain, middle, hidden, cotangent, mixed)
 
 
 def turn_halves(value):
@@ -955,108 +1020,125 @@
 
 
 def attention_back_kernel(
-    length, dbranch, wo, q, k, v, lse, h1, wq, wk, wv, cosine, sine, *rest, first
+    length, dbranch, wo, q, k, v, lse, h1, wq, wk, wv, cosine, sine, tokens, *rest
 ):
-    grads, dh1, dh_s = rest[-3:]
+    mine, theirs, dh1, dh_s, g_s = rest[-5:]
+    c = length[1]
     step = pl.program_id(0)
     low = jnp.bfloat16
     full = jnp.float32
     rows = dbranch.shape[0]
-    blocks = rows // ROW_BLOCK
-    dmixed = mm(dbranch[...], wo[...]).astype(low)
-    lane = lax.broadcasted_iota(jnp.int32, (rows, 128), 1)
-    kept = lse[...]
-    query, key, value = q[...], k[...], v[...]
-    columns = [
-        jnp.sum(jnp.where(lane == (step + first) * PAIR * GROUP + i, kept, 0.0), axis=1, keepdims=True)
-        for i in range(PAIR * GROUP)
-    ]
-    masks = [block_mask(block, length[0]) for block in range(blocks)]
-    dq = [[] for _ in range(PAIR * GROUP)]
-    dks, dvs = [], []
-    for head in range(PAIR):
-        key_h = key[:, head * HEAD_SIZE : (head + 1) * HEAD_SIZE]
-        value_h = value[:, head * HEAD_SIZE : (head + 1) * HEAD_SIZE]
-        dk = [None] * blocks
-        dv = [None] * blocks
-        for block in range(blocks):
-            keys = (block + 1) * ROW_BLOCK
-            at = slice(block * ROW_BLOCK, (block + 1) * ROW_BLOCK)
-            query_h = heads_of(query[at], head * GROUP, GROUP)
-            dmixed_h = heads_of(dmixed[at], head * GROUP, GROUP)
-            log_total = jnp.concatenate(
-                [columns[head * GROUP + i][at] for i in range(GROUP)], axis=0
-            )
-            scores = multiply_transposed(query_h, key_h[:keys]) * score_scale
-            scores = jnp.where(masks[block], scores, masked_score)
-            probs = jnp.exp(scores - log_total)
-            dprobs = multiply_transposed(dmixed_h, value_h[:keys])
-            delta = jnp.sum(probs * dprobs, axis=1, keepdims=True)
-            dscores = (probs * (dprobs - delta)).astype(low)
-            dquery = mm(dscores, key_h[:keys]) * score_scale
-            dkey = contract_rows(dscores, query_h) * score_scale
-            dvalue = contract_rows(probs.astype(low), dmixed_h)
-            for i in range(GROUP):
-                dq[head * GROUP + i].append(dquery[i * ROW_BLOCK : (i + 1) * ROW_BLOCK])
-            for b in range(block + 1):
-                part = slice(b * ROW_BLOCK, (b + 1) * ROW_BLOCK)
-                dk[b] = dkey[part] if dk[b] is None else dk[b] + dkey[part]
-                dv[b] = dvalue[part] if dv[b] is None else dv[b] + dvalue[part]
-        dks.append(jnp.concatenate(dk, axis=0))
-        dvs.append(jnp.concatenate(dv, axis=0))
-    cos = cosine[...]
-    sin = sine[...]
-    dquery = jnp.concatenate([jnp.concatenate(o, axis=0) for o in dq], axis=1)
-    dquery = (dquery * cos - turn_halves(dquery * sin)).astype(low)
-    dkey = jnp.concatenate(dks, axis=1)
-    dkey = (dkey * cos[:, :KEY_LANES] - turn_halves(dkey * sin[:, :KEY_LANES])).astype(low)
-    dvalue = jnp.concatenate(dvs, axis=1).astype(low)
-    hidden = h1[...]
-    grads[:, :QUERY_LANES] = contract_rows(hidden, dquery).astype(low)
-    both = contract_rows(hidden, jnp.concatenate([dkey, dvalue], axis=1)).astype(low)
-    grads[:, QUERY_LANES:] = both
-    term = (
-        multiply_transposed(dquery, wq[...])
-        + multiply_transposed(dkey, wk[...])
-        + multiply_transposed(dvalue, wv[...])
-    )
-
-    @pl.when(step == 0)
+    split = (Z_SIZE * Y_SIZE * X_SIZE, C_SIZE, h1.shape[1] // (Z_SIZE * Y_SIZE * X_SIZE * C_SIZE))
+
+    @pl.when(step < pl.num_programs(0) - 1)
     def _():
-        dh_s[...] = term
-
-    @pl.when(step > 0)
-    def _():
-        dh_s[...] += term
+        blocks = rows // ROW_BLOCK
+        dmixed = mm(dbranch[...], wo[...]).astype(low)
+        lane = lax.broadcasted_iota(jnp.int32, (rows, 128), 1)
+        kept = lse[...]
+        query, key, value = q[...], k[...], v[...]
+        columns = [
+            jnp.sum(jnp.where(lane == step * PAIR * GROUP + i, kept, 0.0), axis=1, keepdims=True)
+            for i in range(PAIR * GROUP)
+        ]
+        masks = [block_mask(block, length[0]) for block in range(blocks)]
+        dq = [[] for _ in range(PAIR * GROUP)]
+        dks, dvs = [], []
+        for head in range(PAIR):
+            key_h = key[:, head * HEAD_SIZE : (head + 1) * HEAD_SIZE]
+            value_h = value[:, head * HEAD_SIZE : (head + 1) * HEAD_SIZE]
+            dk = [None] * blocks
+            dv = [None] * blocks
+            for block in range(blocks):
+                keys = (block + 1) * ROW_BLOCK
+                at = slice(block * ROW_BLOCK, (block + 1) * ROW_BLOCK)
+                query_h = heads_of(query[at], head * GROUP, GROUP)
+                dmixed_h = heads_of(dmixed[at], head * GROUP, GROUP)
+                log_total = jnp.concatenate(
+                    [columns[head * GROUP + i][at] for i in range(GROUP)], axis=0
+                )
+                scores = multiply_transposed(query_h, key_h[:keys]) * score_scale
+                scores = jnp.where(masks[block], scores, masked_score)
+                probs = jnp.exp(scores - log_total)
+                dprobs = multiply_transposed(dmixed_h, value_h[:keys])
+                delta = jnp.sum(probs * dprobs, axis=1, keepdims=True)
+                dscores = (probs * (dprobs - delta)).astype(low)
+                dquery = mm(dscores, key_h[:keys]) * score_scale
+                dkey = contract_rows(dscores, query_h) * score_scale
+                dvalue = contract_rows(probs.astype(low), dmixed_h)
+                for i in range(GROUP):
+                    dq[head * GROUP + i].append(dquery[i * ROW_BLOCK : (i + 1) * ROW_BLOCK])
+                for b in range(block + 1):
+                    part = slice(b * ROW_BLOCK, (b + 1) * ROW_BLOCK)
+                    dk[b] = dkey[part] if dk[b] is None else dk[b] + dkey[part]
+                    dv[b] = dvalue[part] if dv[b] is None else dv[b] + dvalue[part]
+            dks.append(jnp.concatenate(dk, axis=0))
+            dvs.append(jnp.concatenate(dv, axis=0))
+        cos = cosine[...]
+        sin = sine[...]
+        dquery = jnp.concatenate([jnp.concatenate(o, axis=0) for o in dq], axis=1)
+        dquery = (dquery * cos - turn_halves(dquery * sin)).astype(low)
+        dkey = jnp.concatenate(dks, axis=1)
+        dkey = (dkey * cos[:, :KEY_LANES] - turn_halves(dkey * sin[:, :KEY_LANES])).astype(low)
+        dvalue = jnp.concatenate(dvs, axis=1).astype(low)
+        hidden = h1[...]
+        got = contract_rows(hidden, dquery).astype(low)
+        g_s[:, :, :, :QUERY_LANES] = got.reshape(*split, QUERY_LANES)
+        got = contract_rows(hidden, jnp.concatenate([dkey, dvalue], axis=1)).astype(low)
+        g_s[:, :, :, QUERY_LANES:] = got.reshape(*split, 2 * KEY_LANES)
+        mine[...] = g_s[:, c]
+        theirs[...] = g_s[:, 1 - c]
+        term = (
+            multiply_transposed(dquery, wq[...])
+            + multiply_transposed(dkey, wk[...])
+            + multiply_transposed(dvalue, wv[...])
+        )
+
+        @pl.when(step == 0)
+        def _():
+            dh_s[...] = term
+
+        @pl.when(step > 0)
+        def _():
+            dh_s[...] += term
 
     @pl.when(step == pl.num_programs(0) - 1)
     def _():
-        dh1[...] = dh_s[...]
+        total = dh_s[...]
+        dh1[...] = total
+        value = tokens[...].astype(full)
+        product = (total * (value * rms_inverse(value))).astype(low)
+        column = contract_rows(product, jnp.ones((rows, 128), low)).astype(low)
+        g_s[:, :, :, :128] = column.reshape(*split, 128)
+        mine[:, :, :128] = g_s[:, c, :, :128]
+        theirs[:, :, :128] = g_s[:, 1 - c, :, :128]
 
 
 def attention_backward(
-    length, dbranch, out_t, q, k, v, lse, h1, weight, cosine, sine, first, steps, after=()
+    length, dbranch, q, k, v, lse, h1, weight, out_at, cosine, sine, tokens, after=()
 ):
     rows, width = dbranch.shape
-    pairs = KEY_VALUE_HEADS // PAIR
+    steps = KEY_VALUE_HEADS // PAIR
     low = jnp.bfloat16
     full = jnp.float32
     query_total = QUERY_HEADS * HEAD_SIZE
     key_total = KEY_VALUE_HEADS * HEAD_SIZE
     key_at = query_total // KEY_LANES
-    value_at = key_at + pairs
+    value_at = key_at + steps
     whole = lambda shape: pl.BlockSpec(shape, lambda i, n: (0, 0))
-    cols = lambda lanes, at: pl.BlockSpec((width, lanes), lambda i, n: (0, at + first + i))
-    part = lambda lanes: pl.BlockSpec((rows, lanes), lambda i, n: (0, first + i))
+    cols = lambda lanes, at: pl.BlockSpec((width, lanes), lambda i, n: (0, at + jnp.minimum(i, steps - 1)))
+    part = lambda lanes: pl.BlockSpec((rows, lanes), lambda i, n: (0, jnp.minimum(i, steps - 1)))
     lanes = QUERY_LANES + 2 * KEY_LANES
+    blocks = Z_SIZE * Y_SIZE * X_SIZE
+    per = width // (blocks * C_SIZE)
     return pl.pallas_call(
-        functools.partial(attention_back_kernel, first=first),
+        attention_back_kernel,
         grid_spec=pltpu.PrefetchScalarGridSpec(
             num_scalar_prefetch=1,
-            grid=(steps,),
+            grid=(steps + 1,),
             in_specs=[
                 whole((rows, width)),
-                cols(QUERY_LANES, 0),
+                cols(QUERY_LANES, out_at // QUERY_LANES),
                 part(QUERY_LANES),
                 part(KEY_LANES),
                 part(KEY_LANES),
@@ -1067,13 +1149,22 @@
                 cols(KEY_LANES, value_at),
                 whole((rows, QUERY_LANES)),
                 whole((rows, QUERY_LANES)),
+                whole((rows, width)),
             ]
             + [pl.BlockSpec(memory_space=pl.ANY)] * len(after),
-            out_specs=[pl.BlockSpec((width, lanes), lambda i, n: (0, i)), whole((rows, width))],
-            scratch_shapes=[pltpu.VMEM((rows, width), full)],
+            out_specs=[
+                pl.BlockSpec((blocks, per, lanes), lambda i, n: (0, 0, i)),
+                pl.BlockSpec((blocks, per, lanes), lambda i, n: (0, 0, i)),
+                whole((rows, width)),
+            ],
+            scratch_shapes=[
+                pltpu.VMEM((rows, width), full),
+                pltpu.VMEM((blocks, C_SIZE, per, lanes), low),
+            ],
         ),
         out_shape=[
-            jax.ShapeDtypeStruct((width, steps * lanes), low),
+            jax.ShapeDtypeStruct((blocks, per, steps * lanes + 128), low),
+            jax.ShapeDtypeStruct((blocks, per, steps * lanes + 128), low),
             jax.ShapeDtypeStruct((rows, width), full),
         ],
         compiler_params=pltpu.CompilerParams(vmem_limit_bytes=48 * 1024 * 1024),
@@ -1085,7 +1176,7 @@
             transcendentals=QUERY_HEADS * rows * rows,
         ),
         name="attention_backward",
-    )(length, dbranch, out_t, q, k, v, lse, h1, weight, weight, weight, cosine, sine, *after)
+    )(length, dbranch, weight, q, k, v, lse, h1, weight, weight, weight, cosine, sine, tokens, *after)
 
 
 def combine_kernel(slots, values, *rest):
@@ -1135,16 +1226,6 @@
     )(slots, values, *after)
 
 
-def line_terms(own, moved):
-    return [own[0].astype(jnp.float32) + moved[0].astype(jnp.float32)] + [
-        plus(own[s], moved[s]).astype(jnp.bfloat16) for s in range(1, Z_SIZE)
-    ]
-
-
-def line_first(terms):
-    return terms[1], terms[3]
-
-
 def weight_chunks(gate_up_weight, down_weight):
     experts, rows = gate_up_weight.shape[0], gate_up_weight.shape[1]
     gate, upper = gate_up_weight[..., :FF], gate_up_weight[..., FF:]
@@ -1160,55 +1241,66 @@
     ]
 
 
-def along_z(own, got, z):
-    result = jnp.zeros((Z_SIZE, *own.shape), own.dtype)
-    result = lax.dynamic_update_slice_in_dim(result, own[None], z, 0)
-    for step in range(1, Z_SIZE):
-        result = lax.dynamic_update_slice_in_dim(
-            result, got[step - 1][None], (z + Z_SIZE - step) % Z_SIZE, 0
-        )
-    return result
-
-
-def shift_sends(rounds, chunk, z, steps=(1, 2, 3), axis=0):
-    return [
-        move(
-            rounds.gate(lax.dynamic_index_in_dim(chunk, (z + step) % Z_SIZE, axis, keepdims=False)),
-            pairs_shift(step),
-        )
-        for step in steps
-    ]
+def finish_kernel(*refs):
+    parts, gate_up, down = refs[:5], refs[-2], refs[-1]
+    half = FF // 2
+    full = jnp.float32
+    for z_from in range(Z_SIZE):
+        for j in range(5):
+            expert, side = divmod(HALF_ORDER[z_from][j], 2)
+            cols = slice(side * half, (side + 1) * half)
+            gate_up[expert, :, cols] = parts[j][z_from, :, :half].astype(full)
+            cols_up = slice(FF + side * half, FF + (side + 1) * half)
+            gate_up[expert, :, cols_up] = parts[j][z_from, :, half : 2 * half].astype(full)
+            down[expert, :, cols] = parts[j][z_from, :, 2 * half :].astype(full)
+
+
+def finish_grads(backs, after):
+    rows = backs[0].shape[1]
+    experts = EXPERTS // (X_SIZE * C_SIZE)
+    vmem = pl.BlockSpec(memory_space=pltpu.VMEM)
+    return pl.pallas_call(
+        finish_kernel,
+        in_specs=[vmem] * 5 + [pl.BlockSpec(memory_space=pl.ANY)] * len(after),
+        out_specs=[vmem, vmem],
+        out_shape=[
+            jax.ShapeDtypeStruct((experts, rows, 2 * FF), jnp.float32),
+            jax.ShapeDtypeStruct((experts, rows, FF), jnp.float32),
+        ],
+        compiler_params=pltpu.CompilerParams(vmem_limit_bytes=40 * 1024 * 1024),
+        cost_estimate=pl.CostEstimate(
+            flops=0, bytes_accessed=experts * rows * FF * 18, transcendentals=0
+        ),
+        name="finish_grads",
+    )(*backs, *after)
 
 
 class DenseScatter:
-    def __init__(self, rounds, term, place):
-        self.rounds, self.place = rounds, place
-        z, y, x, c = place
-        rows, n = term.shape
-        rows = rows // (Z_SIZE * Y_SIZE * X_SIZE * C_SIZE)
-        blocks = term.reshape(Z_SIZE, Y_SIZE, X_SIZE, C_SIZE, rows, n)
-
-        def block(at_y, at_x, at_c):
-            got = lax.dynamic_slice(
-                blocks, (0, at_y, at_x, at_c, 0, 0), (Z_SIZE, 1, 1, 1, rows, n)
-            )
-            return got.reshape(Z_SIZE, rows, n)
-
-        order = [(y, x), (y, 1 - x), (1 - y, x), (1 - y, 1 - x)]
-        self.mine = [block(at_y, at_x, c) for at_y, at_x in order]
-        self.theirs = jnp.stack([block(at_y, at_x, 1 - c) for at_y, at_x in order])
+    def __init__(self, mine, theirs, place):
+        shape = (Z_SIZE, Y_SIZE, X_SIZE, *mine.shape[1:])
+        self.mine, self.theirs, self.place = mine.reshape(shape), theirs.reshape(shape), place
+
+    def block(self, other_y, other_x):
+        y = 1 - self.place[1] if other_y else self.place[1]
+        x = 1 - self.place[2] if other_x else self.place[2]
+        size = (Z_SIZE, 1, 1, *self.mine.shape[3:])
+        got = [
+            lax.dynamic_slice(a, (0, y, x, 0, 0), size).reshape(Z_SIZE, *size[3:])
+            for a in (self.mine, self.got)
+        ]
+        return plus(*got)
 
     def cores(self):
-        self.got = move(self.rounds.gate(self.theirs), PAIRS_C)
+        self.got = move(self.theirs, PAIRS_C)
         return [self.got]
 
     def first(self):
         low = jnp.bfloat16
         zs = Z_SIZE // 2
         self.near, self.to_x, self.to_y, far = [
-            plus(self.mine[i], self.got[i]) for i in range(4)
+            self.block(*at) for at in ((False, False), (False, True), (True, False), (True, True))
         ]
-        gate = self.rounds.gate
+        gate = lambda value: value
         self.via_x = move(gate(far[:zs].astype(low)), PAIRS_X)
         self.via_y = move(gate(far[zs:].astype(low)), PAIRS_Y)
         self.x_a = move(gate(self.to_x[:zs].astype(low)), PAIRS_X)
@@ -1218,37 +1310,44 @@
     def second(self):
         low = jnp.bfloat16
         zs = Z_SIZE // 2
-        gate = self.rounds.gate
+        gate = lambda value: value
         self.x_b = move(gate(plus(self.to_x[zs:], self.via_y).astype(low)), PAIRS_X)
         self.y_a = move(gate(plus(self.to_y[:zs], self.via_x).astype(low)), PAIRS_Y)
         return [self.x_b, self.y_a]
 
     def along(self):
         zs = Z_SIZE // 2
-        z = self.place[0]
-        total = jnp.concatenate(
+        self.total = jnp.concatenate(
             [
                 plus(self.near[:zs], self.x_a) + self.y_a.astype(jnp.float32),
                 plus(self.near[zs:], self.x_b) + self.y_b.astype(jnp.float32),
             ]
         ).astype(jnp.bfloat16)
-        self.own = lax.dynamic_index_in_dim(total, z, 0, keepdims=False)
-        self.parts = shift_sends(self.rounds, total, z)
-        return self.parts
+        self.parts = trade(self.total)
+        return [self.parts]
 
     def result(self):
-        return plus(self.own, self.parts[0]) + plus(self.parts[1], self.parts[2])
+        return jnp.sum(self.parts.astype(jnp.float32), axis=0)
+
+
+def of_core(term, c):
+    rows = term.shape[0] // (Z_SIZE * Y_SIZE * X_SIZE * C_SIZE)
+    blocks = term.reshape(Z_SIZE * Y_SIZE * X_SIZE, C_SIZE, rows, term.shape[1])
+    return lax.dynamic_index_in_dim(blocks, c, 1, keepdims=False)
 
 
 def plus(a, b):
     return a.astype(jnp.float32) + b.astype(jnp.float32)
 
 
-def ring_total(own, x_a, second):
-    y_b, y_a, x_b = second
+def ring_total(own, first, second, h):
+    x_a, y_b = first
+    x_b, y_a = second
     return jnp.concatenate(
-        [plus(own[0], x_a) + y_a.astype(jnp.float32), plus(own[1], x_b) + y_b.astype(jnp.float32)],
-        axis=1,
+        [
+            plus(own[0][h], x_a[h]) + y_a[h].astype(jnp.float32),
+            plus(own[1][h], x_b[h]) + y_b[h].astype(jnp.float32),
+        ]
     ).astype(jnp.bfloat16)
 
 
@@ -1288,61 +1387,47 @@
         [router_weight, first_gain[:, None], second_gain[:, None]], axis=1
     )
     small = jnp.pad(small, ((0, 0), (0, 128 - small.shape[1])))
-    shard = jnp.concatenate([qkv_weight, small], axis=1)
-    out_shard = out_weight.T
+    shard = jnp.concatenate([qkv_weight, small, out_weight.T], axis=1)
     table = slot_table.astype(low)
 
-    got = [move(shard, pairs_shift(s)) for s in steps]
-    tables = [move(table, pairs_shift(s)) for s in steps]
+    block = spread(shard)
+    tables = spread(table)
     cuts = weight_chunks(gate_up_weight, down_weight)
-    rounds.close(*got, *tables, *cuts)
+    rounds.close(block, tables)
 
     near, far, moved = [None] * 5, [None] * 5, [None] * 5
 
     def send_half(q):
-        return shift_sends(rounds, cuts[q], z)
-
-    def keep_half(q, got):
-        moved[q] = along_z(lax.dynamic_index_in_dim(cuts[q], z, 0, keepdims=False), got, z)
+        moved[q] = trade(gate(cuts[q]))
+        return [moved[q]]
 
     def send_near(q):
-        moved[q] = gate(moved[q])
         near[q] = (move(moved[q], PAIRS_X), move(moved[q], PAIRS_Y))
         return near[q]
 
     def send_far(q):
-        far[q] = (move(gate(near[q][1][:zs]), PAIRS_X), move(gate(near[q][0][zs:]), PAIRS_Y))
-        return far[q]
-
-    block = gate(along_z(shard, got, z))
-    out_got = [move(s, pairs_shift(i + 1)) for i, s in enumerate([gate(out_shard)] * 3)]
-    half_got = send_half(0)
+        far[q] = move(near[q][1], PAIRS_X) if q % 2 == 0 else move(near[q][0], PAIRS_Y)
+        return [far[q]]
+
     from_x, from_y = move(block, PAIRS_X), move(block, PAIRS_Y)
     block_c = move(block, PAIRS_C)
-    tables = jnp.stack([table] + tables)
-    tables_c = move(gate(tables), PAIRS_C)
-    rounds.close(from_x, from_y, block_c, *out_got, *half_got, tables_c)
-    keep_half(0, half_got)
-    far_a, far_b = move(gate(from_y[:zs]), PAIRS_X), move(gate(from_x[zs:]), PAIRS_Y)
-    from_x_c, from_y_c = move(gate(from_x), PAIRS_C), move(gate(from_y), PAIRS_C)
-    out_block = gate(along_z(out_shard, out_got, z))
-    out_x, out_y = move(out_block, PAIRS_X), move(out_block, PAIRS_Y)
-    out_block_c = move(out_block, PAIRS_C)
-    half_got = send_half(1)
-    rounds.close(far_a, far_b, from_x_c, from_y_c, out_x, out_y, out_block_c, *half_got)
-    keep_half(1, half_got)
-    far_a_c, far_b_c = move(gate(far_a), PAIRS_C), move(gate(far_b), PAIRS_C)
-    out_far_a, out_far_b = move(gate(out_y[:zs]), PAIRS_X), move(gate(out_x[zs:]), PAIRS_Y)
-    out_x_c, out_y_c = move(gate(out_x), PAIRS_C), move(gate(out_y), PAIRS_C)
-    half_got = send_half(2)
-    rounds.close(far_a_c, far_b_c, out_far_a, out_far_b, out_x_c, out_y_c, *half_got, *send_near(0))
-    keep_half(2, half_got)
-    first_pack = dense_assemble(
+    tables_c = move(tables, PAIRS_C)
+    rounds.close(from_x, from_y, block_c, tables_c, *send_half(0))
+    far_a, far_b = move(from_y[:zs], PAIRS_X), move(from_x[zs:], PAIRS_Y)
+    from_x_c, from_y_c = move(from_x, PAIRS_C), move(from_y, PAIRS_C)
+    rounds.close(far_a, far_b, from_x_c, from_y_c, *send_half(1))
+    far_a_c, far_b_c = move(far_a, PAIRS_C), move(far_b, PAIRS_C)
+    moved[0] = gate(moved[0])
+    send_half(2)
+    pack = dense_assemble(
         place,
         (block, from_x, from_y, far_a, far_b),
         (block_c, from_x_c, from_y_c, far_a_c, far_b_c),
     )
-    small_full = first_pack[:, qkv_weight.shape[1] :]
+    rounds.close(pack, moved[2], *send_near(0))
+    out_at = qkv_weight.shape[1] + small.shape[1]
+    out_t = pack[:, out_at:]
+    small_full = pack[:, qkv_weight.shape[1] : out_at]
     router_full = small_full[:, :EXPERTS]
     gain_one = small_full[:, EXPERTS].astype(full)
     gain_two = small_full[:, EXPERTS + 1].astype(full)
@@ -1353,19 +1438,13 @@
     cosine_table, sine_table = rope_tables(sequence_length)
     cosine_table = jnp.tile(cosine_table, (1, QUERY_LANES // HEAD_SIZE))
     sine_table = jnp.tile(sine_table, (1, QUERY_LANES // HEAD_SIZE))
-    out_far_a_c, out_far_b_c = move(gate(out_far_a), PAIRS_C), move(gate(out_far_b), PAIRS_C)
-    half_got = send_half(3)
     hidden_one, query_rows, keys, value_rows, mixed, log_totals = attention_forward(
-        lengths, tokens, gain_one[None, :], first_pack, cosine_table, sine_table, rounds.after()
-    )
-    rounds.close(out_far_a_c, out_far_b_c, *half_got, *send_near(1), mixed)
-    keep_half(3, half_got)
-    out_t = dense_assemble(
-        place,
-        (out_block, out_x, out_y, out_far_a, out_far_b),
-        (out_block_c, out_x_c, out_y_c, out_far_a_c, out_far_b_c),
-    )
-    half_got = send_half(4)
+        lengths, tokens, gain_one[None, :], pack, cosine_table, sine_table, rounds.after()
+    )
+    moved[1] = gate(moved[1])
+    rounds.close(*send_half(3), *send_near(1), mixed)
+    moved[2] = gate(moved[2])
+    send_half(4)
     branch = multiply_transposed(mixed, out_t)
     middle = inputs + residual_scale * branch
     inverse_two = rms_inverse(middle)
@@ -1373,38 +1452,21 @@
     hidden_two = (normal_two * gain_two).astype(low)
     grad_out = cotangent.astype(full)
 
-    rounds.close(*half_got, *send_near(2), hidden_two)
-    keep_half(4, half_got)
-    sent = gate(hidden_two)
-    up, down = line_hop(1, sent, sent)
-    own_c = move(sent, PAIRS_C)
-    rounds.close(up, down, own_c, *send_near(3), *send_far(0))
-    hops, hops_c = [(up, down)], []
-    for step, sends in ((2, lambda: (*send_near(4), *send_far(1))), (3, lambda: (*send_far(2), *send_far(3)))):
-        up, down = gate(hops[-1][0]), gate(hops[-1][1])
-        hops[-1] = (up, down)
-        hops_c.append((move(up, PAIRS_C), move(down, PAIRS_C)))
-        hops.append(line_hop(step, up, down))
-        rounds.close(*hops_c[-1], *hops[-1], *sends())
-    up, down = hops[-1]
-    hops_c.append((move(gate(up), PAIRS_C), move(gate(down), PAIRS_C)))
-    rounds.close(*hops_c[-1], *send_far(4))
-
-    def gathered(own, own_c, hops, hops_c):
-        return line_blocks(
-            z,
-            (own, *[h[0] for h in hops], *[h[1] for h in hops]),
-            (own_c, *[h[0] for h in hops_c], *[h[1] for h in hops_c]),
-        )
-
-    rows_in = gathered(hidden_two, own_c, hops, hops_c)
-    rings = [
-        (
-            [p for q in range(*cut) for p in (moved[q], near[q][1])],
-            [p for q in range(*cut) for p in (near[q][0], *far[q])],
-        )
-        for cut in UNIT_HALVES
-    ]
+    rounds.close(moved[4], *send_near(2))
+    rows_own = spread(gate(hidden_two))
+    moved[3] = gate(moved[3])
+    rounds.close(*send_near(3))
+    moved[4] = gate(moved[4])
+    rounds.close(*send_near(4))
+    for first, second in ((0, 1), (2, 3)):
+        near[first] = (near[first][0], gate(near[first][1]))
+        near[second] = (gate(near[second][0]), near[second][1])
+        rounds.close(*send_far(first), *send_far(second))
+    rounds.close(rows_own)
+    rows_own = gate(rows_own)
+    rows_other = move(rows_own, PAIRS_C)
+    rounds.close(rows_other)
+    rows_in = join_rows([rows_other], [rows_own])
     slots_in = jnp.concatenate([tables_c, tables], axis=0).astype(jnp.int32)
     logits_in = jnp.einsum("de,itd->iet", router_full, rows_in, preferred_element_type=full)
     chosen_in = slots_in >= 0
@@ -1427,6 +1489,12 @@
     buffer = None
     saved = {}
 
+    def ring(pair, own):
+        halves = range(*UNIT_HALVES[pair])
+        if own:
+            return [p for q in halves for p in (moved[q], near[q][1])]
+        return [p for q in halves for p in (near[q][0], far[q])]
+
     def run_forward(pair, own):
         nonlocal buffer
         at = pair + (pairs if own else 0)
@@ -1437,33 +1505,27 @@
             unit_slots[at],
             unit_gates[at],
             rows_in,
-            rings[pair][0 if own else 1],
+            ring(pair, own),
             buffer,
             rounds.after(),
         )
 
-    sent = gate(cotangent)
-    dy_c = move(sent, PAIRS_C)
-    dy_hops, dy_hops_c = [], []
-    up = down = sent
+    dy_own = spread(gate(cotangent))
+    late = [(4,), (), ()]
     for pair in range(pairs):
-        if pair > 0:
-            up, down = gate(up), gate(down)
-            dy_hops[-1] = (up, down)
-            dy_hops_c.append((move(up, PAIRS_C), move(down, PAIRS_C)))
-        up, down = line_hop(pair + 1, up, down)
-        dy_hops.append((up, down))
+        sent = []
+        for q in late[pair]:
+            near[q] = tuple(gate(part) for part in near[q])
+            sent += send_far(q)
         run_forward(pair, False)
         run_forward(pair, True)
-        rounds.close(up, down, saved[pair + pairs][0], *(dy_hops_c[-1] if dy_hops_c else (dy_c,)))
-    up, down = gate(up), gate(down)
-    dy_hops[-1] = (up, down)
-    dy_hops_c.append((move(up, PAIRS_C), move(down, PAIRS_C)))
+        rounds.close(saved[pair + pairs][0], *sent)
     mix_other, mix_own = combine(all_slots, buffer, rounds.after())
-    rounds.close(mix_other, *dy_hops_c[-1])
-    mix_moved = move(gate(mix_other), PAIRS_C)
-    grads_in = gathered(cotangent, dy_c, dy_hops, dy_hops_c)
-    rounds.close(mix_moved, grads_in)
+    rounds.close(mix_other, dy_own)
+    mix_moved = move(mix_other, PAIRS_C)
+    dy_other = move(dy_own, PAIRS_C)
+    rounds.close(mix_moved, dy_other)
+    grads_in = join_rows([dy_other], [dy_own])
 
     back = None
     grads = [[None, None] for _ in units]
@@ -1479,7 +1541,7 @@
             unit_gates[at],
             grads_in,
             *saved[at],
-            rings[pair][0 if own else 1],
+            ring(pair, own),
             back,
             rounds.after(),
         )
@@ -1503,140 +1565,87 @@
         return seconds[u]
 
     def total_of(u):
-        x_b, y_a = seconds[u]
-        x_a, y_b = firsts[u]
-        return ring_total(grads[u][1], x_a, (y_b, y_a, x_b))
-
-    def hop_sum(step, terms, up, down):
-        up = move(gate(up), pairs_up_below(step - 1))
-        down = move(gate(down), pairs_down_above(Z_SIZE - step))
-        return up, down
-
-    terms = line_terms(mix_own, mix_moved)
-    up, down = hop_sum(1, terms, terms[1], terms[3])
+        return [ring_total(grads[u][1], firsts[u], seconds[u], h) for h in range(sizes[u])]
+
+    terms = plus(mix_own, mix_moved).astype(low)
+    mix_got = trade(gate(terms))
     run_back(0, False)
-    rounds.close(up, down, grads[0][0][0])
-    up, down = hop_sum(2, terms, plus(terms[2], up).astype(low), plus(terms[2], down).astype(low))
+    rounds.close(grads[0][0][0])
     run_back(0, True)
-    rounds.close(up, down, grads[0][1][0], *send_via(0))
-    up, down = hop_sum(3, terms, plus(terms[3], up).astype(low), plus(terms[1], down).astype(low))
+    rounds.close(grads[0][1][0], *send_via(0))
     run_back(1, False)
-    rounds.close(up, down, grads[1][0][0], *send_first(0))
-    output = (middle + residual_scale * (terms[0] + plus(up, down))).astype(low)
+    rounds.close(grads[1][0][0], *send_first(0))
     run_back(1, True)
-    rounds.close(grads[1][1][0], *send_second(0))
-    totals = [total_of(0), None, None]
-    backs = [[], [], []]
-
-    def send_back(u, step):
-        backs[u] += shift_sends(rounds, totals[u], z, (step,), 1)
-        return backs[u][-1:]
+    rounds.close(mix_got, grads[1][1][0], *send_second(0))
+    mixture = jnp.sum(mix_got.astype(full), axis=0)
+    output = (middle + residual_scale * mixture).astype(low)
+    totals = total_of(0)
+    backs = []
+
+    def send_back():
+        q = len(backs)
+        backs.append(trade(gate(totals[q])))
+        return backs[-1:]
 
     run_back(2, False)
-    rounds.close(grads[2][0][0], *send_via(1), *send_back(0, 1))
+    rounds.close(grads[2][0][0], *send_via(1), *send_back())
     run_back(2, True)
-    rounds.close(grads[2][1][0], *send_first(1), *send_back(0, 2))
+    rounds.close(grads[2][1][0], *send_first(1), *send_back())
     copy_other, copy_own = combine(all_slots, back, rounds.after())
-    rounds.close(copy_other, *send_second(1), *send_back(0, 3))
-    copy_moved = move(gate(copy_other), PAIRS_C)
-    rounds.close(copy_moved, *send_via(2))
-    terms = line_terms(copy_own, copy_moved)
-    up, down = hop_sum(1, terms, terms[1], terms[3])
-    totals[1] = total_of(1)
-    rounds.close(up, down, *send_first(2))
-    up, down = hop_sum(2, terms, plus(terms[2], up).astype(low), plus(terms[2], down).astype(low))
-    rounds.close(up, down, *send_second(2))
-    up, down = hop_sum(3, terms, plus(terms[3], up).astype(low), plus(terms[1], down).astype(low))
-    rounds.close(up, down)
-    copy_sum = terms[0] + plus(up, down)
-    totals[2] = total_of(2)
-    grad_gates = copy_sum[:, width : width + EXPERTS] + copy_sum[:, width + 64 : width + 64 + EXPERTS]
-    copy_sum = copy_sum[:, :width]
-
+    rounds.close(copy_other, *send_second(1), *send_via(2))
+    copy_moved = move(copy_other, PAIRS_C)
+    rounds.close(copy_moved)
+    copy_got = trade(plus(copy_own, copy_moved).astype(low))
+    rounds.close(copy_got)
+    totals += total_of(1)
     chosen = (slot_table >= 0).T
     gates = dense_gates(jnp.dot(hidden_two, router_full, preferred_element_type=full), chosen)
-    grad_logits = (
-        gates * (grad_gates - jnp.sum(gates * grad_gates, axis=-1, keepdims=True))
-    ).astype(low)
-    grad_hidden_two = copy_sum + multiply_transposed(grad_logits, router_full)
-    router_term = contract_rows(hidden_two, grad_logits)
-    second_term, grad_norm_two = norm_backward(
-        grad_hidden_two, normal_two, inverse_two, gain_two
-    )
-    grad_middle = grad_out + grad_norm_two
-    branch_gradient = (residual_scale * grad_middle).astype(low)
-    small_term = jnp.concatenate([router_term, second_term[:, None]], axis=1)
-    out_pack = jnp.concatenate(
-        [
-            contract_rows(branch_gradient, mixed),
-            jnp.pad(small_term, ((0, 0), (0, 128 - small_term.shape[1]))),
-        ],
-        axis=1,
-    ).astype(low)
-    out_scatter = DenseScatter(rounds, out_pack, place)
-
-    def run_attention(first):
-        return attention_backward(
-            lengths,
-            branch_gradient,
-            out_t,
-            query_rows,
-            keys,
-            value_rows,
-            log_totals,
-            hidden_one,
-            first_pack,
-            cosine_table,
-            sine_table,
-            first,
-            2,
-            rounds.after(),
-        )
-
-    rounds.close(out_scatter.theirs, branch_gradient, *send_back(1, 1))
-    qkv_terms = [None, None]
-    qkv_terms[0], part_one = run_attention(0)
-    rounds.close(part_one, *out_scatter.cores(), *send_back(1, 2))
-    qkv_terms[1], part_two = run_attention(2)
-    qkv_scatter = [DenseScatter(rounds, qkv_terms[0], place)]
-    rounds.close(part_two, *out_scatter.first(), *qkv_scatter[0].cores(), *send_back(1, 3))
-    grad_hidden_one = part_one + part_two
-    first_term, grad_norm_one = norm_backward(
+    grad_middle, branch_gradient, out_mine, out_theirs = middle_backward(
+        c,
+        copy_got,
+        jnp.pad(gates, ((0, 0), (0, 128 - EXPERTS))),
+        pack,
+        qkv_weight.shape[1],
+        gain_two[None, :],
+        middle,
+        hidden_two,
+        cotangent,
+        mixed,
+    )
+    out_scatter = DenseScatter(out_mine, out_theirs, place)
+    rounds.close(out_scatter.theirs, branch_gradient)
+    qkv_mine, qkv_theirs, grad_hidden_one = attention_backward(
+        jnp.concatenate([lengths, c[None]]),
+        branch_gradient,
+        query_rows,
+        keys,
+        value_rows,
+        log_totals,
+        hidden_one,
+        pack,
+        out_at,
+        cosine_table,
+        sine_table,
+        tokens,
+        rounds.after(),
+    )
+    rounds.close(grad_hidden_one, *out_scatter.cores(), *send_back(), *send_first(2))
+    qkv_scatter = DenseScatter(qkv_mine, qkv_theirs, place)
+    rounds.close(*qkv_scatter.cores(), *out_scatter.first(), *send_back(), *send_second(2))
+    totals += total_of(2)
+    rounds.close(*qkv_scatter.first(), *out_scatter.second(), *send_back())
+    rounds.close(*qkv_scatter.second(), *out_scatter.along())
+    qkv_scatter.along()
+    gate_up_grads, down_grads = finish_grads(backs, [qkv_scatter.total])
+    down_grads = down_grads.transpose(0, 2, 1)
+    _, grad_norm_one = norm_backward(
         grad_hidden_one, normal_one, inverse_one, gain_one
     )
     grad_input = grad_middle + grad_norm_one
 
-    first_pack_term = jnp.pad(first_term[:, None], ((0, 0), (0, 127))).astype(low)
-    qkv_scatter.append(
-        DenseScatter(rounds, jnp.concatenate([qkv_terms[1], first_pack_term], axis=1), place)
-    )
-    sent = [*out_scatter.second(), *qkv_scatter[0].first(), *qkv_scatter[1].cores()]
-    for step in steps:
-        sent += send_back(2, step)
-    rounds.close(*sent)
-    rounds.close(*out_scatter.along(), *qkv_scatter[0].second(), *qkv_scatter[1].first())
-    rounds.close(*qkv_scatter[0].along(), *qkv_scatter[1].second())
-    qkv_scatter[1].along()
-    back = jnp.concatenate(
-        [
-            along_z(lax.dynamic_index_in_dim(totals[u], z, 1, keepdims=False), backs[u], z)
-            for u in units
-        ],
-        axis=1,
-    ).reshape(Z_SIZE * 5, rows, -1)
-    weight_sums = jnp.stack([back[HALF_PLACE[q]] for q in range(Z_SIZE * 5)]).astype(full)
-    weight_sums = weight_sums.reshape(EXPERTS // (X_SIZE * C_SIZE), 2, rows, 3 * FF // 2)
-    parts = [
-        weight_sums[..., i * FF // 2 : (i + 1) * FF // 2].transpose(0, 2, 1, 3).reshape(-1, rows, FF)
-        for i in range(3)
-    ]
-    gate_up_grads = jnp.concatenate(parts[:2], axis=-1)
-    down_grads = parts[2].transpose(0, 2, 1)
-
-    qkv_sums = [scatter.result() for scatter in qkv_scatter]
-    first_sum = qkv_sums[-1][:, -128]
-    qkv_sums[-1] = qkv_sums[-1][:, :-128]
-    qkv_sum = jnp.concatenate(qkv_sums, axis=1)
+    qkv_sum = qkv_scatter.result()
+    first_sum = qkv_sum[:, -128]
+    qkv_sum = qkv_sum[:, :-128]
     qkv_sum = qkv_sum.reshape(qkv_sum.shape[0], -1, QUERY_LANES + 2 * KEY_LANES)
     qkv_sum = jnp.concatenate(
         [

time: 1280 us -> 1130 us (0.88)
  local copies, waits for them, and re-layouts: 211 us -> 101 us
  waiting for transfers between devices: 307 us -> 394 us
  starting transfers between devices: 204 us -> 135 us
  other arithmetic: 146 us -> 95.7 us
  Pallas kernels: 366 us -> 380 us
    all_to_all x0 -> x18, waiting for transfers between devices: none -> 159 us  [trade(): lax.all_to_all(value, 'dp', split_axis=0, concat_axis=0, axis_index_group...]
    ppermute x160 -> x61, starting transfers between devices: 204 us -> 50.6 us  [move(): return lax.ppermute(value, MESH_AXES, pairs)]
    all_to_all x0 -> x18, starting transfers between devices: none -> 84.8 us  [trade(): lax.all_to_all(value, 'dp', split_axis=0, concat_axis=0, axis_index_group...]
    ppermute x160 -> x61, waiting for transfers between devices: 307 us -> 235 us  [move(): return lax.ppermute(value, MESH_AXES, pairs)]
    unnamed x537 -> x311, local copies, waits for them, and re-layouts: 96.9 us -> 51.3 us
    dynamic_update_slice x36 -> x0, local copies, waits for them, and re-layouts: 40 us -> none  [the longest x30 33.1 us: along_z(): lax.dynamic_update_slice_in_dim(result, got[step - 1][None], (z + Z_SIZE...]
    slice x25 -> x4, local copies, waits for them, and re-layouts: 32.2 us -> 1.91 us  [the longest x2 1.25 us: body(): far_a, far_b = (move(from_y[:zs], PAIRS_X), move(from_x[zs:], PAIRS_Y))]
    convert_element_type x11 -> x3, other arithmetic: 38.8 us -> 17.5 us  [the longest x1 7.42 us: body(): terms = plus(mix_own, mix_moved).astype(low)]
  transfers between devices with their start and end apart: 160 -> 79, of which waited for: 48 -> 38; matrix products, arithmetic and copies ran while one was open for 24% -> 12% of each run, Pallas kernels for 26% -> 31%
where the time goes in v3:
time: 1130 us; the launch traced here: 1120 us
  waiting for transfers between devices  394 us (35%)
  Pallas kernels  380 us (34%)
  starting transfers between devices  135 us (12%)
  local copies, waits for them, and re-layouts  101 us (9%)
  other arithmetic  95.7 us (8%)
    ppermute x61, waiting for transfers between devices, move(): return lax.ppermute(value, MESH_AXES, pairs)  235 us
    all_to_all x18, waiting for transfers between devices, trade(): lax.all_to_all(value, 'dp', split_axis=0, concat_axis=0, axis_index_group...  159 us
    pallas_call x6, Pallas kernels, expert_backward(): pl.pallas_call(functools.partial(expert_back_kernel, count=len(pieces), w...  143 us
    pallas_call x6, Pallas kernels, expert_forward(): pl.pallas_call(functools.partial(expert_forward_kernel, count=len(pieces)...  91.6 us
    all_to_all x18, starting transfers between devices, trade(): lax.all_to_all(value, 'dp', split_axis=0, concat_axis=0, axis_index_group...  84.8 us
    unnamed x311, local copies, waits for them, and re-layouts  51.3 us
    ppermute x61, starting transfers between devices, move(): return lax.ppermute(value, MESH_AXES, pairs)  50.6 us
    pallas_call x2, Pallas kernels, combine(): pl.pallas_call(combine_kernel, grid=(sources,), in_specs=[pl.BlockSpec((1...  38.2 us
  transfers between devices with their start and end apart: 79, of which 38 were waited for; matrix products, arithmetic and copies ran while one was open for 12% of the time, Pallas kernels for 31%

profile of v3, /device:TPU:0, one launch (start us, length us, event | category | flops | bytes accessed | tf_op | source)
XLA Modules:
  0.0 1119.5 jit_solution(5193035777547150750)
XLA Ops:
  29.7 27.5 %all-to-all-done.refs_0_ = bf16[4,48,4224]{2,1,0:T(8,128)(2,1)S(1)} async-done(((bf16[4,48,4224]{2,1,0:T(8,128)(2,1)}), bf16[4,48,4224]{2,1,0:T(8,128)(2,1)S(1)}, u32[]{:S(2)}, u32[]{:S(2)}) %all-to-all-start) | async-done | bytes 1622048 | tf_op jit(solution)/shard_map/all_to_all | solution.py:371
  70.2 29.7 %collective-permute-done.refs_1_.refs_0_ = bf16[4,48,4224]{2,1,0:T(8,128)(2,1)S(1)} collective-permute-done((bf16[4,48,4224]{2,1,0:T(8,128)(2,1)S(1)}, bf16[4,48,4224]{2,1,0:T(8,128)(2,1)S(1)}, u32[]{:S(2)}, u32[]{:S(2)}) %collective-permute-start) | collective-permute-done | bytes 1622048 | tf_op jit(solution)/shard_map/ppermute | solution.py:406
  115.3 14.3 %collective-permute-done.2.refs_3_.refs_0_ = bf16[2,48,4224]{2,1,0:T(8,128)(2,1)S(1)} collective-permute-done((bf16[2,48,4224]{2,1,0:T(8,128)(2,1)S(1)}, bf16[2,48,4224]{2,1,0:T(8,128)(2,1)S(1)}, u32[]{:S(2)}, u32[]{:S(2)}) %collective-permute-start.2) | collective-permute-done | bytes 811040 | tf_op jit(solution)/shard_map/ppermute | solution.py:406
  156.2 10.2 collective-permute-done.10.refs_2_.rest_0_
  181.5 18.6 %attention_forward.1 = (bf16[384,1536]{1,0:T(8,128)(2,1)S(1)}, bf16[384,1536]{1,0:T(8,128)(2,1)S(1)}, bf16[384,512]{1,0:T(8,128)(2,1)S(1)}, bf16[384,512]{1,0:T(...) custom-call(s32[1]{0:T(128)S(6)} %copy.285.length, bf16[384,1536]{1,0:T(8,128)(2,1)} %tokens.3, ...), custom_call_target="tpu_custom_call" | custom-call | flops 3925868544 | bytes 13762560 | tf_op jit(solution)/shard_map/attention_forward/pallas_call | solution.py:978
  219.0 16.7 %collective-permute-done.14.refs_1_.rest_0_ = bf16[4,192,768]{2,1,0:T(8,128)(2,1)S(1)} collective-permute-done((bf16[4,192,768]{2,1,0:T(8,128)(2,1)}, bf16[4,192,768]{2,1,0:T(8,128)(2,1)S(1)}, u32[]{:S(2)}, u32[]{:S(2)}) %collective-permute-start.14) | collective-permute-done | bytes 1179680 | tf_op jit(solution)/shard_map/ppermute | solution.py:406
  247.6 25.6 %collective-permute-done.16.refs_0_ = bf16[4,192,768]{2,1,0:T(8,128)(2,1)S(1)} collective-permute-done((bf16[4,192,768]{2,1,0:T(8,128)(2,1)}, bf16[4,192,768]{2,1,0:T(8,128)(2,1)S(1)}, u32[]{:S(2)}, u32[]{:S(2)}) %collective-permute-start.16) | collective-permute-done | bytes 1179680 | tf_op jit(solution)/shard_map/ppermute | solution.py:406
  277.3 24.7 %collective-permute-done.18.refs_0_ = bf16[4,192,768]{2,1,0:T(8,128)(2,1)S(1)} collective-permute-done((bf16[4,192,768]{2,1,0:T(8,128)(2,1)}, bf16[4,192,768]{2,1,0:T(8,128)(2,1)S(1)}, u32[]{:S(2)}, u32[]{:S(2)}) %collective-permute-start.18) | collective-permute-done | bytes 1179680 | tf_op jit(solution)/shard_map/ppermute | solution.py:406
  306.2 23.8 %collective-permute-done.20.refs_0_.rest_1_ = bf16[4,192,768]{2,1,0:T(8,128)(2,1)S(1)} collective-permute-done((bf16[4,192,768]{2,1,0:T(8,128)(2,1)}, bf16[4,192,768]{2,1,0:T(8,128)(2,1)S(1)}, u32[]{:S(2)}, u32[]{:S(2)}) %collective-permute-start.20) | collective-permute-done | bytes 1179680 | tf_op jit(solution)/shard_map/ppermute | solution.py:406
  334.1 23.0 %collective-permute-done.22.refs_0_.rest_1_ = bf16[4,192,768]{2,1,0:T(8,128)(2,1)S(1)} collective-permute-done((bf16[4,192,768]{2,1,0:T(8,128)(2,1)}, bf16[4,192,768]{2,1,0:T(8,128)(2,1)S(1)}, u32[]{:S(2)}, u32[]{:S(2)}) %collective-permute-start.22) | collective-permute-done | bytes 1179680 | tf_op jit(solution)/shard_map/ppermute | solution.py:406
  391.5 16.4 %expert_forward.6 = (bf16[8,960,1536]{2,1,0:T(8,128)(2,1)}, bf16[1280,1536]{1,0:T(8,128)(2,1)}, f32[1280,1024]{1,0:T(8,128)}) custom-call(s32[2]{0:T(128)} %pad_add_fusion.6.info, s32[8,1,384]{2,1,0:T(1,128)} %copy-done.148, f32[8,1,384]{2,1,0:T(1,128)} %get-tuple-element.286.gates, bf16[8,384,1536]{2,1,0:T(8,128)(2,1)} %copy-done, ...), custom_call_target="tpu_custom_call" | custom-call | flops 7549747200 | bytes 27262976 | tf_op jit(solution)/shard_map/expert_forward/pallas_call | solution.py:579
  407.9 16.5 %expert_forward.7 = (bf16[8,960,1536]{2,1,0:T(8,128)(2,1)}, bf16[1280,1536]{1,0:T(8,128)(2,1)}, f32[1280,1024]{1,0:T(8,128)}) custom-call(s32[2]{0:T(128)} %pad_add_fusion.5.info, s32[8,1,384]{2,1,0:T(1,128)} %copy-done.145, f32[8,1,384]{2,1,0:T(1,128)} %get-tuple-element.287.gates, bf16[8,384,1536]{2,1,0:T(8,128)(2,1)} %copy-done, ...), custom_call_target="tpu_custom_call", output_to_operand_aliasing={{0}: (8, {})} | custom-call | flops 7549747200 | bytes 27262976 | tf_op jit(solution)/shard_map/expert_forward/pallas_call | solution.py:579
  426.0 16.4 %expert_forward.8 = (bf16[8,960,1536]{2,1,0:T(8,128)(2,1)}, bf16[1280,1536]{1,0:T(8,128)(2,1)}, f32[1280,1024]{1,0:T(8,128)}) custom-call(s32[2]{0:T(128)} %pad_add_fusion.4.info, s32[8,1,384]{2,1,0:T(1,128)} %copy-done.144, f32[8,1,384]{2,1,0:T(1,128)} %get-tuple-element.288.gates, bf16[8,384,1536]{2,1,0:T(8,128)(2,1)} %copy-done, ...), custom_call_target="tpu_custom_call", output_to_operand_aliasing={{0}: (8, {})} | custom-call | flops 7549747200 | bytes 27262976 | tf_op jit(solution)/shard_map/expert_forward/pallas_call | solution.py:579
  442.4 16.4 %expert_forward.9 = (bf16[8,960,1536]{2,1,0:T(8,128)(2,1)}, bf16[1280,1536]{1,0:T(8,128)(2,1)}, f32[1280,1024]{1,0:T(8,128)}) custom-call(s32[2]{0:T(128)} %pad_add_fusion.3.info, s32[8,1,384]{2,1,0:T(1,128)} %copy-done.143, f32[8,1,384]{2,1,0:T(1,128)} %get-tuple-element.289.gates, bf16[8,384,1536]{2,1,0:T(8,128)(2,1)} %copy-done, ...), custom_call_target="tpu_custom_call", output_to_operand_aliasing={{0}: (8, {})} | custom-call | flops 7549747200 | bytes 27262976 | tf_op jit(solution)/shard_map/expert_forward/pallas_call | solution.py:579
  459.4 12.9 %expert_forward.10 = (bf16[8,960,1536]{2,1,0:T(8,128)(2,1)}, bf16[1280,1536]{1,0:T(8,128)(2,1)}, f32[1280,512]{1,0:T(8,128)}) custom-call(s32[2]{0:T(128)} %pad_add_fusion.2.info, s32[8,1,384]{2,1,0:T(1,128)} %copy-done.137, f32[8,1,384]{2,1,0:T(1,128)} %get-tuple-element.290.gates, bf16[8,384,1536]{2,1,0:T(8,128)(2,1)} %copy-done, ...), custom_call_target="tpu_custom_call", output_to_operand_aliasing={{0}: (6, {})} | custom-call | flops 4529848320 | bytes 22282240 | tf_op jit(solution)/shard_map/expert_forward/pallas_call | solution.py:579
  472.3 13.0 %expert_forward.11 = (bf16[8,960,1536]{2,1,0:T(8,128)(2,1)}, bf16[1280,1536]{1,0:T(8,128)(2,1)}, f32[1280,512]{1,0:T(8,128)}) custom-call(s32[2]{0:T(128)} %pad_add_fusion.1.info, s32[8,1,384]{2,1,0:T(1,128)} %copy-done.136, f32[8,1,384]{2,1,0:T(1,128)} %get-tuple-element.291.gates, bf16[8,384,1536]{2,1,0:T(8,128)(2,1)} %copy-done, ...), custom_call_target="tpu_custom_call", output_to_operand_aliasing={{0}: (6, {})} | custom-call | flops 4529848320 | bytes 22282240 | tf_op jit(solution)/shard_map/expert_forward/pallas_call | solution.py:579
  485.9 18.3 %combine.2 = (bf16[4,384,1536]{2,1,0:T(8,128)(2,1)}, bf16[4,384,1536]{2,1,0:T(8,128)(2,1)}) custom-call(s32[8,6,384]{2,1,0:T(8,128)} %concatenate.129.slots, bf16[8,960,1536]{2,1,0:T(8,128)(2,1)} %get-tuple-element.84.values, f32[8,128]{1,0:T(8,128)} %join.43.rest_0_.refs_2_), custom_call_target="tpu_custom_call" | custom-call | flops 9059696640 | bytes 33030144 | tf_op jit(solution)/shard_map/combine/pallas_call | solution.py:1205
  533.5 26.2 %expert_backward.6 = (bf16[8,960,1664]{2,1,0:T(8,128)(2,1)}, bf16[2,2,192,768]{3,2,1,0:T(8,128)(2,1)}, bf16[2,2,192,768]{3,2,1,0:T(8,128)(2,1)}, bf16[2,2,192,76...) custom-call(s32[2]{0:T(128)} %pad_add_fusion.6.info, s32[8,1,384]{2,1,0:T(1,128)} %copy-done.148, ...), custom_call_target="tpu_custom_call" | custom-call | flops 13589544960 | bytes 31981568 | tf_op jit(solution)/shard_map/expert_backward/pallas_call | solution.py:732
  561.8 26.3 %expert_backward.7 = (bf16[8,960,1664]{2,1,0:T(8,128)(2,1)}, bf16[2,2,192,768]{3,2,1,0:T(8,128)(2,1)}, bf16[2,2,192,768]{3,2,1,0:T(8,128)(2,1)}, bf16[2,2,192,76...) custom-call(s32[2]{0:T(128)} %pad_add_fusion.5.info, s32[8,1,384]{2,1,0:T(1,128)} %copy-done.145, ...), custom_call_target="tpu_custom_call", output_to_operand_aliasing={{0}: (10, {})} | custom-call | flops 13589544960 | bytes 31981568 | tf_op jit(solution)/shard_map/expert_backward/pallas_call | solution.py:732
  597.1 26.3 %expert_backward.8 = (bf16[8,960,1664]{2,1,0:T(8,128)(2,1)}, bf16[2,2,192,768]{3,2,1,0:T(8,128)(2,1)}, bf16[2,2,192,768]{3,2,1,0:T(8,128)(2,1)}, bf16[2,2,192,76...) custom-call(s32[2]{0:T(128)} %pad_add_fusion.4.info, s32[8,1,384]{2,1,0:T(1,128)} %copy-done.144, ...), custom_call_target="tpu_custom_call", output_to_operand_aliasing={{0}: (10, {})} | custom-call | flops 13589544960 | bytes 31981568 | tf_op jit(solution)/shard_map/expert_backward/pallas_call | solution.py:732
  627.0 26.6 %expert_backward.9 = (bf16[8,960,1664]{2,1,0:T(8,128)(2,1)}, bf16[2,2,192,768]{3,2,1,0:T(8,128)(2,1)}, bf16[2,2,192,768]{3,2,1,0:T(8,128)(2,1)}, bf16[2,2,192,76...) custom-call(s32[2]{0:T(128)} %pad_add_fusion.3.info, s32[8,1,384]{2,1,0:T(1,128)} %copy-done.143, ...), custom_call_target="tpu_custom_call", output_to_operand_aliasing={{0}: (10, {})} | custom-call | flops 13589544960 | bytes 31981568 | tf_op jit(solution)/shard_map/expert_backward/pallas_call | solution.py:732
  669.8 18.9 %expert_backward.10 = (bf16[8,960,1664]{2,1,0:T(8,128)(2,1)}, bf16[1,2,192,768]{3,2,1,0:T(8,128)(2,1)}, bf16[1,2,192,768]{3,2,1,0:T(8,128)(2,1)}, bf16[1,2,192,7...) custom-call(s32[2]{0:T(128)} %pad_add_fusion.2.info, s32[8,1,384]{2,1,0:T(1,128)} %copy-done.137, ...), custom_call_target="tpu_custom_call", output_to_operand_aliasing={{0}: (8, {})} | custom-call | flops 7549747200 | bytes 24641536 | tf_op jit(solution)/shard_map/expert_backward/pallas_call | solution.py:732
  700.6 19.0 %expert_backward.11 = (bf16[8,960,1664]{2,1,0:T(8,128)(2,1)}, bf16[1,2,192,768]{3,2,1,0:T(8,128)(2,1)}, bf16[1,2,192,768]{3,2,1,0:T(8,128)(2,1)}, bf16[1,2,192,7...) custom-call(s32[2]{0:T(128)} %pad_add_fusion.1.info, s32[8,1,384]{2,1,0:T(1,128)} %copy-done.136, ...), custom_call_target="tpu_custom_call", output_to_operand_aliasing={{0}: (8, {})} | custom-call | flops 7549747200 | bytes 24641536 | tf_op jit(solution)/shard_map/expert_backward/pallas_call | solution.py:732
  727.7 19.9 %combine.3 = (bf16[4,384,1664]{2,1,0:T(8,128)(2,1)}, bf16[4,384,1664]{2,1,0:T(8,128)(2,1)}) custom-call(s32[8,6,384]{2,1,0:T(8,128)} %concatenate.129.slots, bf16[8,960,1664]{2,1,0:T(8,128)(2,1)} %get-tuple-element.115.values, f32[8,128]{1,0:T(8,128)} %join.51.rest_0_.refs_1_.refs_5_), custom_call_target="tpu_custom_call" | custom-call | flops 9814671360 | bytes 35782656 | tf_op jit(solution)/shard_map/combine/pallas_call | solution.py:1205
  747.6 8.7 collective-permute-done.38.refs_0_
  782.7 100.7 %all-to-all-done.12.got.refs_0_ = bf16[4,384,1664]{2,1,0:T(8,128)(2,1)} async-done(((bf16[4,384,1664]{2,1,0:T(8,128)(2,1)}), bf16[4,384,1664]{2,1,0:T(8,128)(2,1)}, u32[]{:S(2)}, u32[]{:S(2)}) %all-to-all-start.12) | async-done | bytes 5111840 | tf_op jit(solution)/shard_map/all_to_all | solution.py:371
  883.4 13.7 %middle_backward.1 = (f32[384,1536]{1,0:T(8,128)}, bf16[384,1536]{1,0:T(8,128)(2,1)}, bf16[16,48,1664]{2,1,0:T(8,128)(2,1)}, bf16[16,48,1664]{2,1,0:T(8,128)(2,1)}) custom-call(s32[1]{0:T(128)} %bitcast.2.c_ref, bf16[4,384,1664]{2,1,0:T(8,128)(2,1)} %all-to-all-done.12.got.refs_0_, f32[384,128]{1,0:T(8,128)} %pad.9.gates, bf16[1536,4224]{1,0:T(8,128)(2,1)} %bitcast.324, ...), custom_call_target="tpu_custom_call" | custom-call | flops 2264924160 | bytes 23592960 | tf_op jit(solution)/shard_map/middle_backward/pallas_call | solution.py:836
  922.6 36.0 %attention_backward.1 = (bf16[16,48,2688]{2,1,0:T(8,128)(2,1)}, bf16[16,48,2688]{2,1,0:T(8,128)(2,1)}, f32[384,1536]{1,0:T(8,128)}) custom-call(s32[2]{0:T(128)S(1)} %pad_add_fusion.7.length, bf16[384,1536]{1,0:T(8,128)(2,1)S(1)} %copy-done.26, bf16[1536,4224]{1,0:T(8,128)(2,1)} %bitcast.325, bf16[384,1536]{1,0:T(8,128)(2,1)S(1)} %copy-done.32, ...), custom_call_target="tpu_custom_call" | custom-call | flops 10116661248 | bytes 28704768 | tf_op jit(solution)/shard_map/attention_backward/pallas_call | solution.py:1134
  986.3 9.8 all-to-all-done.15.refs_2_
  1005.6 10.6 collective-permute-done.59.refs_7_
  1052.5 10.7 collective-permute-done.47
  1079.3 11.1 all-to-all-done.17.refs_4_
  (652 shorter events, 427.8 us)
Async XLA Ops:
  16.8 40.4 %all-to-all-start = ((bf16[4,48,4224]{2,1,0:T(8,128)(2,1)}), bf16[4,48,4224]{2,1,0:T(8,128)(2,1)S(1)}, u32[]{:S(2)}, u32[]{:S(2)}) async-start(bf16[4,48,4224]{2,1,0:T(8,128)(2,1)} %broadcast_in_dim.39), calls=%async_computation | async-start | bytes 3244032 | tf_op jit(solution)/shard_map/all_to_all | solution.py:371
  58.9 43.3 %all-to-all-start.2 = ((bf16[4,192,768]{2,1,0:T(8,128)(2,1)}), bf16[4,192,768]{2,1,0:T(8,128)(2,1)}, u32[]{:S(2)}, u32[]{:S(2)}) async-start(bf16[4,192,768]{2,1,0:T(8,128)(2,1)} %tie.43), calls=%async_computation.2 | async-start | bytes 2359296 | tf_op jit(solution)/shard_map/all_to_all | solution.py:371
  63.4 36.5 %collective-permute-start = (bf16[4,48,4224]{2,1,0:T(8,128)(2,1)S(1)}, bf16[4,48,4224]{2,1,0:T(8,128)(2,1)S(1)}, u32[]{:S(2)}, u32[]{:S(2)}) collective-permute-start(bf16[4,48,4224]{2,1,0:T(8,128)(2,1)S(1)} %copy-done.3), channel_id=1, source_target_pairs={{0,2},{1,3},{2,0},{3,1},{4,6},{5,7},{6,4},{7,5},{8,10},{9,11},{10,... | collective-permute-start | bytes 4866056 | tf_op jit(solution)/shard_map/ppermute | solution.py:406
  65.0 36.1 %collective-permute-start.1 = (bf16[4,48,4224]{2,1,0:T(8,128)(2,1)S(1)}, bf16[4,48,4224]{2,1,0:T(8,128)(2,1)S(1)}, u32[]{:S(2)}, u32[]{:S(2)}) collective-permute-start(bf16[4,48,4224]{2,1,0:T(8,128)(2,1)S(1)} %copy-done.3), channel_id=1, source_target_pairs={{0,4},{1,5},{2,6},{3,7},{4,0},{5,1},{6,2},{7,3},{8,12},{9,13},{10,... | collective-permute-start | bytes 4866056 | tf_op jit(solution)/shard_map/ppermute | solution.py:406
  66.5 35.8 %collective-permute-start.4 = (bf16[4,48,4224]{2,1,0:T(8,128)(2,1)S(1)}, bf16[4,48,4224]{2,1,0:T(8,128)(2,1)}, u32[]{:S(2)}, u32[]{:S(2)}) collective-permute-start(bf16[4,48,4224]{2,1,0:T(8,128)(2,1)S(1)} %copy-done.3), channel_id=1, source_target_pairs={{0,1},{1,0},{2,3},{3,2},{4,5},{5,4},{6,7},{7,6},{8,9},{9,8},{10,11... | collective-permute-start | bytes 4866056 | tf_op jit(solution)/shard_map/ppermute | solution.py:406
  102.9 31.3 %all-to-all-start.3 = ((bf16[4,192,768]{2,1,0:T(8,128)(2,1)}), bf16[4,192,768]{2,1,0:T(8,128)(2,1)}, u32[]{:S(2)}, u32[]{:S(2)}) async-start(bf16[4,192,768]{2,1,0:T(8,128)(2,1)} %tie.44), calls=%async_computation.3 | async-start | bytes 2359296 | tf_op jit(solution)/shard_map/all_to_all | solution.py:371
  134.8 32.4 %all-to-all-start.4 = ((bf16[4,192,768]{2,1,0:T(8,128)(2,1)}), bf16[4,192,768]{2,1,0:T(8,128)(2,1)}, u32[]{:S(2)}, u32[]{:S(2)}) async-start(bf16[4,192,768]{2,1,0:T(8,128)(2,1)} %tie.45), calls=%async_computation.4 | async-start | bytes 2359296 | tf_op jit(solution)/shard_map/all_to_all | solution.py:371
  167.7 35.6 %all-to-all-start.5 = ((bf16[4,192,768]{2,1,0:T(8,128)(2,1)}), bf16[4,192,768]{2,1,0:T(8,128)(2,1)}, u32[]{:S(2)}, u32[]{:S(2)}) async-start(bf16[4,192,768]{2,1,0:T(8,128)(2,1)} %tie.47), calls=%async_computation.5 | async-start | bytes 2359296 | tf_op jit(solution)/shard_map/all_to_all | solution.py:371
  173.1 30.2 %collective-permute-start.12 = (bf16[4,192,768]{2,1,0:T(8,128)(2,1)}, bf16[4,192,768]{2,1,0:T(8,128)(2,1)}, u32[]{:S(2)}, u32[]{:S(2)}) collective-permute-start(bf16[4,192,768]{2,1,0:T(8,128)(2,1)} %tie.48.rest_2_), channel_id=1, source_target_pairs={{0,2},{1,3},{2,0},{3,1},{4,6},{5,7},{6,4},{7,5},{8,10},{9,11},{10,... | collective-permute-start | bytes 3538952 | tf_op jit(solution)/shard_map/ppermute | solution.py:406
  204.3 32.3 %all-to-all-start.6 = ((bf16[4,192,768]{2,1,0:T(8,128)(2,1)}), bf16[4,192,768]{2,1,0:T(8,128)(2,1)}, u32[]{:S(2)}, u32[]{:S(2)}) async-start(bf16[4,192,768]{2,1,0:T(8,128)(2,1)} %tie.49), calls=%async_computation.6 | async-start | bytes 2359296 | tf_op jit(solution)/shard_map/all_to_all | solution.py:371
  241.1 118.6 %all-to-all-start.7 = ((bf16[4,384,1536]{2,1,0:T(8,128)(2,1)}), bf16[4,384,1536]{2,1,0:T(8,128)(2,1)}, u32[]{:S(2)}, u32[]{:S(2)}) async-start(bf16[4,384,1536]{2,1,0:T(8,128)(2,1)} %broadcast_in_dim.44), calls=%async_computation.7 | async-start | bytes 9437184 | tf_op jit(solution)/shard_map/all_to_all | solution.py:371
  373.0 131.3 %all-to-all-start.8 = ((bf16[4,384,1536]{2,1,0:T(8,128)(2,1)}), bf16[4,384,1536]{2,1,0:T(8,128)(2,1)}, u32[]{:S(2)}, u32[]{:S(2)}) async-start(bf16[4,384,1536]{2,1,0:T(8,128)(2,1)} %broadcast_in_dim.47), calls=%async_computation.8 | async-start | bytes 9437184 | tf_op jit(solution)/shard_map/all_to_all | solution.py:371
  380.2 44.1 %collective-permute-start.25 = (bf16[4,192,768]{2,1,0:T(8,128)(2,1)}, bf16[4,192,768]{2,1,0:T(8,128)(2,1)S(1)}, u32[]{:S(2)}, u32[]{:S(2)}) collective-permute-start(bf16[4,192,768]{2,1,0:T(8,128)(2,1)} %tie.59.rest_1_), channel_id=1, source_target_pairs={{0,2},{1,3},{2,0},{3,1},{4,6},{5,7},{6,4},{7,5},{8,10},{9,11},{10,... | collective-permute-start | bytes 3538952 | tf_op jit(solution)/shard_map/ppermute | solution.py:406
  521.1 138.4 %all-to-all-start.9 = ((bf16[4,384,1536]{2,1,0:T(8,128)(2,1)}), bf16[4,384,1536]{2,1,0:T(8,128)(2,1)}, u32[]{:S(2)}, u32[]{:S(2)}) async-start(bf16[4,384,1536]{2,1,0:T(8,128)(2,1)} %tie.62), calls=%async_computation.9 | async-start | bytes 9437184 | tf_op jit(solution)/shard_map/all_to_all | solution.py:371
  590.8 32.6 %collective-permute-start.30 = (bf16[2,2,192,768]{3,2,1,0:T(8,128)(2,1)}, bf16[2,2,192,768]{3,2,1,0:T(8,128)(2,1)}, u32[]{:S(2)}, u32[]{:S(2)}) collective-permute-start(bf16[2,2,192,768]{3,2,1,0:T(8,128)(2,1)} %tie.65), channel_id=1, source_target_pairs={{0,2},{1,3},{2,0},{3,1},{4,6},{5,7},{6,4},{7,5},{8,10},{9,11},{10,... | collective-permute-start | bytes 3538952 | tf_op jit(solution)/shard_map/ppermute | solution.py:406
  591.8 31.6 %collective-permute-start.31 = (bf16[2,2,192,768]{3,2,1,0:T(8,128)(2,1)}, bf16[2,2,192,768]{3,2,1,0:T(8,128)(2,1)S(1)}, u32[]{:S(2)}, u32[]{:S(2)}) collective-permute-start(bf16[2,2,192,768]{3,2,1,0:T(8,128)(2,1)} %tie.66), channel_id=1, source_target_pairs={{0,4},{1,5},{2,6},{3,7},{4,0},{5,1},{6,2},{7,3},{8,12},{9,13},{10,... | collective-permute-start | bytes 3538952 | tf_op jit(solution)/shard_map/ppermute | solution.py:406
  625.1 32.0 %collective-permute-start.32 = (bf16[2,2,192,768]{3,2,1,0:T(8,128)(2,1)}, bf16[2,2,192,768]{3,2,1,0:T(8,128)(2,1)S(1)}, u32[]{:S(2)}, u32[]{:S(2)}) collective-permute-start(bf16[2,2,192,768]{3,2,1,0:T(8,128)(2,1)} %tie.67), channel_id=1, source_target_pairs={{0,2},{1,3},{2,0},{3,1},{4,6},{5,7},{6,4},{7,5},{8,10},{9,11},{10,... | collective-permute-start | bytes 3538952 | tf_op jit(solution)/shard_map/ppermute | solution.py:406
  660.1 32.5 %all-to-all-start.10 = ((bf16[4,192,768]{2,1,0:T(8,128)(2,1)}), bf16[4,192,768]{2,1,0:T(8,128)(2,1)S(1)}, u32[]{:S(2)}, u32[]{:S(2)}) async-start(bf16[4,192,768]{2,1,0:T(8,128)(2,1)} %tie.71), calls=%async_computation.10 | async-start | bytes 2359296 | tf_op jit(solution)/shard_map/all_to_all | solution.py:371
  694.2 31.5 %all-to-all-start.11 = ((bf16[4,192,768]{2,1,0:T(8,128)(2,1)}), bf16[4,192,768]{2,1,0:T(8,128)(2,1)S(1)}, u32[]{:S(2)}, u32[]{:S(2)}) async-start(bf16[4,192,768]{2,1,0:T(8,128)(2,1)} %tie.74), calls=%async_computation.11 | async-start | bytes 2359296 | tf_op jit(solution)/shard_map/all_to_all | solution.py:371
  764.6 118.8 %all-to-all-start.12 = ((bf16[4,384,1664]{2,1,0:T(8,128)(2,1)}), bf16[4,384,1664]{2,1,0:T(8,128)(2,1)}, u32[]{:S(2)}, u32[]{:S(2)}) async-start(bf16[4,384,1664]{2,1,0:T(8,128)(2,1)} %add_convert_fusion), calls=%async_computation.12 | async-start | bytes 10223616 | tf_op jit(solution)/shard_map/all_to_all | solution.py:371
  777.8 130.4 %collective-permute-start.39 = (bf16[2,2,192,768]{3,2,1,0:T(8,128)(2,1)}, bf16[2,2,192,768]{3,2,1,0:T(8,128)(2,1)S(1)}, u32[]{:S(2)}, u32[]{:S(2)}) collective-permute-start(bf16[2,2,192,768]{3,2,1,0:T(8,128)(2,1)} %tie.75), channel_id=1, source_target_pairs={{0,2},{1,3},{2,0},{3,1},{4,6},{5,7},{6,4},{7,5},{8,10},{9,11},{10,... | collective-permute-start | bytes 3538952 | tf_op jit(solution)/shard_map/ppermute | solution.py:406
  778.8 129.3 %collective-permute-start.40 = (bf16[2,2,192,768]{3,2,1,0:T(8,128)(2,1)}, bf16[2,2,192,768]{3,2,1,0:T(8,128)(2,1)}, u32[]{:S(2)}, u32[]{:S(2)}) collective-permute-start(bf16[2,2,192,768]{3,2,1,0:T(8,128)(2,1)} %tie.76), channel_id=1, source_target_pairs={{0,4},{1,5},{2,6},{3,7},{4,0},{5,1},{6,2},{7,3},{8,12},{9,13},{10,... | collective-permute-start | bytes 3538952 | tf_op jit(solution)/shard_map/ppermute | solution.py:406
  779.3 126.0 %collective-permute-start.42 = (bf16[1,2,192,768]{3,2,1,0:T(8,128)(2,1)}, bf16[1,2,192,768]{3,2,1,0:T(8,128)(2,1)S(1)}, u32[]{:S(2)}, u32[]{:S(2)}) collective-permute-start(bf16[1,2,192,768]{3,2,1,0:T(8,128)(2,1)} %tie.78), channel_id=1, source_target_pairs={{0,4},{1,5},{2,6},{3,7},{4,0},{5,1},{6,2},{7,3},{8,12},{9,13},{10,... | collective-permute-start | bytes 1769480 | tf_op jit(solution)/shard_map/ppermute | solution.py:406
  781.7 124.6 %collective-permute-start.41 = (bf16[1,2,192,768]{3,2,1,0:T(8,128)(2,1)}, bf16[1,2,192,768]{3,2,1,0:T(8,128)(2,1)S(1)}, u32[]{:S(2)}, u32[]{:S(2)}) collective-permute-start(bf16[1,2,192,768]{3,2,1,0:T(8,128)(2,1)} %tie.77), channel_id=1, source_target_pairs={{0,2},{1,3},{2,0},{3,1},{4,6},{5,7},{6,4},{7,5},{8,10},{9,11},{10,... | collective-permute-start | bytes 1769480 | tf_op jit(solution)/shard_map/ppermute | solution.py:406
  900.5 68.2 %collective-permute-start.50 = (bf16[4,2,2,48,1664]{4,3,0,2,1:T(8,128)(2,1)}, bf16[4,2,2,48,1664]{4,3,0,2,1:T(8,128)(2,1)}, u32[]{:S(2)}, u32[]{:S(2)}) collective-permute-start(bf16[4,2,2,48,1664]{4,3,0,2,1:T(8,128)(2,1)} %copy.203), channel_id=1, source_target_pairs={{0,1},{1,0},{2,3},{3,2},{4,5},{5,4},{6,7},{7,6},{8,9},{9,8},{10,11... | collective-permute-start | bytes 7667720 | tf_op jit(solution)/shard_map/ppermute | solution.py:406
  963.0 64.9 %collective-permute-start.43 = (bf16[4,2,2,48,2688]{4,3,0,2,1:T(8,128)(2,1)}, bf16[4,2,2,48,2688]{4,3,0,2,1:T(8,128)(2,1)}, u32[]{:S(2)}, u32[]{:S(2)}) collective-permute-start(bf16[4,2,2,48,2688]{4,3,0,2,1:T(8,128)(2,1)} %copy.198), channel_id=1, source_target_pairs={{0,1},{1,0},{2,3},{3,2},{4,5},{5,4},{6,7},{7,6},{8,9},{9,8},{10,11... | collective-permute-start | bytes 12386312 | tf_op jit(solution)/shard_map/ppermute | solution.py:406
  963.4 32.6 %all-to-all-start.15 = ((bf16[4,192,768]{2,1,0:T(8,128)(2,1)}), bf16[4,192,768]{2,1,0:T(8,128)(2,1)S(1)}, u32[]{:S(2)}, u32[]{:S(2)}) async-start(bf16[4,192,768]{2,1,0:T(8,128)(2,1)} %tie.79), calls=%async_computation.15 | async-start | bytes 2359296 | tf_op jit(solution)/shard_map/all_to_all | solution.py:371
  974.5 46.1 %collective-permute-start.51 = (bf16[2,48,1664]{2,1,0:T(8,128)(2,1)}, bf16[2,48,1664]{2,1,0:T(8,128)(2,1)}, u32[]{:S(2)}, u32[]{:S(2)}) collective-permute-start(bf16[2,48,1664]{2,1,0:T(8,128)(2,1)} %fusion.59), channel_id=1, source_target_pairs={{0,2},{1,3},{2,0},{3,1},{4,6},{5,7},{6,4},{7,5},{8,10},{9,11},{10,... | collective-permute-start | bytes 958472 | tf_op jit(solution)/shard_map/ppermute | solution.py:406
  983.5 37.1 %collective-permute-start.56 = (bf16[2,48,1664]{2,1,0:T(8,128)(2,1)}, bf16[2,48,1664]{2,1,0:T(8,128)(2,1)}, u32[]{:S(2)}, u32[]{:S(2)}) collective-permute-start(bf16[2,48,1664]{2,1,0:T(8,128)(2,1)} %fusion.60), channel_id=1, source_target_pairs={{0,4},{1,5},{2,6},{3,7},{4,0},{5,1},{6,2},{7,3},{8,12},{9,13},{10,... | collective-permute-start | bytes 958472 | tf_op jit(solution)/shard_map/ppermute | solution.py:406
  997.7 45.9 %all-to-all-start.16 = ((bf16[4,192,768]{2,1,0:T(8,128)(2,1)}), bf16[4,192,768]{2,1,0:T(8,128)(2,1)S(1)}, u32[]{:S(2)}, u32[]{:S(2)}) async-start(bf16[4,192,768]{2,1,0:T(8,128)(2,1)} %tie.82), calls=%async_computation.16 | async-start | bytes 2359296 | tf_op jit(solution)/shard_map/all_to_all | solution.py:371
  1035.3 40.1 %collective-permute-start.44 = (bf16[2,48,2688]{2,1,0:T(8,128)(2,1)}, bf16[2,48,2688]{2,1,0:T(8,128)(2,1)}, u32[]{:S(2)}, u32[]{:S(2)}) collective-permute-start(bf16[2,48,2688]{2,1,0:T(8,128)(2,1)} %fusion.51), channel_id=1, source_target_pairs={{0,2},{1,3},{2,0},{3,1},{4,6},{5,7},{6,4},{7,5},{8,10},{9,11},{10,... | collective-permute-start | bytes 1548296 | tf_op jit(solution)/shard_map/ppermute | solution.py:406
  1037.1 38.2 %collective-permute-start.49 = (bf16[2,48,2688]{2,1,0:T(8,128)(2,1)}, bf16[2,48,2688]{2,1,0:T(8,128)(2,1)}, u32[]{:S(2)}, u32[]{:S(2)}) collective-permute-start(bf16[2,48,2688]{2,1,0:T(8,128)(2,1)} %fusion.52), channel_id=1, source_target_pairs={{0,4},{1,5},{2,6},{3,7},{4,0},{5,1},{6,2},{7,3},{8,12},{9,13},{10,... | collective-permute-start | bytes 1548296 | tf_op jit(solution)/shard_map/ppermute | solution.py:406
  (199 other events, 1450.5 us)

commit v4 on v3

--- a/solution.py
+++ b/solution.py
@@ -799,24 +799,22 @@
     dmiddle[...] = grad
     branch = (residual_scale * grad).astype(low)
     dbranch[...] = branch
-    blocks = g_s.shape[0]
-    per = g_s.shape[2]
+    per = g_s.shape[3]
     step = width // Z_SIZE
-    rows = blocks // Z_SIZE
+    rows = Y_SIZE * X_SIZE
     for z in range(Z_SIZE):
         part = slice(z * step, (z + 1) * step)
-        here = slice(z * rows, (z + 1) * rows)
         term = contract_rows(branch[:, part], mixed[...]).astype(low)
-        g_s[here, :, :, :width] = term.reshape(rows, C_SIZE, per, width)
+        g_s[:, z, :, :, :width] = term.reshape(rows, C_SIZE, per, width)
         router = contract_rows(hidden[:, part], grad_logits)
         product = (dh2[:, part] * normal[:, part]).astype(low)
         second = contract_rows(product, jnp.ones((length, 128), low))
         lane = lax.broadcasted_iota(jnp.int32, router.shape, 1)
         router = jnp.where(lane == EXPERTS, second, router).astype(low)
-        g_s[here, :, :, width:] = router.reshape(rows, C_SIZE, per, 128)
+        g_s[:, z, :, :, width:] = router.reshape(rows, C_SIZE, per, 128)
     copies = [
-        pltpu.make_async_copy(g_s.at[:, c], mine, sem.at[0]),
-        pltpu.make_async_copy(g_s.at[:, 1 - c], theirs, sem.at[1]),
+        pltpu.make_async_copy(g_s.at[:, :, c], mine, sem.at[0]),
+        pltpu.make_async_copy(g_s.at[:, :, 1 - c], theirs, sem.at[1]),
     ]
     for copy in copies:
         copy.start()
@@ -827,11 +825,11 @@
 def middle_backward(c, got, gates, pack, small_at, gain, middle, hidden, cotangent, mixed):
     length, width = middle.shape
     low = jnp.bfloat16
-    blocks = Z_SIZE * Y_SIZE * X_SIZE
-    per = width // (blocks * C_SIZE)
+    blocks = (Y_SIZE * X_SIZE, Z_SIZE)
+    per = width // (Y_SIZE * X_SIZE * Z_SIZE * C_SIZE)
     any_spec = pl.BlockSpec(memory_space=pl.ANY)
     whole = lambda a: pl.BlockSpec(a.shape, lambda i, n: (0,) * a.ndim)
-    split = jax.ShapeDtypeStruct((blocks, per, width + 128), low)
+    split = jax.ShapeDtypeStruct((*blocks, per, width + 128), low)
     rows = pl.BlockSpec((length, width), lambda i, n: (0, 0))
     return pl.pallas_call(
         middle_back_kernel,
@@ -850,7 +848,7 @@
             ],
             out_specs=[rows, rows, any_spec, any_spec],
             scratch_shapes=[
-                pltpu.VMEM((blocks, C_SIZE, per, width + 128), low),
+                pltpu.VMEM((*blocks, C_SIZE, per, width + 128), low),
                 pltpu.SemaphoreType.DMA((2,)),
             ],
         ),
@@ -1028,7 +1026,8 @@
     low = jnp.bfloat16
     full = jnp.float32
     rows = dbranch.shape[0]
-    split = (Z_SIZE * Y_SIZE * X_SIZE, C_SIZE, h1.shape[1] // (Z_SIZE * Y_SIZE * X_SIZE * C_SIZE))
+    span = h1.shape[1] // Z_SIZE
+    split = (Y_SIZE * X_SIZE, C_SIZE, span // (Y_SIZE * X_SIZE * C_SIZE))
 
     @pl.when(step < pl.num_programs(0) - 1)
     def _():
@@ -1083,11 +1082,15 @@
         dvalue = jnp.concatenate(dvs, axis=1).astype(low)
         hidden = h1[...]
         got = contract_rows(hidden, dquery).astype(low)
-        g_s[:, :, :, :QUERY_LANES] = got.reshape(*split, QUERY_LANES)
+        for z in range(Z_SIZE):
+            part = got[z * span : (z + 1) * span]
+            g_s[:, z, :, :, :QUERY_LANES] = part.reshape(*split, QUERY_LANES)
         got = contract_rows(hidden, jnp.concatenate([dkey, dvalue], axis=1)).astype(low)
-        g_s[:, :, :, QUERY_LANES:] = got.reshape(*split, 2 * KEY_LANES)
-        mine[...] = g_s[:, c]
-        theirs[...] = g_s[:, 1 - c]
+        for z in range(Z_SIZE):
+            part = got[z * span : (z + 1) * span]
+            g_s[:, z, :, :, QUERY_LANES:] = part.reshape(*split, 2 * KEY_LANES)
+        mine[...] = g_s[:, :, c]
+        theirs[...] = g_s[:, :, 1 - c]
         term = (
             multiply_transposed(dquery, wq[...])
             + multiply_transposed(dkey, wk[...])
@@ -1109,9 +1112,11 @@
         value = tokens[...].astype(full)
         product = (total * (value * rms_inverse(value))).astype(low)
         column = contract_rows(product, jnp.ones((rows, 128), low)).astype(low)
-        g_s[:, :, :, :128] = column.reshape(*split, 128)
-        mine[:, :, :128] = g_s[:, c, :, :128]
-        theirs[:, :, :128] = g_s[:, 1 - c, :, :128]
+        for z in range(Z_SIZE):
+            part = column[z * span : (z + 1) * span]
+            g_s[:, z, :, :, :128] = part.reshape(*split, 128)
+        mine[:, :, :, :128] = g_s[:, :, c, :, :128]
+        theirs[:, :, :, :128] = g_s[:, :, 1 - c, :, :128]
 
 
 def attention_backward(
@@ -1129,8 +1134,8 @@
     cols = lambda lanes, at: pl.BlockSpec((width, lanes), lambda i, n: (0, at + jnp.minimum(i, steps - 1)))
     part = lambda lanes: pl.BlockSpec((rows, lanes), lambda i, n: (0, jnp.minimum(i, steps - 1)))
     lanes = QUERY_LANES + 2 * KEY_LANES
-    blocks = Z_SIZE * Y_SIZE * X_SIZE
-    per = width // (blocks * C_SIZE)
+    blocks = (Y_SIZE * X_SIZE, Z_SIZE)
+    per = width // (Y_SIZE * X_SIZE * Z_SIZE * C_SIZE)
     return pl.pallas_call(
         attention_back_kernel,
         grid_spec=pltpu.PrefetchScalarGridSpec(
@@ -1153,18 +1158,18 @@
             ]
             + [pl.BlockSpec(memory_space=pl.ANY)] * len(after),
             out_specs=[
-                pl.BlockSpec((blocks, per, lanes), lambda i, n: (0, 0, i)),
-                pl.BlockSpec((blocks, per, lanes), lambda i, n: (0, 0, i)),
+                pl.BlockSpec((*blocks, per, lanes), lambda i, n: (0, 0, 0, i)),
+                pl.BlockSpec((*blocks, per, lanes), lambda i, n: (0, 0, 0, i)),
                 whole((rows, width)),
             ],
             scratch_shapes=[
                 pltpu.VMEM((rows, width), full),
-                pltpu.VMEM((blocks, C_SIZE, per, lanes), low),
+                pltpu.VMEM((*blocks, C_SIZE, per, lanes), low),
             ],
         ),
         out_shape=[
-            jax.ShapeDtypeStruct((blocks, per, steps * lanes + 128), low),
-            jax.ShapeDtypeStruct((blocks, per, steps * lanes + 128), low),
+            jax.ShapeDtypeStruct((*blocks, per, steps * lanes + 128), low),
+            jax.ShapeDtypeStruct((*blocks, per, steps * lanes + 128), low),
             jax.ShapeDtypeStruct((rows, width), full),
         ],
         compiler_params=pltpu.CompilerParams(vmem_limit_bytes=48 * 1024 * 1024),
@@ -1242,17 +1247,21 @@
 
 
 def finish_kernel(*refs):
-    parts, gate_up, down = refs[:5], refs[-2], refs[-1]
+    gate_up, down = refs[-2:]
+    rows = gate_up.shape[1]
+    places = [(ref, i) for ref in refs[:4] for i in range(ref.shape[1] // rows)]
     half = FF // 2
     full = jnp.float32
     for z_from in range(Z_SIZE):
         for j in range(5):
             expert, side = divmod(HALF_ORDER[z_from][j], 2)
+            part, i = places[j]
+            at = slice(i * rows, (i + 1) * rows)
             cols = slice(side * half, (side + 1) * half)
-            gate_up[expert, :, cols] = parts[j][z_from, :, :half].astype(full)
+            gate_up[expert, :, cols] = part[z_from, at, :half].astype(full)
             cols_up = slice(FF + side * half, FF + (side + 1) * half)
-            gate_up[expert, :, cols_up] = parts[j][z_from, :, half : 2 * half].astype(full)
-            down[expert, :, cols] = parts[j][z_from, :, 2 * half :].astype(full)
+            gate_up[expert, :, cols_up] = part[z_from, at, half : 2 * half].astype(full)
+            down[expert, :, cols] = part[z_from, at, 2 * half :].astype(full)
 
 
 def finish_grads(backs, after):
@@ -1261,7 +1270,7 @@
     vmem = pl.BlockSpec(memory_space=pltpu.VMEM)
     return pl.pallas_call(
         finish_kernel,
-        in_specs=[vmem] * 5 + [pl.BlockSpec(memory_space=pl.ANY)] * len(after),
+        in_specs=[vmem] * len(backs) + [pl.BlockSpec(memory_space=pl.ANY)] * len(after),
         out_specs=[vmem, vmem],
         out_shape=[
             jax.ShapeDtypeStruct((experts, rows, 2 * FF), jnp.float32),
@@ -1277,15 +1286,15 @@
 
 class DenseScatter:
     def __init__(self, mine, theirs, place):
-        shape = (Z_SIZE, Y_SIZE, X_SIZE, *mine.shape[1:])
+        shape = (Y_SIZE, X_SIZE, *mine.shape[1:])
         self.mine, self.theirs, self.place = mine.reshape(shape), theirs.reshape(shape), place
 
     def block(self, other_y, other_x):
         y = 1 - self.place[1] if other_y else self.place[1]
         x = 1 - self.place[2] if other_x else self.place[2]
-        size = (Z_SIZE, 1, 1, *self.mine.shape[3:])
+        size = (1, 1, *self.mine.shape[2:])
         got = [
-            lax.dynamic_slice(a, (0, y, x, 0, 0), size).reshape(Z_SIZE, *size[3:])
+            lax.dynamic_slice(a, (y, x, 0, 0, 0), size).reshape(size[2:])
             for a in (self.mine, self.got)
         ]
         return plus(*got)
@@ -1315,25 +1324,17 @@
         self.y_a = move(gate(plus(self.to_y[:zs], self.via_x).astype(low)), PAIRS_Y)
         return [self.x_b, self.y_a]
 
-    def along(self):
+    def sum_up(self):
         zs = Z_SIZE // 2
-        self.total = jnp.concatenate(
+        return jnp.concatenate(
             [
                 plus(self.near[:zs], self.x_a) + self.y_a.astype(jnp.float32),
                 plus(self.near[zs:], self.x_b) + self.y_b.astype(jnp.float32),
             ]
         ).astype(jnp.bfloat16)
-        self.parts = trade(self.total)
-        return [self.parts]
 
     def result(self):
         return jnp.sum(self.parts.astype(jnp.float32), axis=0)
-
-
-def of_core(term, c):
-    rows = term.shape[0] // (Z_SIZE * Y_SIZE * X_SIZE * C_SIZE)
-    blocks = term.reshape(Z_SIZE * Y_SIZE * X_SIZE, C_SIZE, rows, term.shape[1])
-    return lax.dynamic_index_in_dim(blocks, c, 1, keepdims=False)
 
 
 def plus(a, b):
@@ -1519,13 +1520,14 @@
             sent += send_far(q)
         run_forward(pair, False)
         run_forward(pair, True)
-        rounds.close(saved[pair + pairs][0], *sent)
+        rounds.close(saved[pair + pairs][0], *sent, *([dy_own] if pair == 2 else []))
+    dy_own = gate(dy_own)
+    dy_other = move(dy_own, PAIRS_C)
     mix_other, mix_own = combine(all_slots, buffer, rounds.after())
-    rounds.close(mix_other, dy_own)
+    rounds.close(mix_other, dy_other)
     mix_moved = move(mix_other, PAIRS_C)
-    dy_other = move(dy_own, PAIRS_C)
-    rounds.close(mix_moved, dy_other)
     grads_in = join_rows([dy_other], [dy_own])
+    rounds.close(mix_moved, grads_in)
 
     back = None
     grads = [[None, None] for _ in units]
@@ -1582,22 +1584,24 @@
     totals = total_of(0)
     backs = []
 
-    def send_back():
-        q = len(backs)
-        backs.append(trade(gate(totals[q])))
+    def send_back(*parts):
+        backs.append(trade(gate(parts[0] if len(parts) == 1 else jnp.concatenate(parts, axis=1))))
         return backs[-1:]
 
     run_back(2, False)
-    rounds.close(grads[2][0][0], *send_via(1), *send_back())
+    rounds.close(grads[2][0][0], *send_via(1), *send_back(totals[0]))
     run_back(2, True)
-    rounds.close(grads[2][1][0], *send_first(1), *send_back())
+    rounds.close(grads[2][1][0], *send_first(1), *send_back(totals[1]))
     copy_other, copy_own = combine(all_slots, back, rounds.after())
     rounds.close(copy_other, *send_second(1), *send_via(2))
     copy_moved = move(copy_other, PAIRS_C)
     rounds.close(copy_moved)
     copy_got = trade(plus(copy_own, copy_moved).astype(low))
-    rounds.close(copy_got)
-    totals += total_of(1)
+    rounds.close(*send_first(2))
+    rounds.close(*send_second(2))
+    totals += total_of(1) + total_of(2)
+    rounds.close(copy_got, output, totals[2])
+    copy_got = gate(copy_got)
     chosen = (slot_table >= 0).T
     gates = dense_gates(jnp.dot(hidden_two, router_full, preferred_element_type=full), chosen)
     grad_middle, branch_gradient, out_mine, out_theirs = middle_backward(
@@ -1613,7 +1617,7 @@
         mixed,
     )
     out_scatter = DenseScatter(out_mine, out_theirs, place)
-    rounds.close(out_scatter.theirs, branch_gradient)
+    out_scatter.cores()
     qkv_mine, qkv_theirs, grad_hidden_one = attention_backward(
         jnp.concatenate([lengths, c[None]]),
         branch_gradient,
@@ -1629,14 +1633,17 @@
         tokens,
         rounds.after(),
     )
-    rounds.close(grad_hidden_one, *out_scatter.cores(), *send_back(), *send_first(2))
-    qkv_scatter = DenseScatter(qkv_mine, qkv_theirs, place)
-    rounds.close(*qkv_scatter.cores(), *out_scatter.first(), *send_back(), *send_second(2))
-    totals += total_of(2)
-    rounds.close(*qkv_scatter.first(), *out_scatter.second(), *send_back())
-    rounds.close(*qkv_scatter.second(), *out_scatter.along())
-    qkv_scatter.along()
-    gate_up_grads, down_grads = finish_grads(backs, [qkv_scatter.total])
+    rounds.close(grad_hidden_one, *send_back(totals[2]), *out_scatter.first())
+    qkv_scatter = DenseScatter(qkv_mine, gate(qkv_theirs), place)
+    sent = send_back(*totals[3:])
+    rounds.close(*qkv_scatter.cores(), *out_scatter.second())
+    rounds.close(*qkv_scatter.first())
+    rounds.close(*qkv_scatter.second(), *sent)
+    both = jnp.concatenate([out_scatter.sum_up(), qkv_scatter.sum_up()], axis=-1)
+    parts = trade(both)
+    out_scatter.parts = parts[..., : width + 128]
+    qkv_scatter.parts = parts[..., width + 128 :]
+    gate_up_grads, down_grads = finish_grads(backs, [both])
     down_grads = down_grads.transpose(0, 2, 1)
     _, grad_norm_one = norm_backward(
         grad_hidden_one, normal_one, inverse_one, gain_one

time: 1130 us -> 1070 us (0.947)
  local copies, waits for them, and re-layouts: 101 us -> 64.5 us
  waiting for transfers between devices: 394 us -> 374 us
    all_to_all x18 -> x16, waiting for transfers between devices: 159 us -> 105 us  [trade(): lax.all_to_all(value, 'dp', split_axis=0, concat_axis=0, axis_index_group...]
    ppermute x61, waiting for transfers between devices: 235 us -> 269 us  [move(): return lax.ppermute(value, MESH_AXES, pairs)]
    unnamed x311 -> x263, local copies, waits for them, and re-layouts: 51.3 us -> 35.3 us
    all_to_all x18 -> x16, starting transfers between devices: 84.8 us -> 76 us  [trade(): lax.all_to_all(value, 'dp', split_axis=0, concat_axis=0, axis_index_group...]
  transfers between devices with their start and end apart: 79 -> 77, of which waited for: 38 -> 40; matrix products, arithmetic and copies ran while one was open for 12% -> 10% of each run, Pallas kernels for 31% -> 32%
where the time goes in v4:
time: 1070 us
  Pallas kernels  388 us (36%)
  waiting for transfers between devices  374 us (35%)
  starting transfers between devices  129 us (12%)
  other arithmetic  96.3 us (9%)
  local copies, waits for them, and re-layouts  64.5 us (6%)
  matrix products  11.4 us (1%)
    ppermute x61, waiting for transfers between devices, move(): return lax.ppermute(value, MESH_AXES, pairs)  269 us
    pallas_call x6, Pallas kernels, expert_backward(): pl.pallas_call(functools.partial(expert_back_kernel, count=len(pieces), w...  143 us
    all_to_all x16, waiting for transfers between devices, trade(): lax.all_to_all(value, 'dp', split_axis=0, concat_axis=0, axis_index_group...  105 us
    pallas_call x6, Pallas kernels, expert_forward(): pl.pallas_call(functools.partial(expert_forward_kernel, count=len(pieces)...  100 us
    all_to_all x16, starting transfers between devices, trade(): lax.all_to_all(value, 'dp', split_axis=0, concat_axis=0, axis_index_group...  76 us
    ppermute x61, starting transfers between devices, move(): return lax.ppermute(value, MESH_AXES, pairs)  52.6 us
    pallas_call x2, Pallas kernels, combine(): pl.pallas_call(combine_kernel, grid=(sources,), in_specs=[pl.BlockSpec((1...  38 us
    pallas_call x1, Pallas kernels, attention_backward(): pl.pallas_call(attention_back_kernel, grid_spec=pltpu.PrefetchScalarGridS...  35.4 us
  transfers between devices with their start and end apart: 77, of which 40 were waited for; matrix products, arithmetic and copies ran while one was open for 10% of the time, Pallas kernels for 32%

profile of v4, /device:TPU:0, one launch (start us, length us, event | category | flops | bytes accessed | tf_op | source)
XLA Modules:
  0.0 1065.9 jit_solution(14739642163141777823)
XLA Ops:
  29.7 27.5 %all-to-all-done.refs_0_ = bf16[4,48,4224]{2,1,0:T(8,128)(2,1)S(1)} async-done(((bf16[4,48,4224]{2,1,0:T(8,128)(2,1)}), bf16[4,48,4224]{2,1,0:T(8,128)(2,1)S(1)}, u32[]{:S(2)}, u32[]{:S(2)}) %all-to-all-start) | async-done | bytes 1622048 | tf_op jit(solution)/shard_map/all_to_all | solution.py:371
  70.1 29.7 %collective-permute-done.refs_1_.refs_0_ = bf16[4,48,4224]{2,1,0:T(8,128)(2,1)S(1)} collective-permute-done((bf16[4,48,4224]{2,1,0:T(8,128)(2,1)S(1)}, bf16[4,48,4224]{2,1,0:T(8,128)(2,1)S(1)}, u32[]{:S(2)}, u32[]{:S(2)}) %collective-permute-start) | collective-permute-done | bytes 1622048 | tf_op jit(solution)/shard_map/ppermute | solution.py:406
  115.2 14.3 %collective-permute-done.2.refs_3_.refs_0_ = bf16[2,48,4224]{2,1,0:T(8,128)(2,1)S(1)} collective-permute-done((bf16[2,48,4224]{2,1,0:T(8,128)(2,1)S(1)}, bf16[2,48,4224]{2,1,0:T(8,128)(2,1)S(1)}, u32[]{:S(2)}, u32[]{:S(2)}) %collective-permute-start.2) | collective-permute-done | bytes 811040 | tf_op jit(solution)/shard_map/ppermute | solution.py:406
  156.1 10.2 collective-permute-done.10.refs_2_.rest_0_
  181.5 18.6 %attention_forward.1 = (bf16[384,1536]{1,0:T(8,128)(2,1)S(1)}, bf16[384,1536]{1,0:T(8,128)(2,1)S(1)}, bf16[384,512]{1,0:T(8,128)(2,1)S(1)}, bf16[384,512]{1,0:T(...) custom-call(s32[1]{0:T(128)S(6)} %copy.218.length, bf16[384,1536]{1,0:T(8,128)(2,1)} %tokens.3, ...), custom_call_target="tpu_custom_call" | custom-call | flops 3925868544 | bytes 13762560 | tf_op jit(solution)/shard_map/attention_forward/pallas_call | solution.py:976
  218.7 16.4 %collective-permute-done.14.refs_1_.rest_0_ = bf16[4,192,768]{2,1,0:T(8,128)(2,1)S(1)} collective-permute-done((bf16[4,192,768]{2,1,0:T(8,128)(2,1)}, bf16[4,192,768]{2,1,0:T(8,128)(2,1)S(1)}, u32[]{:S(2)}, u32[]{:S(2)}) %collective-permute-start.14) | collective-permute-done | bytes 1179680 | tf_op jit(solution)/shard_map/ppermute | solution.py:406
  247.0 25.5 %collective-permute-done.16.refs_0_ = bf16[4,192,768]{2,1,0:T(8,128)(2,1)S(1)} collective-permute-done((bf16[4,192,768]{2,1,0:T(8,128)(2,1)}, bf16[4,192,768]{2,1,0:T(8,128)(2,1)S(1)}, u32[]{:S(2)}, u32[]{:S(2)}) %collective-permute-start.16) | collective-permute-done | bytes 1179680 | tf_op jit(solution)/shard_map/ppermute | solution.py:406
  275.7 24.7 %collective-permute-done.18.refs_0_ = bf16[4,192,768]{2,1,0:T(8,128)(2,1)S(1)} collective-permute-done((bf16[4,192,768]{2,1,0:T(8,128)(2,1)}, bf16[4,192,768]{2,1,0:T(8,128)(2,1)S(1)}, u32[]{:S(2)}, u32[]{:S(2)}) %collective-permute-start.18) | collective-permute-done | bytes 1179680 | tf_op jit(solution)/shard_map/ppermute | solution.py:406
  303.5 23.9 %collective-permute-done.20.refs_0_.rest_1_ = bf16[4,192,768]{2,1,0:T(8,128)(2,1)S(1)} collective-permute-done((bf16[4,192,768]{2,1,0:T(8,128)(2,1)}, bf16[4,192,768]{2,1,0:T(8,128)(2,1)S(1)}, u32[]{:S(2)}, u32[]{:S(2)}) %collective-permute-start.20) | collective-permute-done | bytes 1179680 | tf_op jit(solution)/shard_map/ppermute | solution.py:406
  330.5 23.1 %collective-permute-done.22.refs_0_.rest_1_ = bf16[4,192,768]{2,1,0:T(8,128)(2,1)S(1)} collective-permute-done((bf16[4,192,768]{2,1,0:T(8,128)(2,1)}, bf16[4,192,768]{2,1,0:T(8,128)(2,1)S(1)}, u32[]{:S(2)}, u32[]{:S(2)}) %collective-permute-start.22) | collective-permute-done | bytes 1179680 | tf_op jit(solution)/shard_map/ppermute | solution.py:406
  389.9 16.4 %expert_forward.6 = (bf16[8,960,1536]{2,1,0:T(8,128)(2,1)}, bf16[1280,1536]{1,0:T(8,128)(2,1)}, f32[1280,1024]{1,0:T(8,128)}) custom-call(s32[2]{0:T(128)} %pad_add_fusion.6.info, s32[8,1,384]{2,1,0:T(1,128)} %copy-done.124, f32[8,1,384]{2,1,0:T(1,128)} %get-tuple-element.286.gates, bf16[8,384,1536]{2,1,0:T(8,128)(2,1)} %copy-done, ...), custom_call_target="tpu_custom_call" | custom-call | flops 7549747200 | bytes 27262976 | tf_op jit(solution)/shard_map/expert_forward/pallas_call | solution.py:579
  406.3 16.4 %expert_forward.7 = (bf16[8,960,1536]{2,1,0:T(8,128)(2,1)}, bf16[1280,1536]{1,0:T(8,128)(2,1)}, f32[1280,1024]{1,0:T(8,128)}) custom-call(s32[2]{0:T(128)} %pad_add_fusion.5.info, s32[8,1,384]{2,1,0:T(1,128)} %copy-done.121, f32[8,1,384]{2,1,0:T(1,128)} %get-tuple-element.287.gates, bf16[8,384,1536]{2,1,0:T(8,128)(2,1)} %copy-done, ...), custom_call_target="tpu_custom_call", output_to_operand_aliasing={{0}: (8, {})} | custom-call | flops 7549747200 | bytes 27262976 | tf_op jit(solution)/shard_map/expert_forward/pallas_call | solution.py:579
  424.3 16.4 %expert_forward.8 = (bf16[8,960,1536]{2,1,0:T(8,128)(2,1)}, bf16[1280,1536]{1,0:T(8,128)(2,1)}, f32[1280,1024]{1,0:T(8,128)}) custom-call(s32[2]{0:T(128)} %pad_add_fusion.4.info, s32[8,1,384]{2,1,0:T(1,128)} %copy-done.120, f32[8,1,384]{2,1,0:T(1,128)} %get-tuple-element.288.gates, bf16[8,384,1536]{2,1,0:T(8,128)(2,1)} %copy-done, ...), custom_call_target="tpu_custom_call", output_to_operand_aliasing={{0}: (8, {})} | custom-call | flops 7549747200 | bytes 27262976 | tf_op jit(solution)/shard_map/expert_forward/pallas_call | solution.py:579
  440.7 16.4 %expert_forward.9 = (bf16[8,960,1536]{2,1,0:T(8,128)(2,1)}, bf16[1280,1536]{1,0:T(8,128)(2,1)}, f32[1280,1024]{1,0:T(8,128)}) custom-call(s32[2]{0:T(128)} %pad_add_fusion.3.info, s32[8,1,384]{2,1,0:T(1,128)} %copy-done.119, f32[8,1,384]{2,1,0:T(1,128)} %get-tuple-element.289.gates, bf16[8,384,1536]{2,1,0:T(8,128)(2,1)} %copy-done, ...), custom_call_target="tpu_custom_call", output_to_operand_aliasing={{0}: (8, {})} | custom-call | flops 7549747200 | bytes 27262976 | tf_op jit(solution)/shard_map/expert_forward/pallas_call | solution.py:579
  457.8 12.9 %expert_forward.10 = (bf16[8,960,1536]{2,1,0:T(8,128)(2,1)}, bf16[1280,1536]{1,0:T(8,128)(2,1)}, f32[1280,512]{1,0:T(8,128)}) custom-call(s32[2]{0:T(128)} %pad_add_fusion.2.info, s32[8,1,384]{2,1,0:T(1,128)} %copy-done.115, f32[8,1,384]{2,1,0:T(1,128)} %get-tuple-element.290.gates, bf16[8,384,1536]{2,1,0:T(8,128)(2,1)} %copy-done, ...), custom_call_target="tpu_custom_call", output_to_operand_aliasing={{0}: (6, {})} | custom-call | flops 4529848320 | bytes 22282240 | tf_op jit(solution)/shard_map/expert_forward/pallas_call | solution.py:579
  470.7 21.6 %expert_forward.11 = (bf16[8,960,1536]{2,1,0:T(8,128)(2,1)}, bf16[1280,1536]{1,0:T(8,128)(2,1)}, f32[1280,512]{1,0:T(8,128)}) custom-call(s32[2]{0:T(128)} %pad_add_fusion.1.info, s32[8,1,384]{2,1,0:T(1,128)} %copy-done.114, f32[8,1,384]{2,1,0:T(1,128)} %get-tuple-element.291.gates, bf16[8,384,1536]{2,1,0:T(8,128)(2,1)} %copy-done, ...), custom_call_target="tpu_custom_call", output_to_operand_aliasing={{0}: (6, {})} | custom-call | flops 4529848320 | bytes 22282240 | tf_op jit(solution)/shard_map/expert_forward/pallas_call | solution.py:579
  492.9 18.2 %combine.2 = (bf16[4,384,1536]{2,1,0:T(8,128)(2,1)}, bf16[4,384,1536]{2,1,0:T(8,128)(2,1)}) custom-call(s32[8,6,384]{2,1,0:T(8,128)} %concatenate.135.slots, bf16[8,960,1536]{2,1,0:T(8,128)(2,1)} %get-tuple-element.84.values, f32[8,128]{1,0:T(8,128)} %join.43.rest_0_.refs_1_.refs_2_), custom_call_target="tpu_custom_call" | custom-call | flops 9059696640 | bytes 33030144 | tf_op jit(solution)/shard_map/combine/pallas_call | solution.py:1210
  532.6 26.2 %expert_backward.6 = (bf16[8,960,1664]{2,1,0:T(8,128)(2,1)}, bf16[2,2,192,768]{3,2,1,0:T(8,128)(2,1)}, bf16[2,2,192,768]{3,2,1,0:T(8,128)(2,1)}, bf16[2,2,192,76...) custom-call(s32[2]{0:T(128)} %pad_add_fusion.6.info, s32[8,1,384]{2,1,0:T(1,128)} %copy-done.124, ...), custom_call_target="tpu_custom_call" | custom-call | flops 13589544960 | bytes 31981568 | tf_op jit(solution)/shard_map/expert_backward/pallas_call | solution.py:732
  561.0 26.3 %expert_backward.7 = (bf16[8,960,1664]{2,1,0:T(8,128)(2,1)}, bf16[2,2,192,768]{3,2,1,0:T(8,128)(2,1)}, bf16[2,2,192,768]{3,2,1,0:T(8,128)(2,1)}, bf16[2,2,192,76...) custom-call(s32[2]{0:T(128)} %pad_add_fusion.5.info, s32[8,1,384]{2,1,0:T(1,128)} %copy-done.121, ...), custom_call_target="tpu_custom_call", output_to_operand_aliasing={{0}: (10, {})} | custom-call | flops 13589544960 | bytes 31981568 | tf_op jit(solution)/shard_map/expert_backward/pallas_call | solution.py:732
  595.9 26.5 %expert_backward.8 = (bf16[8,960,1664]{2,1,0:T(8,128)(2,1)}, bf16[2,2,192,768]{3,2,1,0:T(8,128)(2,1)}, bf16[2,2,192,768]{3,2,1,0:T(8,128)(2,1)}, bf16[2,2,192,76...) custom-call(s32[2]{0:T(128)} %pad_add_fusion.4.info, s32[8,1,384]{2,1,0:T(1,128)} %copy-done.120, ...), custom_call_target="tpu_custom_call", output_to_operand_aliasing={{0}: (10, {})} | custom-call | flops 13589544960 | bytes 31981568 | tf_op jit(solution)/shard_map/expert_backward/pallas_call | solution.py:732
  625.9 26.2 %expert_backward.9 = (bf16[8,960,1664]{2,1,0:T(8,128)(2,1)}, bf16[2,2,192,768]{3,2,1,0:T(8,128)(2,1)}, bf16[2,2,192,768]{3,2,1,0:T(8,128)(2,1)}, bf16[2,2,192,76...) custom-call(s32[2]{0:T(128)} %pad_add_fusion.3.info, s32[8,1,384]{2,1,0:T(1,128)} %copy-done.119, ...), custom_call_target="tpu_custom_call", output_to_operand_aliasing={{0}: (10, {})} | custom-call | flops 13589544960 | bytes 31981568 | tf_op jit(solution)/shard_map/expert_backward/pallas_call | solution.py:732
  668.4 19.1 %expert_backward.10 = (bf16[8,960,1664]{2,1,0:T(8,128)(2,1)}, bf16[1,2,192,768]{3,2,1,0:T(8,128)(2,1)}, bf16[1,2,192,768]{3,2,1,0:T(8,128)(2,1)}, bf16[1,2,192,7...) custom-call(s32[2]{0:T(128)} %pad_add_fusion.2.info, s32[8,1,384]{2,1,0:T(1,128)} %copy-done.115, ...), custom_call_target="tpu_custom_call", output_to_operand_aliasing={{0}: (8, {})} | custom-call | flops 7549747200 | bytes 24641536 | tf_op jit(solution)/shard_map/expert_backward/pallas_call | solution.py:732
  699.6 19.0 %expert_backward.11 = (bf16[8,960,1664]{2,1,0:T(8,128)(2,1)}, bf16[1,2,192,768]{3,2,1,0:T(8,128)(2,1)}, bf16[1,2,192,768]{3,2,1,0:T(8,128)(2,1)}, bf16[1,2,192,7...) custom-call(s32[2]{0:T(128)} %pad_add_fusion.1.info, s32[8,1,384]{2,1,0:T(1,128)} %copy-done.114, ...), custom_call_target="tpu_custom_call", output_to_operand_aliasing={{0}: (8, {})} | custom-call | flops 7549747200 | bytes 24641536 | tf_op jit(solution)/shard_map/expert_backward/pallas_call | solution.py:732
  725.5 19.9 %combine.3 = (bf16[4,384,1664]{2,1,0:T(8,128)(2,1)}, bf16[4,384,1664]{2,1,0:T(8,128)(2,1)}) custom-call(s32[8,6,384]{2,1,0:T(8,128)} %concatenate.135.slots, bf16[8,960,1664]{2,1,0:T(8,128)(2,1)} %get-tuple-element.115.values, f32[8,128]{1,0:T(8,128)} %join.51.rest_0_.refs_1_.refs_5_), custom_call_target="tpu_custom_call" | custom-call | flops 9814671360 | bytes 35782656 | tf_op jit(solution)/shard_map/combine/pallas_call | solution.py:1210
  787.9 27.0 %collective-permute-done.41.refs_4_ = bf16[1,2,192,768]{3,2,1,0:T(8,128)(2,1)S(1)} collective-permute-done((bf16[1,2,192,768]{3,2,1,0:T(8,128)(2,1)}, bf16[1,2,192,768]{3,2,1,0:T(8,128)(2,1)S(1)}, u32[]{:S(2)}, u32[]{:S(2)}) %collective-permute-start.41) | collective-permute-done | bytes 589856 | tf_op jit(solution)/shard_map/ppermute | solution.py:406
  849.0 32.4 %all-to-all-done.12.refs_0_ = bf16[4,384,1664]{2,1,0:T(8,128)(2,1)} async-done(((bf16[4,384,1664]{2,1,0:T(8,128)(2,1)}), bf16[4,384,1664]{2,1,0:T(8,128)(2,1)}, u32[]{:S(2)}, u32[]{:S(2)}) %all-to-all-start.12) | async-done | bytes 5111840 | tf_op jit(solution)/shard_map/all_to_all | solution.py:371
  882.1 13.8 %middle_backward.1 = (f32[384,1536]{1,0:T(8,128)}, bf16[384,1536]{1,0:T(8,128)(2,1)}, bf16[4,4,48,1664]{3,2,1,0:T(8,128)(2,1)}, bf16[4,4,48,1664]{3,2,1,0:T(8,128)(2,1)}) custom-call(s32[1]{0:T(128)} %bitcast.2.c_ref, bf16[4,384,1664]{2,1,0:T(8,128)(2,1)} %tie.86.got, f32[384,128]{1,0:T(8,128)} %pad.9.gates, bf16[1536,4224]{1,0:T(8,128)(2,1)} %bitcast.308, ...), custom_call_target="tpu_custom_call" | custom-call | flops 2264924160 | bytes 23592960 | tf_op jit(solution)/shard_map/middle_backward/pallas_call | solution.py:834
  911.7 35.4 %attention_backward.1 = (bf16[4,4,48,2688]{3,2,1,0:T(8,128)(2,1)}, bf16[4,4,48,2688]{3,2,1,0:T(8,128)(2,1)}, f32[384,1536]{1,0:T(8,128)}) custom-call(s32[2]{0:T(128)S(1)} %pad_add_fusion.7.length, bf16[384,1536]{1,0:T(8,128)(2,1)S(1)} %copy-done.26, bf16[1536,4224]{1,0:T(8,128)(2,1)} %bitcast.309, bf16[384,1536]{1,0:T(8,128)(2,1)S(1)} %get-tuple-element.130.q, ...), custom_call_target="tpu_custom_call" | custom-call | flops 10116661248 | bytes 28704768 | tf_op jit(solution)/shard_map/attention_backward/pallas_call | solution.py:1139
  970.4 11.9 %collective-permute-done.56 = bf16[2,48,2688]{2,1,0:T(8,128)(2,1)S(1)} collective-permute-done((bf16[2,48,2688]{2,1,0:T(8,128)(2,1)S(1)}, bf16[2,48,2688]{2,1,0:T(8,128)(2,1)S(1)}, u32[]{:S(2)}, u32[]{:S(2)}) %collective-permute-start.56) | collective-permute-done | bytes 516128 | tf_op jit(solution)/shard_map/ppermute | solution.py:406
  982.9 11.3 %collective-permute-done.58 = bf16[2,48,2688]{2,1,0:T(8,128)(2,1)S(1)} collective-permute-done((bf16[2,48,2688]{2,1,0:T(8,128)(2,1)S(1)}, bf16[2,48,2688]{2,1,0:T(8,128)(2,1)S(1)}, u32[]{:S(2)}, u32[]{:S(2)}) %collective-permute-start.58) | collective-permute-done | bytes 516128 | tf_op jit(solution)/shard_map/ppermute | solution.py:406
  1005.7 10.4 all-to-all-done.15.refs_3_
  1031.8 27.3 %all-to-all-done.14 = bf16[4,48,4352]{2,1,0:T(8,128)(2,1)} async-done(((bf16[4,48,4352]{2,1,0:T(8,128)(2,1)}), bf16[4,48,4352]{2,1,0:T(8,128)(2,1)}, u32[]{:S(2)}, u32[]{:S(2)}) %all-to-all-start.14) | async-done | bytes 1671200 | tf_op jit(solution)/shard_map/all_to_all | solution.py:371
  (596 shorter events, 397.4 us)
Async XLA Ops:
  16.8 40.4 %all-to-all-start = ((bf16[4,48,4224]{2,1,0:T(8,128)(2,1)}), bf16[4,48,4224]{2,1,0:T(8,128)(2,1)S(1)}, u32[]{:S(2)}, u32[]{:S(2)}) async-start(bf16[4,48,4224]{2,1,0:T(8,128)(2,1)} %broadcast_in_dim.39), calls=%async_computation | async-start | bytes 3244032 | tf_op jit(solution)/shard_map/all_to_all | solution.py:371
  58.9 43.3 %all-to-all-start.2 = ((bf16[4,192,768]{2,1,0:T(8,128)(2,1)}), bf16[4,192,768]{2,1,0:T(8,128)(2,1)}, u32[]{:S(2)}, u32[]{:S(2)}) async-start(bf16[4,192,768]{2,1,0:T(8,128)(2,1)} %tie.45), calls=%async_computation.2 | async-start | bytes 2359296 | tf_op jit(solution)/shard_map/all_to_all | solution.py:371
  63.4 36.5 %collective-permute-start = (bf16[4,48,4224]{2,1,0:T(8,128)(2,1)S(1)}, bf16[4,48,4224]{2,1,0:T(8,128)(2,1)S(1)}, u32[]{:S(2)}, u32[]{:S(2)}) collective-permute-start(bf16[4,48,4224]{2,1,0:T(8,128)(2,1)S(1)} %copy-done.3), channel_id=1, source_target_pairs={{0,2},{1,3},{2,0},{3,1},{4,6},{5,7},{6,4},{7,5},{8,10},{9,11},{10,... | collective-permute-start | bytes 4866056 | tf_op jit(solution)/shard_map/ppermute | solution.py:406
  65.0 36.1 %collective-permute-start.1 = (bf16[4,48,4224]{2,1,0:T(8,128)(2,1)S(1)}, bf16[4,48,4224]{2,1,0:T(8,128)(2,1)S(1)}, u32[]{:S(2)}, u32[]{:S(2)}) collective-permute-start(bf16[4,48,4224]{2,1,0:T(8,128)(2,1)S(1)} %copy-done.3), channel_id=1, source_target_pairs={{0,4},{1,5},{2,6},{3,7},{4,0},{5,1},{6,2},{7,3},{8,12},{9,13},{10,... | collective-permute-start | bytes 4866056 | tf_op jit(solution)/shard_map/ppermute | solution.py:406
  66.5 35.8 %collective-permute-start.4 = (bf16[4,48,4224]{2,1,0:T(8,128)(2,1)S(1)}, bf16[4,48,4224]{2,1,0:T(8,128)(2,1)}, u32[]{:S(2)}, u32[]{:S(2)}) collective-permute-start(bf16[4,48,4224]{2,1,0:T(8,128)(2,1)S(1)} %copy-done.3), channel_id=1, source_target_pairs={{0,1},{1,0},{2,3},{3,2},{4,5},{5,4},{6,7},{7,6},{8,9},{9,8},{10,11... | collective-permute-start | bytes 4866056 | tf_op jit(solution)/shard_map/ppermute | solution.py:406
  102.8 31.3 %all-to-all-start.3 = ((bf16[4,192,768]{2,1,0:T(8,128)(2,1)}), bf16[4,192,768]{2,1,0:T(8,128)(2,1)}, u32[]{:S(2)}, u32[]{:S(2)}) async-start(bf16[4,192,768]{2,1,0:T(8,128)(2,1)} %tie.46), calls=%async_computation.3 | async-start | bytes 2359296 | tf_op jit(solution)/shard_map/all_to_all | solution.py:371
  134.7 32.4 %all-to-all-start.4 = ((bf16[4,192,768]{2,1,0:T(8,128)(2,1)}), bf16[4,192,768]{2,1,0:T(8,128)(2,1)}, u32[]{:S(2)}, u32[]{:S(2)}) async-start(bf16[4,192,768]{2,1,0:T(8,128)(2,1)} %tie.47), calls=%async_computation.4 | async-start | bytes 2359296 | tf_op jit(solution)/shard_map/all_to_all | solution.py:371
  167.7 35.7 %all-to-all-start.5 = ((bf16[4,192,768]{2,1,0:T(8,128)(2,1)}), bf16[4,192,768]{2,1,0:T(8,128)(2,1)}, u32[]{:S(2)}, u32[]{:S(2)}) async-start(bf16[4,192,768]{2,1,0:T(8,128)(2,1)} %tie.49), calls=%async_computation.5 | async-start | bytes 2359296 | tf_op jit(solution)/shard_map/all_to_all | solution.py:371
  204.0 32.1 %all-to-all-start.6 = ((bf16[4,192,768]{2,1,0:T(8,128)(2,1)}), bf16[4,192,768]{2,1,0:T(8,128)(2,1)}, u32[]{:S(2)}, u32[]{:S(2)}) async-start(bf16[4,192,768]{2,1,0:T(8,128)(2,1)} %tie.51), calls=%async_computation.6 | async-start | bytes 2359296 | tf_op jit(solution)/shard_map/all_to_all | solution.py:371
  240.5 114.8 %all-to-all-start.7 = ((bf16[4,384,1536]{2,1,0:T(8,128)(2,1)}), bf16[4,384,1536]{2,1,0:T(8,128)(2,1)}, u32[]{:S(2)}, u32[]{:S(2)}) async-start(bf16[4,384,1536]{2,1,0:T(8,128)(2,1)} %broadcast_in_dim.44), calls=%async_computation.7 | async-start | bytes 9437184 | tf_op jit(solution)/shard_map/all_to_all | solution.py:371
  368.5 123.8 %all-to-all-start.8 = ((bf16[4,384,1536]{2,1,0:T(8,128)(2,1)}), bf16[4,384,1536]{2,1,0:T(8,128)(2,1)}, u32[]{:S(2)}, u32[]{:S(2)}) async-start(bf16[4,384,1536]{2,1,0:T(8,128)(2,1)} %broadcast_in_dim.47), calls=%async_computation.8 | async-start | bytes 9437184 | tf_op jit(solution)/shard_map/all_to_all | solution.py:371
  378.4 44.3 %collective-permute-start.25 = (bf16[4,192,768]{2,1,0:T(8,128)(2,1)}, bf16[4,192,768]{2,1,0:T(8,128)(2,1)S(1)}, u32[]{:S(2)}, u32[]{:S(2)}) collective-permute-start(bf16[4,192,768]{2,1,0:T(8,128)(2,1)} %tie.61.rest_1_), channel_id=1, source_target_pairs={{0,2},{1,3},{2,0},{3,1},{4,6},{5,7},{6,4},{7,5},{8,10},{9,11},{10,... | collective-permute-start | bytes 3538952 | tf_op jit(solution)/shard_map/ppermute | solution.py:406
  527.7 130.4 %all-to-all-start.9 = ((bf16[4,384,1536]{2,1,0:T(8,128)(2,1)}), bf16[4,384,1536]{2,1,0:T(8,128)(2,1)}, u32[]{:S(2)}, u32[]{:S(2)}) async-start(bf16[4,384,1536]{2,1,0:T(8,128)(2,1)} %tie.65), calls=%async_computation.9 | async-start | bytes 9437184 | tf_op jit(solution)/shard_map/all_to_all | solution.py:371
  589.3 33.1 %collective-permute-start.30 = (bf16[2,2,192,768]{3,2,1,0:T(8,128)(2,1)}, bf16[2,2,192,768]{3,2,1,0:T(8,128)(2,1)}, u32[]{:S(2)}, u32[]{:S(2)}) collective-permute-start(bf16[2,2,192,768]{3,2,1,0:T(8,128)(2,1)} %tie.68), channel_id=1, source_target_pairs={{0,2},{1,3},{2,0},{3,1},{4,6},{5,7},{6,4},{7,5},{8,10},{9,11},{10,... | collective-permute-start | bytes 3538952 | tf_op jit(solution)/shard_map/ppermute | solution.py:406
  590.3 32.1 %collective-permute-start.31 = (bf16[2,2,192,768]{3,2,1,0:T(8,128)(2,1)}, bf16[2,2,192,768]{3,2,1,0:T(8,128)(2,1)S(1)}, u32[]{:S(2)}, u32[]{:S(2)}) collective-permute-start(bf16[2,2,192,768]{3,2,1,0:T(8,128)(2,1)} %tie.69), channel_id=1, source_target_pairs={{0,4},{1,5},{2,6},{3,7},{4,0},{5,1},{6,2},{7,3},{8,12},{9,13},{10,... | collective-permute-start | bytes 3538952 | tf_op jit(solution)/shard_map/ppermute | solution.py:406
  624.0 31.5 %collective-permute-start.32 = (bf16[2,2,192,768]{3,2,1,0:T(8,128)(2,1)}, bf16[2,2,192,768]{3,2,1,0:T(8,128)(2,1)S(1)}, u32[]{:S(2)}, u32[]{:S(2)}) collective-permute-start(bf16[2,2,192,768]{3,2,1,0:T(8,128)(2,1)} %tie.70), channel_id=1, source_target_pairs={{0,2},{1,3},{2,0},{3,1},{4,6},{5,7},{6,4},{7,5},{8,10},{9,11},{10,... | collective-permute-start | bytes 3538952 | tf_op jit(solution)/shard_map/ppermute | solution.py:406
  658.6 32.1 %all-to-all-start.10 = ((bf16[4,192,768]{2,1,0:T(8,128)(2,1)}), bf16[4,192,768]{2,1,0:T(8,128)(2,1)S(1)}, u32[]{:S(2)}, u32[]{:S(2)}) async-start(bf16[4,192,768]{2,1,0:T(8,128)(2,1)} %tie.74), calls=%async_computation.10 | async-start | bytes 2359296 | tf_op jit(solution)/shard_map/all_to_all | solution.py:371
  692.3 31.6 %all-to-all-start.11 = ((bf16[4,192,768]{2,1,0:T(8,128)(2,1)}), bf16[4,192,768]{2,1,0:T(8,128)(2,1)S(1)}, u32[]{:S(2)}, u32[]{:S(2)}) async-start(bf16[4,192,768]{2,1,0:T(8,128)(2,1)} %tie.77), calls=%async_computation.11 | async-start | bytes 2359296 | tf_op jit(solution)/shard_map/all_to_all | solution.py:371
  762.5 119.0 %all-to-all-start.12 = ((bf16[4,384,1664]{2,1,0:T(8,128)(2,1)}), bf16[4,384,1664]{2,1,0:T(8,128)(2,1)}, u32[]{:S(2)}, u32[]{:S(2)}) async-start(bf16[4,384,1664]{2,1,0:T(8,128)(2,1)} %add_convert_fusion), calls=%async_computation.12 | async-start | bytes 10223616 | tf_op jit(solution)/shard_map/all_to_all | solution.py:371
  773.3 41.5 %collective-permute-start.40 = (bf16[2,2,192,768]{3,2,1,0:T(8,128)(2,1)}, bf16[2,2,192,768]{3,2,1,0:T(8,128)(2,1)}, u32[]{:S(2)}, u32[]{:S(2)}) collective-permute-start(bf16[2,2,192,768]{3,2,1,0:T(8,128)(2,1)} %tie.79), channel_id=1, source_target_pairs={{0,2},{1,3},{2,0},{3,1},{4,6},{5,7},{6,4},{7,5},{8,10},{9,11},{10,... | collective-permute-start | bytes 3538952 | tf_op jit(solution)/shard_map/ppermute | solution.py:406
  774.3 40.6 %collective-permute-start.39 = (bf16[2,2,192,768]{3,2,1,0:T(8,128)(2,1)}, bf16[2,2,192,768]{3,2,1,0:T(8,128)(2,1)}, u32[]{:S(2)}, u32[]{:S(2)}) collective-permute-start(bf16[2,2,192,768]{3,2,1,0:T(8,128)(2,1)} %tie.78), channel_id=1, source_target_pairs={{0,4},{1,5},{2,6},{3,7},{4,0},{5,1},{6,2},{7,3},{8,12},{9,13},{10,... | collective-permute-start | bytes 3538952 | tf_op jit(solution)/shard_map/ppermute | solution.py:406
  778.6 36.3 %collective-permute-start.41 = (bf16[1,2,192,768]{3,2,1,0:T(8,128)(2,1)}, bf16[1,2,192,768]{3,2,1,0:T(8,128)(2,1)S(1)}, u32[]{:S(2)}, u32[]{:S(2)}) collective-permute-start(bf16[1,2,192,768]{3,2,1,0:T(8,128)(2,1)} %tie.80), channel_id=1, source_target_pairs={{0,4},{1,5},{2,6},{3,7},{4,0},{5,1},{6,2},{7,3},{8,12},{9,13},{10,... | collective-permute-start | bytes 1769480 | tf_op jit(solution)/shard_map/ppermute | solution.py:406
  779.1 35.7 %collective-permute-start.42 = (bf16[1,2,192,768]{3,2,1,0:T(8,128)(2,1)}, bf16[1,2,192,768]{3,2,1,0:T(8,128)(2,1)S(1)}, u32[]{:S(2)}, u32[]{:S(2)}) collective-permute-start(bf16[1,2,192,768]{3,2,1,0:T(8,128)(2,1)} %tie.81), channel_id=1, source_target_pairs={{0,2},{1,3},{2,0},{3,1},{4,6},{5,7},{6,4},{7,5},{8,10},{9,11},{10,... | collective-permute-start | bytes 1769480 | tf_op jit(solution)/shard_map/ppermute | solution.py:406
  896.0 51.0 %all-to-all-start.13 = ((bf16[4,192,768]{2,1,0:T(8,128)(2,1)}), bf16[4,192,768]{2,1,0:T(8,128)(2,1)S(1)}, u32[]{:S(2)}, u32[]{:S(2)}) async-start(bf16[4,192,768]{2,1,0:T(8,128)(2,1)} %tie.87), calls=%async_computation.13 | async-start | bytes 2359296 | tf_op jit(solution)/shard_map/all_to_all | solution.py:371
  906.0 41.0 %collective-permute-start.49 = (bf16[2,48,1664]{2,1,0:T(8,128)(2,1)}, bf16[2,48,1664]{2,1,0:T(8,128)(2,1)}, u32[]{:S(2)}, u32[]{:S(2)}) collective-permute-start(bf16[2,48,1664]{2,1,0:T(8,128)(2,1)} %get-tuple-element.283), channel_id=1, source_target_pairs={{0,2},{1,3},{2,0},{3,1},{4,6},{5,7},{6,4},{7,5},{8,10},{9,11},{10,... | collective-permute-start | bytes 958472 | tf_op jit(solution)/shard_map/ppermute | solution.py:406
  907.0 40.1 %collective-permute-start.51 = (bf16[2,48,1664]{2,1,0:T(8,128)(2,1)}, bf16[2,48,1664]{2,1,0:T(8,128)(2,1)}, u32[]{:S(2)}, u32[]{:S(2)}) collective-permute-start(bf16[2,48,1664]{2,1,0:T(8,128)(2,1)} %get-tuple-element.282), channel_id=1, source_target_pairs={{0,4},{1,5},{2,6},{3,7},{4,0},{5,1},{6,2},{7,3},{8,12},{9,13},{10,... | collective-permute-start | bytes 958472 | tf_op jit(solution)/shard_map/ppermute | solution.py:406
  909.2 37.9 %collective-permute-start.48 = (bf16[2,48,1664]{2,1,0:T(8,128)(2,1)}, bf16[2,48,1664]{2,1,0:T(8,128)(2,1)}, u32[]{:S(2)}, u32[]{:S(2)}) collective-permute-start(bf16[2,48,1664]{2,1,0:T(8,128)(2,1)} %fusion.59), channel_id=1, source_target_pairs={{0,2},{1,3},{2,0},{3,1},{4,6},{5,7},{6,4},{7,5},{8,10},{9,11},{10,... | collective-permute-start | bytes 958472 | tf_op jit(solution)/shard_map/ppermute | solution.py:406
  911.0 36.1 %collective-permute-start.53 = (bf16[2,48,1664]{2,1,0:T(8,128)(2,1)}, bf16[2,48,1664]{2,1,0:T(8,128)(2,1)}, u32[]{:S(2)}, u32[]{:S(2)}) collective-permute-start(bf16[2,48,1664]{2,1,0:T(8,128)(2,1)} %fusion.60), channel_id=1, source_target_pairs={{0,4},{1,5},{2,6},{3,7},{4,0},{5,1},{6,2},{7,3},{8,12},{9,13},{10,... | collective-permute-start | bytes 958472 | tf_op jit(solution)/shard_map/ppermute | solution.py:406
  955.6 39.2 %collective-permute-start.50 = (bf16[2,48,1664]{2,1,0:T(8,128)(2,1)S(1)}, bf16[2,48,1664]{2,1,0:T(8,128)(2,1)S(1)}, u32[]{:S(2)}, u32[]{:S(2)}) collective-permute-start(bf16[2,48,1664]{2,1,0:T(8,128)(2,1)S(1)} %fusion.37), channel_id=1, source_target_pairs={{0,4},{1,5},{2,6},{3,7},{4,0},{5,1},{6,2},{7,3},{8,12},{9,13},{10,... | collective-permute-start | bytes 958472 | tf_op jit(solution)/shard_map/ppermute | solution.py:406
  958.1 37.9 %collective-permute-start.52 = (bf16[2,48,1664]{2,1,0:T(8,128)(2,1)S(1)}, bf16[2,48,1664]{2,1,0:T(8,128)(2,1)}, u32[]{:S(2)}, u32[]{:S(2)}) collective-permute-start(bf16[2,48,1664]{2,1,0:T(8,128)(2,1)S(1)} %fusion.32), channel_id=1, source_target_pairs={{0,2},{1,3},{2,0},{3,1},{4,6},{5,7},{6,4},{7,5},{8,10},{9,11},{10,... | collective-permute-start | bytes 958472 | tf_op jit(solution)/shard_map/ppermute | solution.py:406
  959.2 56.9 %all-to-all-start.15 = ((bf16[4,384,768]{2,1,0:T(8,128)(2,1)}), bf16[4,384,768]{2,1,0:T(8,128)(2,1)S(1)}, u32[]{:S(2)}, u32[]{:S(2)}) async-start(bf16[4,384,768]{2,1,0:T(8,128)(2,1)} %tie.89), calls=%async_computation.15 | async-start | bytes 4718592 | tf_op jit(solution)/shard_map/all_to_all | solution.py:371
  1016.1 43.0 %all-to-all-start.14 = ((bf16[4,48,4352]{2,1,0:T(8,128)(2,1)}), bf16[4,48,4352]{2,1,0:T(8,128)(2,1)}, u32[]{:S(2)}, u32[]{:S(2)}) async-start(bf16[4,48,4352]{2,1,0:T(8,128)(2,1)} %maximum_maximum_fusion.1.refs_4_), calls=%async_computation.14 | async-start | bytes 3342336 | tf_op jit(solution)/shard_map/all_to_all | solution.py:371
  (173 other events, 1378.4 us)

commit v5 on v4

--- a/solution.py
+++ b/solution.py
@@ -1185,46 +1185,34 @@
 
 
 def combine_kernel(slots, values, *rest):
-    other, own, p_s = rest[-3:]
-    step = pl.program_id(0)
+    out, p_s = rest[-2:]
     length = slots.shape[2]
     iota = lax.broadcasted_iota(jnp.int32, (WIDE, length), 0)
     for u in range(slots.shape[1]):
         pick = iota == slots[0, u : u + 1, :]
         p_s[u * WIDE : (u + 1) * WIDE, :] = jnp.where(pick, 1.0, 0.0).astype(jnp.bfloat16)
-    result = contract_rows(p_s[...], values[0]).astype(jnp.bfloat16)
-
-    @pl.when(step < Z_SIZE)
-    def _():
-        other[0] = result
-
-    @pl.when(step >= Z_SIZE)
-    def _():
-        own[0] = result
-
-
-def combine(slots, values, after=()):
-    sources, units, length = slots.shape
+    out[0] = contract_rows(p_s[...], values[0]).astype(jnp.bfloat16)
+
+
+def combine(slots, values, first, after=()):
+    _, units, length = slots.shape
     n = values.shape[-1]
     low = jnp.bfloat16
     return pl.pallas_call(
         combine_kernel,
-        grid=(sources,),
+        grid=(Z_SIZE,),
         in_specs=[
-            pl.BlockSpec((1, units, length), lambda i: (i, 0, 0)),
-            pl.BlockSpec((1, units * WIDE, n), lambda i: (i, 0, 0)),
+            pl.BlockSpec((1, units, length), lambda i: (first + i, 0, 0)),
+            pl.BlockSpec((1, units * WIDE, n), lambda i: (first + i, 0, 0)),
         ]
         + [pl.BlockSpec(memory_space=pl.ANY)] * len(after),
-        out_specs=[
-            pl.BlockSpec((1, length, n), lambda i: (jnp.minimum(i, Z_SIZE - 1), 0, 0)),
-            pl.BlockSpec((1, length, n), lambda i: (jnp.maximum(i - Z_SIZE, 0), 0, 0)),
-        ],
-        out_shape=[jax.ShapeDtypeStruct((Z_SIZE, length, n), low)] * 2,
+        out_specs=pl.BlockSpec((1, length, n), lambda i: (i, 0, 0)),
+        out_shape=jax.ShapeDtypeStruct((Z_SIZE, length, n), low),
         scratch_shapes=[pltpu.VMEM((units * WIDE, length), low)],
         compiler_params=pltpu.CompilerParams(vmem_limit_bytes=60 * 1024 * 1024),
         cost_estimate=pl.CostEstimate(
-            flops=2 * sources * units * WIDE * length * n,
-            bytes_accessed=sources * (units * WIDE + length) * n * 2,
+            flops=2 * Z_SIZE * units * WIDE * length * n,
+            bytes_accessed=Z_SIZE * (units * WIDE + length) * n * 2,
             transcendentals=0,
         ),
         name="combine",
@@ -1410,10 +1398,13 @@
         far[q] = move(near[q][1], PAIRS_X) if q % 2 == 0 else move(near[q][0], PAIRS_Y)
         return [far[q]]
 
+    cosine_table, sine_table = rope_tables(sequence_length)
+    cosine_table = jnp.tile(cosine_table, (1, QUERY_LANES // HEAD_SIZE))
+    sine_table = jnp.tile(sine_table, (1, QUERY_LANES // HEAD_SIZE))
     from_x, from_y = move(block, PAIRS_X), move(block, PAIRS_Y)
     block_c = move(block, PAIRS_C)
     tables_c = move(tables, PAIRS_C)
-    rounds.close(from_x, from_y, block_c, tables_c, *send_half(0))
+    rounds.close(from_x, from_y, block_c, tables_c, cosine_table, sine_table, *send_half(0))
     far_a, far_b = move(from_y[:zs], PAIRS_X), move(from_x[zs:], PAIRS_Y)
     from_x_c, from_y_c = move(from_x, PAIRS_C), move(from_y, PAIRS_C)
     rounds.close(far_a, far_b, from_x_c, from_y_c, *send_half(1))
@@ -1436,9 +1427,6 @@
     inputs = tokens.astype(full)
     inverse_one = rms_inverse(inputs)
     normal_one = inputs * inverse_one
-    cosine_table, sine_table = rope_tables(sequence_length)
-    cosine_table = jnp.tile(cosine_table, (1, QUERY_LANES // HEAD_SIZE))
-    sine_table = jnp.tile(sine_table, (1, QUERY_LANES // HEAD_SIZE))
     hidden_one, query_rows, keys, value_rows, mixed, log_totals = attention_forward(
         lengths, tokens, gain_one[None, :], pack, cosine_table, sine_table, rounds.after()
     )
@@ -1523,11 +1511,12 @@
         rounds.close(saved[pair + pairs][0], *sent, *([dy_own] if pair == 2 else []))
     dy_own = gate(dy_own)
     dy_other = move(dy_own, PAIRS_C)
-    mix_other, mix_own = combine(all_slots, buffer, rounds.after())
+    mix_other = combine(all_slots, buffer, 0, rounds.after())
     rounds.close(mix_other, dy_other)
     mix_moved = move(mix_other, PAIRS_C)
+    mix_own = combine(all_slots, buffer, Z_SIZE, rounds.after())
     grads_in = join_rows([dy_other], [dy_own])
-    rounds.close(mix_moved, grads_in)
+    rounds.close(mix_moved, mix_own, grads_in)
 
     back = None
     grads = [[None, None] for _ in units]
@@ -1592,15 +1581,17 @@
     rounds.close(grads[2][0][0], *send_via(1), *send_back(totals[0]))
     run_back(2, True)
     rounds.close(grads[2][1][0], *send_first(1), *send_back(totals[1]))
-    copy_other, copy_own = combine(all_slots, back, rounds.after())
-    rounds.close(copy_other, *send_second(1), *send_via(2))
+    copy_other = combine(all_slots, back, 0, rounds.after())
+    rounds.close(copy_other)
     copy_moved = move(copy_other, PAIRS_C)
-    rounds.close(copy_moved)
+    copy_own = combine(all_slots, back, Z_SIZE, rounds.after())
+    rounds.close(copy_moved, copy_own, *send_second(1), *send_via(2))
     copy_got = trade(plus(copy_own, copy_moved).astype(low))
     rounds.close(*send_first(2))
     rounds.close(*send_second(2))
     totals += total_of(1) + total_of(2)
-    rounds.close(copy_got, output, totals[2])
+    last_total = jnp.concatenate(totals[3:], axis=1)
+    rounds.close(copy_got, output, totals[2], last_total)
     copy_got = gate(copy_got)
     chosen = (slot_table >= 0).T
     gates = dense_gates(jnp.dot(hidden_two, router_full, preferred_element_type=full), chosen)
@@ -1635,7 +1626,7 @@
     )
     rounds.close(grad_hidden_one, *send_back(totals[2]), *out_scatter.first())
     qkv_scatter = DenseScatter(qkv_mine, gate(qkv_theirs), place)
-    sent = send_back(*totals[3:])
+    sent = send_back(last_total)
     rounds.close(*qkv_scatter.cores(), *out_scatter.second())
     rounds.close(*qkv_scatter.first())
     rounds.close(*qkv_scatter.second(), *sent)

time: 1070 us -> 1060 us (level); the launches traced: 1070 us -> 1050 us
  waiting for transfers between devices: 374 us -> 353 us
    ppermute x61, waiting for transfers between devices: 269 us -> 253 us  [move(): return lax.ppermute(value, MESH_AXES, pairs)]
    unnamed x263 -> x253, local copies, waits for them, and re-layouts: 35.3 us -> 28.5 us
    pallas_call x2 -> x4, Pallas kernels: 38 us -> 40.4 us  [combine(): pl.pallas_call(combine_kernel, grid=(Z_SIZE,), in_specs=[pl.BlockSpec((1,...]
  transfers between devices with their start and end apart: 77 -> 77, of which waited for: 40 -> 38; matrix products, arithmetic and copies ran while one was open for 10% -> 11% of each run, Pallas kernels for 32% -> 33%
where the time goes in v5:
time: 1060 us; the launch traced here: 1050 us
  Pallas kernels  382 us (36%)
  waiting for transfers between devices  353 us (33%)
  starting transfers between devices  134 us (13%)
  other arithmetic  97.2 us (9%)
  local copies, waits for them, and re-layouts  63.8 us (6%)
  matrix products  11.4 us (1%)
    ppermute x61, waiting for transfers between devices, move(): return lax.ppermute(value, MESH_AXES, pairs)  253 us
    pallas_call x6, Pallas kernels, expert_backward(): pl.pallas_call(functools.partial(expert_back_kernel, count=len(pieces), w...  143 us
    all_to_all x16, waiting for transfers between devices, trade(): lax.all_to_all(value, 'dp', split_axis=0, concat_axis=0, axis_index_group...  100 us
    pallas_call x6, Pallas kernels, expert_forward(): pl.pallas_call(functools.partial(expert_forward_kernel, count=len(pieces)...  92 us
    all_to_all x16, starting transfers between devices, trade(): lax.all_to_all(value, 'dp', split_axis=0, concat_axis=0, axis_index_group...  76.5 us
    ppermute x61, starting transfers between devices, move(): return lax.ppermute(value, MESH_AXES, pairs)  57.7 us
    pallas_call x4, Pallas kernels, combine(): pl.pallas_call(combine_kernel, grid=(Z_SIZE,), in_specs=[pl.BlockSpec((1,...  40.4 us
    pallas_call x1, Pallas kernels, attention_backward(): pl.pallas_call(attention_back_kernel, grid_spec=pltpu.PrefetchScalarGridS...  35.4 us
  transfers between devices with their start and end apart: 77, of which 38 were waited for; matrix products, arithmetic and copies ran while one was open for 11% of the time, Pallas kernels for 33%

profile of v5, /device:TPU:0, one launch (start us, length us, event | category | flops | bytes accessed | tf_op | source)
XLA Modules:
  0.0 1045.1 jit_solution(4117978186357446328)
XLA Ops:
  29.8 27.4 %all-to-all-done.refs_0_ = bf16[4,48,4224]{2,1,0:T(8,128)(2,1)S(1)} async-done(((bf16[4,48,4224]{2,1,0:T(8,128)(2,1)}), bf16[4,48,4224]{2,1,0:T(8,128)(2,1)S(1)}, u32[]{:S(2)}, u32[]{:S(2)}) %all-to-all-start) | async-done | bytes 1622048 | tf_op jit(solution)/shard_map/all_to_all | solution.py:371
  75.9 24.0 %collective-permute-done.refs_1_.refs_0_ = bf16[4,48,4224]{2,1,0:T(8,128)(2,1)S(1)} collective-permute-done((bf16[4,48,4224]{2,1,0:T(8,128)(2,1)S(1)}, bf16[4,48,4224]{2,1,0:T(8,128)(2,1)S(1)}, u32[]{:S(2)}, u32[]{:S(2)}) %collective-permute-start) | collective-permute-done | bytes 1622048 | tf_op jit(solution)/shard_map/ppermute | solution.py:406
  114.6 13.8 %collective-permute-done.2.refs_3_.refs_0_ = bf16[2,48,4224]{2,1,0:T(8,128)(2,1)S(1)} collective-permute-done((bf16[2,48,4224]{2,1,0:T(8,128)(2,1)S(1)}, bf16[2,48,4224]{2,1,0:T(8,128)(2,1)S(1)}, u32[]{:S(2)}, u32[]{:S(2)}) %collective-permute-start.2) | collective-permute-done | bytes 811040 | tf_op jit(solution)/shard_map/ppermute | solution.py:406
  154.6 10.8 %collective-permute-done.10.refs_2_.rest_0_ = bf16[4,192,768]{2,1,0:T(8,128)(2,1)} collective-permute-done((bf16[4,192,768]{2,1,0:T(8,128)(2,1)}, bf16[4,192,768]{2,1,0:T(8,128)(2,1)}, u32[]{:S(2)}, u32[]{:S(2)}) %collective-permute-start.10) | collective-permute-done | bytes 1179680 | tf_op jit(solution)/shard_map/ppermute | solution.py:406
  178.1 18.6 %attention_forward.1 = (bf16[384,1536]{1,0:T(8,128)(2,1)S(1)}, bf16[384,1536]{1,0:T(8,128)(2,1)S(1)}, bf16[384,512]{1,0:T(8,128)(2,1)S(1)}, bf16[384,512]{1,0:T(...) custom-call(s32[1]{0:T(128)S(6)} %copy.228.length, bf16[384,1536]{1,0:T(8,128)(2,1)} %tokens.3, ...), custom_call_target="tpu_custom_call" | custom-call | flops 3925868544 | bytes 13762560 | tf_op jit(solution)/shard_map/attention_forward/pallas_call | solution.py:976
  215.8 16.3 %collective-permute-done.14.refs_1_.rest_0_ = bf16[4,192,768]{2,1,0:T(8,128)(2,1)S(1)} collective-permute-done((bf16[4,192,768]{2,1,0:T(8,128)(2,1)}, bf16[4,192,768]{2,1,0:T(8,128)(2,1)S(1)}, u32[]{:S(2)}, u32[]{:S(2)}) %collective-permute-start.14) | collective-permute-done | bytes 1179680 | tf_op jit(solution)/shard_map/ppermute | solution.py:406
  245.3 24.3 %collective-permute-done.16.refs_0_ = bf16[4,192,768]{2,1,0:T(8,128)(2,1)S(1)} collective-permute-done((bf16[4,192,768]{2,1,0:T(8,128)(2,1)}, bf16[4,192,768]{2,1,0:T(8,128)(2,1)S(1)}, u32[]{:S(2)}, u32[]{:S(2)}) %collective-permute-start.16) | collective-permute-done | bytes 1179680 | tf_op jit(solution)/shard_map/ppermute | solution.py:406
  273.8 23.6 %collective-permute-done.18.refs_0_ = bf16[4,192,768]{2,1,0:T(8,128)(2,1)S(1)} collective-permute-done((bf16[4,192,768]{2,1,0:T(8,128)(2,1)}, bf16[4,192,768]{2,1,0:T(8,128)(2,1)S(1)}, u32[]{:S(2)}, u32[]{:S(2)}) %collective-permute-start.18) | collective-permute-done | bytes 1179680 | tf_op jit(solution)/shard_map/ppermute | solution.py:406
  301.6 22.8 %collective-permute-done.20.refs_0_.rest_1_ = bf16[4,192,768]{2,1,0:T(8,128)(2,1)S(1)} collective-permute-done((bf16[4,192,768]{2,1,0:T(8,128)(2,1)}, bf16[4,192,768]{2,1,0:T(8,128)(2,1)S(1)}, u32[]{:S(2)}, u32[]{:S(2)}) %collective-permute-start.20) | collective-permute-done | bytes 1179680 | tf_op jit(solution)/shard_map/ppermute | solution.py:406
  328.5 22.0 %collective-permute-done.22.refs_0_.rest_1_ = bf16[4,192,768]{2,1,0:T(8,128)(2,1)S(1)} collective-permute-done((bf16[4,192,768]{2,1,0:T(8,128)(2,1)}, bf16[4,192,768]{2,1,0:T(8,128)(2,1)S(1)}, u32[]{:S(2)}, u32[]{:S(2)}) %collective-permute-start.22) | collective-permute-done | bytes 1179680 | tf_op jit(solution)/shard_map/ppermute | solution.py:406
  386.4 16.4 %expert_forward.6 = (bf16[8,960,1536]{2,1,0:T(8,128)(2,1)}, bf16[1280,1536]{1,0:T(8,128)(2,1)}, f32[1280,1024]{1,0:T(8,128)}) custom-call(s32[2]{0:T(128)} %pad_add_fusion.6.info, s32[8,1,384]{2,1,0:T(1,128)} %get-tuple-element.289.slots, f32[8,1,384]{2,1,0:T(1,128)} %get-tuple-element.278.gates, bf16[8,384,1536]{2,1,0:T(8,128)(2,1)} %copy-done, ...), custom_call_target="tpu_custom_call" | custom-call | flops 7549747200 | bytes 27262976 | tf_op jit(solution)/shard_map/expert_forward/pallas_call | solution.py:579
  402.9 16.5 %expert_forward.7 = (bf16[8,960,1536]{2,1,0:T(8,128)(2,1)}, bf16[1280,1536]{1,0:T(8,128)(2,1)}, f32[1280,1024]{1,0:T(8,128)}) custom-call(s32[2]{0:T(128)} %pad_add_fusion.5.info, s32[8,1,384]{2,1,0:T(1,128)} %get-tuple-element.286.slots, f32[8,1,384]{2,1,0:T(1,128)} %get-tuple-element.279.gates, ...), custom_call_target="tpu_custom_call", output_to_operand_aliasing={{0}: (8, {})} | custom-call | flops 7549747200 | bytes 27262976 | tf_op jit(solution)/shard_map/expert_forward/pallas_call | solution.py:579
  421.0 16.4 %expert_forward.8 = (bf16[8,960,1536]{2,1,0:T(8,128)(2,1)}, bf16[1280,1536]{1,0:T(8,128)(2,1)}, f32[1280,1024]{1,0:T(8,128)}) custom-call(s32[2]{0:T(128)} %pad_add_fusion.4.info, s32[8,1,384]{2,1,0:T(1,128)} %get-tuple-element.288.slots, f32[8,1,384]{2,1,0:T(1,128)} %get-tuple-element.280.gates, ...), custom_call_target="tpu_custom_call", output_to_operand_aliasing={{0}: (8, {})} | custom-call | flops 7549747200 | bytes 27262976 | tf_op jit(solution)/shard_map/expert_forward/pallas_call | solution.py:579
  437.5 16.5 %expert_forward.9 = (bf16[8,960,1536]{2,1,0:T(8,128)(2,1)}, bf16[1280,1536]{1,0:T(8,128)(2,1)}, f32[1280,1024]{1,0:T(8,128)}) custom-call(s32[2]{0:T(128)} %pad_add_fusion.3.info, s32[8,1,384]{2,1,0:T(1,128)} %get-tuple-element.285.slots, f32[8,1,384]{2,1,0:T(1,128)} %get-tuple-element.281.gates, ...), custom_call_target="tpu_custom_call", output_to_operand_aliasing={{0}: (8, {})} | custom-call | flops 7549747200 | bytes 27262976 | tf_op jit(solution)/shard_map/expert_forward/pallas_call | solution.py:579
  454.5 13.0 %expert_forward.10 = (bf16[8,960,1536]{2,1,0:T(8,128)(2,1)}, bf16[1280,1536]{1,0:T(8,128)(2,1)}, f32[1280,512]{1,0:T(8,128)}) custom-call(s32[2]{0:T(128)} %pad_add_fusion.2.info, s32[8,1,384]{2,1,0:T(1,128)} %get-tuple-element.287.slots, f32[8,1,384]{2,1,0:T(1,128)} %get-tuple-element.282.gates, ...), custom_call_target="tpu_custom_call", output_to_operand_aliasing={{0}: (6, {})} | custom-call | flops 4529848320 | bytes 22282240 | tf_op jit(solution)/shard_map/expert_forward/pallas_call | solution.py:579
  467.6 13.1 %expert_forward.11 = (bf16[8,960,1536]{2,1,0:T(8,128)(2,1)}, bf16[1280,1536]{1,0:T(8,128)(2,1)}, f32[1280,512]{1,0:T(8,128)}) custom-call(s32[2]{0:T(128)} %pad_add_fusion.1.info, s32[8,1,384]{2,1,0:T(1,128)} %get-tuple-element.284.slots, f32[8,1,384]{2,1,0:T(1,128)} %get-tuple-element.283.gates, ...), custom_call_target="tpu_custom_call", output_to_operand_aliasing={{0}: (6, {})} | custom-call | flops 4529848320 | bytes 22282240 | tf_op jit(solution)/shard_map/expert_forward/pallas_call | solution.py:579
  482.8 9.7 combine.4.refs_0_
  523.2 26.1 %expert_backward.6 = (bf16[8,960,1664]{2,1,0:T(8,128)(2,1)}, bf16[2,2,192,768]{3,2,1,0:T(8,128)(2,1)}, bf16[2,2,192,768]{3,2,1,0:T(8,128)(2,1)}, bf16[2,2,192,76...) custom-call(s32[2]{0:T(128)} %pad_add_fusion.6.info, s32[8,1,384]{2,1,0:T(1,128)} %get-tuple-element.289.slots, ...), custom_call_target="tpu_custom_call" | custom-call | flops 13589544960 | bytes 31981568 | tf_op jit(solution)/shard_map/expert_backward/pallas_call | solution.py:732
  552.3 26.3 %expert_backward.7 = (bf16[8,960,1664]{2,1,0:T(8,128)(2,1)}, bf16[2,2,192,768]{3,2,1,0:T(8,128)(2,1)}, bf16[2,2,192,768]{3,2,1,0:T(8,128)(2,1)}, bf16[2,2,192,76...) custom-call(s32[2]{0:T(128)} %pad_add_fusion.5.info, ...), custom_call_target="tpu_custom_call", output_to_operand_aliasing={{0}: (10, {})} | custom-call | flops 13589544960 | bytes 31981568 | tf_op jit(solution)/shard_map/expert_backward/pallas_call | solution.py:732
  587.0 26.3 %expert_backward.8 = (bf16[8,960,1664]{2,1,0:T(8,128)(2,1)}, bf16[2,2,192,768]{3,2,1,0:T(8,128)(2,1)}, bf16[2,2,192,768]{3,2,1,0:T(8,128)(2,1)}, bf16[2,2,192,76...) custom-call(s32[2]{0:T(128)} %pad_add_fusion.4.info, ...), custom_call_target="tpu_custom_call", output_to_operand_aliasing={{0}: (10, {})} | custom-call | flops 13589544960 | bytes 31981568 | tf_op jit(solution)/shard_map/expert_backward/pallas_call | solution.py:732
  616.7 26.6 %expert_backward.9 = (bf16[8,960,1664]{2,1,0:T(8,128)(2,1)}, bf16[2,2,192,768]{3,2,1,0:T(8,128)(2,1)}, bf16[2,2,192,768]{3,2,1,0:T(8,128)(2,1)}, bf16[2,2,192,76...) custom-call(s32[2]{0:T(128)} %pad_add_fusion.3.info, ...), custom_call_target="tpu_custom_call", output_to_operand_aliasing={{0}: (10, {})} | custom-call | flops 13589544960 | bytes 31981568 | tf_op jit(solution)/shard_map/expert_backward/pallas_call | solution.py:732
  659.6 19.0 %expert_backward.10 = (bf16[8,960,1664]{2,1,0:T(8,128)(2,1)}, bf16[1,2,192,768]{3,2,1,0:T(8,128)(2,1)}, bf16[1,2,192,768]{3,2,1,0:T(8,128)(2,1)}, bf16[1,2,192,7...) custom-call(s32[2]{0:T(128)} %pad_add_fusion.2.info, ...), custom_call_target="tpu_custom_call", output_to_operand_aliasing={{0}: (8, {})} | custom-call | flops 7549747200 | bytes 24641536 | tf_op jit(solution)/shard_map/expert_backward/pallas_call | solution.py:732
  691.0 19.1 %expert_backward.11 = (bf16[8,960,1664]{2,1,0:T(8,128)(2,1)}, bf16[1,2,192,768]{3,2,1,0:T(8,128)(2,1)}, bf16[1,2,192,768]{3,2,1,0:T(8,128)(2,1)}, bf16[1,2,192,7...) custom-call(s32[2]{0:T(128)} %pad_add_fusion.1.info, ...), custom_call_target="tpu_custom_call", output_to_operand_aliasing={{0}: (8, {})} | custom-call | flops 7549747200 | bytes 24641536 | tf_op jit(solution)/shard_map/expert_backward/pallas_call | solution.py:732
  717.4 10.5 %combine.6.refs_0_ = bf16[4,384,1664]{2,1,0:T(8,128)(2,1)} custom-call(s32[8,6,384]{2,1,0:T(8,128)} %concatenate.135.slots, bf16[8,960,1664]{2,1,0:T(8,128)(2,1)} %get-tuple-element.109.values, f32[8,128]{1,0:T(8,128)} %join.51.rest_0_.refs_1_), custom_call_target="tpu_custom_call" | custom-call | flops 4907335680 | bytes 17891328 | tf_op jit(solution)/shard_map/combine/pallas_call | solution.py:1201
  728.6 10.6 %combine.7.refs_1_ = bf16[4,384,1664]{2,1,0:T(8,128)(2,1)} custom-call(s32[8,6,384]{2,1,0:T(8,128)} %concatenate.135.slots, bf16[8,960,1664]{2,1,0:T(8,128)(2,1)} %get-tuple-element.109.values, f32[8,128]{1,0:T(8,128)} %join.52.rest_0_.refs_1_.refs_6_), custom_call_target="tpu_custom_call" | custom-call | flops 4907335680 | bytes 17891328 | tf_op jit(solution)/shard_map/combine/pallas_call | solution.py:1201
  771.8 26.7 %collective-permute-done.41.refs_4_ = bf16[1,2,192,768]{3,2,1,0:T(8,128)(2,1)S(1)} collective-permute-done((bf16[1,2,192,768]{3,2,1,0:T(8,128)(2,1)}, bf16[1,2,192,768]{3,2,1,0:T(8,128)(2,1)S(1)}, u32[]{:S(2)}, u32[]{:S(2)}) %collective-permute-start.41) | collective-permute-done | bytes 589856 | tf_op jit(solution)/shard_map/ppermute | solution.py:406
  837.4 28.4 %all-to-all-done.12.refs_0_ = bf16[4,384,1664]{2,1,0:T(8,128)(2,1)} async-done(((bf16[4,384,1664]{2,1,0:T(8,128)(2,1)}), bf16[4,384,1664]{2,1,0:T(8,128)(2,1)}, u32[]{:S(2)}, u32[]{:S(2)}) %all-to-all-start.12) | async-done | bytes 5111840 | tf_op jit(solution)/shard_map/all_to_all | solution.py:371
  866.4 13.8 %middle_backward.1 = (f32[384,1536]{1,0:T(8,128)}, bf16[384,1536]{1,0:T(8,128)(2,1)}, bf16[4,4,48,1664]{3,2,1,0:T(8,128)(2,1)}, bf16[4,4,48,1664]{3,2,1,0:T(8,128)(2,1)}) custom-call(s32[1]{0:T(128)} %bitcast.2.c_ref, bf16[4,384,1664]{2,1,0:T(8,128)(2,1)} %tie.86.got, f32[384,128]{1,0:T(8,128)} %pad.9.gates, bf16[1536,4224]{1,0:T(8,128)(2,1)} %bitcast.308, ...), custom_call_target="tpu_custom_call" | custom-call | flops 2264924160 | bytes 23592960 | tf_op jit(solution)/shard_map/middle_backward/pallas_call | solution.py:834
  896.0 35.4 %attention_backward.1 = (bf16[4,4,48,2688]{3,2,1,0:T(8,128)(2,1)}, bf16[4,4,48,2688]{3,2,1,0:T(8,128)(2,1)}, f32[384,1536]{1,0:T(8,128)}) custom-call(s32[2]{0:T(128)S(1)} %pad_add_fusion.7.length, bf16[384,1536]{1,0:T(8,128)(2,1)S(1)} %copy-done.24, bf16[1536,4224]{1,0:T(8,128)(2,1)} %bitcast.309, bf16[384,1536]{1,0:T(8,128)(2,1)S(1)} %get-tuple-element.123.q, ...), custom_call_target="tpu_custom_call" | custom-call | flops 10116661248 | bytes 28704768 | tf_op jit(solution)/shard_map/attention_backward/pallas_call | solution.py:1139
  950.5 11.4 %collective-permute-done.56 = bf16[2,48,2688]{2,1,0:T(8,128)(2,1)S(1)} collective-permute-done((bf16[2,48,2688]{2,1,0:T(8,128)(2,1)S(1)}, bf16[2,48,2688]{2,1,0:T(8,128)(2,1)S(1)}, u32[]{:S(2)}, u32[]{:S(2)}) %collective-permute-start.56) | collective-permute-done | bytes 516128 | tf_op jit(solution)/shard_map/ppermute | solution.py:406
  963.0 10.8 %collective-permute-done.58 = bf16[2,48,2688]{2,1,0:T(8,128)(2,1)S(1)} collective-permute-done((bf16[2,48,2688]{2,1,0:T(8,128)(2,1)S(1)}, bf16[2,48,2688]{2,1,0:T(8,128)(2,1)S(1)}, u32[]{:S(2)}, u32[]{:S(2)}) %collective-permute-start.58) | collective-permute-done | bytes 516128 | tf_op jit(solution)/shard_map/ppermute | solution.py:406
  1011.1 27.3 %all-to-all-done.14 = bf16[4,48,4352]{2,1,0:T(8,128)(2,1)} async-done(((bf16[4,48,4352]{2,1,0:T(8,128)(2,1)}), bf16[4,48,4352]{2,1,0:T(8,128)(2,1)}, u32[]{:S(2)}, u32[]{:S(2)}) %all-to-all-start.14) | async-done | bytes 1671200 | tf_op jit(solution)/shard_map/all_to_all | solution.py:371
  (588 shorter events, 418.3 us)
Async XLA Ops:
  16.8 40.4 %all-to-all-start = ((bf16[4,48,4224]{2,1,0:T(8,128)(2,1)}), bf16[4,48,4224]{2,1,0:T(8,128)(2,1)S(1)}, u32[]{:S(2)}, u32[]{:S(2)}) async-start(bf16[4,48,4224]{2,1,0:T(8,128)(2,1)} %broadcast_in_dim.39), calls=%async_computation | async-start | bytes 3244032 | tf_op jit(solution)/shard_map/all_to_all | solution.py:371
  58.9 42.2 %all-to-all-start.2 = ((bf16[4,192,768]{2,1,0:T(8,128)(2,1)}), bf16[4,192,768]{2,1,0:T(8,128)(2,1)}, u32[]{:S(2)}, u32[]{:S(2)}) async-start(bf16[4,192,768]{2,1,0:T(8,128)(2,1)} %tie.45), calls=%async_computation.2 | async-start | bytes 2359296 | tf_op jit(solution)/shard_map/all_to_all | solution.py:371
  63.4 36.5 %collective-permute-start = (bf16[4,48,4224]{2,1,0:T(8,128)(2,1)S(1)}, bf16[4,48,4224]{2,1,0:T(8,128)(2,1)S(1)}, u32[]{:S(2)}, u32[]{:S(2)}) collective-permute-start(bf16[4,48,4224]{2,1,0:T(8,128)(2,1)S(1)} %copy-done.3), channel_id=1, source_target_pairs={{0,2},{1,3},{2,0},{3,1},{4,6},{5,7},{6,4},{7,5},{8,10},{9,11},{10,... | collective-permute-start | bytes 4866056 | tf_op jit(solution)/shard_map/ppermute | solution.py:406
  64.9 36.2 %collective-permute-start.1 = (bf16[4,48,4224]{2,1,0:T(8,128)(2,1)S(1)}, bf16[4,48,4224]{2,1,0:T(8,128)(2,1)}, u32[]{:S(2)}, u32[]{:S(2)}) collective-permute-start(bf16[4,48,4224]{2,1,0:T(8,128)(2,1)S(1)} %copy-done.3), channel_id=1, source_target_pairs={{0,4},{1,5},{2,6},{3,7},{4,0},{5,1},{6,2},{7,3},{8,12},{9,13},{10,... | collective-permute-start | bytes 4866056 | tf_op jit(solution)/shard_map/ppermute | solution.py:406
  66.4 34.7 %collective-permute-start.4 = (bf16[4,48,4224]{2,1,0:T(8,128)(2,1)S(1)}, bf16[4,48,4224]{2,1,0:T(8,128)(2,1)}, u32[]{:S(2)}, u32[]{:S(2)}) collective-permute-start(bf16[4,48,4224]{2,1,0:T(8,128)(2,1)S(1)} %copy-done.3), channel_id=1, source_target_pairs={{0,1},{1,0},{2,3},{3,2},{4,5},{5,4},{6,7},{7,6},{8,9},{9,8},{10,11... | collective-permute-start | bytes 4866056 | tf_op jit(solution)/shard_map/ppermute | solution.py:406
  101.8 31.5 %all-to-all-start.3 = ((bf16[4,192,768]{2,1,0:T(8,128)(2,1)}), bf16[4,192,768]{2,1,0:T(8,128)(2,1)}, u32[]{:S(2)}, u32[]{:S(2)}) async-start(bf16[4,192,768]{2,1,0:T(8,128)(2,1)} %tie.46), calls=%async_computation.3 | async-start | bytes 2359296 | tf_op jit(solution)/shard_map/all_to_all | solution.py:371
  133.8 32.8 %all-to-all-start.4 = ((bf16[4,192,768]{2,1,0:T(8,128)(2,1)}), bf16[4,192,768]{2,1,0:T(8,128)(2,1)}, u32[]{:S(2)}, u32[]{:S(2)}) async-start(bf16[4,192,768]{2,1,0:T(8,128)(2,1)} %tie.47), calls=%async_computation.4 | async-start | bytes 2359296 | tf_op jit(solution)/shard_map/all_to_all | solution.py:371
  167.2 32.7 %all-to-all-start.5 = ((bf16[4,192,768]{2,1,0:T(8,128)(2,1)}), bf16[4,192,768]{2,1,0:T(8,128)(2,1)}, u32[]{:S(2)}, u32[]{:S(2)}) async-start(bf16[4,192,768]{2,1,0:T(8,128)(2,1)} %tie.49), calls=%async_computation.5 | async-start | bytes 2359296 | tf_op jit(solution)/shard_map/all_to_all | solution.py:371
  200.5 32.7 %all-to-all-start.6 = ((bf16[4,192,768]{2,1,0:T(8,128)(2,1)}), bf16[4,192,768]{2,1,0:T(8,128)(2,1)}, u32[]{:S(2)}, u32[]{:S(2)}) async-start(bf16[4,192,768]{2,1,0:T(8,128)(2,1)} %tie.51), calls=%async_computation.6 | async-start | bytes 2359296 | tf_op jit(solution)/shard_map/all_to_all | solution.py:371
  237.6 114.6 %all-to-all-start.7 = ((bf16[4,384,1536]{2,1,0:T(8,128)(2,1)}), bf16[4,384,1536]{2,1,0:T(8,128)(2,1)}, u32[]{:S(2)}, u32[]{:S(2)}) async-start(bf16[4,384,1536]{2,1,0:T(8,128)(2,1)} %broadcast_in_dim.44), calls=%async_computation.7 | async-start | bytes 9437184 | tf_op jit(solution)/shard_map/all_to_all | solution.py:371
  365.4 115.3 %all-to-all-start.8 = ((bf16[4,384,1536]{2,1,0:T(8,128)(2,1)}), bf16[4,384,1536]{2,1,0:T(8,128)(2,1)}, u32[]{:S(2)}, u32[]{:S(2)}) async-start(bf16[4,384,1536]{2,1,0:T(8,128)(2,1)} %broadcast_in_dim.47), calls=%async_computation.8 | async-start | bytes 9437184 | tf_op jit(solution)/shard_map/all_to_all | solution.py:371
  375.1 44.3 %collective-permute-start.25 = (bf16[4,192,768]{2,1,0:T(8,128)(2,1)}, bf16[4,192,768]{2,1,0:T(8,128)(2,1)S(1)}, u32[]{:S(2)}, u32[]{:S(2)}) collective-permute-start(bf16[4,192,768]{2,1,0:T(8,128)(2,1)} %tie.61.rest_1_), channel_id=1, source_target_pairs={{0,2},{1,3},{2,0},{3,1},{4,6},{5,7},{6,4},{7,5},{8,10},{9,11},{10,... | collective-permute-start | bytes 3538952 | tf_op jit(solution)/shard_map/ppermute | solution.py:406
  518.2 130.9 %all-to-all-start.9 = ((bf16[4,384,1536]{2,1,0:T(8,128)(2,1)}), bf16[4,384,1536]{2,1,0:T(8,128)(2,1)}, u32[]{:S(2)}, u32[]{:S(2)}) async-start(bf16[4,384,1536]{2,1,0:T(8,128)(2,1)} %tie.65), calls=%async_computation.9 | async-start | bytes 9437184 | tf_op jit(solution)/shard_map/all_to_all | solution.py:371
  580.2 33.1 %collective-permute-start.30 = (bf16[2,2,192,768]{3,2,1,0:T(8,128)(2,1)}, bf16[2,2,192,768]{3,2,1,0:T(8,128)(2,1)}, u32[]{:S(2)}, u32[]{:S(2)}) collective-permute-start(bf16[2,2,192,768]{3,2,1,0:T(8,128)(2,1)} %tie.68), channel_id=1, source_target_pairs={{0,2},{1,3},{2,0},{3,1},{4,6},{5,7},{6,4},{7,5},{8,10},{9,11},{10,... | collective-permute-start | bytes 3538952 | tf_op jit(solution)/shard_map/ppermute | solution.py:406
  581.5 31.9 %collective-permute-start.31 = (bf16[2,2,192,768]{3,2,1,0:T(8,128)(2,1)}, bf16[2,2,192,768]{3,2,1,0:T(8,128)(2,1)S(1)}, u32[]{:S(2)}, u32[]{:S(2)}) collective-permute-start(bf16[2,2,192,768]{3,2,1,0:T(8,128)(2,1)} %tie.69), channel_id=1, source_target_pairs={{0,4},{1,5},{2,6},{3,7},{4,0},{5,1},{6,2},{7,3},{8,12},{9,13},{10,... | collective-permute-start | bytes 3538952 | tf_op jit(solution)/shard_map/ppermute | solution.py:406
  614.9 31.8 %collective-permute-start.32 = (bf16[2,2,192,768]{3,2,1,0:T(8,128)(2,1)}, bf16[2,2,192,768]{3,2,1,0:T(8,128)(2,1)S(1)}, u32[]{:S(2)}, u32[]{:S(2)}) collective-permute-start(bf16[2,2,192,768]{3,2,1,0:T(8,128)(2,1)} %tie.70), channel_id=1, source_target_pairs={{0,2},{1,3},{2,0},{3,1},{4,6},{5,7},{6,4},{7,5},{8,10},{9,11},{10,... | collective-permute-start | bytes 3538952 | tf_op jit(solution)/shard_map/ppermute | solution.py:406
  649.8 32.9 %all-to-all-start.10 = ((bf16[4,192,768]{2,1,0:T(8,128)(2,1)}), bf16[4,192,768]{2,1,0:T(8,128)(2,1)S(1)}, u32[]{:S(2)}, u32[]{:S(2)}) async-start(bf16[4,192,768]{2,1,0:T(8,128)(2,1)} %tie.74), calls=%async_computation.10 | async-start | bytes 2359296 | tf_op jit(solution)/shard_map/all_to_all | solution.py:371
  684.3 31.6 %all-to-all-start.11 = ((bf16[4,192,768]{2,1,0:T(8,128)(2,1)}), bf16[4,192,768]{2,1,0:T(8,128)(2,1)S(1)}, u32[]{:S(2)}, u32[]{:S(2)}) async-start(bf16[4,192,768]{2,1,0:T(8,128)(2,1)} %tie.77), calls=%async_computation.11 | async-start | bytes 2359296 | tf_op jit(solution)/shard_map/all_to_all | solution.py:371
  746.6 119.2 %all-to-all-start.12 = ((bf16[4,384,1664]{2,1,0:T(8,128)(2,1)}), bf16[4,384,1664]{2,1,0:T(8,128)(2,1)}, u32[]{:S(2)}, u32[]{:S(2)}) async-start(bf16[4,384,1664]{2,1,0:T(8,128)(2,1)} %add_convert_fusion), calls=%async_computation.12 | async-start | bytes 10223616 | tf_op jit(solution)/shard_map/all_to_all | solution.py:371
  757.3 41.9 %collective-permute-start.40 = (bf16[2,2,192,768]{3,2,1,0:T(8,128)(2,1)}, bf16[2,2,192,768]{3,2,1,0:T(8,128)(2,1)}, u32[]{:S(2)}, u32[]{:S(2)}) collective-permute-start(bf16[2,2,192,768]{3,2,1,0:T(8,128)(2,1)} %tie.79), channel_id=1, source_target_pairs={{0,2},{1,3},{2,0},{3,1},{4,6},{5,7},{6,4},{7,5},{8,10},{9,11},{10,... | collective-permute-start | bytes 3538952 | tf_op jit(solution)/shard_map/ppermute | solution.py:406
  758.3 41.0 %collective-permute-start.39 = (bf16[2,2,192,768]{3,2,1,0:T(8,128)(2,1)}, bf16[2,2,192,768]{3,2,1,0:T(8,128)(2,1)}, u32[]{:S(2)}, u32[]{:S(2)}) collective-permute-start(bf16[2,2,192,768]{3,2,1,0:T(8,128)(2,1)} %tie.78), channel_id=1, source_target_pairs={{0,4},{1,5},{2,6},{3,7},{4,0},{5,1},{6,2},{7,3},{8,12},{9,13},{10,... | collective-permute-start | bytes 3538952 | tf_op jit(solution)/shard_map/ppermute | solution.py:406
  762.1 36.5 %collective-permute-start.41 = (bf16[1,2,192,768]{3,2,1,0:T(8,128)(2,1)}, bf16[1,2,192,768]{3,2,1,0:T(8,128)(2,1)S(1)}, u32[]{:S(2)}, u32[]{:S(2)}) collective-permute-start(bf16[1,2,192,768]{3,2,1,0:T(8,128)(2,1)} %tie.80), channel_id=1, source_target_pairs={{0,2},{1,3},{2,0},{3,1},{4,6},{5,7},{6,4},{7,5},{8,10},{9,11},{10,... | collective-permute-start | bytes 1769480 | tf_op jit(solution)/shard_map/ppermute | solution.py:406
  763.0 36.2 %collective-permute-start.42 = (bf16[1,2,192,768]{3,2,1,0:T(8,128)(2,1)}, bf16[1,2,192,768]{3,2,1,0:T(8,128)(2,1)S(1)}, u32[]{:S(2)}, u32[]{:S(2)}) collective-permute-start(bf16[1,2,192,768]{3,2,1,0:T(8,128)(2,1)} %tie.81), channel_id=1, source_target_pairs={{0,4},{1,5},{2,6},{3,7},{4,0},{5,1},{6,2},{7,3},{8,12},{9,13},{10,... | collective-permute-start | bytes 1769480 | tf_op jit(solution)/shard_map/ppermute | solution.py:406
  880.4 51.1 %all-to-all-start.13 = ((bf16[4,192,768]{2,1,0:T(8,128)(2,1)}), bf16[4,192,768]{2,1,0:T(8,128)(2,1)S(1)}, u32[]{:S(2)}, u32[]{:S(2)}) async-start(bf16[4,192,768]{2,1,0:T(8,128)(2,1)} %tie.87), calls=%async_computation.13 | async-start | bytes 2359296 | tf_op jit(solution)/shard_map/all_to_all | solution.py:371
  890.4 41.1 %collective-permute-start.49 = (bf16[2,48,1664]{2,1,0:T(8,128)(2,1)}, bf16[2,48,1664]{2,1,0:T(8,128)(2,1)}, u32[]{:S(2)}, u32[]{:S(2)}) collective-permute-start(bf16[2,48,1664]{2,1,0:T(8,128)(2,1)} %get-tuple-element.275), channel_id=1, source_target_pairs={{0,2},{1,3},{2,0},{3,1},{4,6},{5,7},{6,4},{7,5},{8,10},{9,11},{10,... | collective-permute-start | bytes 958472 | tf_op jit(solution)/shard_map/ppermute | solution.py:406
  891.3 40.1 %collective-permute-start.51 = (bf16[2,48,1664]{2,1,0:T(8,128)(2,1)}, bf16[2,48,1664]{2,1,0:T(8,128)(2,1)}, u32[]{:S(2)}, u32[]{:S(2)}) collective-permute-start(bf16[2,48,1664]{2,1,0:T(8,128)(2,1)} %get-tuple-element.274), channel_id=1, source_target_pairs={{0,4},{1,5},{2,6},{3,7},{4,0},{5,1},{6,2},{7,3},{8,12},{9,13},{10,... | collective-permute-start | bytes 958472 | tf_op jit(solution)/shard_map/ppermute | solution.py:406
  893.1 38.4 %collective-permute-start.48 = (bf16[2,48,1664]{2,1,0:T(8,128)(2,1)}, bf16[2,48,1664]{2,1,0:T(8,128)(2,1)}, u32[]{:S(2)}, u32[]{:S(2)}) collective-permute-start(bf16[2,48,1664]{2,1,0:T(8,128)(2,1)} %fusion.59), channel_id=1, source_target_pairs={{0,2},{1,3},{2,0},{3,1},{4,6},{5,7},{6,4},{7,5},{8,10},{9,11},{10,... | collective-permute-start | bytes 958472 | tf_op jit(solution)/shard_map/ppermute | solution.py:406
  894.8 36.7 %collective-permute-start.53 = (bf16[2,48,1664]{2,1,0:T(8,128)(2,1)}, bf16[2,48,1664]{2,1,0:T(8,128)(2,1)}, u32[]{:S(2)}, u32[]{:S(2)}) collective-permute-start(bf16[2,48,1664]{2,1,0:T(8,128)(2,1)} %fusion.60), channel_id=1, source_target_pairs={{0,4},{1,5},{2,6},{3,7},{4,0},{5,1},{6,2},{7,3},{8,12},{9,13},{10,... | collective-permute-start | bytes 958472 | tf_op jit(solution)/shard_map/ppermute | solution.py:406
  935.5 39.4 %collective-permute-start.50 = (bf16[2,48,1664]{2,1,0:T(8,128)(2,1)S(1)}, bf16[2,48,1664]{2,1,0:T(8,128)(2,1)S(1)}, u32[]{:S(2)}, u32[]{:S(2)}) collective-permute-start(bf16[2,48,1664]{2,1,0:T(8,128)(2,1)S(1)} %fusion.37), channel_id=1, source_target_pairs={{0,4},{1,5},{2,6},{3,7},{4,0},{5,1},{6,2},{7,3},{8,12},{9,13},{10,... | collective-permute-start | bytes 958472 | tf_op jit(solution)/shard_map/ppermute | solution.py:406
  937.5 38.6 %collective-permute-start.52 = (bf16[2,48,1664]{2,1,0:T(8,128)(2,1)S(1)}, bf16[2,48,1664]{2,1,0:T(8,128)(2,1)}, u32[]{:S(2)}, u32[]{:S(2)}) collective-permute-start(bf16[2,48,1664]{2,1,0:T(8,128)(2,1)S(1)} %fusion.32), channel_id=1, source_target_pairs={{0,2},{1,3},{2,0},{3,1},{4,6},{5,7},{6,4},{7,5},{8,10},{9,11},{10,... | collective-permute-start | bytes 958472 | tf_op jit(solution)/shard_map/ppermute | solution.py:406
  938.6 56.8 %all-to-all-start.15 = ((bf16[4,384,768]{2,1,0:T(8,128)(2,1)}), bf16[4,384,768]{2,1,0:T(8,128)(2,1)S(1)}, u32[]{:S(2)}, u32[]{:S(2)}) async-start(bf16[4,384,768]{2,1,0:T(8,128)(2,1)} %tie.89), calls=%async_computation.15 | async-start | bytes 4718592 | tf_op jit(solution)/shard_map/all_to_all | solution.py:371
  995.4 43.0 %all-to-all-start.14 = ((bf16[4,48,4352]{2,1,0:T(8,128)(2,1)}), bf16[4,48,4352]{2,1,0:T(8,128)(2,1)}, u32[]{:S(2)}, u32[]{:S(2)}) async-start(bf16[4,48,4352]{2,1,0:T(8,128)(2,1)} %maximum_maximum_fusion.1.refs_4_), calls=%async_computation.14 | async-start | bytes 3342336 | tf_op jit(solution)/shard_map/all_to_all | solution.py:371
  (168 other events, 1376.7 us)

commit v6 on v5

--- a/solution.py
+++ b/solution.py
@@ -1432,8 +1432,6 @@
     )
     moved[1] = gate(moved[1])
     rounds.close(*send_half(3), *send_near(1), mixed)
-    moved[2] = gate(moved[2])
-    send_half(4)
     branch = multiply_transposed(mixed, out_t)
     middle = inputs + residual_scale * branch
     inverse_two = rms_inverse(middle)
@@ -1441,12 +1439,11 @@
     hidden_two = (normal_two * gain_two).astype(low)
     grad_out = cotangent.astype(full)
 
-    rounds.close(moved[4], *send_near(2))
     rows_own = spread(gate(hidden_two))
+    moved[2] = gate(moved[2])
+    rounds.close(*send_near(2))
     moved[3] = gate(moved[3])
     rounds.close(*send_near(3))
-    moved[4] = gate(moved[4])
-    rounds.close(*send_near(4))
     for first, second in ((0, 1), (2, 3)):
         near[first] = (near[first][0], gate(near[first][1]))
         near[second] = (gate(near[second][0]), near[second][1])
@@ -1454,7 +1451,7 @@
     rounds.close(rows_own)
     rows_own = gate(rows_own)
     rows_other = move(rows_own, PAIRS_C)
-    rounds.close(rows_other)
+    rounds.close(rows_other, *send_half(4))
     rows_in = join_rows([rows_other], [rows_own])
     slots_in = jnp.concatenate([tables_c, tables], axis=0).astype(jnp.int32)
     logits_in = jnp.einsum("de,itd->iet", router_full, rows_in, preferred_element_type=full)
@@ -1500,12 +1497,14 @@
         )
 
     dy_own = spread(gate(cotangent))
-    late = [(4,), (), ()]
     for pair in range(pairs):
         sent = []
-        for q in late[pair]:
-            near[q] = tuple(gate(part) for part in near[q])
-            sent += send_far(q)
+        if pair == 0:
+            moved[4] = gate(moved[4])
+            sent += send_near(4)
+        if pair == 1:
+            near[4] = tuple(gate(part) for part in near[4])
+            sent += send_far(4)
         run_forward(pair, False)
         run_forward(pair, True)
         rounds.close(saved[pair + pairs][0], *sent, *([dy_own] if pair == 2 else []))

time: 1060 us -> 1050 us (level)
    all_to_all x16, waiting for transfers between devices: 100 us -> 127 us  [trade(): lax.all_to_all(value, 'dp', split_axis=0, concat_axis=0, axis_index_group...]
    ppermute x61, waiting for transfers between devices: 253 us -> 229 us  [move(): return lax.ppermute(value, MESH_AXES, pairs)]
    unnamed x253 -> x257, local copies, waits for them, and re-layouts: 28.5 us -> 31 us
where the time goes in v6:
time: 1050 us; the launch traced here: 1040 us
  Pallas kernels  382 us (36%)
  waiting for transfers between devices  356 us (34%)
  starting transfers between devices  128 us (12%)
  other arithmetic  97.7 us (9%)
  local copies, waits for them, and re-layouts  66.9 us (6%)
  matrix products  11.8 us (1%)
    ppermute x61, waiting for transfers between devices, move(): return lax.ppermute(value, MESH_AXES, pairs)  229 us
    pallas_call x6, Pallas kernels, expert_backward(): pl.pallas_call(functools.partial(expert_back_kernel, count=len(pieces), w...  143 us
    all_to_all x16, waiting for transfers between devices, trade(): lax.all_to_all(value, 'dp', split_axis=0, concat_axis=0, axis_index_group...  127 us
    pallas_call x6, Pallas kernels, expert_forward(): pl.pallas_call(functools.partial(expert_forward_kernel, count=len(pieces)...  92.2 us
    all_to_all x16, starting transfers between devices, trade(): lax.all_to_all(value, 'dp', split_axis=0, concat_axis=0, axis_index_group...  75.1 us
    ppermute x61, starting transfers between devices, move(): return lax.ppermute(value, MESH_AXES, pairs)  52.5 us
    pallas_call x4, Pallas kernels, combine(): pl.pallas_call(combine_kernel, grid=(Z_SIZE,), in_specs=[pl.BlockSpec((1,...  40.4 us
    pallas_call x1, Pallas kernels, attention_backward(): pl.pallas_call(attention_back_kernel, grid_spec=pltpu.PrefetchScalarGridS...  35.4 us
  transfers between devices with their start and end apart: 77, of which 38 were waited for; matrix products, arithmetic and copies ran while one was open for 11% of the time, Pallas kernels for 33%

profile of v6, /device:TPU:0, one launch (start us, length us, event | category | flops | bytes accessed | tf_op | source)
XLA Modules:
  0.0 1044.9 jit_solution(6809971380515782092)
XLA Ops:
  29.7 27.5 %all-to-all-done.refs_0_ = bf16[4,48,4224]{2,1,0:T(8,128)(2,1)S(1)} async-done(((bf16[4,48,4224]{2,1,0:T(8,128)(2,1)}), bf16[4,48,4224]{2,1,0:T(8,128)(2,1)S(1)}, u32[]{:S(2)}, u32[]{:S(2)}) %all-to-all-start) | async-done | bytes 1622048 | tf_op jit(solution)/shard_map/all_to_all | solution.py:371
  75.9 23.9 %collective-permute-done.refs_1_.refs_0_ = bf16[4,48,4224]{2,1,0:T(8,128)(2,1)S(1)} collective-permute-done((bf16[4,48,4224]{2,1,0:T(8,128)(2,1)S(1)}, bf16[4,48,4224]{2,1,0:T(8,128)(2,1)S(1)}, u32[]{:S(2)}, u32[]{:S(2)}) %collective-permute-start) | collective-permute-done | bytes 1622048 | tf_op jit(solution)/shard_map/ppermute | solution.py:406
  115.3 13.2 %collective-permute-done.2.refs_3_.refs_0_ = bf16[2,48,4224]{2,1,0:T(8,128)(2,1)S(1)} collective-permute-done((bf16[2,48,4224]{2,1,0:T(8,128)(2,1)S(1)}, bf16[2,48,4224]{2,1,0:T(8,128)(2,1)S(1)}, u32[]{:S(2)}, u32[]{:S(2)}) %collective-permute-start.2) | collective-permute-done | bytes 811040 | tf_op jit(solution)/shard_map/ppermute | solution.py:406
  174.4 18.7 %attention_forward.1 = (bf16[384,1536]{1,0:T(8,128)(2,1)S(1)}, bf16[384,1536]{1,0:T(8,128)(2,1)S(1)}, bf16[384,512]{1,0:T(8,128)(2,1)S(1)}, bf16[384,512]{1,0:T(...) custom-call(s32[1]{0:T(128)S(6)} %copy.228.length, bf16[384,1536]{1,0:T(8,128)(2,1)} %tokens.3, ...), custom_call_target="tpu_custom_call" | custom-call | flops 3925868544 | bytes 13762560 | tf_op jit(solution)/shard_map/attention_forward/pallas_call | solution.py:976
  212.7 25.8 %collective-permute-done.14.refs_1_.refs_0_ = bf16[4,192,768]{2,1,0:T(8,128)(2,1)S(1)} collective-permute-done((bf16[4,192,768]{2,1,0:T(8,128)(2,1)}, bf16[4,192,768]{2,1,0:T(8,128)(2,1)S(1)}, u32[]{:S(2)}, u32[]{:S(2)}) %collective-permute-start.14) | collective-permute-done | bytes 1179680 | tf_op jit(solution)/shard_map/ppermute | solution.py:406
  241.5 24.9 %collective-permute-done.16.refs_0_ = bf16[4,192,768]{2,1,0:T(8,128)(2,1)S(1)} collective-permute-done((bf16[4,192,768]{2,1,0:T(8,128)(2,1)}, bf16[4,192,768]{2,1,0:T(8,128)(2,1)S(1)}, u32[]{:S(2)}, u32[]{:S(2)}) %collective-permute-start.16) | collective-permute-done | bytes 1179680 | tf_op jit(solution)/shard_map/ppermute | solution.py:406
  269.4 24.1 %collective-permute-done.18.refs_0_.rest_1_ = bf16[4,192,768]{2,1,0:T(8,128)(2,1)S(1)} collective-permute-done((bf16[4,192,768]{2,1,0:T(8,128)(2,1)}, bf16[4,192,768]{2,1,0:T(8,128)(2,1)S(1)}, u32[]{:S(2)}, u32[]{:S(2)}) %collective-permute-start.18) | collective-permute-done | bytes 1179680 | tf_op jit(solution)/shard_map/ppermute | solution.py:406
  296.3 23.6 %collective-permute-done.20.refs_0_.rest_1_ = bf16[4,192,768]{2,1,0:T(8,128)(2,1)S(1)} collective-permute-done((bf16[4,192,768]{2,1,0:T(8,128)(2,1)}, bf16[4,192,768]{2,1,0:T(8,128)(2,1)S(1)}, u32[]{:S(2)}, u32[]{:S(2)}) %collective-permute-start.20) | collective-permute-done | bytes 1179680 | tf_op jit(solution)/shard_map/ppermute | solution.py:406
  330.9 25.8 %all-to-all-done.7.refs_1_.refs_0_ = bf16[4,192,768]{2,1,0:T(8,128)(2,1)S(1)} async-done(((bf16[4,192,768]{2,1,0:T(8,128)(2,1)}), bf16[4,192,768]{2,1,0:T(8,128)(2,1)S(1)}, u32[]{:S(2)}, u32[]{:S(2)}) %all-to-all-start.7) | async-done | bytes 1179680 | tf_op jit(solution)/shard_map/all_to_all | solution.py:371
  383.5 16.4 %expert_forward.6 = (bf16[8,960,1536]{2,1,0:T(8,128)(2,1)}, bf16[1280,1536]{1,0:T(8,128)(2,1)}, f32[1280,1024]{1,0:T(8,128)}) custom-call(s32[2]{0:T(128)} %pad_add_fusion.3.info, s32[8,1,384]{2,1,0:T(1,128)} %get-tuple-element.289.slots, f32[8,1,384]{2,1,0:T(1,128)} %get-tuple-element.281.gates, bf16[8,384,1536]{2,1,0:T(8,128)(2,1)} %copy-done, ...), custom_call_target="tpu_custom_call" | custom-call | flops 7549747200 | bytes 27262976 | tf_op jit(solution)/shard_map/expert_forward/pallas_call | solution.py:579
  399.9 16.5 %expert_forward.7 = (bf16[8,960,1536]{2,1,0:T(8,128)(2,1)}, bf16[1280,1536]{1,0:T(8,128)(2,1)}, f32[1280,1024]{1,0:T(8,128)}) custom-call(s32[2]{0:T(128)} %pad_add_fusion.2.info, s32[8,1,384]{2,1,0:T(1,128)} %get-tuple-element.286.slots, f32[8,1,384]{2,1,0:T(1,128)} %get-tuple-element.282.gates, ...), custom_call_target="tpu_custom_call", output_to_operand_aliasing={{0}: (8, {})} | custom-call | flops 7549747200 | bytes 27262976 | tf_op jit(solution)/shard_map/expert_forward/pallas_call | solution.py:579
  419.1 16.5 %expert_forward.8 = (bf16[8,960,1536]{2,1,0:T(8,128)(2,1)}, bf16[1280,1536]{1,0:T(8,128)(2,1)}, f32[1280,1024]{1,0:T(8,128)}) custom-call(s32[2]{0:T(128)} %pad_add_fusion.6.info, s32[8,1,384]{2,1,0:T(1,128)} %get-tuple-element.288.slots, f32[8,1,384]{2,1,0:T(1,128)} %get-tuple-element.278.gates, ...), custom_call_target="tpu_custom_call", output_to_operand_aliasing={{0}: (8, {})} | custom-call | flops 7549747200 | bytes 27262976 | tf_op jit(solution)/shard_map/expert_forward/pallas_call | solution.py:579
  435.6 16.5 %expert_forward.9 = (bf16[8,960,1536]{2,1,0:T(8,128)(2,1)}, bf16[1280,1536]{1,0:T(8,128)(2,1)}, f32[1280,1024]{1,0:T(8,128)}) custom-call(s32[2]{0:T(128)} %pad_add_fusion.5.info, s32[8,1,384]{2,1,0:T(1,128)} %get-tuple-element.285.slots, f32[8,1,384]{2,1,0:T(1,128)} %get-tuple-element.279.gates, ...), custom_call_target="tpu_custom_call", output_to_operand_aliasing={{0}: (8, {})} | custom-call | flops 7549747200 | bytes 27262976 | tf_op jit(solution)/shard_map/expert_forward/pallas_call | solution.py:579
  453.7 13.0 %expert_forward.10 = (bf16[8,960,1536]{2,1,0:T(8,128)(2,1)}, bf16[1280,1536]{1,0:T(8,128)(2,1)}, f32[1280,512]{1,0:T(8,128)}) custom-call(s32[2]{0:T(128)} %pad_add_fusion.4.info, s32[8,1,384]{2,1,0:T(1,128)} %get-tuple-element.287.slots, f32[8,1,384]{2,1,0:T(1,128)} %get-tuple-element.280.gates, ...), custom_call_target="tpu_custom_call", output_to_operand_aliasing={{0}: (6, {})} | custom-call | flops 4529848320 | bytes 22282240 | tf_op jit(solution)/shard_map/expert_forward/pallas_call | solution.py:579
  466.7 13.4 %expert_forward.11 = (bf16[8,960,1536]{2,1,0:T(8,128)(2,1)}, bf16[1280,1536]{1,0:T(8,128)(2,1)}, f32[1280,512]{1,0:T(8,128)}) custom-call(s32[2]{0:T(128)} %pad_add_fusion.1.info, s32[8,1,384]{2,1,0:T(1,128)} %get-tuple-element.284.slots, f32[8,1,384]{2,1,0:T(1,128)} %get-tuple-element.283.gates, ...), custom_call_target="tpu_custom_call", output_to_operand_aliasing={{0}: (6, {})} | custom-call | flops 4529848320 | bytes 22282240 | tf_op jit(solution)/shard_map/expert_forward/pallas_call | solution.py:579
  482.2 9.7 combine.4.refs_0_
  499.9 9.7 combine.5.refs_1_
  522.7 26.2 %expert_backward.6 = (bf16[8,960,1664]{2,1,0:T(8,128)(2,1)}, bf16[2,2,192,768]{3,2,1,0:T(8,128)(2,1)}, bf16[2,2,192,768]{3,2,1,0:T(8,128)(2,1)}, bf16[2,2,192,76...) custom-call(s32[2]{0:T(128)} %pad_add_fusion.3.info, s32[8,1,384]{2,1,0:T(1,128)} %get-tuple-element.289.slots, ...), custom_call_target="tpu_custom_call" | custom-call | flops 13589544960 | bytes 31981568 | tf_op jit(solution)/shard_map/expert_backward/pallas_call | solution.py:732
  552.2 26.3 %expert_backward.7 = (bf16[8,960,1664]{2,1,0:T(8,128)(2,1)}, bf16[2,2,192,768]{3,2,1,0:T(8,128)(2,1)}, bf16[2,2,192,768]{3,2,1,0:T(8,128)(2,1)}, bf16[2,2,192,76...) custom-call(s32[2]{0:T(128)} %pad_add_fusion.2.info, ...), custom_call_target="tpu_custom_call", output_to_operand_aliasing={{0}: (10, {})} | custom-call | flops 13589544960 | bytes 31981568 | tf_op jit(solution)/shard_map/expert_backward/pallas_call | solution.py:732
  586.8 26.3 %expert_backward.8 = (bf16[8,960,1664]{2,1,0:T(8,128)(2,1)}, bf16[2,2,192,768]{3,2,1,0:T(8,128)(2,1)}, bf16[2,2,192,768]{3,2,1,0:T(8,128)(2,1)}, bf16[2,2,192,76...) custom-call(s32[2]{0:T(128)} %pad_add_fusion.6.info, ...), custom_call_target="tpu_custom_call", output_to_operand_aliasing={{0}: (10, {})} | custom-call | flops 13589544960 | bytes 31981568 | tf_op jit(solution)/shard_map/expert_backward/pallas_call | solution.py:732
  616.6 26.5 %expert_backward.9 = (bf16[8,960,1664]{2,1,0:T(8,128)(2,1)}, bf16[2,2,192,768]{3,2,1,0:T(8,128)(2,1)}, bf16[2,2,192,768]{3,2,1,0:T(8,128)(2,1)}, bf16[2,2,192,76...) custom-call(s32[2]{0:T(128)} %pad_add_fusion.5.info, ...), custom_call_target="tpu_custom_call", output_to_operand_aliasing={{0}: (10, {})} | custom-call | flops 13589544960 | bytes 31981568 | tf_op jit(solution)/shard_map/expert_backward/pallas_call | solution.py:732
  659.4 18.9 %expert_backward.10 = (bf16[8,960,1664]{2,1,0:T(8,128)(2,1)}, bf16[1,2,192,768]{3,2,1,0:T(8,128)(2,1)}, bf16[1,2,192,768]{3,2,1,0:T(8,128)(2,1)}, bf16[1,2,192,7...) custom-call(s32[2]{0:T(128)} %pad_add_fusion.4.info, ...), custom_call_target="tpu_custom_call", output_to_operand_aliasing={{0}: (8, {})} | custom-call | flops 7549747200 | bytes 24641536 | tf_op jit(solution)/shard_map/expert_backward/pallas_call | solution.py:732
  690.8 19.0 %expert_backward.11 = (bf16[8,960,1664]{2,1,0:T(8,128)(2,1)}, bf16[1,2,192,768]{3,2,1,0:T(8,128)(2,1)}, bf16[1,2,192,768]{3,2,1,0:T(8,128)(2,1)}, bf16[1,2,192,7...) custom-call(s32[2]{0:T(128)} %pad_add_fusion.1.info, ...), custom_call_target="tpu_custom_call", output_to_operand_aliasing={{0}: (8, {})} | custom-call | flops 7549747200 | bytes 24641536 | tf_op jit(solution)/shard_map/expert_backward/pallas_call | solution.py:732
  717.2 10.5 %combine.6.refs_0_ = bf16[4,384,1664]{2,1,0:T(8,128)(2,1)} custom-call(s32[8,6,384]{2,1,0:T(8,128)} %concatenate.135.slots, bf16[8,960,1664]{2,1,0:T(8,128)(2,1)} %get-tuple-element.109.values, f32[8,128]{1,0:T(8,128)} %join.49.rest_0_.refs_1_), custom_call_target="tpu_custom_call" | custom-call | flops 4907335680 | bytes 17891328 | tf_op jit(solution)/shard_map/combine/pallas_call | solution.py:1201
  728.3 10.5 %combine.7.refs_1_ = bf16[4,384,1664]{2,1,0:T(8,128)(2,1)} custom-call(s32[8,6,384]{2,1,0:T(8,128)} %concatenate.135.slots, bf16[8,960,1664]{2,1,0:T(8,128)(2,1)} %get-tuple-element.109.values, f32[8,128]{1,0:T(8,128)} %join.50.rest_0_.refs_1_.refs_6_), custom_call_target="tpu_custom_call" | custom-call | flops 4907335680 | bytes 17891328 | tf_op jit(solution)/shard_map/combine/pallas_call | solution.py:1201
  771.6 26.7 %collective-permute-done.41.refs_4_ = bf16[1,2,192,768]{3,2,1,0:T(8,128)(2,1)S(1)} collective-permute-done((bf16[1,2,192,768]{3,2,1,0:T(8,128)(2,1)}, bf16[1,2,192,768]{3,2,1,0:T(8,128)(2,1)S(1)}, u32[]{:S(2)}, u32[]{:S(2)}) %collective-permute-start.41) | collective-permute-done | bytes 589856 | tf_op jit(solution)/shard_map/ppermute | solution.py:406
  837.2 28.4 %all-to-all-done.12.refs_0_ = bf16[4,384,1664]{2,1,0:T(8,128)(2,1)} async-done(((bf16[4,384,1664]{2,1,0:T(8,128)(2,1)}), bf16[4,384,1664]{2,1,0:T(8,128)(2,1)}, u32[]{:S(2)}, u32[]{:S(2)}) %all-to-all-start.12) | async-done | bytes 5111840 | tf_op jit(solution)/shard_map/all_to_all | solution.py:371
  866.2 13.7 %middle_backward.1 = (f32[384,1536]{1,0:T(8,128)}, bf16[384,1536]{1,0:T(8,128)(2,1)}, bf16[4,4,48,1664]{3,2,1,0:T(8,128)(2,1)}, bf16[4,4,48,1664]{3,2,1,0:T(8,128)(2,1)}) custom-call(s32[1]{0:T(128)} %bitcast.2.c_ref, bf16[4,384,1664]{2,1,0:T(8,128)(2,1)} %tie.86.got, f32[384,128]{1,0:T(8,128)} %pad.9.gates, bf16[1536,4224]{1,0:T(8,128)(2,1)} %bitcast.308, ...), custom_call_target="tpu_custom_call" | custom-call | flops 2264924160 | bytes 23592960 | tf_op jit(solution)/shard_map/middle_backward/pallas_call | solution.py:834
  895.8 35.4 %attention_backward.1 = (bf16[4,4,48,2688]{3,2,1,0:T(8,128)(2,1)}, bf16[4,4,48,2688]{3,2,1,0:T(8,128)(2,1)}, f32[384,1536]{1,0:T(8,128)}) custom-call(s32[2]{0:T(128)S(1)} %pad_add_fusion.7.length, bf16[384,1536]{1,0:T(8,128)(2,1)S(1)} %copy-done.23, bf16[1536,4224]{1,0:T(8,128)(2,1)} %bitcast.309, bf16[384,1536]{1,0:T(8,128)(2,1)S(1)} %get-tuple-element.123.q, ...), custom_call_target="tpu_custom_call" | custom-call | flops 10116661248 | bytes 28704768 | tf_op jit(solution)/shard_map/attention_backward/pallas_call | solution.py:1139
  950.2 11.4 %collective-permute-done.56 = bf16[2,48,2688]{2,1,0:T(8,128)(2,1)S(1)} collective-permute-done((bf16[2,48,2688]{2,1,0:T(8,128)(2,1)S(1)}, bf16[2,48,2688]{2,1,0:T(8,128)(2,1)S(1)}, u32[]{:S(2)}, u32[]{:S(2)}) %collective-permute-start.56) | collective-permute-done | bytes 516128 | tf_op jit(solution)/shard_map/ppermute | solution.py:406
  962.7 10.8 %collective-permute-done.58 = bf16[2,48,2688]{2,1,0:T(8,128)(2,1)S(1)} collective-permute-done((bf16[2,48,2688]{2,1,0:T(8,128)(2,1)S(1)}, bf16[2,48,2688]{2,1,0:T(8,128)(2,1)S(1)}, u32[]{:S(2)}, u32[]{:S(2)}) %collective-permute-start.58) | collective-permute-done | bytes 516128 | tf_op jit(solution)/shard_map/ppermute | solution.py:406
  1010.9 27.3 %all-to-all-done.14 = bf16[4,48,4352]{2,1,0:T(8,128)(2,1)} async-done(((bf16[4,48,4352]{2,1,0:T(8,128)(2,1)}), bf16[4,48,4352]{2,1,0:T(8,128)(2,1)}, u32[]{:S(2)}, u32[]{:S(2)}) %all-to-all-start.14) | async-done | bytes 1671200 | tf_op jit(solution)/shard_map/all_to_all | solution.py:371
  (591 shorter events, 404.4 us)
Async XLA Ops:
  16.8 40.4 %all-to-all-start = ((bf16[4,48,4224]{2,1,0:T(8,128)(2,1)}), bf16[4,48,4224]{2,1,0:T(8,128)(2,1)S(1)}, u32[]{:S(2)}, u32[]{:S(2)}) async-start(bf16[4,48,4224]{2,1,0:T(8,128)(2,1)} %broadcast_in_dim.39), calls=%async_computation | async-start | bytes 3244032 | tf_op jit(solution)/shard_map/all_to_all | solution.py:371
  58.9 42.2 %all-to-all-start.2 = ((bf16[4,192,768]{2,1,0:T(8,128)(2,1)}), bf16[4,192,768]{2,1,0:T(8,128)(2,1)}, u32[]{:S(2)}, u32[]{:S(2)}) async-start(bf16[4,192,768]{2,1,0:T(8,128)(2,1)} %tie.45), calls=%async_computation.2 | async-start | bytes 2359296 | tf_op jit(solution)/shard_map/all_to_all | solution.py:371
  63.4 36.5 %collective-permute-start = (bf16[4,48,4224]{2,1,0:T(8,128)(2,1)S(1)}, bf16[4,48,4224]{2,1,0:T(8,128)(2,1)S(1)}, u32[]{:S(2)}, u32[]{:S(2)}) collective-permute-start(bf16[4,48,4224]{2,1,0:T(8,128)(2,1)S(1)} %copy-done.3), channel_id=1, source_target_pairs={{0,2},{1,3},{2,0},{3,1},{4,6},{5,7},{6,4},{7,5},{8,10},{9,11},{10,... | collective-permute-start | bytes 4866056 | tf_op jit(solution)/shard_map/ppermute | solution.py:406
  64.9 36.2 %collective-permute-start.1 = (bf16[4,48,4224]{2,1,0:T(8,128)(2,1)S(1)}, bf16[4,48,4224]{2,1,0:T(8,128)(2,1)}, u32[]{:S(2)}, u32[]{:S(2)}) collective-permute-start(bf16[4,48,4224]{2,1,0:T(8,128)(2,1)S(1)} %copy-done.3), channel_id=1, source_target_pairs={{0,4},{1,5},{2,6},{3,7},{4,0},{5,1},{6,2},{7,3},{8,12},{9,13},{10,... | collective-permute-start | bytes 4866056 | tf_op jit(solution)/shard_map/ppermute | solution.py:406
  66.5 34.7 %collective-permute-start.4 = (bf16[4,48,4224]{2,1,0:T(8,128)(2,1)S(1)}, bf16[4,48,4224]{2,1,0:T(8,128)(2,1)}, u32[]{:S(2)}, u32[]{:S(2)}) collective-permute-start(bf16[4,48,4224]{2,1,0:T(8,128)(2,1)S(1)} %copy-done.3), channel_id=1, source_target_pairs={{0,1},{1,0},{2,3},{3,2},{4,5},{5,4},{6,7},{7,6},{8,9},{9,8},{10,11... | collective-permute-start | bytes 4866056 | tf_op jit(solution)/shard_map/ppermute | solution.py:406
  133.8 32.8 %all-to-all-start.4 = ((bf16[4,192,768]{2,1,0:T(8,128)(2,1)}), bf16[4,192,768]{2,1,0:T(8,128)(2,1)}, u32[]{:S(2)}, u32[]{:S(2)}) async-start(bf16[4,192,768]{2,1,0:T(8,128)(2,1)} %tie.47), calls=%async_computation.4 | async-start | bytes 2359296 | tf_op jit(solution)/shard_map/all_to_all | solution.py:371
  167.2 34.1 %collective-permute-start.12 = (bf16[4,192,768]{2,1,0:T(8,128)(2,1)}, bf16[4,192,768]{2,1,0:T(8,128)(2,1)}, u32[]{:S(2)}, u32[]{:S(2)}) collective-permute-start(bf16[4,192,768]{2,1,0:T(8,128)(2,1)} %tie.50.rest_2_), channel_id=1, source_target_pairs={{0,2},{1,3},{2,0},{3,1},{4,6},{5,7},{6,4},{7,5},{8,10},{9,11},{10,... | collective-permute-start | bytes 3538952 | tf_op jit(solution)/shard_map/ppermute | solution.py:406
  168.3 33.0 %collective-permute-start.13 = (bf16[4,192,768]{2,1,0:T(8,128)(2,1)}, bf16[4,192,768]{2,1,0:T(8,128)(2,1)}, u32[]{:S(2)}, u32[]{:S(2)}) collective-permute-start(bf16[4,192,768]{2,1,0:T(8,128)(2,1)} %tie.50.rest_2_), channel_id=1, source_target_pairs={{0,4},{1,5},{2,6},{3,7},{4,0},{5,1},{6,2},{7,3},{8,12},{9,13},{10,... | collective-permute-start | bytes 3538952 | tf_op jit(solution)/shard_map/ppermute | solution.py:406
  169.8 32.1 %all-to-all-start.5 = ((bf16[4,192,768]{2,1,0:T(8,128)(2,1)}), bf16[4,192,768]{2,1,0:T(8,128)(2,1)}, u32[]{:S(2)}, u32[]{:S(2)}) async-start(bf16[4,192,768]{2,1,0:T(8,128)(2,1)} %tie.49), calls=%async_computation.5 | async-start | bytes 2359296 | tf_op jit(solution)/shard_map/all_to_all | solution.py:371
  206.3 115.2 %all-to-all-start.6 = ((bf16[4,384,1536]{2,1,0:T(8,128)(2,1)}), bf16[4,384,1536]{2,1,0:T(8,128)(2,1)}, u32[]{:S(2)}, u32[]{:S(2)}) async-start(bf16[4,384,1536]{2,1,0:T(8,128)(2,1)} %broadcast_in_dim.44), calls=%async_computation.6 | async-start | bytes 9437184 | tf_op jit(solution)/shard_map/all_to_all | solution.py:371
  322.3 34.5 %collective-permute-start.22 = (bf16[4,384,1536]{2,1,0:T(8,128)(2,1)}, bf16[4,384,1536]{2,1,0:T(8,128)(2,1)}, u32[]{:S(2)}, u32[]{:S(2)}) collective-permute-start(bf16[4,384,1536]{2,1,0:T(8,128)(2,1)} %tie.58.refs_1_), channel_id=1, source_target_pairs={{0,1},{1,0},{2,3},{3,2},{4,5},{5,4},{6,7},{7,6},{8,9},{9,8},{10,11... | collective-permute-start | bytes 14155784 | tf_op jit(solution)/shard_map/ppermute | solution.py:406
  362.2 117.9 %all-to-all-start.8 = ((bf16[4,384,1536]{2,1,0:T(8,128)(2,1)}), bf16[4,384,1536]{2,1,0:T(8,128)(2,1)}, u32[]{:S(2)}, u32[]{:S(2)}) async-start(bf16[4,384,1536]{2,1,0:T(8,128)(2,1)} %broadcast_in_dim.47), calls=%async_computation.8 | async-start | bytes 9437184 | tf_op jit(solution)/shard_map/all_to_all | solution.py:371
  372.0 44.4 %collective-permute-start.23 = (bf16[4,192,768]{2,1,0:T(8,128)(2,1)}, bf16[4,192,768]{2,1,0:T(8,128)(2,1)}, u32[]{:S(2)}, u32[]{:S(2)}) collective-permute-start(bf16[4,192,768]{2,1,0:T(8,128)(2,1)} %tie.60.rest_0_), channel_id=1, source_target_pairs={{0,4},{1,5},{2,6},{3,7},{4,0},{5,1},{6,2},{7,3},{8,12},{9,13},{10,... | collective-permute-start | bytes 3538952 | tf_op jit(solution)/shard_map/ppermute | solution.py:406
  372.0 44.4 %collective-permute-start.24 = (bf16[4,192,768]{2,1,0:T(8,128)(2,1)}, bf16[4,192,768]{2,1,0:T(8,128)(2,1)S(1)}, u32[]{:S(2)}, u32[]{:S(2)}) collective-permute-start(bf16[4,192,768]{2,1,0:T(8,128)(2,1)} %tie.60.rest_0_), channel_id=1, source_target_pairs={{0,2},{1,3},{2,0},{3,1},{4,6},{5,7},{6,4},{7,5},{8,10},{9,11},{10,... | collective-permute-start | bytes 3538952 | tf_op jit(solution)/shard_map/ppermute | solution.py:406
  418.1 33.9 %collective-permute-start.25 = (bf16[4,192,768]{2,1,0:T(8,128)(2,1)}, bf16[4,192,768]{2,1,0:T(8,128)(2,1)S(1)}, u32[]{:S(2)}, u32[]{:S(2)}) collective-permute-start(bf16[4,192,768]{2,1,0:T(8,128)(2,1)} %tie.61.rest_1_), channel_id=1, source_target_pairs={{0,2},{1,3},{2,0},{3,1},{4,6},{5,7},{6,4},{7,5},{8,10},{9,11},{10,... | collective-permute-start | bytes 3538952 | tf_op jit(solution)/shard_map/ppermute | solution.py:406
  517.6 131.3 %all-to-all-start.9 = ((bf16[4,384,1536]{2,1,0:T(8,128)(2,1)}), bf16[4,384,1536]{2,1,0:T(8,128)(2,1)}, u32[]{:S(2)}, u32[]{:S(2)}) async-start(bf16[4,384,1536]{2,1,0:T(8,128)(2,1)} %tie.65), calls=%async_computation.9 | async-start | bytes 9437184 | tf_op jit(solution)/shard_map/all_to_all | solution.py:371
  580.1 33.0 %collective-permute-start.30 = (bf16[2,2,192,768]{3,2,1,0:T(8,128)(2,1)}, bf16[2,2,192,768]{3,2,1,0:T(8,128)(2,1)}, u32[]{:S(2)}, u32[]{:S(2)}) collective-permute-start(bf16[2,2,192,768]{3,2,1,0:T(8,128)(2,1)} %tie.68), channel_id=1, source_target_pairs={{0,2},{1,3},{2,0},{3,1},{4,6},{5,7},{6,4},{7,5},{8,10},{9,11},{10,... | collective-permute-start | bytes 3538952 | tf_op jit(solution)/shard_map/ppermute | solution.py:406
  649.5 32.9 %all-to-all-start.10 = ((bf16[4,192,768]{2,1,0:T(8,128)(2,1)}), bf16[4,192,768]{2,1,0:T(8,128)(2,1)S(1)}, u32[]{:S(2)}, u32[]{:S(2)}) async-start(bf16[4,192,768]{2,1,0:T(8,128)(2,1)} %tie.74), calls=%async_computation.10 | async-start | bytes 2359296 | tf_op jit(solution)/shard_map/all_to_all | solution.py:371
  746.4 119.2 %all-to-all-start.12 = ((bf16[4,384,1664]{2,1,0:T(8,128)(2,1)}), bf16[4,384,1664]{2,1,0:T(8,128)(2,1)}, u32[]{:S(2)}, u32[]{:S(2)}) async-start(bf16[4,384,1664]{2,1,0:T(8,128)(2,1)} %add_convert_fusion), calls=%async_computation.12 | async-start | bytes 10223616 | tf_op jit(solution)/shard_map/all_to_all | solution.py:371
  757.1 41.9 %collective-permute-start.40 = (bf16[2,2,192,768]{3,2,1,0:T(8,128)(2,1)}, bf16[2,2,192,768]{3,2,1,0:T(8,128)(2,1)}, u32[]{:S(2)}, u32[]{:S(2)}) collective-permute-start(bf16[2,2,192,768]{3,2,1,0:T(8,128)(2,1)} %tie.79), channel_id=1, source_target_pairs={{0,2},{1,3},{2,0},{3,1},{4,6},{5,7},{6,4},{7,5},{8,10},{9,11},{10,... | collective-permute-start | bytes 3538952 | tf_op jit(solution)/shard_map/ppermute | solution.py:406
  758.0 41.0 %collective-permute-start.39 = (bf16[2,2,192,768]{3,2,1,0:T(8,128)(2,1)}, bf16[2,2,192,768]{3,2,1,0:T(8,128)(2,1)}, u32[]{:S(2)}, u32[]{:S(2)}) collective-permute-start(bf16[2,2,192,768]{3,2,1,0:T(8,128)(2,1)} %tie.78), channel_id=1, source_target_pairs={{0,4},{1,5},{2,6},{3,7},{4,0},{5,1},{6,2},{7,3},{8,12},{9,13},{10,... | collective-permute-start | bytes 3538952 | tf_op jit(solution)/shard_map/ppermute | solution.py:406
  761.9 36.4 %collective-permute-start.41 = (bf16[1,2,192,768]{3,2,1,0:T(8,128)(2,1)}, bf16[1,2,192,768]{3,2,1,0:T(8,128)(2,1)S(1)}, u32[]{:S(2)}, u32[]{:S(2)}) collective-permute-start(bf16[1,2,192,768]{3,2,1,0:T(8,128)(2,1)} %tie.80), channel_id=1, source_target_pairs={{0,2},{1,3},{2,0},{3,1},{4,6},{5,7},{6,4},{7,5},{8,10},{9,11},{10,... | collective-permute-start | bytes 1769480 | tf_op jit(solution)/shard_map/ppermute | solution.py:406
  762.8 36.1 %collective-permute-start.42 = (bf16[1,2,192,768]{3,2,1,0:T(8,128)(2,1)}, bf16[1,2,192,768]{3,2,1,0:T(8,128)(2,1)S(1)}, u32[]{:S(2)}, u32[]{:S(2)}) collective-permute-start(bf16[1,2,192,768]{3,2,1,0:T(8,128)(2,1)} %tie.81), channel_id=1, source_target_pairs={{0,4},{1,5},{2,6},{3,7},{4,0},{5,1},{6,2},{7,3},{8,12},{9,13},{10,... | collective-permute-start | bytes 1769480 | tf_op jit(solution)/shard_map/ppermute | solution.py:406
  880.1 51.1 %all-to-all-start.13 = ((bf16[4,192,768]{2,1,0:T(8,128)(2,1)}), bf16[4,192,768]{2,1,0:T(8,128)(2,1)S(1)}, u32[]{:S(2)}, u32[]{:S(2)}) async-start(bf16[4,192,768]{2,1,0:T(8,128)(2,1)} %tie.87), calls=%async_computation.13 | async-start | bytes 2359296 | tf_op jit(solution)/shard_map/all_to_all | solution.py:371
  890.1 41.1 %collective-permute-start.49 = (bf16[2,48,1664]{2,1,0:T(8,128)(2,1)}, bf16[2,48,1664]{2,1,0:T(8,128)(2,1)}, u32[]{:S(2)}, u32[]{:S(2)}) collective-permute-start(bf16[2,48,1664]{2,1,0:T(8,128)(2,1)} %get-tuple-element.275), channel_id=1, source_target_pairs={{0,2},{1,3},{2,0},{3,1},{4,6},{5,7},{6,4},{7,5},{8,10},{9,11},{10,... | collective-permute-start | bytes 958472 | tf_op jit(solution)/shard_map/ppermute | solution.py:406
  891.1 40.1 %collective-permute-start.51 = (bf16[2,48,1664]{2,1,0:T(8,128)(2,1)}, bf16[2,48,1664]{2,1,0:T(8,128)(2,1)}, u32[]{:S(2)}, u32[]{:S(2)}) collective-permute-start(bf16[2,48,1664]{2,1,0:T(8,128)(2,1)} %get-tuple-element.274), channel_id=1, source_target_pairs={{0,4},{1,5},{2,6},{3,7},{4,0},{5,1},{6,2},{7,3},{8,12},{9,13},{10,... | collective-permute-start | bytes 958472 | tf_op jit(solution)/shard_map/ppermute | solution.py:406
  892.9 38.3 %collective-permute-start.48 = (bf16[2,48,1664]{2,1,0:T(8,128)(2,1)}, bf16[2,48,1664]{2,1,0:T(8,128)(2,1)}, u32[]{:S(2)}, u32[]{:S(2)}) collective-permute-start(bf16[2,48,1664]{2,1,0:T(8,128)(2,1)} %fusion.59), channel_id=1, source_target_pairs={{0,2},{1,3},{2,0},{3,1},{4,6},{5,7},{6,4},{7,5},{8,10},{9,11},{10,... | collective-permute-start | bytes 958472 | tf_op jit(solution)/shard_map/ppermute | solution.py:406
  894.6 36.6 %collective-permute-start.53 = (bf16[2,48,1664]{2,1,0:T(8,128)(2,1)}, bf16[2,48,1664]{2,1,0:T(8,128)(2,1)}, u32[]{:S(2)}, u32[]{:S(2)}) collective-permute-start(bf16[2,48,1664]{2,1,0:T(8,128)(2,1)} %fusion.60), channel_id=1, source_target_pairs={{0,4},{1,5},{2,6},{3,7},{4,0},{5,1},{6,2},{7,3},{8,12},{9,13},{10,... | collective-permute-start | bytes 958472 | tf_op jit(solution)/shard_map/ppermute | solution.py:406
  935.2 39.4 %collective-permute-start.50 = (bf16[2,48,1664]{2,1,0:T(8,128)(2,1)S(1)}, bf16[2,48,1664]{2,1,0:T(8,128)(2,1)S(1)}, u32[]{:S(2)}, u32[]{:S(2)}) collective-permute-start(bf16[2,48,1664]{2,1,0:T(8,128)(2,1)S(1)} %fusion.37), channel_id=1, source_target_pairs={{0,4},{1,5},{2,6},{3,7},{4,0},{5,1},{6,2},{7,3},{8,12},{9,13},{10,... | collective-permute-start | bytes 958472 | tf_op jit(solution)/shard_map/ppermute | solution.py:406
  937.2 38.5 %collective-permute-start.52 = (bf16[2,48,1664]{2,1,0:T(8,128)(2,1)S(1)}, bf16[2,48,1664]{2,1,0:T(8,128)(2,1)}, u32[]{:S(2)}, u32[]{:S(2)}) collective-permute-start(bf16[2,48,1664]{2,1,0:T(8,128)(2,1)S(1)} %fusion.32), channel_id=1, source_target_pairs={{0,2},{1,3},{2,0},{3,1},{4,6},{5,7},{6,4},{7,5},{8,10},{9,11},{10,... | collective-permute-start | bytes 958472 | tf_op jit(solution)/shard_map/ppermute | solution.py:406
  938.4 56.8 %all-to-all-start.15 = ((bf16[4,384,768]{2,1,0:T(8,128)(2,1)}), bf16[4,384,768]{2,1,0:T(8,128)(2,1)S(1)}, u32[]{:S(2)}, u32[]{:S(2)}) async-start(bf16[4,384,768]{2,1,0:T(8,128)(2,1)} %tie.89), calls=%async_computation.15 | async-start | bytes 4718592 | tf_op jit(solution)/shard_map/all_to_all | solution.py:371
  995.2 43.0 %all-to-all-start.14 = ((bf16[4,48,4352]{2,1,0:T(8,128)(2,1)}), bf16[4,48,4352]{2,1,0:T(8,128)(2,1)}, u32[]{:S(2)}, u32[]{:S(2)}) async-start(bf16[4,48,4352]{2,1,0:T(8,128)(2,1)} %maximum_maximum_fusion.1.refs_4_), calls=%async_computation.14 | async-start | bytes 3342336 | tf_op jit(solution)/shard_map/all_to_all | solution.py:371
  (170 other events, 1406.4 us)
